TPU v7x, 32 devices: a whole 2x2x4 slice. The times are simulated.
32 devices in a mesh: seq: 2 (over x), pipe: 4 (over y, core), dp: 4 (over z).
Axes of the slice: x: 2, y: 2, z: 4, core: 2. Of those that a mesh axis runs over, the one named last changes fastest.
Arguments:
- segment_input: bfloat16 [4, 512, 3072], P('pipe', ('dp', 'seq')), parts along dimension 1
- output_grad: bfloat16 [4, 512, 3072], P('pipe', ('dp', 'seq')), parts along dimension 1, may hold values from -6 to 6
- qkv_weight: bfloat16 [4, 3072, 16, 384], P('pipe', None, 'seq')
- out_weight: bfloat16 [4, 2048, 3072], P('pipe', 'seq'), may hold values from -0.125 to 0.125
- query_gain: float32 [4, 128], P('pipe')
- key_gain: float32 [4, 128], P('pipe')
- gate_scale: float32 [4, 3072], P('pipe'), may hold values from -4 to 4
- neighbours: int32 [8, 27], P('dp'), parts along dimension 0, may hold values from -1 to 1
- tile_slot: int32 [8], P('dp'), parts along dimension 0, may hold values from 0 to 1, as said below
Outputs:
- segment_output: bfloat16 [4, 512, 3072], P('pipe', ('dp', 'seq')), parts along dimension 1
- input_grad: bfloat16 [4, 512, 3072], P('pipe', ('dp', 'seq')), parts along dimension 1
- gate_grad: float32 [16, 3072], P(('dp', 'pipe'), 'seq'), parts along dimension 0
There are 4 independent parts, one for each index of `dp`. A program takes and returns all parts, laid end to end along the dimension named above; an argument that names none is the same for every part. Nothing has to cross between parts.
Inputs may be any that keep to these rules, and one draw needn't show every extreme that they name: `tile_slot`: A permutation of 0 to 1.
All inputs are finite; a program needn't handle non-finite values.
Results may differ from a plain program's by a relative error of at most 0.02.
Values may be sent and summed in bfloat16 or wider, within the bound.
No kernel may reach another device: no remote copies, remote signals or barrier semaphores. Data moves between devices by JAX's collectives and lax.ppermute only.
A program may use at most 128 MiB of HBM per device.

v0:
```python
import functools
import math

import jax
import jax.numpy as jnp
from jax import lax
from jax.experimental import pallas as pl
from jax.experimental.pallas import tpu as pltpu
from jax.sharding import PartitionSpec as P

TILE = 64
EPSILON = 1e-06
F32 = jnp.float32
BF16 = jnp.bfloat16
VMEM_LIMIT = 44 * 1024 * 1024


def passed_along(block, axis, distance):
    devices = range(lax.axis_size(axis))
    route = [((i - distance) % len(devices), i) for i in devices]
    return lax.ppermute(block, axis, route)


def slot_lists(neighbours, tile_slot):
    tile_count = tile_slot.shape[0]
    numbering = jnp.arange(tile_count, dtype=jnp.int32)
    placed = (tile_slot[:, None] == numbering[None, :]).astype(jnp.int32)
    tile_of_slot = jnp.sum(placed * numbering[:, None], axis=0)
    chosen = (tile_of_slot[:, None] == numbering[None, :]).astype(jnp.int32)
    listed_tiles = jnp.sum(chosen[:, :, None] * neighbours[None, :, :], axis=1)
    key_valid = listed_tiles >= 0
    safe_tiles = jnp.maximum(listed_tiles, 0)
    matches = (safe_tiles[:, :, None] == numbering[None, None, :]).astype(jnp.int32)
    key_slots = jnp.sum(matches * tile_slot[None, None, :], axis=2)
    return (key_slots, key_valid)


def block_tiles(tile_count):
    return math.gcd(tile_count, max(1, 512 // TILE))


def unit_norm(values):
    spread = jnp.sqrt(jnp.mean(values * values, axis=-1, keepdims=True) + EPSILON)
    return (values / spread, spread)


def probabilities(query_block, key_rows, block_valid):
    scores = jnp.einsum(
        "aihd,ajhd->ahij", query_block, key_rows, preferred_element_type=jnp.float32
    ) * (1.0 / math.sqrt(query_block.shape[-1]))
    key_mask = jnp.repeat(block_valid, TILE, axis=1)
    scores = jnp.where(key_mask[:, None, None, :], scores, -jnp.inf)
    row_max = jnp.max(scores, axis=-1, keepdims=True)
    weights = jnp.exp(scores - row_max)
    return (weights / jnp.sum(weights, axis=-1, keepdims=True)).astype(jnp.bfloat16)


def gathered(tiles_array, block_slots):
    picked = tiles_array[block_slots]
    return picked.reshape(block_slots.shape[0], -1, tiles_array.shape[2], tiles_array.shape[3])


def attend_both(query_tiles, key_tiles, value_tiles, grad_tiles, key_slots, key_valid):
    tile_count = query_tiles.shape[0]
    span = block_tiles(tile_count)
    scale_factor = 1.0 / math.sqrt(query_tiles.shape[-1])
    empty_grad = jnp.zeros(query_tiles.shape, jnp.float32)

    def per_block(accumulators, block_index):
        key_total, value_total = accumulators
        first_tile = block_index * span
        query_block = lax.dynamic_slice_in_dim(query_tiles, first_tile, span, 0)
        grad_block = lax.dynamic_slice_in_dim(grad_tiles, first_tile, span, 0)
        block_slots = lax.dynamic_slice_in_dim(key_slots, first_tile, span, 0)
        block_valid = lax.dynamic_slice_in_dim(key_valid, first_tile, span, 0)
        key_rows = gathered(key_tiles, block_slots)
        value_rows = gathered(value_tiles, block_slots)
        weights = probabilities(query_block, key_rows, block_valid)
        attended = jnp.einsum(
            "ahij,ajhd->aihd", weights, value_rows, preferred_element_type=jnp.float32
        )
        value_part = jnp.einsum(
            "ahij,aihd->ajhd", weights, grad_block, preferred_element_type=jnp.float32
        )
        prob_grad = jnp.einsum(
            "aihd,ajhd->ahij", grad_block, value_rows, preferred_element_type=jnp.float32
        )
        weights_wide = weights.astype(jnp.float32)
        row_delta = jnp.sum(weights_wide * prob_grad, axis=-1, keepdims=True)
        score_grad = (weights_wide * (prob_grad - row_delta) * scale_factor).astype(jnp.bfloat16)
        query_part = jnp.einsum(
            "ahij,ajhd->aihd", score_grad, key_rows, preferred_element_type=jnp.float32
        )
        key_part = jnp.einsum(
            "ahij,aihd->ajhd", score_grad, query_block, preferred_element_type=jnp.float32
        )
        block_shape = (span, block_slots.shape[1]) + query_tiles.shape[1:]
        key_total = key_total.at[block_slots].add(key_part.reshape(block_shape))
        value_total = value_total.at[block_slots].add(value_part.reshape(block_shape))
        return ((key_total, value_total), (attended, query_part))

    totals, parts = lax.scan(
        per_block, (empty_grad, empty_grad), jnp.arange(tile_count // span, dtype=jnp.int32)
    )
    flat_shape = (-1,) + query_tiles.shape[2:]
    return (
        parts[0].reshape(flat_shape),
        parts[1].reshape(flat_shape),
        totals[0].reshape(flat_shape),
        totals[1].reshape(flat_shape),
    )


def general_body(
    segment_input,
    output_grad,
    qkv_weight,
    out_weight,
    query_gain,
    key_gain,
    gate_scale,
    neighbours,
    tile_slot,
):
    key_slots, key_valid = slot_lists(neighbours, tile_slot)
    stream = segment_input[0]
    upstream = output_grad[0]
    model_width = stream.shape[1]
    head_dim = query_gain.shape[1]
    local_heads = qkv_weight.shape[2]
    local_width = local_heads * head_dim
    proj_weight = qkv_weight[0].reshape(model_width, local_heads * 3 * head_dim)
    out_local = out_weight[0]
    gate_row = gate_scale[0]
    query_weights = query_gain[0]
    key_weights = key_gain[0]
    projected = jnp.dot(
        lax.all_gather(stream, "seq", axis=0, tiled=True),
        proj_weight,
        preferred_element_type=jnp.float32,
    )
    all_tokens = projected.shape[0]
    projected = projected.reshape(all_tokens, local_heads, 3, head_dim)
    query_unit, query_spread = unit_norm(projected[:, :, 0])
    key_unit, key_spread = unit_norm(projected[:, :, 1])
    queries = (query_unit * query_weights).astype(jnp.bfloat16)
    keys_normed = (key_unit * key_weights).astype(jnp.bfloat16)
    value_rows = projected[:, :, 2].astype(jnp.bfloat16)
    scaled = (upstream.astype(jnp.float32) * gate_row).astype(jnp.bfloat16)
    attended_grad = jnp.einsum(
        "td,cd->tc",
        lax.all_gather(scaled, "seq", axis=0, tiled=True),
        out_local,
        preferred_element_type=jnp.float32,
    ).astype(jnp.bfloat16)

    def as_tiles(values):
        return values.reshape(-1, TILE, local_heads, head_dim)

    attended, query_grad, key_grad, value_grad = attend_both(
        as_tiles(queries),
        as_tiles(keys_normed),
        as_tiles(value_rows),
        as_tiles(attended_grad),
        key_slots,
        key_valid,
    )
    attended_low = attended.astype(jnp.bfloat16).reshape(all_tokens, local_width)
    rows = attended_low
    attention_out = lax.psum_scatter(
        jnp.dot(rows, out_local, preferred_element_type=jnp.float32),
        "seq",
        scatter_dimension=0,
        tiled=True,
    )
    section_out = (stream.astype(jnp.float32) + gate_row * attention_out).astype(jnp.bfloat16)
    segment_output = passed_along(section_out, "pipe", 1)
    gate_local = lax.psum_scatter(
        jnp.sum(upstream.astype(jnp.float32) * attention_out, axis=0),
        "seq",
        scatter_dimension=0,
        tiled=True,
    )
    query_scaled = query_grad * query_weights
    query_part_grad = (
        query_scaled - query_unit * jnp.mean(query_scaled * query_unit, axis=-1, keepdims=True)
    ) / query_spread
    key_scaled = key_grad * key_weights
    key_part_grad = (
        key_scaled - key_unit * jnp.mean(key_scaled * key_unit, axis=-1, keepdims=True)
    ) / key_spread
    projected_grad = (
        jnp.stack([query_part_grad, key_part_grad, value_grad], axis=2)
        .astype(jnp.bfloat16)
        .reshape(all_tokens, local_heads * 3 * head_dim)
    )
    rows = projected_grad
    stream_grad = lax.psum_scatter(
        jnp.einsum("tc,dc->td", rows, proj_weight, preferred_element_type=jnp.float32).astype(
            jnp.bfloat16
        ),
        "seq",
        scatter_dimension=0,
        tiled=True,
    ).astype(jnp.float32)
    token_grad = (upstream.astype(jnp.float32) + stream_grad).astype(jnp.bfloat16)
    input_grad = passed_along(token_grad, "pipe", -1)
    return (segment_output[None], input_grad[None], gate_local[None])


def dot_nn(a, b):
    return lax.dot_general(a, b, (((1,), (0,)), ((), ())), preferred_element_type=F32)


def dot_nt(a, b):
    return lax.dot_general(a, b, (((1,), (1,)), ((), ())), preferred_element_type=F32)


def dot_tn(a, b):
    return lax.dot_general(a, b, (((0,), (0,)), ((), ())), preferred_element_type=F32)


def params(limit=VMEM_LIMIT):
    return pltpu.CompilerParams(vmem_limit_bytes=limit)


def regroup_kernel(weight_ref, out_ref):
    heads = weight_ref.shape[1]
    width = weight_ref.shape[2]
    by_head = jnp.swapaxes(weight_ref[...], 0, 1)
    for head in range(heads):
        left = (head % 2) * width
        out_ref[head // 2, :, left : left + width] = by_head[head]


def regroup(weight, rows):
    depth, heads, width = weight.shape
    pairs = heads // 2
    return pl.pallas_call(
        regroup_kernel,
        grid=(depth // rows,),
        out_shape=jax.ShapeDtypeStruct((pairs, depth, 2 * width), weight.dtype),
        in_specs=[pl.BlockSpec((rows, heads, width), lambda i: (i, 0, 0))],
        out_specs=pl.BlockSpec((pairs, rows, 2 * width), lambda i: (0, i, 0)),
        compiler_params=params(),
        cost_estimate=pl.CostEstimate(
            flops=0, bytes_accessed=4 * depth * heads * width, transcendentals=0
        ),
        name="regroup",
    )(weight)


def listed_slots(neighbours_ref, tile_slot_ref):
    tiles, places = neighbours_ref.shape
    one, zero = jnp.int32(1), jnp.int32(0)
    allowed = [[zero] * tiles for _ in range(tiles)]
    for t in range(tiles):
        for u in range(tiles):
            listed = zero
            for k in range(places):
                listed = jnp.where(neighbours_ref[t, k] == u, one, listed)
            for r in range(tiles):
                for c in range(tiles):
                    here = (tile_slot_ref[t] == r) & (tile_slot_ref[u] == c)
                    allowed[r][c] = jnp.where(here, listed, allowed[r][c])
    return allowed


def forward_kernel(
    neighbours_ref,
    tile_slot_ref,
    own_ref,
    other_ref,
    weight_ref,
    out_weight_ref,
    query_gain_ref,
    key_gain_ref,
    gate_ref,
    projected_ref,
    probs_ref,
    attention_ref,
    kept_ref,
    sent_ref,
    tokens_ref,
    bias_ref,
):
    step = pl.program_id(0)
    local = own_ref.shape[0]
    tokens = 2 * local
    width = query_gain_ref.shape[1]
    heads = probs_ref.shape[0]

    @pl.when(step == 0)
    def _():
        tokens_ref[:local, :] = own_ref[...]
        tokens_ref[local:, :] = other_ref[...]
        allowed = listed_slots(neighbours_ref, tile_slot_ref)
        mine = lax.axis_index("seq")
        row_half = lax.broadcasted_iota(jnp.int32, (tokens, tokens), 0) // local
        column_half = lax.broadcasted_iota(jnp.int32, (tokens, tokens), 1) // local
        row_slot = jnp.where(row_half == 0, mine, 1 - mine)
        column_slot = jnp.where(column_half == 0, mine, 1 - mine)
        table = jnp.zeros((tokens, tokens), jnp.int32)
        for r in range(2):
            for c in range(2):
                table = jnp.where((row_slot == r) & (column_slot == c), allowed[r][c], table)
        bias_ref[...] = jnp.where(table > 0, 0.0, -jnp.inf).astype(F32)

    projected = dot_nn(tokens_ref[...], weight_ref[0])
    projected_ref[0] = projected
    scale_factor = 1.0 / math.sqrt(width)
    bias = bias_ref[...]
    attended = []
    for head in range(heads):
        left = head * 3 * width
        query = projected[:, left : left + width]
        key = projected[:, left + width : left + 2 * width]
        value = projected[:, left + 2 * width : left + 3 * width].astype(BF16)
        query_inverse = lax.rsqrt(jnp.mean(query * query, axis=-1, keepdims=True) + EPSILON)
        key_inverse = lax.rsqrt(jnp.mean(key * key, axis=-1, keepdims=True) + EPSILON)
        queries = (query * query_inverse * query_gain_ref[...]).astype(BF16)
        keys = (key * key_inverse * key_gain_ref[...]).astype(BF16)
        scores = dot_nt(queries, keys) * scale_factor + bias
        row_max = jnp.max(scores, axis=-1, keepdims=True)
        weights = jnp.exp(scores - row_max)
        probs = (weights / jnp.sum(weights, axis=-1, keepdims=True)).astype(BF16)
        probs_ref[head] = probs
        attended.append(dot_nn(probs, value).astype(BF16))
    share = dot_nn(jnp.concatenate(attended, axis=1), out_weight_ref[...])

    @pl.when(step == 0)
    def _():
        attention_ref[...] = share

    @pl.when(step > 0)
    def _():
        attention_ref[...] += share

    @pl.when(step == pl.num_programs(0) - 1)
    def _():
        gate = gate_ref[...]
        kept_ref[...] = (own_ref[...].astype(F32) + gate * attention_ref[:local, :]).astype(BF16)
        sent_ref[...] = (gate * attention_ref[local:, :]).astype(BF16)


def forward(neighbours, tile_slot, own, other, weight, out_weight, query_gain, key_gain, gate):
    local, model = own.shape
    pairs, _, wide = weight.shape
    head_dim = query_gain.shape[1]
    tokens = 2 * local
    whole = lambda i: (0, 0)
    smem = pl.BlockSpec(memory_space=pltpu.SMEM)
    return pl.pallas_call(
        forward_kernel,
        grid=(pairs,),
        out_shape=(
            jax.ShapeDtypeStruct((pairs, tokens, wide), F32),
            jax.ShapeDtypeStruct((2 * pairs, tokens, tokens), BF16),
            jax.ShapeDtypeStruct((tokens, model), F32),
            jax.ShapeDtypeStruct((local, model), BF16),
            jax.ShapeDtypeStruct((local, model), BF16),
        ),
        in_specs=[
            smem,
            smem,
            pl.BlockSpec((local, model), whole),
            pl.BlockSpec((local, model), whole),
            pl.BlockSpec((1, model, wide), lambda i: (i, 0, 0)),
            pl.BlockSpec((2 * head_dim, model), lambda i: (i, 0)),
            pl.BlockSpec((1, head_dim), whole),
            pl.BlockSpec((1, head_dim), whole),
            pl.BlockSpec((1, model), whole),
        ],
        out_specs=(
            pl.BlockSpec((1, tokens, wide), lambda i: (i, 0, 0)),
            pl.BlockSpec((2, tokens, tokens), lambda i: (i, 0, 0)),
            pl.BlockSpec((tokens, model), whole),
            pl.BlockSpec((local, model), whole),
            pl.BlockSpec((local, model), whole),
        ),
        scratch_shapes=[pltpu.VMEM((tokens, model), BF16), pltpu.VMEM((tokens, tokens), F32)],
        compiler_params=params(),
        cost_estimate=pl.CostEstimate(
            flops=2 * tokens * model * pairs * (wide + 2 * head_dim),
            bytes_accessed=2 * model * pairs * (wide + 2 * head_dim),
            transcendentals=0,
        ),
        name="attention_forward",
    )(neighbours, tile_slot, own, other, weight, out_weight, query_gain, key_gain, gate)


def backward_kernel(
    own_ref,
    other_ref,
    out_weight_ref,
    projected_ref,
    probs_ref,
    attention_ref,
    query_gain_ref,
    key_gain_ref,
    gate_ref,
    grad_ref,
    gate_grad_ref,
    scaled_ref,
):
    step = pl.program_id(0)
    local = own_ref.shape[0]
    width = query_gain_ref.shape[1]
    heads = probs_ref.shape[0]
    columns = attention_ref.shape[1]

    @pl.when(step == 0)
    def _():
        gate = gate_ref[...]
        scaled_ref[:local, :] = (own_ref[...].astype(F32) * gate).astype(BF16)
        scaled_ref[local:, :] = (other_ref[...].astype(F32) * gate).astype(BF16)

    part = pl.ds(pl.multiple_of(step * columns, columns), columns)
    gate_grad_ref[...] = jnp.sum(
        own_ref[:, part].astype(F32) * attention_ref[:local, :], axis=0, keepdims=True
    ) + jnp.sum(other_ref[:, part].astype(F32) * attention_ref[local:, :], axis=0, keepdims=True)

    attended_grad = dot_nt(scaled_ref[...], out_weight_ref[...]).astype(BF16)
    scale_factor = 1.0 / math.sqrt(width)
    for head in range(heads):
        left = head * 3 * width
        query = projected_ref[0, :, left : left + width]
        key = projected_ref[0, :, left + width : left + 2 * width]
        value = projected_ref[0, :, left + 2 * width : left + 3 * width].astype(BF16)
        query_inverse = lax.rsqrt(jnp.mean(query * query, axis=-1, keepdims=True) + EPSILON)
        key_inverse = lax.rsqrt(jnp.mean(key * key, axis=-1, keepdims=True) + EPSILON)
        query_unit = query * query_inverse
        key_unit = key * key_inverse
        queries = (query_unit * query_gain_ref[...]).astype(BF16)
        keys = (key_unit * key_gain_ref[...]).astype(BF16)
        grad = attended_grad[:, head * width : (head + 1) * width]
        probs = probs_ref[head]
        probs_wide = probs.astype(F32)
        value_grad = dot_tn(probs, grad)
        prob_grad = dot_nt(grad, value)
        row_delta = jnp.sum(probs_wide * prob_grad, axis=-1, keepdims=True)
        score_grad = (probs_wide * (prob_grad - row_delta) * scale_factor).astype(BF16)
        query_scaled = dot_nn(score_grad, keys) * query_gain_ref[...]
        key_scaled = dot_tn(score_grad, queries) * key_gain_ref[...]
        query_mean = jnp.mean(query_scaled * query_unit, axis=-1, keepdims=True)
        key_mean = jnp.mean(key_scaled * key_unit, axis=-1, keepdims=True)
        grad_ref[0, :, left : left + width] = (
            (query_scaled - query_unit * query_mean) * query_inverse
        ).astype(BF16)
        grad_ref[0, :, left + width : left + 2 * width] = (
            (key_scaled - key_unit * key_mean) * key_inverse
        ).astype(BF16)
        grad_ref[0, :, left + 2 * width : left + 3 * width] = value_grad.astype(BF16)


def backward(own, other, out_weight, projected, probs, attention, query_gain, key_gain, gate):
    local, model = own.shape
    pairs, tokens, wide = projected.shape
    head_dim = query_gain.shape[1]
    whole = lambda i: (0, 0)
    return pl.pallas_call(
        backward_kernel,
        grid=(pairs,),
        out_shape=(
            jax.ShapeDtypeStruct((pairs, tokens, wide), BF16),
            jax.ShapeDtypeStruct((1, model), F32),
        ),
        in_specs=[
            pl.BlockSpec((local, model), whole),
            pl.BlockSpec((local, model), whole),
            pl.BlockSpec((2 * head_dim, model), lambda i: (i, 0)),
            pl.BlockSpec((1, tokens, wide), lambda i: (i, 0, 0)),
            pl.BlockSpec((2, tokens, tokens), lambda i: (i, 0, 0)),
            pl.BlockSpec((tokens, model // pairs), lambda i: (0, i)),
            pl.BlockSpec((1, head_dim), whole),
            pl.BlockSpec((1, head_dim), whole),
            pl.BlockSpec((1, model), whole),
        ],
        out_specs=(
            pl.BlockSpec((1, tokens, wide), lambda i: (i, 0, 0)),
            pl.BlockSpec((1, model // pairs), lambda i: (0, i)),
        ),
        scratch_shapes=[pltpu.VMEM((tokens, model), BF16)],
        compiler_params=params(),
        cost_estimate=pl.CostEstimate(
            flops=2 * tokens * model * pairs * 2 * head_dim,
            bytes_accessed=2 * model * pairs * 2 * head_dim,
            transcendentals=0,
        ),
        name="attention_backward",
    )(own, other, out_weight, projected, probs, attention, query_gain, key_gain, gate)


def input_grad_kernel(grad_ref, weight_ref, own_ref, kept_ref, sent_ref):
    local = own_ref.shape[0]
    total = dot_nt(grad_ref[0], weight_ref[0])
    for pair in range(1, grad_ref.shape[0]):
        total += dot_nt(grad_ref[pair], weight_ref[pair])
    kept_ref[...] = (own_ref[...].astype(F32) + total[:local]).astype(BF16)
    sent_ref[...] = total[local:].astype(BF16)


def input_grad_part(grad, weight, own, part, parts, block):
    local, model = own.shape
    pairs, tokens, wide = grad.shape
    columns = model // parts
    first = part * columns // block
    out = jax.ShapeDtypeStruct((local, columns), BF16)
    out_spec = pl.BlockSpec((local, block), lambda i: (0, i))
    return pl.pallas_call(
        input_grad_kernel,
        grid=(columns // block,),
        out_shape=(out, out),
        in_specs=[
            pl.BlockSpec((pairs, tokens, wide), lambda i: (0, 0, 0)),
            pl.BlockSpec((pairs, block, wide), lambda i: (0, i + first, 0)),
            pl.BlockSpec((local, block), lambda i: (0, i + first)),
        ],
        out_specs=(out_spec, out_spec),
        compiler_params=params(),
        cost_estimate=pl.CostEstimate(
            flops=2 * tokens * columns * pairs * wide,
            bytes_accessed=2 * columns * pairs * wide,
            transcendentals=0,
        ),
        name="input_grad",
    )(grad, weight, own)


def routed(block, seq_step, pipe_step):
    seq_size, pipe_size = lax.axis_size("seq"), lax.axis_size("pipe")
    route = []
    for i in range(seq_size):
        for j in range(pipe_size):
            target = (i + seq_step) % seq_size * pipe_size + (j + pipe_step) % pipe_size
            route.append((i * pipe_size + j, target))
    return lax.ppermute(block, ("seq", "pipe"), route)


def pair_body(
    segment_input,
    output_grad,
    qkv_weight,
    out_weight,
    query_gain,
    key_gain,
    gate_scale,
    neighbours,
    tile_slot,
):
    stream = segment_input[0]
    upstream = output_grad[0]
    out_local = out_weight[0]
    model = stream.shape[1]
    other_stream = routed(stream, 1, 0)
    weight = regroup(qkv_weight[0], 256)
    other_stream, upstream_after = lax.optimization_barrier((other_stream, upstream))
    other_upstream = routed(upstream_after, 1, 0)
    projected, probs, attention, kept, sent = forward(
        neighbours,
        tile_slot,
        stream,
        other_stream,
        weight,
        out_local,
        query_gain,
        key_gain,
        gate_scale,
    )
    kept = routed(kept, 0, 1)
    sent = routed(sent, 1, 1)
    grad, gate_share = backward(
        upstream,
        other_upstream,
        out_local,
        projected,
        probs,
        attention,
        query_gain,
        key_gain,
        gate_scale,
    )
    other_gate = routed(gate_share, 1, 0)
    parts = 2
    pieces = []
    for part in range(parts):
        one, two = input_grad_part(grad, weight, upstream, part, parts, 512)
        pieces.append((routed(one, 0, -1), routed(two, 1, -1)))
    segment_output = (kept.astype(F32) + sent.astype(F32)).astype(BF16)
    input_grad = jnp.concatenate(
        [(a.astype(F32) + b.astype(F32)).astype(BF16) for a, b in pieces], axis=1
    )
    half = model // lax.axis_size("seq")
    gate_total = lax.dynamic_slice_in_dim(
        gate_share + other_gate, lax.axis_index("seq") * half, half, 1
    )
    return (segment_output[None], input_grad[None], gate_total)


def solution(mesh):
    in_specs = (
        P("pipe", ("dp", "seq"), None),
        P("pipe", ("dp", "seq"), None),
        P("pipe", None, "seq", None),
        P("pipe", "seq", None),
        P("pipe", None),
        P("pipe", None),
        P("pipe", None),
        P("dp", None),
        P("dp"),
    )
    out_specs = (
        P("pipe", ("dp", "seq"), None),
        P("pipe", ("dp", "seq"), None),
        P(("dp", "pipe"), "seq"),
    )

    def body(*args):
        one_tile_each = args[0].shape[1] == TILE and args[8].shape[0] == 2
        if mesh.shape["seq"] == 2 and one_tile_each and args[2].shape[2] % 2 == 0:
            return pair_body(*args)
        return general_body(*args)

    return jax.shard_map(body, mesh=mesh, in_specs=in_specs, out_specs=out_specs, check_vma=False)
```

profile of v0, /device:TPU:1, one launch (start us, length us, event | category | flops | bytes accessed | tf_op | source)
XLA Modules:
  0.0 81.0 jit_solution(1722970935362182572)
XLA Ops:
  0.6 2.1 %collective-permute-start = (bf16[64,3072]{1,0:T(8,128)(2,1)}, bf16[64,3072]{1,0:T(8,128)(2,1)S(1)}, u32[]{:S(2)}, u32[]{:S(2)}) collective-permute-start(bf16[64,3072]{1,0:T(8,128)(2,1)} %bitcast.12), channel_id=1, source_target_pairs={{0,16},{4,20},{8,24},{12,28},{16,0},{20,4},{24,8},{28,12},{1,17},{... | collective-permute-start | bytes 1179656 | tf_op jit(solution)/shard_map/ppermute | solution.py:537
  2.7 9.1 %collective-permute-done.other_ref = bf16[64,3072]{1,0:T(8,128)(2,1)S(1)} collective-permute-done((bf16[64,3072]{1,0:T(8,128)(2,1)}, bf16[64,3072]{1,0:T(8,128)(2,1)S(1)}, u32[]{:S(2)}, u32[]{:S(2)}) %collective-permute-start) | collective-permute-done | bytes 393248 | tf_op jit(solution)/shard_map/ppermute | solution.py:537
  11.8 1.1 %collective-permute-start.3 = (bf16[64,3072]{1,0:T(8,128)(2,1)}, bf16[64,3072]{1,0:T(8,128)(2,1)}, u32[]{:S(2)}, u32[]{:S(2)}) collective-permute-start(bf16[64,3072]{1,0:T(8,128)(2,1)} %bitcast.8), channel_id=1, source_target_pairs={{0,16},{4,20},{8,24},{12,28},{16,0},{20,4},{24,8},{28,12},{1,17},{... | collective-permute-start | bytes 1179656 | tf_op jit(solution)/shard_map/ppermute | solution.py:537
  12.9 0.0 copy-start.8
  13.0 18.7 %regroup.1.weight_ref = bf16[4,3072,768]{2,1,0:T(8,128)(2,1)} custom-call(bf16[3072,8,384]{2,1,0:T(8,128)(2,1)} %bitcast.16), custom_call_target="tpu_custom_call" | custom-call | bytes 37748736 | tf_op jit(solution)/shard_map/regroup/pallas_call | solution.py:239
  31.7 0.0 copy-done.4
  31.7 0.0 copy-start
  31.7 13.4 %attention_forward.1 = (f32[4,128,768]{2,1,0:T(8,128)S(1)}, bf16[8,128,128]{2,1,0:T(8,128)(2,1)S(1)}, f32[128,3072]{1,0:T(8,128)S(1)}, bf16[64,3072]{1,0:T(8,128)(2,1)}, bf16[64,3072]{1,0:T(8,128)(2,1)}) custom-call(s32[2,27]{1,0:T(2,128)S(1)} %copy-done.8, s32[2]{0:T(128)S(1)} %copy-done.9, bf16[64,3072]{1,0:T(8,128)(2,1)S(1)} %bitcast.13, ...), custom_call_target="tpu_custom_call" | custom-call | flops 3221225472 | bytes 25165824 | tf_op jit(solution)/shard_map/attention_forward/pallas_call | solution.py:353
  45.1 0.7 copy-done.2
  45.8 2.9 %collective-permute-start.2 = (bf16[64,3072]{1,0:T(8,128)(2,1)}, bf16[64,3072]{1,0:T(8,128)(2,1)}, u32[]{:S(2)}, u32[]{:S(2)}) collective-permute-start(bf16[64,3072]{1,0:T(8,128)(2,1)} %get-tuple-element.18), channel_id=1, source_target_pairs={{0,20},{4,24},{8,28},{12,16},{16,4},{20,8},{24,12},{28,0},{1,21},{... | collective-permute-start | bytes 1179656 | tf_op jit(solution)/shard_map/ppermute | solution.py:537
  48.7 0.0 collective-permute-start.1
  48.7 0.0 collective-permute-done.3.other_ref
  48.7 0.9 %copy-done.3 = bf16[8,128,128]{2,1,0:T(8,128)(2,1)S(1)} copy-done((bf16[8,128,128]{2,1,0:T(8,128)(2,1)S(1)}, bf16[8,128,128]{2,1,0:T(8,128)(2,1)}, u32[]{:S(2)}) %copy-start.3) | copy-done | bytes 262168
  49.7 0.7 copy-done.7
  50.3 7.8 %attention_backward.1 = (bf16[4,128,768]{2,1,0:T(8,128)(2,1)S(1)}, f32[1,3072]{1,0:T(1,128)S(1)}) custom-call(bf16[64,3072]{1,0:T(8,128)(2,1)S(1)} %bitcast.9, bf16[64,3072]{1,0:T(8,128)(2,1)} %collective-permute-done.3.other_ref, bf16[1024,3072]{1,0:T(8,128)(2,1)} %bitcast.15, f32[4,128,768]{2,1,0:T(8,128)S(1)} %get-tuple-element.20.projected_ref, ...), custom_call_target="tpu_custom_call" | custom-call | flops 805306368 | bytes 6291456 | tf_op jit(solution)/shard_map/attention_backward/pallas_call | solution.py:461
  58.2 6.1 %input_grad.3 = (bf16[64,1536]{1,0:T(8,128)(2,1)S(1)}, bf16[64,1536]{1,0:T(8,128)(2,1)S(1)}) custom-call(bf16[4,128,768]{2,1,0:T(8,128)(2,1)S(1)} %get-tuple-element.23.grad_ref, bf16[4,3072,768]{2,1,0:T(8,128)(2,1)} %regroup.1.weight_ref, bf16[64,3072]{1,0:T(8,128)(2,1)S(1)} %bitcast.10), custom_call_target="tpu_custom_call" | custom-call | flops 1207959552 | bytes 9437184 | tf_op jit(solution)/shard_map/input_grad/pallas_call | solution.py:510
  64.3 1.6 %collective-permute-start.7 = (bf16[64,1536]{1,0:T(8,128)(2,1)S(1)}, bf16[64,1536]{1,0:T(8,128)(2,1)S(1)}, u32[]{:S(2)}, u32[]{:S(2)}) collective-permute-start(bf16[64,1536]{1,0:T(8,128)(2,1)S(1)} %get-tuple-element.27), channel_id=1, source_target_pairs={{0,28},{4,16},{8,20},{12,24},{16,12},{20,0},{24,4},{28,8},{1,29},{... | collective-permute-start | bytes 589832 | tf_op jit(solution)/shard_map/ppermute | solution.py:537
  65.9 0.0 collective-permute-start.6
  65.9 6.1 %input_grad.2 = (bf16[64,1536]{1,0:T(8,128)(2,1)S(1)}, bf16[64,1536]{1,0:T(8,128)(2,1)S(1)}) custom-call(bf16[4,128,768]{2,1,0:T(8,128)(2,1)S(1)} %get-tuple-element.23.grad_ref, bf16[4,3072,768]{2,1,0:T(8,128)(2,1)} %regroup.1.weight_ref, bf16[64,3072]{1,0:T(8,128)(2,1)S(1)} %bitcast.11), custom_call_target="tpu_custom_call" | custom-call | flops 1207959552 | bytes 9437184 | tf_op jit(solution)/shard_map/input_grad/pallas_call | solution.py:510
  72.0 0.6 collective-permute-start.5
  72.6 0.0 collective-permute-done.2
  72.6 1.1 %collective-permute-start.4 = (bf16[64,1536]{1,0:T(8,128)(2,1)S(1)}, bf16[64,1536]{1,0:T(8,128)(2,1)S(1)}, u32[]{:S(2)}, u32[]{:S(2)}) collective-permute-start(bf16[64,1536]{1,0:T(8,128)(2,1)S(1)} %get-tuple-element.24), channel_id=1, source_target_pairs={{0,12},{4,0},{8,4},{12,8},{16,28},{20,16},{24,20},{28,24},{1,13},{... | collective-permute-start | bytes 589832 | tf_op jit(solution)/shard_map/ppermute | solution.py:537
  73.7 0.0 collective-permute-done.1
  73.7 1.2 %collective-permute-start.8 = (f32[1,3072]{1,0:T(1,128)S(1)}, f32[1,3072]{1,0:T(1,128)S(1)}, u32[]{:S(2)}, u32[]{:S(2)}) collective-permute-start(f32[1,3072]{1,0:T(1,128)S(1)} %get-tuple-element.28), channel_id=1, source_target_pairs={{0,16},{4,20},{8,24},{12,28},{16,0},{20,4},{24,8},{28,12},{1,17},{... | collective-permute-start | bytes 36872 | tf_op jit(solution)/shard_map/ppermute | solution.py:537
  74.8 2.0 %fusion = bf16[1,64,3072]{2,1,0:T(8,128)(2,1)} fusion(bf16[64,3072]{1,0:T(8,128)(2,1)} %collective-permute-done.2, bf16[64,3072]{1,0:T(8,128)(2,1)} %collective-permute-done.1), kind=kLoop, calls=%fused_computation.1 | loop fusion | flops 786432 | bytes 1179648 | tf_op jit(solution)/shard_map/broadcast_in_dim | solution.py:597
  76.8 1.7 %collective-permute-done.8 = f32[1,3072]{1,0:T(1,128)S(1)} collective-permute-done((f32[1,3072]{1,0:T(1,128)S(1)}, f32[1,3072]{1,0:T(1,128)S(1)}, u32[]{:S(2)}, u32[]{:S(2)}) %collective-permute-start.8) | collective-permute-done | bytes 12320 | tf_op jit(solution)/shard_map/ppermute | solution.py:537
  78.5 0.6 dynamic-slice_add_fusion
  79.1 0.0 collective-permute-done.7
  79.1 0.0 collective-permute-done.6
  79.2 1.0 %collective-permute-done.5 = bf16[64,1536]{1,0:T(8,128)(2,1)S(1)} collective-permute-done((bf16[64,1536]{1,0:T(8,128)(2,1)S(1)}, bf16[64,1536]{1,0:T(8,128)(2,1)S(1)}, u32[]{:S(2)}, u32[]{:S(2)}) %collective-permute-start.5) | collective-permute-done | bytes 196640 | tf_op jit(solution)/shard_map/ppermute | solution.py:537
  80.2 0.0 collective-permute-done.4
  80.2 0.8 maximum_bitcast_fusion
  (16 shorter events, 0.1 us)
Async XLA Ops:
  0.6 11.2 %collective-permute-start = (bf16[64,3072]{1,0:T(8,128)(2,1)}, bf16[64,3072]{1,0:T(8,128)(2,1)S(1)}, u32[]{:S(2)}, u32[]{:S(2)}) collective-permute-start(bf16[64,3072]{1,0:T(8,128)(2,1)} %bitcast.12), channel_id=1, source_target_pairs={{0,16},{4,20},{8,24},{12,28},{16,0},{20,4},{24,8},{28,12},{1,17},{... | collective-permute-start | bytes 1179656 | tf_op jit(solution)/shard_map/ppermute | solution.py:537
  11.8 36.9 %collective-permute-start.3 = (bf16[64,3072]{1,0:T(8,128)(2,1)}, bf16[64,3072]{1,0:T(8,128)(2,1)}, u32[]{:S(2)}, u32[]{:S(2)}) collective-permute-start(bf16[64,3072]{1,0:T(8,128)(2,1)} %bitcast.8), channel_id=1, source_target_pairs={{0,16},{4,20},{8,24},{12,28},{16,0},{20,4},{24,8},{28,12},{1,17},{... | collective-permute-start | bytes 1179656 | tf_op jit(solution)/shard_map/ppermute | solution.py:537
  12.9 18.7 %copy-start.1 = (bf16[1,64,3072]{2,1,0:T(8,128)(2,1)S(1)}, bf16[1,64,3072]{2,1,0:T(8,128)(2,1)}, u32[]{:S(2)}) copy-start(bf16[1,64,3072]{2,1,0:T(8,128)(2,1)} %param.9) | copy-start | bytes 1179652
  12.9 18.7 %copy-start.4 = (f32[1,3072]{1,0:T(1,128)S(1)}, f32[1,3072]{1,0:T(1,128)}, u32[]{:S(2)}) copy-start(f32[1,3072]{1,0:T(1,128)} %gate_ref.3) | copy-start | bytes 36868
  12.9 18.7 %copy-start.5 = (f32[1,128]{1,0:T(1,128)S(1)}, f32[1,128]{1,0:T(1,128)}, u32[]{:S(2)}) copy-start(f32[1,128]{1,0:T(1,128)} %query_gain_ref.3) | copy-start | bytes 1540
  12.9 18.7 %copy-start.6 = (f32[1,128]{1,0:T(1,128)S(1)}, f32[1,128]{1,0:T(1,128)}, u32[]{:S(2)}) copy-start(f32[1,128]{1,0:T(1,128)} %key_gain_ref.3) | copy-start | bytes 1540
  12.9 18.7 %copy-start.8 = (s32[2,27]{1,0:T(2,128)S(1)}, s32[2,27]{1,0:T(2,128)}, u32[]{:S(2)}) copy-start(s32[2,27]{1,0:T(2,128)} %neighbours_ref.1) | copy-start | bytes 652
  13.0 18.7 %copy-start.9 = (s32[2]{0:T(128)S(1)}, s32[2]{0:T(128)}, u32[]{:S(2)}) copy-start(s32[2]{0:T(128)} %tile_slot_ref.1) | copy-start | bytes 28
  31.7 17.0 %copy-start = (bf16[1,64,3072]{2,1,0:T(8,128)(2,1)S(1)}, bf16[1,64,3072]{2,1,0:T(8,128)(2,1)}, u32[]{:S(2)}) copy-start(bf16[1,64,3072]{2,1,0:T(8,128)(2,1)} %param.10) | copy-start | bytes 1179652
  45.1 0.7 copy-start.2
  45.8 26.8 %collective-permute-start.2 = (bf16[64,3072]{1,0:T(8,128)(2,1)}, bf16[64,3072]{1,0:T(8,128)(2,1)}, u32[]{:S(2)}, u32[]{:S(2)}) collective-permute-start(bf16[64,3072]{1,0:T(8,128)(2,1)} %get-tuple-element.18), channel_id=1, source_target_pairs={{0,20},{4,24},{8,28},{12,16},{16,4},{20,8},{24,12},{28,0},{1,21},{... | collective-permute-start | bytes 1179656 | tf_op jit(solution)/shard_map/ppermute | solution.py:537
  48.7 25.0 %collective-permute-start.1 = (bf16[64,3072]{1,0:T(8,128)(2,1)}, bf16[64,3072]{1,0:T(8,128)(2,1)}, u32[]{:S(2)}, u32[]{:S(2)}) collective-permute-start(bf16[64,3072]{1,0:T(8,128)(2,1)} %get-tuple-element.17), channel_id=1, source_target_pairs={{0,4},{4,8},{8,12},{12,0},{16,20},{20,24},{24,28},{28,16},{1,5},{5... | collective-permute-start | bytes 1179656 | tf_op jit(solution)/shard_map/ppermute | solution.py:537
  48.7 1.0 %copy-start.3 = (bf16[8,128,128]{2,1,0:T(8,128)(2,1)S(1)}, bf16[8,128,128]{2,1,0:T(8,128)(2,1)}, u32[]{:S(2)}) copy-start(bf16[8,128,128]{2,1,0:T(8,128)(2,1)} %copy-done.2) | copy-start | bytes 786436
  49.7 0.7 copy-start.7
  64.3 14.8 %collective-permute-start.7 = (bf16[64,1536]{1,0:T(8,128)(2,1)S(1)}, bf16[64,1536]{1,0:T(8,128)(2,1)S(1)}, u32[]{:S(2)}, u32[]{:S(2)}) collective-permute-start(bf16[64,1536]{1,0:T(8,128)(2,1)S(1)} %get-tuple-element.27), channel_id=1, source_target_pairs={{0,28},{4,16},{8,20},{12,24},{16,12},{20,0},{24,4},{28,8},{1,29},{... | collective-permute-start | bytes 589832 | tf_op jit(solution)/shard_map/ppermute | solution.py:537
  65.9 13.2 %collective-permute-start.6 = (bf16[64,1536]{1,0:T(8,128)(2,1)S(1)}, bf16[64,1536]{1,0:T(8,128)(2,1)S(1)}, u32[]{:S(2)}, u32[]{:S(2)}) collective-permute-start(bf16[64,1536]{1,0:T(8,128)(2,1)S(1)} %get-tuple-element.26), channel_id=1, source_target_pairs={{0,12},{4,0},{8,4},{12,8},{16,28},{20,16},{24,20},{28,24},{1,13},{... | collective-permute-start | bytes 589832 | tf_op jit(solution)/shard_map/ppermute | solution.py:537
  72.0 8.1 %collective-permute-start.5 = (bf16[64,1536]{1,0:T(8,128)(2,1)S(1)}, bf16[64,1536]{1,0:T(8,128)(2,1)S(1)}, u32[]{:S(2)}, u32[]{:S(2)}) collective-permute-start(bf16[64,1536]{1,0:T(8,128)(2,1)S(1)} %get-tuple-element.25), channel_id=1, source_target_pairs={{0,28},{4,16},{8,20},{12,24},{16,12},{20,0},{24,4},{28,8},{1,29},{... | collective-permute-start | bytes 589832 | tf_op jit(solution)/shard_map/ppermute | solution.py:537
  72.6 7.6 %collective-permute-start.4 = (bf16[64,1536]{1,0:T(8,128)(2,1)S(1)}, bf16[64,1536]{1,0:T(8,128)(2,1)S(1)}, u32[]{:S(2)}, u32[]{:S(2)}) collective-permute-start(bf16[64,1536]{1,0:T(8,128)(2,1)S(1)} %get-tuple-element.24), channel_id=1, source_target_pairs={{0,12},{4,0},{8,4},{12,8},{16,28},{20,16},{24,20},{28,24},{1,13},{... | collective-permute-start | bytes 589832 | tf_op jit(solution)/shard_map/ppermute | solution.py:537
  73.7 4.9 %collective-permute-start.8 = (f32[1,3072]{1,0:T(1,128)S(1)}, f32[1,3072]{1,0:T(1,128)S(1)}, u32[]{:S(2)}, u32[]{:S(2)}) collective-permute-start(f32[1,3072]{1,0:T(1,128)S(1)} %get-tuple-element.28), channel_id=1, source_target_pairs={{0,16},{4,20},{8,24},{12,28},{16,0},{20,4},{24,8},{28,12},{1,17},{... | collective-permute-start | bytes 36872 | tf_op jit(solution)/shard_map/ppermute | solution.py:537
where the time goes:
time: 82.1 us; the launch traced here: 81 us
  Pallas kernels  52.1 us (63%)
  waiting for transfers between devices  11.8 us (14%)
  starting transfers between devices  10.7 us (13%)
  other arithmetic  3.42 us (4%)
  local copies, waits for them, and re-layouts  2.34 us (3%)
    pallas_call x1, Pallas kernels, regroup(): pl.pallas_call(regroup_kernel, grid=(depth // rows,), out_shape=jax.Shape...  18.7 us
    pallas_call x1, Pallas kernels, forward(): pl.pallas_call(forward_kernel, grid=(pairs,), out_shape=(jax.ShapeDtypeSt...  13.4 us
    pallas_call x2, Pallas kernels, input_grad_part(): pl.pallas_call(input_grad_kernel, grid=(columns // block,), out_shape=(ou...  12.2 us
    ppermute x9, waiting for transfers between devices, routed(): return lax.ppermute(block, ('seq', 'pipe'), route)  11.8 us
    ppermute x9, starting transfers between devices, routed(): return lax.ppermute(block, ('seq', 'pipe'), route)  10.7 us
    pallas_call x1, Pallas kernels, backward(): pl.pallas_call(backward_kernel, grid=(pairs,), out_shape=(jax.ShapeDtypeS...  7.81 us
    broadcast_in_dim x2, other arithmetic, pair_body(): return (segment_output[None], input_grad[None], gate_total)  2.72 us
    unnamed x20, local copies, waits for them, and re-layouts  2.34 us
  transfers between devices with their start and end apart: 9, of which 3 were waited for; matrix products, arithmetic and copies ran while one was open for 3% of the time, Pallas kernels for 64%

commit v1 on v0

--- a/solution.py
+++ b/solution.py
@@ -12,7 +12,7 @@
 EPSILON = 1e-06
 F32 = jnp.float32
 BF16 = jnp.bfloat16
-VMEM_LIMIT = 44 * 1024 * 1024
+MIB = 1024 * 1024
 
 
 def passed_along(block, axis, distance):
@@ -220,29 +220,36 @@
     return lax.dot_general(a, b, (((0,), (0,)), ((), ())), preferred_element_type=F32)
 
 
-def params(limit=VMEM_LIMIT):
-    return pltpu.CompilerParams(vmem_limit_bytes=limit)
-
-
-def regroup_kernel(weight_ref, out_ref):
-    heads = weight_ref.shape[1]
-    width = weight_ref.shape[2]
-    by_head = jnp.swapaxes(weight_ref[...], 0, 1)
+def params(mebibytes):
+    return pltpu.CompilerParams(vmem_limit_bytes=mebibytes * MIB)
+
+
+def regroup_kernel(weight_ref, out_ref, wide_ref):
+    rows, heads, width = weight_ref.shape
+    third = wide_ref.shape[2]
+    for part in range(width // third):
+        piece = weight_ref[:, :, part * third : (part + 1) * third].astype(F32)
+        wide_ref[part] = piece.reshape(rows * heads, third)
     for head in range(heads):
-        left = (head % 2) * width
-        out_ref[head // 2, :, left : left + width] = by_head[head]
+        for part in range(width // third):
+            left = (head % 2) * width + part * third
+            out_ref[head // 2, :, left : left + third] = wide_ref[
+                part, pl.ds(head, rows, stride=heads), :
+            ].astype(BF16)
 
 
 def regroup(weight, rows):
     depth, heads, width = weight.shape
     pairs = heads // 2
+    third = width // 3
     return pl.pallas_call(
         regroup_kernel,
         grid=(depth // rows,),
         out_shape=jax.ShapeDtypeStruct((pairs, depth, 2 * width), weight.dtype),
         in_specs=[pl.BlockSpec((rows, heads, width), lambda i: (i, 0, 0))],
         out_specs=pl.BlockSpec((pairs, rows, 2 * width), lambda i: (0, i, 0)),
-        compiler_params=params(),
+        scratch_shapes=[pltpu.VMEM((3, rows * heads, third), F32)],
+        compiler_params=params(46),
         cost_estimate=pl.CostEstimate(
             flops=0, bytes_accessed=4 * depth * heads * width, transcendentals=0
         ),
@@ -379,7 +386,7 @@
             pl.BlockSpec((local, model), whole),
         ),
         scratch_shapes=[pltpu.VMEM((tokens, model), BF16), pltpu.VMEM((tokens, tokens), F32)],
-        compiler_params=params(),
+        compiler_params=params(46),
         cost_estimate=pl.CostEstimate(
             flops=2 * tokens * model * pairs * (wide + 2 * head_dim),
             bytes_accessed=2 * model * pairs * (wide + 2 * head_dim),
@@ -481,7 +488,7 @@
             pl.BlockSpec((1, model // pairs), lambda i: (0, i)),
         ),
         scratch_shapes=[pltpu.VMEM((tokens, model), BF16)],
-        compiler_params=params(),
+        compiler_params=params(46),
         cost_estimate=pl.CostEstimate(
             flops=2 * tokens * model * pairs * 2 * head_dim,
             bytes_accessed=2 * model * pairs * 2 * head_dim,
@@ -493,9 +500,10 @@
 
 def input_grad_kernel(grad_ref, weight_ref, own_ref, kept_ref, sent_ref):
     local = own_ref.shape[0]
-    total = dot_nt(grad_ref[0], weight_ref[0])
+    total = dot_nt(weight_ref[0], grad_ref[0])
     for pair in range(1, grad_ref.shape[0]):
-        total += dot_nt(grad_ref[pair], weight_ref[pair])
+        total += dot_nt(weight_ref[pair], grad_ref[pair])
+    total = total.T
     kept_ref[...] = (own_ref[...].astype(F32) + total[:local]).astype(BF16)
     sent_ref[...] = total[local:].astype(BF16)
 
@@ -517,7 +525,7 @@
             pl.BlockSpec((local, block), lambda i: (0, i + first)),
         ],
         out_specs=(out_spec, out_spec),
-        compiler_params=params(),
+        compiler_params=params(46),
         cost_estimate=pl.CostEstimate(
             flops=2 * tokens * columns * pairs * wide,
             bytes_accessed=2 * columns * pairs * wide,
@@ -553,8 +561,8 @@
     out_local = out_weight[0]
     model = stream.shape[1]
     other_stream = routed(stream, 1, 0)
-    weight = regroup(qkv_weight[0], 256)
-    other_stream, upstream_after = lax.optimization_barrier((other_stream, upstream))
+    weight = regroup(qkv_weight[0], 128)
+    weight, upstream_after = lax.optimization_barrier((weight, upstream))
     other_upstream = routed(upstream_after, 1, 0)
     projected, probs, attention, kept, sent = forward(
         neighbours,
@@ -581,18 +589,18 @@
         gate_scale,
     )
     other_gate = routed(gate_share, 1, 0)
-    parts = 2
-    pieces = []
-    for part in range(parts):
-        one, two = input_grad_part(grad, weight, upstream, part, parts, 512)
-        pieces.append((routed(one, 0, -1), routed(two, 1, -1)))
+    first, second = input_grad_part(grad, weight, upstream, 0, 2, 512)
+    pieces = [(routed(first, 0, -1), routed(second, 1, -1))]
     segment_output = (kept.astype(F32) + sent.astype(F32)).astype(BF16)
-    input_grad = jnp.concatenate(
-        [(a.astype(F32) + b.astype(F32)).astype(BF16) for a, b in pieces], axis=1
-    )
     half = model // lax.axis_size("seq")
     gate_total = lax.dynamic_slice_in_dim(
         gate_share + other_gate, lax.axis_index("seq") * half, half, 1
+    )
+    grad, segment_output, gate_total = lax.optimization_barrier((grad, segment_output, gate_total))
+    first, second = input_grad_part(grad, weight, upstream, 1, 2, 512)
+    pieces.append((routed(first, 0, -1), routed(second, 1, -1)))
+    input_grad = jnp.concatenate(
+        [(a.astype(F32) + b.astype(F32)).astype(BF16) for a, b in pieces], axis=1
     )
     return (segment_output[None], input_grad[None], gate_total)
 

time: 82.1 us -> 76.5 us (0.932)
  waiting for transfers between devices: 11.8 us -> 6.61 us
  Pallas kernels: 52.1 us -> 56.4 us
  local copies, waits for them, and re-layouts: 2.34 us -> 0.03 us
  other arithmetic: 3.42 us -> 2.31 us
  starting transfers between devices: 10.7 us -> 9.68 us
    pallas_call x1, Pallas kernels: 18.7 us -> 24.3 us  [regroup(): pl.pallas_call(regroup_kernel, grid=(depth // rows,), out_shape=jax.Shape...]
    ppermute x9, waiting for transfers between devices: 11.8 us -> 6.61 us  [routed(): return lax.ppermute(block, ('seq', 'pipe'), route)]
    unnamed x20 -> x14, local copies, waits for them, and re-layouts: 2.34 us -> 0.03 us
    broadcast_in_dim x2 -> x1, other arithmetic: 2.72 us -> 0.77 us  [pair_body(): return (segment_output[None], input_grad[None], gate_total)]
    ppermute x9, starting transfers between devices: 10.7 us -> 9.68 us  [routed(): return lax.ppermute(block, ('seq', 'pipe'), route)]
    pallas_call x1, Pallas kernels: 13.4 us -> 12.5 us  [forward(): pl.pallas_call(forward_kernel, grid=(pairs,), out_shape=(jax.ShapeDtypeSt...]
    convert_element_type x0 -> x1, other arithmetic: none -> 0.84 us  [pair_body(): segment_output = (kept.astype(F32) + sent.astype(F32)).astype(BF16)]
  transfers between devices with their start and end apart: 9 -> 9, of which waited for: 3 -> 2; matrix products, arithmetic and copies ran while one was open for 3% -> 2% of each run, Pallas kernels for 64% -> 74%
where the time goes in v1:
time: 76.5 us; the launch traced here: 75.8 us
  Pallas kernels  56.4 us (74%)
  starting transfers between devices  9.68 us (13%)
  waiting for transfers between devices  6.61 us (9%)
  other arithmetic  2.31 us (3%)
    pallas_call x1, Pallas kernels, regroup(): pl.pallas_call(regroup_kernel, grid=(depth // rows,), out_shape=jax.Shape...  24.3 us
    pallas_call x1, Pallas kernels, forward(): pl.pallas_call(forward_kernel, grid=(pairs,), out_shape=(jax.ShapeDtypeSt...  12.5 us
    pallas_call x2, Pallas kernels, input_grad_part(): pl.pallas_call(input_grad_kernel, grid=(columns // block,), out_shape=(ou...  11.8 us
    ppermute x9, starting transfers between devices, routed(): return lax.ppermute(block, ('seq', 'pipe'), route)  9.68 us
    pallas_call x1, Pallas kernels, backward(): pl.pallas_call(backward_kernel, grid=(pairs,), out_shape=(jax.ShapeDtypeS...  7.74 us
    ppermute x9, waiting for transfers between devices, routed(): return lax.ppermute(block, ('seq', 'pipe'), route)  6.61 us
  transfers between devices with their start and end apart: 9, of which 2 were waited for; matrix products, arithmetic and copies ran while one was open for 2% of the time, Pallas kernels for 74%

profile of v1, /device:TPU:1, one launch (start us, length us, event | category | flops | bytes accessed | tf_op | source)
XLA Modules:
  0.0 75.8 jit_solution(6293858755697862425)
XLA Ops:
  0.6 2.1 %collective-permute-start.1 = (bf16[64,3072]{1,0:T(8,128)(2,1)}, bf16[64,3072]{1,0:T(8,128)(2,1)S(1)}, u32[]{:S(2)}, u32[]{:S(2)}) collective-permute-start(bf16[64,3072]{1,0:T(8,128)(2,1)} %bitcast.11), channel_id=1, source_target_pairs={{0,16},{4,20},{8,24},{12,28},{16,0},{20,4},{24,8},{28,12},{1,17},{... | collective-permute-start | bytes 1179656 | tf_op jit(solution)/shard_map/ppermute | solution.py:545
  2.8 0.0 copy-start.4
  2.8 24.3 %regroup.1.weight_ref = bf16[4,3072,768]{2,1,0:T(8,128)(2,1)} custom-call(bf16[3072,8,384]{2,1,0:T(8,128)(2,1)} %bitcast.15), custom_call_target="tpu_custom_call" | custom-call | bytes 37748736 | tf_op jit(solution)/shard_map/regroup/pallas_call | solution.py:245
  27.1 0.0 collective-permute-start
  27.2 0.0 collective-permute-done.1.other_ref
  27.2 0.0 copy-done.2
  27.2 0.0 copy-done.3
  27.2 0.0 copy-done.4
  27.2 0.0 copy-done.5
  27.2 0.0 copy-done.6
  27.2 12.5 %attention_forward.1 = (f32[4,128,768]{2,1,0:T(8,128)S(1)}, bf16[8,128,128]{2,1,0:T(8,128)(2,1)S(1)}, f32[128,3072]{1,0:T(8,128)S(1)}, bf16[64,3072]{1,0:T(8,128)(2,1)S(1)}, bf16[64,3072]{1,0:T(8,128)(2,1)S(1)}) custom-call(s32[2,27]{1,0:T(2,128)S(1)} %copy-done.5, s32[2]{0:T(128)S(1)} %copy-done.6, bf16[64,3072]{1,0:T(8,128)(2,1)S(1)} %bitcast.12, ...), custom_call_target="tpu_custom_call" | custom-call | flops 3221225472 | bytes 25165824 | tf_op jit(solution)/shard_map/attention_forward/pallas_call | solution.py:360
  39.7 2.6 %collective-permute-start.2 = (bf16[64,3072]{1,0:T(8,128)(2,1)S(1)}, bf16[64,3072]{1,0:T(8,128)(2,1)S(1)}, u32[]{:S(2)}, u32[]{:S(2)}) collective-permute-start(bf16[64,3072]{1,0:T(8,128)(2,1)S(1)} %get-tuple-element.25), channel_id=1, source_target_pairs={{0,4},{4,8},{8,12},{12,0},{16,20},{20,24},{24,28},{28,16},{1,5},{5... | collective-permute-start | bytes 1179656 | tf_op jit(solution)/shard_map/ppermute | solution.py:545
  42.3 1.0 %collective-permute-start.3 = (bf16[64,3072]{1,0:T(8,128)(2,1)S(1)}, bf16[64,3072]{1,0:T(8,128)(2,1)S(1)}, u32[]{:S(2)}, u32[]{:S(2)}) collective-permute-start(bf16[64,3072]{1,0:T(8,128)(2,1)S(1)} %get-tuple-element.26), channel_id=1, source_target_pairs={{0,20},{4,24},{8,28},{12,16},{16,4},{20,8},{24,12},{28,0},{1,21},{... | collective-permute-start | bytes 1179656 | tf_op jit(solution)/shard_map/ppermute | solution.py:545
  43.3 0.0 collective-permute-done.other_ref
  43.3 7.7 %attention_backward.1 = (bf16[4,128,768]{2,1,0:T(8,128)(2,1)S(1)}, f32[1,3072]{1,0:T(1,128)S(1)}) custom-call(bf16[64,3072]{1,0:T(8,128)(2,1)S(1)} %bitcast.8, bf16[64,3072]{1,0:T(8,128)(2,1)S(1)} %collective-permute-done.other_ref, bf16[1024,3072]{1,0:T(8,128)(2,1)} %bitcast.14, f32[4,128,768]{2,1,0:T(8,128)S(1)} %get-tuple-element.21.projected_ref, ...), custom_call_target="tpu_custom_call" | custom-call | flops 805306368 | bytes 6291456 | tf_op jit(solution)/shard_map/attention_backward/pallas_call | solution.py:468
  51.0 0.3 collective-permute-start.4
  51.4 5.9 %input_grad.2 = (bf16[64,1536]{1,0:T(8,128)(2,1)S(1)}, bf16[64,1536]{1,0:T(8,128)(2,1)S(1)}) custom-call(bf16[4,128,768]{2,1,0:T(8,128)(2,1)S(1)} %get-tuple-element.31.grad_ref, bf16[4,3072,768]{2,1,0:T(8,128)(2,1)} %regroup.1.weight_ref, bf16[64,3072]{1,0:T(8,128)(2,1)S(1)} %bitcast.9), custom_call_target="tpu_custom_call" | custom-call | flops 1207959552 | bytes 9437184 | tf_op jit(solution)/shard_map/input_grad/pallas_call | solution.py:518
  57.3 0.9 %collective-permute-start.5 = (bf16[64,1536]{1,0:T(8,128)(2,1)S(1)}, bf16[64,1536]{1,0:T(8,128)(2,1)S(1)}, u32[]{:S(2)}, u32[]{:S(2)}) collective-permute-start(bf16[64,1536]{1,0:T(8,128)(2,1)S(1)} %get-tuple-element.29), channel_id=1, source_target_pairs={{0,12},{4,0},{8,4},{12,8},{16,28},{20,16},{24,20},{28,24},{1,13},{... | collective-permute-start | bytes 589832 | tf_op jit(solution)/shard_map/ppermute | solution.py:545
  58.2 1.2 %collective-permute-start.6 = (bf16[64,1536]{1,0:T(8,128)(2,1)S(1)}, bf16[64,1536]{1,0:T(8,128)(2,1)S(1)}, u32[]{:S(2)}, u32[]{:S(2)}) collective-permute-start(bf16[64,1536]{1,0:T(8,128)(2,1)S(1)} %get-tuple-element.30), channel_id=1, source_target_pairs={{0,28},{4,16},{8,20},{12,24},{16,12},{20,0},{24,4},{28,8},{1,29},{... | collective-permute-start | bytes 589832 | tf_op jit(solution)/shard_map/ppermute | solution.py:545
  59.4 0.0 collective-permute-done.4
  59.4 0.6 dynamic-slice_add_fusion
  60.0 0.0 collective-permute-done.2
  60.0 0.0 collective-permute-done.3
  60.0 0.8 %add_convert_fusion = bf16[64,3072]{1,0:T(8,128)(2,1)} fusion(bf16[64,3072]{1,0:T(8,128)(2,1)S(1)} %collective-permute-done.3, bf16[64,3072]{1,0:T(8,128)(2,1)S(1)} %collective-permute-done.2), kind=kLoop, calls=%fused_computation | loop fusion | flops 786432 | bytes 1179648 | tf_op jit(solution)/shard_map/convert_element_type | solution.py:594
  60.9 5.9 %input_grad.3 = (bf16[64,1536]{1,0:T(8,128)(2,1)S(1)}, bf16[64,1536]{1,0:T(8,128)(2,1)S(1)}) custom-call(bf16[4,128,768]{2,1,0:T(8,128)(2,1)S(1)} %get-tuple-element.31.grad_ref, bf16[4,3072,768]{2,1,0:T(8,128)(2,1)} %regroup.1.weight_ref, bf16[64,3072]{1,0:T(8,128)(2,1)S(1)} %bitcast.10), custom_call_target="tpu_custom_call" | custom-call | flops 1207959552 | bytes 9437184 | tf_op jit(solution)/shard_map/input_grad/pallas_call | solution.py:518
  66.8 0.4 collective-permute-start.7
  67.2 1.1 %collective-permute-start.8 = (bf16[64,1536]{1,0:T(8,128)(2,1)S(1)}, bf16[64,1536]{1,0:T(8,128)(2,1)S(1)}, u32[]{:S(2)}, u32[]{:S(2)}) collective-permute-start(bf16[64,1536]{1,0:T(8,128)(2,1)S(1)} %get-tuple-element.33), channel_id=1, source_target_pairs={{0,28},{4,16},{8,20},{12,24},{16,12},{20,0},{24,4},{28,8},{1,29},{... | collective-permute-start | bytes 589832 | tf_op jit(solution)/shard_map/ppermute | solution.py:545
  68.3 0.0 collective-permute-done.5
  68.3 0.0 collective-permute-done.6
  68.3 4.8 %collective-permute-done.7 = bf16[64,1536]{1,0:T(8,128)(2,1)S(1)} collective-permute-done((bf16[64,1536]{1,0:T(8,128)(2,1)S(1)}, bf16[64,1536]{1,0:T(8,128)(2,1)S(1)}, u32[]{:S(2)}, u32[]{:S(2)}) %collective-permute-start.7) | collective-permute-done | bytes 196640 | tf_op jit(solution)/shard_map/ppermute | solution.py:545
  73.1 1.8 %collective-permute-done.8 = bf16[64,1536]{1,0:T(8,128)(2,1)S(1)} collective-permute-done((bf16[64,1536]{1,0:T(8,128)(2,1)S(1)}, bf16[64,1536]{1,0:T(8,128)(2,1)S(1)}, u32[]{:S(2)}, u32[]{:S(2)}) %collective-permute-start.8) | collective-permute-done | bytes 196640 | tf_op jit(solution)/shard_map/ppermute | solution.py:545
  75.0 0.8 %maximum_bitcast_fusion = bf16[1,64,3072]{2,1,0:T(8,128)(2,1)} fusion(bf16[64,1536]{1,0:T(8,128)(2,1)S(1)} %add_convert_fusion.1, bf16[64,1536]{1,0:T(8,128)(2,1)S(1)} %add_convert_fusion.2), kind=kLoop, calls=%fused_computation.1 | loop fusion | flops 786432 | bytes 786432 | tf_op jit(solution)/shard_map/broadcast_in_dim | solution.py:605
  (10 shorter events, 0.1 us)
Async XLA Ops:
  0.6 26.5 %collective-permute-start.1 = (bf16[64,3072]{1,0:T(8,128)(2,1)}, bf16[64,3072]{1,0:T(8,128)(2,1)S(1)}, u32[]{:S(2)}, u32[]{:S(2)}) collective-permute-start(bf16[64,3072]{1,0:T(8,128)(2,1)} %bitcast.11), channel_id=1, source_target_pairs={{0,16},{4,20},{8,24},{12,28},{16,0},{20,4},{24,8},{28,12},{1,17},{... | collective-permute-start | bytes 1179656 | tf_op jit(solution)/shard_map/ppermute | solution.py:545
  2.7 24.4 %copy-start = (bf16[1,64,3072]{2,1,0:T(8,128)(2,1)S(1)}, bf16[1,64,3072]{2,1,0:T(8,128)(2,1)}, u32[]{:S(2)}) copy-start(bf16[1,64,3072]{2,1,0:T(8,128)(2,1)} %param.10) | copy-start | bytes 1179652
  2.7 24.4 %copy-start.1 = (bf16[1,64,3072]{2,1,0:T(8,128)(2,1)S(1)}, bf16[1,64,3072]{2,1,0:T(8,128)(2,1)}, u32[]{:S(2)}) copy-start(bf16[1,64,3072]{2,1,0:T(8,128)(2,1)} %param.9) | copy-start | bytes 1179652
  2.7 24.4 %copy-start.2 = (f32[1,3072]{1,0:T(1,128)S(1)}, f32[1,3072]{1,0:T(1,128)}, u32[]{:S(2)}) copy-start(f32[1,3072]{1,0:T(1,128)} %gate_ref.3) | copy-start | bytes 36868
  2.7 24.4 %copy-start.3 = (f32[1,128]{1,0:T(1,128)S(1)}, f32[1,128]{1,0:T(1,128)}, u32[]{:S(2)}) copy-start(f32[1,128]{1,0:T(1,128)} %query_gain_ref.3) | copy-start | bytes 1540
  2.8 24.4 %copy-start.4 = (f32[1,128]{1,0:T(1,128)S(1)}, f32[1,128]{1,0:T(1,128)}, u32[]{:S(2)}) copy-start(f32[1,128]{1,0:T(1,128)} %key_gain_ref.3) | copy-start | bytes 1540
  2.8 24.4 %copy-start.5 = (s32[2,27]{1,0:T(2,128)S(1)}, s32[2,27]{1,0:T(2,128)}, u32[]{:S(2)}) copy-start(s32[2,27]{1,0:T(2,128)} %neighbours_ref.1) | copy-start | bytes 652
  2.8 24.4 %copy-start.6 = (s32[2]{0:T(128)S(1)}, s32[2]{0:T(128)}, u32[]{:S(2)}) copy-start(s32[2]{0:T(128)} %tile_slot_ref.1) | copy-start | bytes 28
  27.1 16.2 %collective-permute-start = (bf16[64,3072]{1,0:T(8,128)(2,1)S(1)}, bf16[64,3072]{1,0:T(8,128)(2,1)S(1)}, u32[]{:S(2)}, u32[]{:S(2)}) collective-permute-start(bf16[64,3072]{1,0:T(8,128)(2,1)S(1)} %bitcast.7), channel_id=1, source_target_pairs={{0,16},{4,20},{8,24},{12,28},{16,0},{20,4},{24,8},{28,12},{1,17},{... | collective-permute-start | bytes 1179656 | tf_op jit(solution)/shard_map/ppermute | solution.py:545
  39.7 20.3 %collective-permute-start.2 = (bf16[64,3072]{1,0:T(8,128)(2,1)S(1)}, bf16[64,3072]{1,0:T(8,128)(2,1)S(1)}, u32[]{:S(2)}, u32[]{:S(2)}) collective-permute-start(bf16[64,3072]{1,0:T(8,128)(2,1)S(1)} %get-tuple-element.25), channel_id=1, source_target_pairs={{0,4},{4,8},{8,12},{12,0},{16,20},{20,24},{24,28},{28,16},{1,5},{5... | collective-permute-start | bytes 1179656 | tf_op jit(solution)/shard_map/ppermute | solution.py:545
  42.3 17.7 %collective-permute-start.3 = (bf16[64,3072]{1,0:T(8,128)(2,1)S(1)}, bf16[64,3072]{1,0:T(8,128)(2,1)S(1)}, u32[]{:S(2)}, u32[]{:S(2)}) collective-permute-start(bf16[64,3072]{1,0:T(8,128)(2,1)S(1)} %get-tuple-element.26), channel_id=1, source_target_pairs={{0,20},{4,24},{8,28},{12,16},{16,4},{20,8},{24,12},{28,0},{1,21},{... | collective-permute-start | bytes 1179656 | tf_op jit(solution)/shard_map/ppermute | solution.py:545
  51.0 8.4 %collective-permute-start.4 = (f32[1,3072]{1,0:T(1,128)S(1)}, f32[1,3072]{1,0:T(1,128)S(1)}, u32[]{:S(2)}, u32[]{:S(2)}) collective-permute-start(f32[1,3072]{1,0:T(1,128)S(1)} %get-tuple-element.27), channel_id=1, source_target_pairs={{0,16},{4,20},{8,24},{12,28},{16,0},{20,4},{24,8},{28,12},{1,17},{... | collective-permute-start | bytes 36872 | tf_op jit(solution)/shard_map/ppermute | solution.py:545
  57.3 11.0 %collective-permute-start.5 = (bf16[64,1536]{1,0:T(8,128)(2,1)S(1)}, bf16[64,1536]{1,0:T(8,128)(2,1)S(1)}, u32[]{:S(2)}, u32[]{:S(2)}) collective-permute-start(bf16[64,1536]{1,0:T(8,128)(2,1)S(1)} %get-tuple-element.29), channel_id=1, source_target_pairs={{0,12},{4,0},{8,4},{12,8},{16,28},{20,16},{24,20},{28,24},{1,13},{... | collective-permute-start | bytes 589832 | tf_op jit(solution)/shard_map/ppermute | solution.py:545
  58.2 10.0 %collective-permute-start.6 = (bf16[64,1536]{1,0:T(8,128)(2,1)S(1)}, bf16[64,1536]{1,0:T(8,128)(2,1)S(1)}, u32[]{:S(2)}, u32[]{:S(2)}) collective-permute-start(bf16[64,1536]{1,0:T(8,128)(2,1)S(1)} %get-tuple-element.30), channel_id=1, source_target_pairs={{0,28},{4,16},{8,20},{12,24},{16,12},{20,0},{24,4},{28,8},{1,29},{... | collective-permute-start | bytes 589832 | tf_op jit(solution)/shard_map/ppermute | solution.py:545
  66.8 6.3 %collective-permute-start.7 = (bf16[64,1536]{1,0:T(8,128)(2,1)S(1)}, bf16[64,1536]{1,0:T(8,128)(2,1)S(1)}, u32[]{:S(2)}, u32[]{:S(2)}) collective-permute-start(bf16[64,1536]{1,0:T(8,128)(2,1)S(1)} %get-tuple-element.32), channel_id=1, source_target_pairs={{0,12},{4,0},{8,4},{12,8},{16,28},{20,16},{24,20},{28,24},{1,13},{... | collective-permute-start | bytes 589832 | tf_op jit(solution)/shard_map/ppermute | solution.py:545
  67.2 7.7 %collective-permute-start.8 = (bf16[64,1536]{1,0:T(8,128)(2,1)S(1)}, bf16[64,1536]{1,0:T(8,128)(2,1)S(1)}, u32[]{:S(2)}, u32[]{:S(2)}) collective-permute-start(bf16[64,1536]{1,0:T(8,128)(2,1)S(1)} %get-tuple-element.33), channel_id=1, source_target_pairs={{0,28},{4,16},{8,20},{12,24},{16,12},{20,0},{24,4},{28,8},{1,29},{... | collective-permute-start | bytes 589832 | tf_op jit(solution)/shard_map/ppermute | solution.py:545

commit v2 on v1

--- a/solution.py
+++ b/solution.py
@@ -224,37 +224,30 @@
     return pltpu.CompilerParams(vmem_limit_bytes=mebibytes * MIB)
 
 
-def regroup_kernel(weight_ref, out_ref, wide_ref):
+def regroup_kernel(weight_ref, out_ref):
     rows, heads, width = weight_ref.shape
-    third = wide_ref.shape[2]
-    for part in range(width // third):
-        piece = weight_ref[:, :, part * third : (part + 1) * third].astype(F32)
-        wide_ref[part] = piece.reshape(rows * heads, third)
+    first = pl.multiple_of(pl.program_id(0) * rows, rows)
+    by_head = jnp.swapaxes(weight_ref[...], 0, 1)
     for head in range(heads):
-        for part in range(width // third):
-            left = (head % 2) * width + part * third
-            out_ref[head // 2, :, left : left + third] = wide_ref[
-                part, pl.ds(head, rows, stride=heads), :
-            ].astype(BF16)
+        left = (head % 2) * width
+        out_ref[head // 2, pl.ds(first, rows), left : left + width] = by_head[head]
 
 
 def regroup(weight, rows):
     depth, heads, width = weight.shape
     pairs = heads // 2
-    third = width // 3
     return pl.pallas_call(
         regroup_kernel,
         grid=(depth // rows,),
-        out_shape=jax.ShapeDtypeStruct((pairs, depth, 2 * width), weight.dtype),
+        out_shape=pltpu.VMEM((pairs, depth, 2 * width), weight.dtype),
         in_specs=[pl.BlockSpec((rows, heads, width), lambda i: (i, 0, 0))],
-        out_specs=pl.BlockSpec((pairs, rows, 2 * width), lambda i: (0, i, 0)),
-        scratch_shapes=[pltpu.VMEM((3, rows * heads, third), F32)],
-        compiler_params=params(46),
+        out_specs=pl.BlockSpec(memory_space=pltpu.VMEM),
+        compiler_params=params(8),
         cost_estimate=pl.CostEstimate(
             flops=0, bytes_accessed=4 * depth * heads * width, transcendentals=0
         ),
         name="regroup",
-    )(weight)
+    )(pltpu.with_memory_space_constraint(weight, pltpu.HBM))
 
 
 def listed_slots(neighbours_ref, tile_slot_ref):
@@ -313,7 +306,7 @@
                 table = jnp.where((row_slot == r) & (column_slot == c), allowed[r][c], table)
         bias_ref[...] = jnp.where(table > 0, 0.0, -jnp.inf).astype(F32)
 
-    projected = dot_nn(tokens_ref[...], weight_ref[0])
+    projected = dot_nn(tokens_ref[...], weight_ref[step])
     projected_ref[0] = projected
     scale_factor = 1.0 / math.sqrt(width)
     bias = bias_ref[...]
@@ -356,6 +349,7 @@
     head_dim = query_gain.shape[1]
     tokens = 2 * local
     whole = lambda i: (0, 0)
+    weight = pltpu.with_memory_space_constraint(weight, pltpu.VMEM)
     smem = pl.BlockSpec(memory_space=pltpu.SMEM)
     return pl.pallas_call(
         forward_kernel,
@@ -372,7 +366,7 @@
             smem,
             pl.BlockSpec((local, model), whole),
             pl.BlockSpec((local, model), whole),
-            pl.BlockSpec((1, model, wide), lambda i: (i, 0, 0)),
+            pl.BlockSpec(memory_space=pltpu.VMEM),
             pl.BlockSpec((2 * head_dim, model), lambda i: (i, 0)),
             pl.BlockSpec((1, head_dim), whole),
             pl.BlockSpec((1, head_dim), whole),
@@ -386,7 +380,7 @@
             pl.BlockSpec((local, model), whole),
         ),
         scratch_shapes=[pltpu.VMEM((tokens, model), BF16), pltpu.VMEM((tokens, tokens), F32)],
-        compiler_params=params(46),
+        compiler_params=params(16),
         cost_estimate=pl.CostEstimate(
             flops=2 * tokens * model * pairs * (wide + 2 * head_dim),
             bytes_accessed=2 * model * pairs * (wide + 2 * head_dim),
@@ -488,7 +482,7 @@
             pl.BlockSpec((1, model // pairs), lambda i: (0, i)),
         ),
         scratch_shapes=[pltpu.VMEM((tokens, model), BF16)],
-        compiler_params=params(46),
+        compiler_params=params(16),
         cost_estimate=pl.CostEstimate(
             flops=2 * tokens * model * pairs * 2 * head_dim,
             bytes_accessed=2 * model * pairs * 2 * head_dim,
@@ -498,12 +492,12 @@
     )(own, other, out_weight, projected, probs, attention, query_gain, key_gain, gate)
 
 
-def input_grad_kernel(grad_ref, weight_ref, own_ref, kept_ref, sent_ref):
-    local = own_ref.shape[0]
-    total = dot_nt(weight_ref[0], grad_ref[0])
+def input_grad_kernel(first, grad_ref, weight_ref, own_ref, kept_ref, sent_ref):
+    local, block = own_ref.shape
+    rows = pl.ds(pl.multiple_of((pl.program_id(0) + first) * block, block), block)
+    total = dot_nt(grad_ref[0], weight_ref[0, rows, :])
     for pair in range(1, grad_ref.shape[0]):
-        total += dot_nt(weight_ref[pair], grad_ref[pair])
-    total = total.T
+        total += dot_nt(grad_ref[pair], weight_ref[pair, rows, :])
     kept_ref[...] = (own_ref[...].astype(F32) + total[:local]).astype(BF16)
     sent_ref[...] = total[local:].astype(BF16)
 
@@ -515,17 +509,18 @@
     first = part * columns // block
     out = jax.ShapeDtypeStruct((local, columns), BF16)
     out_spec = pl.BlockSpec((local, block), lambda i: (0, i))
+    weight = pltpu.with_memory_space_constraint(weight, pltpu.VMEM)
     return pl.pallas_call(
-        input_grad_kernel,
+        functools.partial(input_grad_kernel, first),
         grid=(columns // block,),
         out_shape=(out, out),
         in_specs=[
             pl.BlockSpec((pairs, tokens, wide), lambda i: (0, 0, 0)),
-            pl.BlockSpec((pairs, block, wide), lambda i: (0, i + first, 0)),
+            pl.BlockSpec(memory_space=pltpu.VMEM),
             pl.BlockSpec((local, block), lambda i: (0, i + first)),
         ],
         out_specs=(out_spec, out_spec),
-        compiler_params=params(46),
+        compiler_params=params(12),
         cost_estimate=pl.CostEstimate(
             flops=2 * tokens * columns * pairs * wide,
             bytes_accessed=2 * columns * pairs * wide,

time: 76.5 us -> 75.3 us (0.984)
  Pallas kernels: 56.4 us -> 39.8 us
  local copies, waits for them, and re-layouts: 0.03 us -> 15.6 us
    unnamed x14 -> x30, local copies, waits for them, and re-layouts: 0.03 us -> 15.6 us
    pallas_call x3, Pallas kernels: 36.2 us -> 24 us  [the longest x1 17 us: regroup(): pl.pallas_call(regroup_kernel, grid=(depth // rows,), out_shape=pltpu.VME...]
    pallas_call x1, Pallas kernels: 12.5 us -> 9.4 us  [forward(): pl.pallas_call(forward_kernel, grid=(pairs,), out_shape=(jax.ShapeDtypeSt...]
    pallas_call x1, Pallas kernels: 7.74 us -> 6.41 us  [backward(): pl.pallas_call(backward_kernel, grid=(pairs,), out_shape=(jax.ShapeDtypeS...]
  transfers between devices with their start and end apart: 9 -> 9, of which waited for: 2 -> 2; matrix products, arithmetic and copies ran while one was open for 2% -> 2% of each run, Pallas kernels for 74% -> 53%
where the time goes in v2:
time: 75.3 us; the launch traced here: 74.8 us
  Pallas kernels  39.8 us (53%)
  local copies, waits for them, and re-layouts  15.6 us (21%)
  starting transfers between devices  9.67 us (13%)
  waiting for transfers between devices  6.63 us (9%)
  other arithmetic  2.31 us (3%)
  between operations  0.8 us (1%)
    pallas_call x1, Pallas kernels, regroup(): pl.pallas_call(regroup_kernel, grid=(depth // rows,), out_shape=pltpu.VME...  17 us
    unnamed x30, local copies, waits for them, and re-layouts  15.6 us
    ppermute x9, starting transfers between devices, routed(): return lax.ppermute(block, ('seq', 'pipe'), route)  9.67 us
    pallas_call x1, Pallas kernels, forward(): pl.pallas_call(forward_kernel, grid=(pairs,), out_shape=(jax.ShapeDtypeSt...  9.4 us
    pallas_call x2, Pallas kernels, input_grad_part(): pl.pallas_call(functools.partial(input_grad_kernel, first), grid=(columns...  6.99 us
    ppermute x9, waiting for transfers between devices, routed(): return lax.ppermute(block, ('seq', 'pipe'), route)  6.63 us
    pallas_call x1, Pallas kernels, backward(): pl.pallas_call(backward_kernel, grid=(pairs,), out_shape=(jax.ShapeDtypeS...  6.41 us
  transfers between devices with their start and end apart: 9, of which 2 were waited for; matrix products, arithmetic and copies ran while one was open for 2% of the time, Pallas kernels for 53%

profile of v2, /device:TPU:1, one launch (start us, length us, event | category | flops | bytes accessed | tf_op | source)
XLA Modules:
  0.0 74.8 jit_solution(16129465363201284129)
XLA Ops:
  0.6 2.1 %collective-permute-start.1 = (bf16[64,3072]{1,0:T(8,128)(2,1)}, bf16[64,3072]{1,0:T(8,128)(2,1)S(1)}, u32[]{:S(2)}, u32[]{:S(2)}) collective-permute-start(bf16[64,3072]{1,0:T(8,128)(2,1)} %bitcast.15), channel_id=1, source_target_pairs={{0,16},{4,20},{8,24},{12,28},{16,0},{20,4},{24,8},{28,12},{1,17},{... | collective-permute-start | bytes 1179656 | tf_op jit(solution)/shard_map/ppermute | solution.py:540
  2.8 17.0 %regroup.1.weight_ref = bf16[4,3072,768]{2,1,0:T(8,128)(2,1)S(1)} custom-call(bf16[3072,8,384]{2,1,0:T(8,128)(2,1)} %bitcast.17), custom_call_target="tpu_custom_call" | custom-call | bytes 37748736 | tf_op jit(solution)/shard_map/regroup/pallas_call | solution.py:239
  19.8 6.4 %copy-done = bf16[4,3072,768]{2,1,0:T(8,128)(2,1)} copy-done((bf16[4,3072,768]{2,1,0:T(8,128)(2,1)}, bf16[4,3072,768]{2,1,0:T(8,128)(2,1)S(1)}, u32[]{:S(2)}) %copy-start) | copy-done | bytes 18874392
  26.2 0.0 collective-permute-start
  26.3 0.0 collective-permute-done.1.other_ref
  26.3 0.0 copy-done.5
  26.3 6.4 %copy-done.1 = bf16[4,3072,768]{2,1,0:T(8,128)(2,1)S(1)} copy-done((bf16[4,3072,768]{2,1,0:T(8,128)(2,1)S(1)}, bf16[4,3072,768]{2,1,0:T(8,128)(2,1)}, u32[]{:S(2)}) %copy-start.1) | copy-done | bytes 18874392
  32.7 2.8 %copy-done.2 = bf16[1,1024,3072]{2,1,0:T(8,128)(2,1)S(1)} copy-done((bf16[1,1024,3072]{2,1,0:T(8,128)(2,1)S(1)}, bf16[1,1024,3072]{2,1,0:T(8,128)(2,1)}, u32[]{:S(2)}) %copy-start.2) | copy-done | bytes 6291480
  35.5 9.4 %attention_forward.1 = (f32[4,128,768]{2,1,0:T(8,128)S(1)}, bf16[8,128,128]{2,1,0:T(8,128)(2,1)S(1)}, f32[128,3072]{1,0:T(8,128)S(1)}, bf16[64,3072]{1,0:T(8,128)(2,1)S(1)}, bf16[64,3072]{1,0:T(8,128)(2,1)S(1)}) custom-call(s32[2,27]{1,0:T(2,128)S(1)} %copy-done.8, s32[2]{0:T(128)S(1)} %copy-done.9, bf16[64,3072]{1,0:T(8,128)(2,1)S(1)} %bitcast.16, ...), custom_call_target="tpu_custom_call" | custom-call | flops 3221225472 | bytes 25165824 | tf_op jit(solution)/shard_map/attention_forward/pallas_call | solution.py:354
  44.9 2.6 %collective-permute-start.2 = (bf16[64,3072]{1,0:T(8,128)(2,1)S(1)}, bf16[64,3072]{1,0:T(8,128)(2,1)S(1)}, u32[]{:S(2)}, u32[]{:S(2)}) collective-permute-start(bf16[64,3072]{1,0:T(8,128)(2,1)S(1)} %get-tuple-element.25), channel_id=1, source_target_pairs={{0,4},{4,8},{8,12},{12,0},{16,20},{20,24},{24,28},{28,16},{1,5},{5... | collective-permute-start | bytes 1179656 | tf_op jit(solution)/shard_map/ppermute | solution.py:540
  47.5 1.0 %collective-permute-start.3 = (bf16[64,3072]{1,0:T(8,128)(2,1)S(1)}, bf16[64,3072]{1,0:T(8,128)(2,1)S(1)}, u32[]{:S(2)}, u32[]{:S(2)}) collective-permute-start(bf16[64,3072]{1,0:T(8,128)(2,1)S(1)} %get-tuple-element.26), channel_id=1, source_target_pairs={{0,20},{4,24},{8,28},{12,16},{16,4},{20,8},{24,12},{28,0},{1,21},{... | collective-permute-start | bytes 1179656 | tf_op jit(solution)/shard_map/ppermute | solution.py:540
  48.5 0.0 collective-permute-done.other_ref
  48.5 6.4 %attention_backward.1 = (bf16[4,128,768]{2,1,0:T(8,128)(2,1)S(1)}, f32[1,3072]{1,0:T(1,128)S(1)}) custom-call(bf16[64,3072]{1,0:T(8,128)(2,1)S(1)} %bitcast.12, bf16[64,3072]{1,0:T(8,128)(2,1)S(1)} %collective-permute-done.other_ref, bf16[1024,3072]{1,0:T(8,128)(2,1)S(1)} %bitcast.10, f32[4,128,768]{2,1,0:T(8,128)S(1)} %get-tuple-element.21.projected_ref, ...), custom_call_target="tpu_custom_call" | custom-call | flops 805306368 | bytes 6291456 | tf_op jit(solution)/shard_map/attention_backward/pallas_call | solution.py:462
  54.9 0.3 collective-permute-start.4
  55.3 0.0 slice-done.3
  55.3 0.0 slice-done.4
  55.3 3.5 %input_grad.2 = (bf16[64,1536]{1,0:T(8,128)(2,1)S(1)}, bf16[64,1536]{1,0:T(8,128)(2,1)S(1)}) custom-call(bf16[4,128,768]{2,1,0:T(8,128)(2,1)S(1)} %get-tuple-element.31.grad_ref, bf16[4,3072,768]{2,1,0:T(8,128)(2,1)S(1)} %bitcast.8, bf16[64,3072]{1,0:T(8,128)(2,1)S(1)} %bitcast.13), custom_call_target="tpu_custom_call" | custom-call | flops 1207959552 | bytes 9437184 | tf_op jit(solution)/shard_map/input_grad/pallas_call | solution.py:513
  58.8 1.0 %collective-permute-start.5 = (bf16[64,1536]{1,0:T(8,128)(2,1)S(1)}, bf16[64,1536]{1,0:T(8,128)(2,1)S(1)}, u32[]{:S(2)}, u32[]{:S(2)}) collective-permute-start(bf16[64,1536]{1,0:T(8,128)(2,1)S(1)} %get-tuple-element.29), channel_id=1, source_target_pairs={{0,12},{4,0},{8,4},{12,8},{16,28},{20,16},{24,20},{28,24},{1,13},{... | collective-permute-start | bytes 589832 | tf_op jit(solution)/shard_map/ppermute | solution.py:540
  59.7 1.2 %collective-permute-start.6 = (bf16[64,1536]{1,0:T(8,128)(2,1)S(1)}, bf16[64,1536]{1,0:T(8,128)(2,1)S(1)}, u32[]{:S(2)}, u32[]{:S(2)}) collective-permute-start(bf16[64,1536]{1,0:T(8,128)(2,1)S(1)} %get-tuple-element.30), channel_id=1, source_target_pairs={{0,28},{4,16},{8,20},{12,24},{16,12},{20,0},{24,4},{28,8},{1,29},{... | collective-permute-start | bytes 589832 | tf_op jit(solution)/shard_map/ppermute | solution.py:540
  60.9 0.0 collective-permute-done.4
  60.9 0.6 dynamic-slice_add_fusion
  61.5 0.0 collective-permute-done.2
  61.5 0.0 collective-permute-done.3
  61.5 0.8 %add_convert_fusion = bf16[64,3072]{1,0:T(8,128)(2,1)} fusion(bf16[64,3072]{1,0:T(8,128)(2,1)S(1)} %collective-permute-done.3, bf16[64,3072]{1,0:T(8,128)(2,1)S(1)} %collective-permute-done.2), kind=kLoop, calls=%fused_computation | loop fusion | flops 786432 | bytes 1179648 | tf_op jit(solution)/shard_map/convert_element_type | solution.py:589
  62.4 3.5 %input_grad.3 = (bf16[64,1536]{1,0:T(8,128)(2,1)S(1)}, bf16[64,1536]{1,0:T(8,128)(2,1)S(1)}) custom-call(bf16[4,128,768]{2,1,0:T(8,128)(2,1)S(1)} %get-tuple-element.31.grad_ref, bf16[4,3072,768]{2,1,0:T(8,128)(2,1)S(1)} %bitcast.8, bf16[64,3072]{1,0:T(8,128)(2,1)S(1)} %bitcast.14), custom_call_target="tpu_custom_call" | custom-call | flops 1207959552 | bytes 9437184 | tf_op jit(solution)/shard_map/input_grad/pallas_call | solution.py:513
  65.9 0.4 collective-permute-start.7
  66.3 1.0 %collective-permute-start.8 = (bf16[64,1536]{1,0:T(8,128)(2,1)S(1)}, bf16[64,1536]{1,0:T(8,128)(2,1)S(1)}, u32[]{:S(2)}, u32[]{:S(2)}) collective-permute-start(bf16[64,1536]{1,0:T(8,128)(2,1)S(1)} %get-tuple-element.33), channel_id=1, source_target_pairs={{0,28},{4,16},{8,20},{12,24},{16,12},{20,0},{24,4},{28,8},{1,29},{... | collective-permute-start | bytes 589832 | tf_op jit(solution)/shard_map/ppermute | solution.py:540
  67.3 0.0 collective-permute-done.5
  67.3 0.0 collective-permute-done.6
  67.4 4.8 %collective-permute-done.7 = bf16[64,1536]{1,0:T(8,128)(2,1)S(1)} collective-permute-done((bf16[64,1536]{1,0:T(8,128)(2,1)S(1)}, bf16[64,1536]{1,0:T(8,128)(2,1)S(1)}, u32[]{:S(2)}, u32[]{:S(2)}) %collective-permute-start.7) | collective-permute-done | bytes 196640 | tf_op jit(solution)/shard_map/ppermute | solution.py:540
  72.2 1.8 %collective-permute-done.8 = bf16[64,1536]{1,0:T(8,128)(2,1)S(1)} collective-permute-done((bf16[64,1536]{1,0:T(8,128)(2,1)S(1)}, bf16[64,1536]{1,0:T(8,128)(2,1)S(1)}, u32[]{:S(2)}, u32[]{:S(2)}) %collective-permute-start.8) | collective-permute-done | bytes 196640 | tf_op jit(solution)/shard_map/ppermute | solution.py:540
  74.0 0.8 %maximum_bitcast_fusion = bf16[1,64,3072]{2,1,0:T(8,128)(2,1)} fusion(bf16[64,1536]{1,0:T(8,128)(2,1)S(1)} %add_convert_fusion.1, bf16[64,1536]{1,0:T(8,128)(2,1)S(1)} %add_convert_fusion.2), kind=kLoop, calls=%fused_computation.1 | loop fusion | flops 786432 | bytes 786432 | tf_op jit(solution)/shard_map/broadcast_in_dim | solution.py:600
  (27 shorter events, 0.1 us)
Async XLA Ops:
  0.6 25.6 %collective-permute-start.1 = (bf16[64,3072]{1,0:T(8,128)(2,1)}, bf16[64,3072]{1,0:T(8,128)(2,1)S(1)}, u32[]{:S(2)}, u32[]{:S(2)}) collective-permute-start(bf16[64,3072]{1,0:T(8,128)(2,1)} %bitcast.15), channel_id=1, source_target_pairs={{0,16},{4,20},{8,24},{12,28},{16,0},{20,4},{24,8},{28,12},{1,17},{... | collective-permute-start | bytes 1179656 | tf_op jit(solution)/shard_map/ppermute | solution.py:540
  2.7 23.5 %copy-start.3 = (bf16[1,64,3072]{2,1,0:T(8,128)(2,1)S(1)}, bf16[1,64,3072]{2,1,0:T(8,128)(2,1)}, u32[]{:S(2)}) copy-start(bf16[1,64,3072]{2,1,0:T(8,128)(2,1)} %param.10) | copy-start | bytes 1179652
  2.7 23.5 %copy-start.4 = (bf16[1,64,3072]{2,1,0:T(8,128)(2,1)S(1)}, bf16[1,64,3072]{2,1,0:T(8,128)(2,1)}, u32[]{:S(2)}) copy-start(bf16[1,64,3072]{2,1,0:T(8,128)(2,1)} %param.9) | copy-start | bytes 1179652
  2.7 23.5 %copy-start.5 = (f32[1,3072]{1,0:T(1,128)S(1)}, f32[1,3072]{1,0:T(1,128)}, u32[]{:S(2)}) copy-start(f32[1,3072]{1,0:T(1,128)} %gate_ref.3) | copy-start | bytes 36868
  2.7 23.5 %copy-start.6 = (f32[1,128]{1,0:T(1,128)S(1)}, f32[1,128]{1,0:T(1,128)}, u32[]{:S(2)}) copy-start(f32[1,128]{1,0:T(1,128)} %query_gain_ref.3) | copy-start | bytes 1540
  2.8 23.5 %copy-start.7 = (f32[1,128]{1,0:T(1,128)S(1)}, f32[1,128]{1,0:T(1,128)}, u32[]{:S(2)}) copy-start(f32[1,128]{1,0:T(1,128)} %key_gain_ref.3) | copy-start | bytes 1540
  2.8 23.5 %copy-start.8 = (s32[2,27]{1,0:T(2,128)S(1)}, s32[2,27]{1,0:T(2,128)}, u32[]{:S(2)}) copy-start(s32[2,27]{1,0:T(2,128)} %neighbours_ref.1) | copy-start | bytes 652
  2.8 23.5 %copy-start.9 = (s32[2]{0:T(128)S(1)}, s32[2]{0:T(128)}, u32[]{:S(2)}) copy-start(s32[2]{0:T(128)} %tile_slot_ref.1) | copy-start | bytes 28
  19.8 6.4 %copy-start = (bf16[4,3072,768]{2,1,0:T(8,128)(2,1)}, bf16[4,3072,768]{2,1,0:T(8,128)(2,1)S(1)}, u32[]{:S(2)}) copy-start(bf16[4,3072,768]{2,1,0:T(8,128)(2,1)S(1)} %regroup.1.weight_ref) | copy-start | bytes 56623108
  26.2 22.3 %collective-permute-start = (bf16[64,3072]{1,0:T(8,128)(2,1)S(1)}, bf16[64,3072]{1,0:T(8,128)(2,1)S(1)}, u32[]{:S(2)}, u32[]{:S(2)}) collective-permute-start(bf16[64,3072]{1,0:T(8,128)(2,1)S(1)} %bitcast.11), channel_id=1, source_target_pairs={{0,16},{4,20},{8,24},{12,28},{16,0},{20,4},{24,8},{28,12},{1,17},{... | collective-permute-start | bytes 1179656 | tf_op jit(solution)/shard_map/ppermute | solution.py:540
  26.3 6.4 %copy-start.1 = (bf16[4,3072,768]{2,1,0:T(8,128)(2,1)S(1)}, bf16[4,3072,768]{2,1,0:T(8,128)(2,1)}, u32[]{:S(2)}) copy-start(bf16[4,3072,768]{2,1,0:T(8,128)(2,1)} %copy-done) | copy-start | bytes 56623108
  32.7 2.8 %copy-start.2 = (bf16[1,1024,3072]{2,1,0:T(8,128)(2,1)S(1)}, bf16[1,1024,3072]{2,1,0:T(8,128)(2,1)}, u32[]{:S(2)}) copy-start(bf16[1,1024,3072]{2,1,0:T(8,128)(2,1)} %param.12) | copy-start | bytes 18874372
  35.5 19.8 %slice-start = ((s8[18874368]{0:T(1024)(128)(4,1)}), s8[2097152]{0:T(1024)(128)(4,1)S(1)}, s32[]{:S(2)}) async-start(s8[18874368]{0:T(1024)(128)(4,1)} %bitcast.7), calls=%async_computation | async-start | bytes 4194304
  35.5 19.8 %slice-start.1 = ((s8[18874368]{0:T(1024)(128)(4,1)}), s8[4194304]{0:T(1024)(128)(4,1)S(1)}, s32[]{:S(2)}) async-start(s8[18874368]{0:T(1024)(128)(4,1)} %bitcast.7), calls=%async_computation.1 | async-start | bytes 8388608
  35.5 19.8 %slice-start.2 = ((s8[18874368]{0:T(1024)(128)(4,1)}), s8[4194304]{0:T(1024)(128)(4,1)S(1)}, s32[]{:S(2)}) async-start(s8[18874368]{0:T(1024)(128)(4,1)} %bitcast.7), calls=%async_computation.2 | async-start | bytes 8388608
  35.5 19.8 %slice-start.3 = ((s8[18874368]{0:T(1024)(128)(4,1)}), s8[4194304]{0:T(1024)(128)(4,1)S(1)}, s32[]{:S(2)}) async-start(s8[18874368]{0:T(1024)(128)(4,1)} %bitcast.7), calls=%async_computation.3 | async-start | bytes 8388608
  44.9 16.6 %collective-permute-start.2 = (bf16[64,3072]{1,0:T(8,128)(2,1)S(1)}, bf16[64,3072]{1,0:T(8,128)(2,1)S(1)}, u32[]{:S(2)}, u32[]{:S(2)}) collective-permute-start(bf16[64,3072]{1,0:T(8,128)(2,1)S(1)} %get-tuple-element.25), channel_id=1, source_target_pairs={{0,4},{4,8},{8,12},{12,0},{16,20},{20,24},{24,28},{28,16},{1,5},{5... | collective-permute-start | bytes 1179656 | tf_op jit(solution)/shard_map/ppermute | solution.py:540
  47.5 14.0 %collective-permute-start.3 = (bf16[64,3072]{1,0:T(8,128)(2,1)S(1)}, bf16[64,3072]{1,0:T(8,128)(2,1)S(1)}, u32[]{:S(2)}, u32[]{:S(2)}) collective-permute-start(bf16[64,3072]{1,0:T(8,128)(2,1)S(1)} %get-tuple-element.26), channel_id=1, source_target_pairs={{0,20},{4,24},{8,28},{12,16},{16,4},{20,8},{24,12},{28,0},{1,21},{... | collective-permute-start | bytes 1179656 | tf_op jit(solution)/shard_map/ppermute | solution.py:540
  48.5 6.8 %slice-start.4 = ((s8[18874368]{0:T(1024)(128)(4,1)}), s8[4194304]{0:T(1024)(128)(4,1)S(1)}, s32[]{:S(2)}) async-start(s8[18874368]{0:T(1024)(128)(4,1)} %bitcast.7), calls=%async_computation.4 | async-start | bytes 8388608
  54.9 6.0 %collective-permute-start.4 = (f32[1,3072]{1,0:T(1,128)S(1)}, f32[1,3072]{1,0:T(1,128)S(1)}, u32[]{:S(2)}, u32[]{:S(2)}) collective-permute-start(f32[1,3072]{1,0:T(1,128)S(1)} %get-tuple-element.27), channel_id=1, source_target_pairs={{0,16},{4,20},{8,24},{12,28},{16,0},{20,4},{24,8},{28,12},{1,17},{... | collective-permute-start | bytes 36872 | tf_op jit(solution)/shard_map/ppermute | solution.py:540
  58.8 8.5 %collective-permute-start.5 = (bf16[64,1536]{1,0:T(8,128)(2,1)S(1)}, bf16[64,1536]{1,0:T(8,128)(2,1)S(1)}, u32[]{:S(2)}, u32[]{:S(2)}) collective-permute-start(bf16[64,1536]{1,0:T(8,128)(2,1)S(1)} %get-tuple-element.29), channel_id=1, source_target_pairs={{0,12},{4,0},{8,4},{12,8},{16,28},{20,16},{24,20},{28,24},{1,13},{... | collective-permute-start | bytes 589832 | tf_op jit(solution)/shard_map/ppermute | solution.py:540
  59.7 7.6 %collective-permute-start.6 = (bf16[64,1536]{1,0:T(8,128)(2,1)S(1)}, bf16[64,1536]{1,0:T(8,128)(2,1)S(1)}, u32[]{:S(2)}, u32[]{:S(2)}) collective-permute-start(bf16[64,1536]{1,0:T(8,128)(2,1)S(1)} %get-tuple-element.30), channel_id=1, source_target_pairs={{0,28},{4,16},{8,20},{12,24},{16,12},{20,0},{24,4},{28,8},{1,29},{... | collective-permute-start | bytes 589832 | tf_op jit(solution)/shard_map/ppermute | solution.py:540
  65.9 6.4 %collective-permute-start.7 = (bf16[64,1536]{1,0:T(8,128)(2,1)S(1)}, bf16[64,1536]{1,0:T(8,128)(2,1)S(1)}, u32[]{:S(2)}, u32[]{:S(2)}) collective-permute-start(bf16[64,1536]{1,0:T(8,128)(2,1)S(1)} %get-tuple-element.32), channel_id=1, source_target_pairs={{0,12},{4,0},{8,4},{12,8},{16,28},{20,16},{24,20},{28,24},{1,13},{... | collective-permute-start | bytes 589832 | tf_op jit(solution)/shard_map/ppermute | solution.py:540
  66.3 7.7 %collective-permute-start.8 = (bf16[64,1536]{1,0:T(8,128)(2,1)S(1)}, bf16[64,1536]{1,0:T(8,128)(2,1)S(1)}, u32[]{:S(2)}, u32[]{:S(2)}) collective-permute-start(bf16[64,1536]{1,0:T(8,128)(2,1)S(1)} %get-tuple-element.33), channel_id=1, source_target_pairs={{0,28},{4,16},{8,20},{12,24},{16,12},{20,0},{24,4},{28,8},{1,29},{... | collective-permute-start | bytes 589832 | tf_op jit(solution)/shard_map/ppermute | solution.py:540

commit v3 on v2

--- a/solution.py
+++ b/solution.py
@@ -224,7 +224,8 @@
     return pltpu.CompilerParams(vmem_limit_bytes=mebibytes * MIB)
 
 
-def regroup_kernel(weight_ref, out_ref):
+def regroup_kernel(weight_ref, out_ref, token_ref):
+    token_ref[...] = jnp.zeros_like(token_ref)
     rows, heads, width = weight_ref.shape
     first = pl.multiple_of(pl.program_id(0) * rows, rows)
     by_head = jnp.swapaxes(weight_ref[...], 0, 1)
@@ -239,9 +240,15 @@
     return pl.pallas_call(
         regroup_kernel,
         grid=(depth // rows,),
-        out_shape=pltpu.VMEM((pairs, depth, 2 * width), weight.dtype),
+        out_shape=(
+            pltpu.VMEM((pairs, depth, 2 * width), weight.dtype),
+            jax.ShapeDtypeStruct((8, 128), F32),
+        ),
         in_specs=[pl.BlockSpec((rows, heads, width), lambda i: (i, 0, 0))],
-        out_specs=pl.BlockSpec(memory_space=pltpu.VMEM),
+        out_specs=(
+            pl.BlockSpec(memory_space=pltpu.VMEM),
+            pl.BlockSpec((8, 128), lambda i: (0, 0)),
+        ),
         compiler_params=params(8),
         cost_estimate=pl.CostEstimate(
             flops=0, bytes_accessed=4 * depth * heads * width, transcendentals=0
@@ -556,8 +563,8 @@
     out_local = out_weight[0]
     model = stream.shape[1]
     other_stream = routed(stream, 1, 0)
-    weight = regroup(qkv_weight[0], 128)
-    weight, upstream_after = lax.optimization_barrier((weight, upstream))
+    weight, regrouped = regroup(qkv_weight[0], 128)
+    regrouped, upstream_after = lax.optimization_barrier((regrouped, upstream))
     other_upstream = routed(upstream_after, 1, 0)
     projected, probs, attention, kept, sent = forward(
         neighbours,

time: 75.3 us -> 75.9 us (level)
  no operation moved by 1% of the time
where the time goes in v3:
time: 75.9 us; the launch traced here: 75.4 us
  Pallas kernels  40.3 us (53%)
  local copies, waits for them, and re-layouts  15.6 us (21%)
  starting transfers between devices  9.67 us (13%)
  waiting for transfers between devices  6.63 us (9%)
  other arithmetic  2.31 us (3%)
  between operations  0.78 us (1%)
    pallas_call x1, Pallas kernels, regroup(): pl.pallas_call(regroup_kernel, grid=(depth // rows,), out_shape=(pltpu.VM...  17.4 us
    unnamed x30, local copies, waits for them, and re-layouts  15.6 us
    ppermute x9, starting transfers between devices, routed(): return lax.ppermute(block, ('seq', 'pipe'), route)  9.67 us
    pallas_call x1, Pallas kernels, forward(): pl.pallas_call(forward_kernel, grid=(pairs,), out_shape=(jax.ShapeDtypeSt...  9.55 us
    pallas_call x2, Pallas kernels, input_grad_part(): pl.pallas_call(functools.partial(input_grad_kernel, first), grid=(columns...  6.99 us
    ppermute x9, waiting for transfers between devices, routed(): return lax.ppermute(block, ('seq', 'pipe'), route)  6.63 us
    pallas_call x1, Pallas kernels, backward(): pl.pallas_call(backward_kernel, grid=(pairs,), out_shape=(jax.ShapeDtypeS...  6.43 us
  transfers between devices with their start and end apart: 9, of which 2 were waited for; matrix products, arithmetic and copies ran while one was open for 2% of the time, Pallas kernels for 53%

profile of v3, /device:TPU:1, one launch (start us, length us, event | category | flops | bytes accessed | tf_op | source)
XLA Modules:
  0.0 75.4 jit_solution(11818401500090072733)
XLA Ops:
  0.6 2.1 %collective-permute-start.1 = (bf16[64,3072]{1,0:T(8,128)(2,1)}, bf16[64,3072]{1,0:T(8,128)(2,1)S(1)}, u32[]{:S(2)}, u32[]{:S(2)}) collective-permute-start(bf16[64,3072]{1,0:T(8,128)(2,1)} %bitcast.15), channel_id=1, source_target_pairs={{0,16},{4,20},{8,24},{12,28},{16,0},{20,4},{24,8},{28,12},{1,17},{... | collective-permute-start | bytes 1179656 | tf_op jit(solution)/shard_map/ppermute | solution.py:547
  2.7 0.1 collective-permute-start
  2.8 0.0 copy-start.8
  2.8 0.0 copy-start.9
  2.8 17.4 %regroup.1 = (bf16[4,3072,768]{2,1,0:T(8,128)(2,1)S(1)}, f32[8,128]{1,0:T(8,128)}) custom-call(bf16[3072,8,384]{2,1,0:T(8,128)(2,1)} %bitcast.17), custom_call_target="tpu_custom_call" | custom-call | bytes 37748736 | tf_op jit(solution)/shard_map/regroup/pallas_call | solution.py:240
  20.2 6.4 %copy-done = bf16[4,3072,768]{2,1,0:T(8,128)(2,1)} copy-done((bf16[4,3072,768]{2,1,0:T(8,128)(2,1)}, bf16[4,3072,768]{2,1,0:T(8,128)(2,1)S(1)}, u32[]{:S(2)}) %copy-start) | copy-done | bytes 18874392
  26.6 0.0 collective-permute-done.1.other_ref
  26.7 6.4 %copy-done.1 = bf16[4,3072,768]{2,1,0:T(8,128)(2,1)S(1)} copy-done((bf16[4,3072,768]{2,1,0:T(8,128)(2,1)S(1)}, bf16[4,3072,768]{2,1,0:T(8,128)(2,1)}, u32[]{:S(2)}) %copy-start.1) | copy-done | bytes 18874392
  33.1 2.8 %copy-done.2 = bf16[1,1024,3072]{2,1,0:T(8,128)(2,1)S(1)} copy-done((bf16[1,1024,3072]{2,1,0:T(8,128)(2,1)S(1)}, bf16[1,1024,3072]{2,1,0:T(8,128)(2,1)}, u32[]{:S(2)}) %copy-start.2) | copy-done | bytes 6291480
  35.9 0.0 slice-start.3
  35.9 9.6 %attention_forward.1 = (f32[4,128,768]{2,1,0:T(8,128)S(1)}, bf16[8,128,128]{2,1,0:T(8,128)(2,1)S(1)}, f32[128,3072]{1,0:T(8,128)S(1)}, bf16[64,3072]{1,0:T(8,128)(2,1)S(1)}, bf16[64,3072]{1,0:T(8,128)(2,1)S(1)}) custom-call(s32[2,27]{1,0:T(2,128)S(1)} %copy-done.8, s32[2]{0:T(128)S(1)} %copy-done.9, bf16[64,3072]{1,0:T(8,128)(2,1)S(1)} %bitcast.16, ...), custom_call_target="tpu_custom_call" | custom-call | flops 3221225472 | bytes 25165824 | tf_op jit(solution)/shard_map/attention_forward/pallas_call | solution.py:361
  45.4 2.6 %collective-permute-start.2 = (bf16[64,3072]{1,0:T(8,128)(2,1)S(1)}, bf16[64,3072]{1,0:T(8,128)(2,1)S(1)}, u32[]{:S(2)}, u32[]{:S(2)}) collective-permute-start(bf16[64,3072]{1,0:T(8,128)(2,1)S(1)} %get-tuple-element.23), channel_id=1, source_target_pairs={{0,4},{4,8},{8,12},{12,0},{16,20},{20,24},{24,28},{28,16},{1,5},{5... | collective-permute-start | bytes 1179656 | tf_op jit(solution)/shard_map/ppermute | solution.py:547
  48.0 1.0 %collective-permute-start.3 = (bf16[64,3072]{1,0:T(8,128)(2,1)S(1)}, bf16[64,3072]{1,0:T(8,128)(2,1)S(1)}, u32[]{:S(2)}, u32[]{:S(2)}) collective-permute-start(bf16[64,3072]{1,0:T(8,128)(2,1)S(1)} %get-tuple-element.24), channel_id=1, source_target_pairs={{0,20},{4,24},{8,28},{12,16},{16,4},{20,8},{24,12},{28,0},{1,21},{... | collective-permute-start | bytes 1179656 | tf_op jit(solution)/shard_map/ppermute | solution.py:547
  49.0 0.0 collective-permute-done.other_ref
  49.0 6.4 %attention_backward.1 = (bf16[4,128,768]{2,1,0:T(8,128)(2,1)S(1)}, f32[1,3072]{1,0:T(1,128)S(1)}) custom-call(bf16[64,3072]{1,0:T(8,128)(2,1)S(1)} %bitcast.12, bf16[64,3072]{1,0:T(8,128)(2,1)S(1)} %collective-permute-done.other_ref, bf16[1024,3072]{1,0:T(8,128)(2,1)S(1)} %bitcast.10, f32[4,128,768]{2,1,0:T(8,128)S(1)} %get-tuple-element.19.projected_ref, ...), custom_call_target="tpu_custom_call" | custom-call | flops 805306368 | bytes 6291456 | tf_op jit(solution)/shard_map/attention_backward/pallas_call | solution.py:469
  55.5 0.3 collective-permute-start.4
  55.8 3.5 %input_grad.2 = (bf16[64,1536]{1,0:T(8,128)(2,1)S(1)}, bf16[64,1536]{1,0:T(8,128)(2,1)S(1)}) custom-call(bf16[4,128,768]{2,1,0:T(8,128)(2,1)S(1)} %get-tuple-element.29.grad_ref, bf16[4,3072,768]{2,1,0:T(8,128)(2,1)S(1)} %bitcast.8, bf16[64,3072]{1,0:T(8,128)(2,1)S(1)} %bitcast.13), custom_call_target="tpu_custom_call" | custom-call | flops 1207959552 | bytes 9437184 | tf_op jit(solution)/shard_map/input_grad/pallas_call | solution.py:520
  59.3 0.9 %collective-permute-start.5 = (bf16[64,1536]{1,0:T(8,128)(2,1)S(1)}, bf16[64,1536]{1,0:T(8,128)(2,1)S(1)}, u32[]{:S(2)}, u32[]{:S(2)}) collective-permute-start(bf16[64,1536]{1,0:T(8,128)(2,1)S(1)} %get-tuple-element.27), channel_id=1, source_target_pairs={{0,12},{4,0},{8,4},{12,8},{16,28},{20,16},{24,20},{28,24},{1,13},{... | collective-permute-start | bytes 589832 | tf_op jit(solution)/shard_map/ppermute | solution.py:547
  60.3 1.2 %collective-permute-start.6 = (bf16[64,1536]{1,0:T(8,128)(2,1)S(1)}, bf16[64,1536]{1,0:T(8,128)(2,1)S(1)}, u32[]{:S(2)}, u32[]{:S(2)}) collective-permute-start(bf16[64,1536]{1,0:T(8,128)(2,1)S(1)} %get-tuple-element.28), channel_id=1, source_target_pairs={{0,28},{4,16},{8,20},{12,24},{16,12},{20,0},{24,4},{28,8},{1,29},{... | collective-permute-start | bytes 589832 | tf_op jit(solution)/shard_map/ppermute | solution.py:547
  61.4 0.0 collective-permute-done.4
  61.4 0.6 dynamic-slice_add_fusion
  62.0 0.0 collective-permute-done.2
  62.0 0.0 collective-permute-done.3
  62.0 0.8 %add_convert_fusion = bf16[64,3072]{1,0:T(8,128)(2,1)} fusion(bf16[64,3072]{1,0:T(8,128)(2,1)S(1)} %collective-permute-done.3, bf16[64,3072]{1,0:T(8,128)(2,1)S(1)} %collective-permute-done.2), kind=kLoop, calls=%fused_computation | loop fusion | flops 786432 | bytes 1179648 | tf_op jit(solution)/shard_map/convert_element_type | solution.py:596
  62.9 3.5 %input_grad.3 = (bf16[64,1536]{1,0:T(8,128)(2,1)S(1)}, bf16[64,1536]{1,0:T(8,128)(2,1)S(1)}) custom-call(bf16[4,128,768]{2,1,0:T(8,128)(2,1)S(1)} %get-tuple-element.29.grad_ref, bf16[4,3072,768]{2,1,0:T(8,128)(2,1)S(1)} %bitcast.8, bf16[64,3072]{1,0:T(8,128)(2,1)S(1)} %bitcast.14), custom_call_target="tpu_custom_call" | custom-call | flops 1207959552 | bytes 9437184 | tf_op jit(solution)/shard_map/input_grad/pallas_call | solution.py:520
  66.4 0.4 collective-permute-start.7
  66.8 1.0 %collective-permute-start.8 = (bf16[64,1536]{1,0:T(8,128)(2,1)S(1)}, bf16[64,1536]{1,0:T(8,128)(2,1)S(1)}, u32[]{:S(2)}, u32[]{:S(2)}) collective-permute-start(bf16[64,1536]{1,0:T(8,128)(2,1)S(1)} %get-tuple-element.31), channel_id=1, source_target_pairs={{0,28},{4,16},{8,20},{12,24},{16,12},{20,0},{24,4},{28,8},{1,29},{... | collective-permute-start | bytes 589832 | tf_op jit(solution)/shard_map/ppermute | solution.py:547
  67.9 0.0 collective-permute-done.5
  67.9 0.0 collective-permute-done.6
  67.9 4.8 %collective-permute-done.7 = bf16[64,1536]{1,0:T(8,128)(2,1)S(1)} collective-permute-done((bf16[64,1536]{1,0:T(8,128)(2,1)S(1)}, bf16[64,1536]{1,0:T(8,128)(2,1)S(1)}, u32[]{:S(2)}, u32[]{:S(2)}) %collective-permute-start.7) | collective-permute-done | bytes 196640 | tf_op jit(solution)/shard_map/ppermute | solution.py:547
  72.7 1.8 %collective-permute-done.8 = bf16[64,1536]{1,0:T(8,128)(2,1)S(1)} collective-permute-done((bf16[64,1536]{1,0:T(8,128)(2,1)S(1)}, bf16[64,1536]{1,0:T(8,128)(2,1)S(1)}, u32[]{:S(2)}, u32[]{:S(2)}) %collective-permute-start.8) | collective-permute-done | bytes 196640 | tf_op jit(solution)/shard_map/ppermute | solution.py:547
  74.6 0.8 %maximum_bitcast_fusion = bf16[1,64,3072]{2,1,0:T(8,128)(2,1)} fusion(bf16[64,1536]{1,0:T(8,128)(2,1)S(1)} %add_convert_fusion.1, bf16[64,1536]{1,0:T(8,128)(2,1)S(1)} %add_convert_fusion.2), kind=kLoop, calls=%fused_computation.1 | loop fusion | flops 786432 | bytes 786432 | tf_op jit(solution)/shard_map/broadcast_in_dim | solution.py:607
  (27 shorter events, 0.1 us)
Async XLA Ops:
  0.6 26.0 %collective-permute-start.1 = (bf16[64,3072]{1,0:T(8,128)(2,1)}, bf16[64,3072]{1,0:T(8,128)(2,1)S(1)}, u32[]{:S(2)}, u32[]{:S(2)}) collective-permute-start(bf16[64,3072]{1,0:T(8,128)(2,1)} %bitcast.15), channel_id=1, source_target_pairs={{0,16},{4,20},{8,24},{12,28},{16,0},{20,4},{24,8},{28,12},{1,17},{... | collective-permute-start | bytes 1179656 | tf_op jit(solution)/shard_map/ppermute | solution.py:547
  2.7 46.3 %collective-permute-start = (bf16[64,3072]{1,0:T(8,128)(2,1)}, bf16[64,3072]{1,0:T(8,128)(2,1)S(1)}, u32[]{:S(2)}, u32[]{:S(2)}) collective-permute-start(bf16[64,3072]{1,0:T(8,128)(2,1)} %bitcast.11), channel_id=1, source_target_pairs={{0,16},{4,20},{8,24},{12,28},{16,0},{20,4},{24,8},{28,12},{1,17},{... | collective-permute-start | bytes 1179656 | tf_op jit(solution)/shard_map/ppermute | solution.py:547
  2.8 23.8 %copy-start.4 = (bf16[1,64,3072]{2,1,0:T(8,128)(2,1)S(1)}, bf16[1,64,3072]{2,1,0:T(8,128)(2,1)}, u32[]{:S(2)}) copy-start(bf16[1,64,3072]{2,1,0:T(8,128)(2,1)} %param.9) | copy-start | bytes 1179652
  2.8 23.8 %copy-start.5 = (f32[1,3072]{1,0:T(1,128)S(1)}, f32[1,3072]{1,0:T(1,128)}, u32[]{:S(2)}) copy-start(f32[1,3072]{1,0:T(1,128)} %gate_ref.3) | copy-start | bytes 36868
  2.8 23.8 %copy-start.6 = (f32[1,128]{1,0:T(1,128)S(1)}, f32[1,128]{1,0:T(1,128)}, u32[]{:S(2)}) copy-start(f32[1,128]{1,0:T(1,128)} %query_gain_ref.3) | copy-start | bytes 1540
  2.8 23.8 %copy-start.7 = (f32[1,128]{1,0:T(1,128)S(1)}, f32[1,128]{1,0:T(1,128)}, u32[]{:S(2)}) copy-start(f32[1,128]{1,0:T(1,128)} %key_gain_ref.3) | copy-start | bytes 1540
  2.8 23.9 %copy-start.8 = (s32[2,27]{1,0:T(2,128)S(1)}, s32[2,27]{1,0:T(2,128)}, u32[]{:S(2)}) copy-start(s32[2,27]{1,0:T(2,128)} %neighbours_ref.1) | copy-start | bytes 652
  2.8 23.9 %copy-start.9 = (s32[2]{0:T(128)S(1)}, s32[2]{0:T(128)}, u32[]{:S(2)}) copy-start(s32[2]{0:T(128)} %tile_slot_ref.1) | copy-start | bytes 28
  20.2 6.4 %copy-start = (bf16[4,3072,768]{2,1,0:T(8,128)(2,1)}, bf16[4,3072,768]{2,1,0:T(8,128)(2,1)S(1)}, u32[]{:S(2)}) copy-start(bf16[4,3072,768]{2,1,0:T(8,128)(2,1)S(1)} %get-tuple-element.18.weight_ref) | copy-start | bytes 56623108
  26.7 6.4 %copy-start.1 = (bf16[4,3072,768]{2,1,0:T(8,128)(2,1)S(1)}, bf16[4,3072,768]{2,1,0:T(8,128)(2,1)}, u32[]{:S(2)}) copy-start(bf16[4,3072,768]{2,1,0:T(8,128)(2,1)} %copy-done) | copy-start | bytes 56623108
  33.1 2.8 %copy-start.2 = (bf16[1,1024,3072]{2,1,0:T(8,128)(2,1)S(1)}, bf16[1,1024,3072]{2,1,0:T(8,128)(2,1)}, u32[]{:S(2)}) copy-start(bf16[1,1024,3072]{2,1,0:T(8,128)(2,1)} %param.12) | copy-start | bytes 18874372
  35.8 13.2 %copy-start.3 = (bf16[1,64,3072]{2,1,0:T(8,128)(2,1)S(1)}, bf16[1,64,3072]{2,1,0:T(8,128)(2,1)}, u32[]{:S(2)}) copy-start(bf16[1,64,3072]{2,1,0:T(8,128)(2,1)} %param.10) | copy-start | bytes 1179652
  35.9 19.9 %slice-start = ((s8[18874368]{0:T(1024)(128)(4,1)}), s8[2097152]{0:T(1024)(128)(4,1)S(1)}, s32[]{:S(2)}) async-start(s8[18874368]{0:T(1024)(128)(4,1)} %bitcast.7), calls=%async_computation | async-start | bytes 4194304
  35.9 19.9 %slice-start.1 = ((s8[18874368]{0:T(1024)(128)(4,1)}), s8[4194304]{0:T(1024)(128)(4,1)S(1)}, s32[]{:S(2)}) async-start(s8[18874368]{0:T(1024)(128)(4,1)} %bitcast.7), calls=%async_computation.1 | async-start | bytes 8388608
  35.9 19.9 %slice-start.2 = ((s8[18874368]{0:T(1024)(128)(4,1)}), s8[4194304]{0:T(1024)(128)(4,1)S(1)}, s32[]{:S(2)}) async-start(s8[18874368]{0:T(1024)(128)(4,1)} %bitcast.7), calls=%async_computation.2 | async-start | bytes 8388608
  35.9 19.9 %slice-start.3 = ((s8[18874368]{0:T(1024)(128)(4,1)}), s8[4194304]{0:T(1024)(128)(4,1)S(1)}, s32[]{:S(2)}) async-start(s8[18874368]{0:T(1024)(128)(4,1)} %bitcast.7), calls=%async_computation.3 | async-start | bytes 8388608
  45.4 16.6 %collective-permute-start.2 = (bf16[64,3072]{1,0:T(8,128)(2,1)S(1)}, bf16[64,3072]{1,0:T(8,128)(2,1)S(1)}, u32[]{:S(2)}, u32[]{:S(2)}) collective-permute-start(bf16[64,3072]{1,0:T(8,128)(2,1)S(1)} %get-tuple-element.23), channel_id=1, source_target_pairs={{0,4},{4,8},{8,12},{12,0},{16,20},{20,24},{24,28},{28,16},{1,5},{5... | collective-permute-start | bytes 1179656 | tf_op jit(solution)/shard_map/ppermute | solution.py:547
  48.0 14.0 %collective-permute-start.3 = (bf16[64,3072]{1,0:T(8,128)(2,1)S(1)}, bf16[64,3072]{1,0:T(8,128)(2,1)S(1)}, u32[]{:S(2)}, u32[]{:S(2)}) collective-permute-start(bf16[64,3072]{1,0:T(8,128)(2,1)S(1)} %get-tuple-element.24), channel_id=1, source_target_pairs={{0,20},{4,24},{8,28},{12,16},{16,4},{20,8},{24,12},{28,0},{1,21},{... | collective-permute-start | bytes 1179656 | tf_op jit(solution)/shard_map/ppermute | solution.py:547
  49.0 6.8 %slice-start.4 = ((s8[18874368]{0:T(1024)(128)(4,1)}), s8[4194304]{0:T(1024)(128)(4,1)S(1)}, s32[]{:S(2)}) async-start(s8[18874368]{0:T(1024)(128)(4,1)} %bitcast.7), calls=%async_computation.4 | async-start | bytes 8388608
  55.5 6.0 %collective-permute-start.4 = (f32[1,3072]{1,0:T(1,128)S(1)}, f32[1,3072]{1,0:T(1,128)S(1)}, u32[]{:S(2)}, u32[]{:S(2)}) collective-permute-start(f32[1,3072]{1,0:T(1,128)S(1)} %get-tuple-element.25), channel_id=1, source_target_pairs={{0,16},{4,20},{8,24},{12,28},{16,0},{20,4},{24,8},{28,12},{1,17},{... | collective-permute-start | bytes 36872 | tf_op jit(solution)/shard_map/ppermute | solution.py:547
  59.3 8.5 %collective-permute-start.5 = (bf16[64,1536]{1,0:T(8,128)(2,1)S(1)}, bf16[64,1536]{1,0:T(8,128)(2,1)S(1)}, u32[]{:S(2)}, u32[]{:S(2)}) collective-permute-start(bf16[64,1536]{1,0:T(8,128)(2,1)S(1)} %get-tuple-element.27), channel_id=1, source_target_pairs={{0,12},{4,0},{8,4},{12,8},{16,28},{20,16},{24,20},{28,24},{1,13},{... | collective-permute-start | bytes 589832 | tf_op jit(solution)/shard_map/ppermute | solution.py:547
  60.3 7.6 %collective-permute-start.6 = (bf16[64,1536]{1,0:T(8,128)(2,1)S(1)}, bf16[64,1536]{1,0:T(8,128)(2,1)S(1)}, u32[]{:S(2)}, u32[]{:S(2)}) collective-permute-start(bf16[64,1536]{1,0:T(8,128)(2,1)S(1)} %get-tuple-element.28), channel_id=1, source_target_pairs={{0,28},{4,16},{8,20},{12,24},{16,12},{20,0},{24,4},{28,8},{1,29},{... | collective-permute-start | bytes 589832 | tf_op jit(solution)/shard_map/ppermute | solution.py:547
  66.4 6.4 %collective-permute-start.7 = (bf16[64,1536]{1,0:T(8,128)(2,1)S(1)}, bf16[64,1536]{1,0:T(8,128)(2,1)S(1)}, u32[]{:S(2)}, u32[]{:S(2)}) collective-permute-start(bf16[64,1536]{1,0:T(8,128)(2,1)S(1)} %get-tuple-element.30), channel_id=1, source_target_pairs={{0,12},{4,0},{8,4},{12,8},{16,28},{20,16},{24,20},{28,24},{1,13},{... | collective-permute-start | bytes 589832 | tf_op jit(solution)/shard_map/ppermute | solution.py:547
  66.8 7.7 %collective-permute-start.8 = (bf16[64,1536]{1,0:T(8,128)(2,1)S(1)}, bf16[64,1536]{1,0:T(8,128)(2,1)S(1)}, u32[]{:S(2)}, u32[]{:S(2)}) collective-permute-start(bf16[64,1536]{1,0:T(8,128)(2,1)S(1)} %get-tuple-element.31), channel_id=1, source_target_pairs={{0,28},{4,16},{8,20},{12,24},{16,12},{20,0},{24,4},{28,8},{1,29},{... | collective-permute-start | bytes 589832 | tf_op jit(solution)/shard_map/ppermute | solution.py:547

commit v4 on v1

--- a/solution.py
+++ b/solution.py
@@ -224,31 +224,39 @@
     return pltpu.CompilerParams(vmem_limit_bytes=mebibytes * MIB)
 
 
-def regroup_kernel(weight_ref, out_ref, wide_ref):
+def regroup_kernel(weight_ref, out_ref, order_ref):
     rows, heads, width = weight_ref.shape
-    third = wide_ref.shape[2]
-    for part in range(width // third):
-        piece = weight_ref[:, :, part * third : (part + 1) * third].astype(F32)
-        wide_ref[part] = piece.reshape(rows * heads, third)
-    for head in range(heads):
-        for part in range(width // third):
-            left = (head % 2) * width + part * third
-            out_ref[head // 2, :, left : left + third] = wide_ref[
-                part, pl.ds(head, rows, stride=heads), :
-            ].astype(BF16)
+    size = order_ref.shape[0]
+    span = size // heads
+
+    @pl.when(pl.program_id(0) == 0)
+    def _():
+        row = lax.broadcasted_iota(jnp.int32, (size, size), 0)
+        column = lax.broadcasted_iota(jnp.int32, (size, size), 1)
+        chosen = column == (row % span) * heads + row // span
+        order_ref[...] = jnp.where(chosen, 1.0, 0.0).astype(BF16)
+
+    order = order_ref[...]
+    for first in range(0, rows, span):
+        piece = weight_ref[first : first + span].reshape(size, width)
+        by_head = dot_nn(order, piece).astype(BF16)
+        for head in range(heads):
+            left = (head % 2) * width
+            out_ref[head // 2, first : first + span, left : left + width] = by_head[
+                head * span : (head + 1) * span
+            ]
 
 
 def regroup(weight, rows):
     depth, heads, width = weight.shape
     pairs = heads // 2
-    third = width // 3
     return pl.pallas_call(
         regroup_kernel,
         grid=(depth // rows,),
         out_shape=jax.ShapeDtypeStruct((pairs, depth, 2 * width), weight.dtype),
         in_specs=[pl.BlockSpec((rows, heads, width), lambda i: (i, 0, 0))],
         out_specs=pl.BlockSpec((pairs, rows, 2 * width), lambda i: (0, i, 0)),
-        scratch_shapes=[pltpu.VMEM((3, rows * heads, third), F32)],
+        scratch_shapes=[pltpu.VMEM((256, 256), BF16)],
         compiler_params=params(46),
         cost_estimate=pl.CostEstimate(
             flops=0, bytes_accessed=4 * depth * heads * width, transcendentals=0
@@ -290,14 +298,18 @@
     sent_ref,
     tokens_ref,
     bias_ref,
+    total_ref,
 ):
     step = pl.program_id(0)
+    part = pl.program_id(1)
+    last_part = pl.num_programs(1) - 1
+    depth = weight_ref.shape[1]
     local = own_ref.shape[0]
     tokens = 2 * local
     width = query_gain_ref.shape[1]
     heads = probs_ref.shape[0]
 
-    @pl.when(step == 0)
+    @pl.when((step == 0) & (part == 0))
     def _():
         tokens_ref[:local, :] = own_ref[...]
         tokens_ref[local:, :] = other_ref[...]
@@ -313,41 +325,57 @@
                 table = jnp.where((row_slot == r) & (column_slot == c), allowed[r][c], table)
         bias_ref[...] = jnp.where(table > 0, 0.0, -jnp.inf).astype(F32)
 
-    projected = dot_nn(tokens_ref[...], weight_ref[0])
-    projected_ref[0] = projected
-    scale_factor = 1.0 / math.sqrt(width)
-    bias = bias_ref[...]
-    attended = []
-    for head in range(heads):
-        left = head * 3 * width
-        query = projected[:, left : left + width]
-        key = projected[:, left + width : left + 2 * width]
-        value = projected[:, left + 2 * width : left + 3 * width].astype(BF16)
-        query_inverse = lax.rsqrt(jnp.mean(query * query, axis=-1, keepdims=True) + EPSILON)
-        key_inverse = lax.rsqrt(jnp.mean(key * key, axis=-1, keepdims=True) + EPSILON)
-        queries = (query * query_inverse * query_gain_ref[...]).astype(BF16)
-        keys = (key * key_inverse * key_gain_ref[...]).astype(BF16)
-        scores = dot_nt(queries, keys) * scale_factor + bias
-        row_max = jnp.max(scores, axis=-1, keepdims=True)
-        weights = jnp.exp(scores - row_max)
-        probs = (weights / jnp.sum(weights, axis=-1, keepdims=True)).astype(BF16)
-        probs_ref[head] = probs
-        attended.append(dot_nn(probs, value).astype(BF16))
-    share = dot_nn(jnp.concatenate(attended, axis=1), out_weight_ref[...])
-
-    @pl.when(step == 0)
+    def attend(product):
+        projected = total_ref[...] + product
+        projected_ref[0] = projected
+        scale_factor = 1.0 / math.sqrt(width)
+        bias = bias_ref[...]
+        attended = []
+        for head in range(heads):
+            left = head * 3 * width
+            query = projected[:, left : left + width]
+            key = projected[:, left + width : left + 2 * width]
+            value = projected[:, left + 2 * width : left + 3 * width].astype(BF16)
+            query_inverse = lax.rsqrt(jnp.mean(query * query, axis=-1, keepdims=True) + EPSILON)
+            key_inverse = lax.rsqrt(jnp.mean(key * key, axis=-1, keepdims=True) + EPSILON)
+            queries = (query * query_inverse * query_gain_ref[...]).astype(BF16)
+            keys = (key * key_inverse * key_gain_ref[...]).astype(BF16)
+            scores = dot_nt(queries, keys) * scale_factor + bias
+            row_max = jnp.max(scores, axis=-1, keepdims=True)
+            weights = jnp.exp(scores - row_max)
+            probs = (weights / jnp.sum(weights, axis=-1, keepdims=True)).astype(BF16)
+            probs_ref[head] = probs
+            attended.append(dot_nn(probs, value).astype(BF16))
+        share = dot_nn(jnp.concatenate(attended, axis=1), out_weight_ref[...])
+
+        @pl.when(step == 0)
+        def _():
+            attention_ref[...] = share
+
+        @pl.when(step > 0)
+        def _():
+            attention_ref[...] += share
+
+        @pl.when(step == pl.num_programs(0) - 1)
+        def _():
+            gate = gate_ref[...]
+            kept_ref[...] = (own_ref[...].astype(F32) + gate * attention_ref[:local, :]).astype(BF16)
+            sent_ref[...] = (gate * attention_ref[local:, :]).astype(BF16)
+
+    columns = pl.ds(pl.multiple_of(part * depth, depth), depth)
+    product = dot_nn(tokens_ref[:, columns], weight_ref[0])
+
+    @pl.when(part == 0)
     def _():
-        attention_ref[...] = share
-
-    @pl.when(step > 0)
+        total_ref[...] = product
+
+    @pl.when((part > 0) & (part < last_part))
     def _():
-        attention_ref[...] += share
-
-    @pl.when(step == pl.num_programs(0) - 1)
+        total_ref[...] += product
+
+    @pl.when(part == last_part)
     def _():
-        gate = gate_ref[...]
-        kept_ref[...] = (own_ref[...].astype(F32) + gate * attention_ref[:local, :]).astype(BF16)
-        sent_ref[...] = (gate * attention_ref[local:, :]).astype(BF16)
+        attend(product)
 
 
 def forward(neighbours, tile_slot, own, other, weight, out_weight, query_gain, key_gain, gate):
@@ -355,11 +383,12 @@
     pairs, _, wide = weight.shape
     head_dim = query_gain.shape[1]
     tokens = 2 * local
-    whole = lambda i: (0, 0)
+    whole = lambda i, k: (0, 0)
+    parts = 4
     smem = pl.BlockSpec(memory_space=pltpu.SMEM)
     return pl.pallas_call(
         forward_kernel,
-        grid=(pairs,),
+        grid=(pairs, parts),
         out_shape=(
             jax.ShapeDtypeStruct((pairs, tokens, wide), F32),
             jax.ShapeDtypeStruct((2 * pairs, tokens, tokens), BF16),
@@ -372,20 +401,24 @@
             smem,
             pl.BlockSpec((local, model), whole),
             pl.BlockSpec((local, model), whole),
-            pl.BlockSpec((1, model, wide), lambda i: (i, 0, 0)),
-            pl.BlockSpec((2 * head_dim, model), lambda i: (i, 0)),
+            pl.BlockSpec((1, model // parts, wide), lambda i, k: (i, k, 0)),
+            pl.BlockSpec((2 * head_dim, model), lambda i, k: (i, 0)),
             pl.BlockSpec((1, head_dim), whole),
             pl.BlockSpec((1, head_dim), whole),
             pl.BlockSpec((1, model), whole),
         ],
         out_specs=(
-            pl.BlockSpec((1, tokens, wide), lambda i: (i, 0, 0)),
-            pl.BlockSpec((2, tokens, tokens), lambda i: (i, 0, 0)),
+            pl.BlockSpec((1, tokens, wide), lambda i, k: (i, 0, 0)),
+            pl.BlockSpec((2, tokens, tokens), lambda i, k: (i, 0, 0)),
             pl.BlockSpec((tokens, model), whole),
             pl.BlockSpec((local, model), whole),
             pl.BlockSpec((local, model), whole),
         ),
-        scratch_shapes=[pltpu.VMEM((tokens, model), BF16), pltpu.VMEM((tokens, tokens), F32)],
+        scratch_shapes=[
+            pltpu.VMEM((tokens, model), BF16),
+            pltpu.VMEM((tokens, tokens), F32),
+            pltpu.VMEM((tokens, wide), F32),
+        ],
         compiler_params=params(46),
         cost_estimate=pl.CostEstimate(
             flops=2 * tokens * model * pairs * (wide + 2 * head_dim),
@@ -500,10 +533,9 @@
 
 def input_grad_kernel(grad_ref, weight_ref, own_ref, kept_ref, sent_ref):
     local = own_ref.shape[0]
-    total = dot_nt(weight_ref[0], grad_ref[0])
+    total = dot_nt(grad_ref[0], weight_ref[0])
     for pair in range(1, grad_ref.shape[0]):
-        total += dot_nt(weight_ref[pair], grad_ref[pair])
-    total = total.T
+        total += dot_nt(grad_ref[pair], weight_ref[pair])
     kept_ref[...] = (own_ref[...].astype(F32) + total[:local]).astype(BF16)
     sent_ref[...] = total[local:].astype(BF16)
 
@@ -589,7 +621,7 @@
         gate_scale,
     )
     other_gate = routed(gate_share, 1, 0)
-    first, second = input_grad_part(grad, weight, upstream, 0, 2, 512)
+    first, second = input_grad_part(grad, weight, upstream, 0, 2, 256)
     pieces = [(routed(first, 0, -1), routed(second, 1, -1))]
     segment_output = (kept.astype(F32) + sent.astype(F32)).astype(BF16)
     half = model // lax.axis_size("seq")
@@ -597,7 +629,7 @@
         gate_share + other_gate, lax.axis_index("seq") * half, half, 1
     )
     grad, segment_output, gate_total = lax.optimization_barrier((grad, segment_output, gate_total))
-    first, second = input_grad_part(grad, weight, upstream, 1, 2, 512)
+    first, second = input_grad_part(grad, weight, upstream, 1, 2, 256)
     pieces.append((routed(first, 0, -1), routed(second, 1, -1)))
     input_grad = jnp.concatenate(
         [(a.astype(F32) + b.astype(F32)).astype(BF16) for a, b in pieces], axis=1

time: 76.5 us -> 86.6 us (1.13)
  Pallas kernels: 56.4 us -> 66.2 us
    pallas_call x1, Pallas kernels: 12.5 us -> 20 us  [forward(): pl.pallas_call(forward_kernel, grid=(pairs, parts), out_shape=(jax.ShapeD...]
    pallas_call x2, Pallas kernels: 11.8 us -> 14.3 us  [input_grad_part(): pl.pallas_call(input_grad_kernel, grid=(columns // block,), out_shape=(ou...]
  transfers between devices with their start and end apart: 9 -> 9, of which waited for: 2 -> 2; matrix products, arithmetic and copies ran while one was open for 2% -> 2% of each run, Pallas kernels for 74% -> 77%
where the time goes in v4:
time: 86.6 us; the launch traced here: 85.6 us
  Pallas kernels  66.2 us (76%)
  starting transfers between devices  9.69 us (11%)
  waiting for transfers between devices  6.61 us (8%)
  other arithmetic  2.31 us (3%)
    pallas_call x1, Pallas kernels, regroup(): pl.pallas_call(regroup_kernel, grid=(depth // rows,), out_shape=jax.Shape...  24.2 us
    pallas_call x1, Pallas kernels, forward(): pl.pallas_call(forward_kernel, grid=(pairs, parts), out_shape=(jax.ShapeD...  20 us
    pallas_call x2, Pallas kernels, input_grad_part(): pl.pallas_call(input_grad_kernel, grid=(columns // block,), out_shape=(ou...  14.3 us
    ppermute x9, starting transfers between devices, routed(): return lax.ppermute(block, ('seq', 'pipe'), route)  9.69 us
    pallas_call x1, Pallas kernels, backward(): pl.pallas_call(backward_kernel, grid=(pairs,), out_shape=(jax.ShapeDtypeS...  7.75 us
    ppermute x9, waiting for transfers between devices, routed(): return lax.ppermute(block, ('seq', 'pipe'), route)  6.61 us
  transfers between devices with their start and end apart: 9, of which 2 were waited for; matrix products, arithmetic and copies ran while one was open for 2% of the time, Pallas kernels for 77%

profile of v4, /device:TPU:1, one launch (start us, length us, event | category | flops | bytes accessed | tf_op | source)
XLA Modules:
  0.0 85.6 jit_solution(179199749755775732)
XLA Ops:
  0.6 2.1 %collective-permute-start.1 = (bf16[64,3072]{1,0:T(8,128)(2,1)}, bf16[64,3072]{1,0:T(8,128)(2,1)S(1)}, u32[]{:S(2)}, u32[]{:S(2)}) collective-permute-start(bf16[64,3072]{1,0:T(8,128)(2,1)} %bitcast.11), channel_id=1, source_target_pairs={{0,16},{4,20},{8,24},{12,28},{16,0},{20,4},{24,8},{28,12},{1,17},{... | collective-permute-start | bytes 1179656 | tf_op jit(solution)/shard_map/ppermute | solution.py:577
  2.8 0.0 copy-start.4
  2.8 0.0 copy-start.5
  2.8 0.0 copy-start.6
  2.8 24.2 %regroup.1.weight_ref = bf16[4,3072,768]{2,1,0:T(8,128)(2,1)} custom-call(bf16[3072,8,384]{2,1,0:T(8,128)(2,1)} %bitcast.15), custom_call_target="tpu_custom_call" | custom-call | bytes 37748736 | tf_op jit(solution)/shard_map/regroup/pallas_call | solution.py:253
  27.0 0.0 copy-done
  27.0 0.0 collective-permute-start
  27.0 0.0 collective-permute-done.1.other_ref
  27.1 0.0 copy-done.2
  27.1 0.0 copy-done.3
  27.1 20.0 %attention_forward.1 = (f32[4,128,768]{2,1,0:T(8,128)S(1)}, bf16[8,128,128]{2,1,0:T(8,128)(2,1)S(1)}, f32[128,3072]{1,0:T(8,128)S(1)}, bf16[64,3072]{1,0:T(8,128)(2,1)S(1)}, bf16[64,3072]{1,0:T(8,128)(2,1)S(1)}) custom-call(s32[2,27]{1,0:T(2,128)S(1)} %copy-done.5, s32[2]{0:T(128)S(1)} %copy-done.6, bf16[64,3072]{1,0:T(8,128)(2,1)S(1)} %bitcast.12, ...), custom_call_target="tpu_custom_call" | custom-call | flops 3221225472 | bytes 25165824 | tf_op jit(solution)/shard_map/attention_forward/pallas_call | solution.py:389
  47.1 2.6 %collective-permute-start.2 = (bf16[64,3072]{1,0:T(8,128)(2,1)S(1)}, bf16[64,3072]{1,0:T(8,128)(2,1)S(1)}, u32[]{:S(2)}, u32[]{:S(2)}) collective-permute-start(bf16[64,3072]{1,0:T(8,128)(2,1)S(1)} %get-tuple-element.25), channel_id=1, source_target_pairs={{0,4},{4,8},{8,12},{12,0},{16,20},{20,24},{24,28},{28,16},{1,5},{5... | collective-permute-start | bytes 1179656 | tf_op jit(solution)/shard_map/ppermute | solution.py:577
  49.7 1.0 %collective-permute-start.3 = (bf16[64,3072]{1,0:T(8,128)(2,1)S(1)}, bf16[64,3072]{1,0:T(8,128)(2,1)S(1)}, u32[]{:S(2)}, u32[]{:S(2)}) collective-permute-start(bf16[64,3072]{1,0:T(8,128)(2,1)S(1)} %get-tuple-element.26), channel_id=1, source_target_pairs={{0,20},{4,24},{8,28},{12,16},{16,4},{20,8},{24,12},{28,0},{1,21},{... | collective-permute-start | bytes 1179656 | tf_op jit(solution)/shard_map/ppermute | solution.py:577
  50.7 0.0 collective-permute-done.other_ref
  50.7 7.7 %attention_backward.1 = (bf16[4,128,768]{2,1,0:T(8,128)(2,1)S(1)}, f32[1,3072]{1,0:T(1,128)S(1)}) custom-call(bf16[64,3072]{1,0:T(8,128)(2,1)S(1)} %bitcast.8, bf16[64,3072]{1,0:T(8,128)(2,1)S(1)} %collective-permute-done.other_ref, bf16[1024,3072]{1,0:T(8,128)(2,1)} %bitcast.14, f32[4,128,768]{2,1,0:T(8,128)S(1)} %get-tuple-element.21.projected_ref, ...), custom_call_target="tpu_custom_call" | custom-call | flops 805306368 | bytes 6291456 | tf_op jit(solution)/shard_map/attention_backward/pallas_call | solution.py:501
  58.5 0.3 collective-permute-start.4
  58.8 7.1 %input_grad.2 = (bf16[64,1536]{1,0:T(8,128)(2,1)S(1)}, bf16[64,1536]{1,0:T(8,128)(2,1)S(1)}) custom-call(bf16[4,128,768]{2,1,0:T(8,128)(2,1)S(1)} %get-tuple-element.31.grad_ref, bf16[4,3072,768]{2,1,0:T(8,128)(2,1)} %regroup.1.weight_ref, bf16[64,3072]{1,0:T(8,128)(2,1)S(1)} %bitcast.9), custom_call_target="tpu_custom_call" | custom-call | flops 1207959552 | bytes 9437184 | tf_op jit(solution)/shard_map/input_grad/pallas_call | solution.py:550
  65.9 0.9 %collective-permute-start.5 = (bf16[64,1536]{1,0:T(8,128)(2,1)S(1)}, bf16[64,1536]{1,0:T(8,128)(2,1)S(1)}, u32[]{:S(2)}, u32[]{:S(2)}) collective-permute-start(bf16[64,1536]{1,0:T(8,128)(2,1)S(1)} %get-tuple-element.29), channel_id=1, source_target_pairs={{0,12},{4,0},{8,4},{12,8},{16,28},{20,16},{24,20},{28,24},{1,13},{... | collective-permute-start | bytes 589832 | tf_op jit(solution)/shard_map/ppermute | solution.py:577
  66.9 1.2 %collective-permute-start.6 = (bf16[64,1536]{1,0:T(8,128)(2,1)S(1)}, bf16[64,1536]{1,0:T(8,128)(2,1)S(1)}, u32[]{:S(2)}, u32[]{:S(2)}) collective-permute-start(bf16[64,1536]{1,0:T(8,128)(2,1)S(1)} %get-tuple-element.30), channel_id=1, source_target_pairs={{0,28},{4,16},{8,20},{12,24},{16,12},{20,0},{24,4},{28,8},{1,29},{... | collective-permute-start | bytes 589832 | tf_op jit(solution)/shard_map/ppermute | solution.py:577
  68.0 0.0 collective-permute-done.4
  68.0 0.6 dynamic-slice_add_fusion
  68.6 0.0 collective-permute-done.2
  68.6 0.0 collective-permute-done.3
  68.6 0.8 add_convert_fusion
  69.5 7.1 %input_grad.3 = (bf16[64,1536]{1,0:T(8,128)(2,1)S(1)}, bf16[64,1536]{1,0:T(8,128)(2,1)S(1)}) custom-call(bf16[4,128,768]{2,1,0:T(8,128)(2,1)S(1)} %get-tuple-element.31.grad_ref, bf16[4,3072,768]{2,1,0:T(8,128)(2,1)} %regroup.1.weight_ref, bf16[64,3072]{1,0:T(8,128)(2,1)S(1)} %bitcast.10), custom_call_target="tpu_custom_call" | custom-call | flops 1207959552 | bytes 9437184 | tf_op jit(solution)/shard_map/input_grad/pallas_call | solution.py:550
  76.6 0.4 collective-permute-start.7
  77.1 1.1 %collective-permute-start.8 = (bf16[64,1536]{1,0:T(8,128)(2,1)S(1)}, bf16[64,1536]{1,0:T(8,128)(2,1)S(1)}, u32[]{:S(2)}, u32[]{:S(2)}) collective-permute-start(bf16[64,1536]{1,0:T(8,128)(2,1)S(1)} %get-tuple-element.33), channel_id=1, source_target_pairs={{0,28},{4,16},{8,20},{12,24},{16,12},{20,0},{24,4},{28,8},{1,29},{... | collective-permute-start | bytes 589832 | tf_op jit(solution)/shard_map/ppermute | solution.py:577
  78.1 0.0 collective-permute-done.5
  78.1 0.0 collective-permute-done.6
  78.2 4.8 %collective-permute-done.7 = bf16[64,1536]{1,0:T(8,128)(2,1)S(1)} collective-permute-done((bf16[64,1536]{1,0:T(8,128)(2,1)S(1)}, bf16[64,1536]{1,0:T(8,128)(2,1)S(1)}, u32[]{:S(2)}, u32[]{:S(2)}) %collective-permute-start.7) | collective-permute-done | bytes 196640 | tf_op jit(solution)/shard_map/ppermute | solution.py:577
  83.0 1.8 %collective-permute-done.8 = bf16[64,1536]{1,0:T(8,128)(2,1)S(1)} collective-permute-done((bf16[64,1536]{1,0:T(8,128)(2,1)S(1)}, bf16[64,1536]{1,0:T(8,128)(2,1)S(1)}, u32[]{:S(2)}, u32[]{:S(2)}) %collective-permute-start.8) | collective-permute-done | bytes 196640 | tf_op jit(solution)/shard_map/ppermute | solution.py:577
  84.8 0.8 maximum_bitcast_fusion
  (10 shorter events, 0.1 us)
Async XLA Ops:
  0.6 26.4 %collective-permute-start.1 = (bf16[64,3072]{1,0:T(8,128)(2,1)}, bf16[64,3072]{1,0:T(8,128)(2,1)S(1)}, u32[]{:S(2)}, u32[]{:S(2)}) collective-permute-start(bf16[64,3072]{1,0:T(8,128)(2,1)} %bitcast.11), channel_id=1, source_target_pairs={{0,16},{4,20},{8,24},{12,28},{16,0},{20,4},{24,8},{28,12},{1,17},{... | collective-permute-start | bytes 1179656 | tf_op jit(solution)/shard_map/ppermute | solution.py:577
  2.7 24.3 %copy-start = (bf16[1,64,3072]{2,1,0:T(8,128)(2,1)S(1)}, bf16[1,64,3072]{2,1,0:T(8,128)(2,1)}, u32[]{:S(2)}) copy-start(bf16[1,64,3072]{2,1,0:T(8,128)(2,1)} %param.10) | copy-start | bytes 1179652
  2.7 24.3 %copy-start.1 = (bf16[1,64,3072]{2,1,0:T(8,128)(2,1)S(1)}, bf16[1,64,3072]{2,1,0:T(8,128)(2,1)}, u32[]{:S(2)}) copy-start(bf16[1,64,3072]{2,1,0:T(8,128)(2,1)} %param.9) | copy-start | bytes 1179652
  2.7 24.3 %copy-start.2 = (f32[1,3072]{1,0:T(1,128)S(1)}, f32[1,3072]{1,0:T(1,128)}, u32[]{:S(2)}) copy-start(f32[1,3072]{1,0:T(1,128)} %gate_ref.3) | copy-start | bytes 36868
  2.7 24.3 %copy-start.3 = (f32[1,128]{1,0:T(1,128)S(1)}, f32[1,128]{1,0:T(1,128)}, u32[]{:S(2)}) copy-start(f32[1,128]{1,0:T(1,128)} %query_gain_ref.3) | copy-start | bytes 1540
  2.8 24.3 %copy-start.4 = (f32[1,128]{1,0:T(1,128)S(1)}, f32[1,128]{1,0:T(1,128)}, u32[]{:S(2)}) copy-start(f32[1,128]{1,0:T(1,128)} %key_gain_ref.3) | copy-start | bytes 1540
  2.8 24.3 %copy-start.5 = (s32[2,27]{1,0:T(2,128)S(1)}, s32[2,27]{1,0:T(2,128)}, u32[]{:S(2)}) copy-start(s32[2,27]{1,0:T(2,128)} %neighbours_ref.1) | copy-start | bytes 652
  2.8 24.3 %copy-start.6 = (s32[2]{0:T(128)S(1)}, s32[2]{0:T(128)}, u32[]{:S(2)}) copy-start(s32[2]{0:T(128)} %tile_slot_ref.1) | copy-start | bytes 28
  27.0 23.7 %collective-permute-start = (bf16[64,3072]{1,0:T(8,128)(2,1)S(1)}, bf16[64,3072]{1,0:T(8,128)(2,1)S(1)}, u32[]{:S(2)}, u32[]{:S(2)}) collective-permute-start(bf16[64,3072]{1,0:T(8,128)(2,1)S(1)} %bitcast.7), channel_id=1, source_target_pairs={{0,16},{4,20},{8,24},{12,28},{16,0},{20,4},{24,8},{28,12},{1,17},{... | collective-permute-start | bytes 1179656 | tf_op jit(solution)/shard_map/ppermute | solution.py:577
  47.1 21.5 %collective-permute-start.2 = (bf16[64,3072]{1,0:T(8,128)(2,1)S(1)}, bf16[64,3072]{1,0:T(8,128)(2,1)S(1)}, u32[]{:S(2)}, u32[]{:S(2)}) collective-permute-start(bf16[64,3072]{1,0:T(8,128)(2,1)S(1)} %get-tuple-element.25), channel_id=1, source_target_pairs={{0,4},{4,8},{8,12},{12,0},{16,20},{20,24},{24,28},{28,16},{1,5},{5... | collective-permute-start | bytes 1179656 | tf_op jit(solution)/shard_map/ppermute | solution.py:577
  49.7 18.9 %collective-permute-start.3 = (bf16[64,3072]{1,0:T(8,128)(2,1)S(1)}, bf16[64,3072]{1,0:T(8,128)(2,1)S(1)}, u32[]{:S(2)}, u32[]{:S(2)}) collective-permute-start(bf16[64,3072]{1,0:T(8,128)(2,1)S(1)} %get-tuple-element.26), channel_id=1, source_target_pairs={{0,20},{4,24},{8,28},{12,16},{16,4},{20,8},{24,12},{28,0},{1,21},{... | collective-permute-start | bytes 1179656 | tf_op jit(solution)/shard_map/ppermute | solution.py:577
  58.5 9.6 %collective-permute-start.4 = (f32[1,3072]{1,0:T(1,128)S(1)}, f32[1,3072]{1,0:T(1,128)S(1)}, u32[]{:S(2)}, u32[]{:S(2)}) collective-permute-start(f32[1,3072]{1,0:T(1,128)S(1)} %get-tuple-element.27), channel_id=1, source_target_pairs={{0,16},{4,20},{8,24},{12,28},{16,0},{20,4},{24,8},{28,12},{1,17},{... | collective-permute-start | bytes 36872 | tf_op jit(solution)/shard_map/ppermute | solution.py:577
  65.9 12.2 %collective-permute-start.5 = (bf16[64,1536]{1,0:T(8,128)(2,1)S(1)}, bf16[64,1536]{1,0:T(8,128)(2,1)S(1)}, u32[]{:S(2)}, u32[]{:S(2)}) collective-permute-start(bf16[64,1536]{1,0:T(8,128)(2,1)S(1)} %get-tuple-element.29), channel_id=1, source_target_pairs={{0,12},{4,0},{8,4},{12,8},{16,28},{20,16},{24,20},{28,24},{1,13},{... | collective-permute-start | bytes 589832 | tf_op jit(solution)/shard_map/ppermute | solution.py:577
  66.9 11.3 %collective-permute-start.6 = (bf16[64,1536]{1,0:T(8,128)(2,1)S(1)}, bf16[64,1536]{1,0:T(8,128)(2,1)S(1)}, u32[]{:S(2)}, u32[]{:S(2)}) collective-permute-start(bf16[64,1536]{1,0:T(8,128)(2,1)S(1)} %get-tuple-element.30), channel_id=1, source_target_pairs={{0,28},{4,16},{8,20},{12,24},{16,12},{20,0},{24,4},{28,8},{1,29},{... | collective-permute-start | bytes 589832 | tf_op jit(solution)/shard_map/ppermute | solution.py:577
  76.6 6.4 %collective-permute-start.7 = (bf16[64,1536]{1,0:T(8,128)(2,1)S(1)}, bf16[64,1536]{1,0:T(8,128)(2,1)S(1)}, u32[]{:S(2)}, u32[]{:S(2)}) collective-permute-start(bf16[64,1536]{1,0:T(8,128)(2,1)S(1)} %get-tuple-element.32), channel_id=1, source_target_pairs={{0,12},{4,0},{8,4},{12,8},{16,28},{20,16},{24,20},{28,24},{1,13},{... | collective-permute-start | bytes 589832 | tf_op jit(solution)/shard_map/ppermute | solution.py:577
  77.1 7.7 %collective-permute-start.8 = (bf16[64,1536]{1,0:T(8,128)(2,1)S(1)}, bf16[64,1536]{1,0:T(8,128)(2,1)S(1)}, u32[]{:S(2)}, u32[]{:S(2)}) collective-permute-start(bf16[64,1536]{1,0:T(8,128)(2,1)S(1)} %get-tuple-element.33), channel_id=1, source_target_pairs={{0,28},{4,16},{8,20},{12,24},{16,12},{20,0},{24,4},{28,8},{1,29},{... | collective-permute-start | bytes 589832 | tf_op jit(solution)/shard_map/ppermute | solution.py:577

commit v5 on v4

--- a/solution.py
+++ b/solution.py
@@ -224,39 +224,79 @@
     return pltpu.CompilerParams(vmem_limit_bytes=mebibytes * MIB)
 
 
-def regroup_kernel(weight_ref, out_ref, order_ref):
-    rows, heads, width = weight_ref.shape
-    size = order_ref.shape[0]
-    span = size // heads
-
-    @pl.when(pl.program_id(0) == 0)
-    def _():
-        row = lax.broadcasted_iota(jnp.int32, (size, size), 0)
-        column = lax.broadcasted_iota(jnp.int32, (size, size), 1)
-        chosen = column == (row % span) * heads + row // span
-        order_ref[...] = jnp.where(chosen, 1.0, 0.0).astype(BF16)
-
-    order = order_ref[...]
-    for first in range(0, rows, span):
-        piece = weight_ref[first : first + span].reshape(size, width)
-        by_head = dot_nn(order, piece).astype(BF16)
+class Copies:
+    def __init__(self, pairs, semaphores, ahead):
+        self.copies = [
+            pltpu.make_async_copy(source, target, semaphores.at[i])
+            for i, (source, target) in enumerate(pairs)
+        ]
+        self.ahead = ahead
+        self.waited = 0
+        for copy in self.copies[:ahead]:
+            copy.start()
+
+    def wait(self, count=1):
+        for _ in range(count):
+            self.copies[self.waited].wait()
+            following = self.waited + self.ahead
+            if following < len(self.copies):
+                self.copies[following].start()
+            self.waited += 1
+
+
+def regroup_kernel(rows, ahead, weight_ref, out_ref, read_ref, written_ref, reads, writes):
+    depth, heads, width = weight_ref.shape
+    steps = depth // rows
+
+    def part(step):
+        return pl.ds(pl.multiple_of(step * rows, rows), rows)
+
+    def read(step):
+        return pltpu.make_async_copy(
+            weight_ref.at[part(step)], read_ref.at[part(step)], reads.at[step]
+        )
+
+    def write(step):
+        return pltpu.make_async_copy(
+            written_ref.at[:, part(step)], out_ref.at[:, part(step)], writes.at[step]
+        )
+
+    for step in range(ahead):
+        read(step).start()
+
+    @pl.loop(0, steps)
+    def _(step):
+        read(step).wait()
+
+        @pl.when(step + ahead < steps)
+        def _():
+            read(step + ahead).start()
+
+        by_head = jnp.swapaxes(read_ref[part(step)], 0, 1)
         for head in range(heads):
             left = (head % 2) * width
-            out_ref[head // 2, first : first + span, left : left + width] = by_head[
-                head * span : (head + 1) * span
-            ]
-
-
-def regroup(weight, rows):
+            written_ref[head // 2, part(step), left : left + width] = by_head[head]
+        write(step).start()
+
+    @pl.loop(0, steps)
+    def _(step):
+        write(step).wait()
+
+
+def regroup(weight, rows, ahead):
     depth, heads, width = weight.shape
-    pairs = heads // 2
+    out = (heads // 2, depth, 2 * width)
     return pl.pallas_call(
-        regroup_kernel,
-        grid=(depth // rows,),
-        out_shape=jax.ShapeDtypeStruct((pairs, depth, 2 * width), weight.dtype),
-        in_specs=[pl.BlockSpec((rows, heads, width), lambda i: (i, 0, 0))],
-        out_specs=pl.BlockSpec((pairs, rows, 2 * width), lambda i: (0, i, 0)),
-        scratch_shapes=[pltpu.VMEM((256, 256), BF16)],
+        functools.partial(regroup_kernel, rows, ahead),
+        out_shape=jax.ShapeDtypeStruct(out, weight.dtype),
+        in_specs=[pl.BlockSpec(memory_space=pl.ANY)],
+        out_specs=pl.BlockSpec(memory_space=pl.ANY),
+        scratch_shapes=[
+            pltpu.VMEM(weight.shape, weight.dtype),
+            pltpu.VMEM(out, weight.dtype),
+            pltpu.SemaphoreType.DMA((depth // rows,)),
+            pltpu.SemaphoreType.DMA((depth // rows,)),
+        ],
         compiler_params=params(46),
         cost_estimate=pl.CostEstimate(
             flops=0, bytes_accessed=4 * depth * heads * width, transcendentals=0
@@ -279,6 +319,12 @@
                     here = (tile_slot_ref[t] == r) & (tile_slot_ref[u] == c)
                     allowed[r][c] = jnp.where(here, listed, allowed[r][c])
     return allowed
+
+
+def normed(rows, gain):
+    inverse = lax.rsqrt(jnp.mean(rows * rows, axis=-1, keepdims=True) + EPSILON)
+    unit = rows * inverse
+    return unit, inverse, (unit * gain).astype(BF16)
 
 
 def forward_kernel(
@@ -297,98 +343,101 @@
     kept_ref,
     sent_ref,
     tokens_ref,
-    bias_ref,
-    total_ref,
+    weight_buffer,
+    out_weight_buffer,
+    semaphores,
 ):
-    step = pl.program_id(0)
-    part = pl.program_id(1)
-    last_part = pl.num_programs(1) - 1
-    depth = weight_ref.shape[1]
-    local = own_ref.shape[0]
+    local, model = own_ref.shape
     tokens = 2 * local
     width = query_gain_ref.shape[1]
-    heads = probs_ref.shape[0]
-
-    @pl.when((step == 0) & (part == 0))
-    def _():
-        tokens_ref[:local, :] = own_ref[...]
-        tokens_ref[local:, :] = other_ref[...]
-        allowed = listed_slots(neighbours_ref, tile_slot_ref)
-        mine = lax.axis_index("seq")
-        row_half = lax.broadcasted_iota(jnp.int32, (tokens, tokens), 0) // local
-        column_half = lax.broadcasted_iota(jnp.int32, (tokens, tokens), 1) // local
-        row_slot = jnp.where(row_half == 0, mine, 1 - mine)
-        column_slot = jnp.where(column_half == 0, mine, 1 - mine)
-        table = jnp.zeros((tokens, tokens), jnp.int32)
-        for r in range(2):
-            for c in range(2):
-                table = jnp.where((row_slot == r) & (column_slot == c), allowed[r][c], table)
-        bias_ref[...] = jnp.where(table > 0, 0.0, -jnp.inf).astype(F32)
-
-    def attend(product):
-        projected = total_ref[...] + product
-        projected_ref[0] = projected
-        scale_factor = 1.0 / math.sqrt(width)
-        bias = bias_ref[...]
+    pairs = weight_ref.shape[0]
+    halves = 2
+    half = model // halves
+
+    def weight_part(pair, index):
+        place = (pair, pl.ds(index * half, half))
+        return weight_ref.at[place], weight_buffer.at[place]
+
+    def out_weight_part(pair):
+        place = pl.ds(pair * 2 * width, 2 * width)
+        return out_weight_ref.at[place], out_weight_buffer.at[place]
+
+    order = [weight_part(0, 0), weight_part(0, 1)]
+    for pair in range(1, pairs):
+        order += [weight_part(pair, 0), weight_part(pair, 1), out_weight_part(pair - 1)]
+    order.append(out_weight_part(pairs - 1))
+    copies = Copies(order, semaphores, 3)
+
+    tokens_ref[:local, :] = own_ref[...]
+    tokens_ref[local:, :] = other_ref[...]
+    allowed = listed_slots(neighbours_ref, tile_slot_ref)
+    mine = lax.axis_index("seq")
+    row_half = lax.broadcasted_iota(jnp.int32, (tokens, tokens), 0) // local
+    column_half = lax.broadcasted_iota(jnp.int32, (tokens, tokens), 1) // local
+    row_slot = jnp.where(row_half == 0, mine, 1 - mine)
+    column_slot = jnp.where(column_half == 0, mine, 1 - mine)
+    table = jnp.zeros((tokens, tokens), jnp.int32)
+    for r in range(2):
+        for c in range(2):
+            table = jnp.where((row_slot == r) & (column_slot == c), allowed[r][c], table)
+    bias = jnp.where(table > 0, 0.0, -jnp.inf).astype(F32)
+
+    def project(pair):
+        total = None
+        for index in range(halves):
+            part = slice(index * half, (index + 1) * half)
+            product = dot_nn(tokens_ref[:, part], weight_buffer[pair, part, :])
+            total = product if total is None else total + product
+        projected_ref[pair] = total
+
+    def attend(pair):
         attended = []
-        for head in range(heads):
+        for head in range(2):
             left = head * 3 * width
-            query = projected[:, left : left + width]
-            key = projected[:, left + width : left + 2 * width]
-            value = projected[:, left + 2 * width : left + 3 * width].astype(BF16)
-            query_inverse = lax.rsqrt(jnp.mean(query * query, axis=-1, keepdims=True) + EPSILON)
-            key_inverse = lax.rsqrt(jnp.mean(key * key, axis=-1, keepdims=True) + EPSILON)
-            queries = (query * query_inverse * query_gain_ref[...]).astype(BF16)
-            keys = (key * key_inverse * key_gain_ref[...]).astype(BF16)
-            scores = dot_nt(queries, keys) * scale_factor + bias
+            _, _, queries = normed(projected_ref[pair, :, left : left + width], query_gain_ref[...])
+            left += width
+            _, _, keys = normed(projected_ref[pair, :, left : left + width], key_gain_ref[...])
+            left += width
+            value = projected_ref[pair, :, left : left + width].astype(BF16)
+            scores = dot_nt(queries, keys) * (1.0 / math.sqrt(width)) + bias
             row_max = jnp.max(scores, axis=-1, keepdims=True)
             weights = jnp.exp(scores - row_max)
             probs = (weights / jnp.sum(weights, axis=-1, keepdims=True)).astype(BF16)
-            probs_ref[head] = probs
+            probs_ref[2 * pair + head] = probs
             attended.append(dot_nn(probs, value).astype(BF16))
-        share = dot_nn(jnp.concatenate(attended, axis=1), out_weight_ref[...])
-
-        @pl.when(step == 0)
-        def _():
+        return jnp.concatenate(attended, axis=1)
+
+    copies.wait(halves)
+    project(0)
+    for pair in range(pairs):
+        if pair + 1 < pairs:
+            copies.wait(halves + 1)
+            project(pair + 1)
+        else:
+            copies.wait()
+        part = slice(pair * 2 * width, (pair + 1) * 2 * width)
+        share = dot_nn(attend(pair), out_weight_buffer[part, :])
+        if pair == 0:
             attention_ref[...] = share
-
-        @pl.when(step > 0)
-        def _():
+        elif pair + 1 < pairs:
             attention_ref[...] += share
-
-        @pl.when(step == pl.num_programs(0) - 1)
-        def _():
+        else:
+            total = attention_ref[...] + share
+            attention_ref[...] = total
             gate = gate_ref[...]
-            kept_ref[...] = (own_ref[...].astype(F32) + gate * attention_ref[:local, :]).astype(BF16)
-            sent_ref[...] = (gate * attention_ref[local:, :]).astype(BF16)
-
-    columns = pl.ds(pl.multiple_of(part * depth, depth), depth)
-    product = dot_nn(tokens_ref[:, columns], weight_ref[0])
-
-    @pl.when(part == 0)
-    def _():
-        total_ref[...] = product
-
-    @pl.when((part > 0) & (part < last_part))
-    def _():
-        total_ref[...] += product
-
-    @pl.when(part == last_part)
-    def _():
-        attend(product)
+            kept_ref[...] = (own_ref[...].astype(F32) + gate * total[:local]).astype(BF16)
+            sent_ref[...] = (gate * total[local:]).astype(BF16)
 
 
 def forward(neighbours, tile_slot, own, other, weight, out_weight, query_gain, key_gain, gate):
     local, model = own.shape
     pairs, _, wide = weight.shape
-    head_dim = query_gain.shape[1]
     tokens = 2 * local
-    whole = lambda i, k: (0, 0)
-    parts = 4
     smem = pl.BlockSpec(memory_space=pltpu.SMEM)
+    vmem = pl.BlockSpec(memory_space=pltpu.VMEM)
+    hbm = pl.BlockSpec(memory_space=pl.ANY)
     return pl.pallas_call(
         forward_kernel,
-        grid=(pairs, parts),
         out_shape=(
             jax.ShapeDtypeStruct((pairs, tokens, wide), F32),
             jax.ShapeDtypeStruct((2 * pairs, tokens, tokens), BF16),
@@ -396,43 +445,53 @@
             jax.ShapeDtypeStruct((local, model), BF16),
             jax.ShapeDtypeStruct((local, model), BF16),
         ),
-        in_specs=[
-            smem,
-            smem,
-            pl.BlockSpec((local, model), whole),
-            pl.BlockSpec((local, model), whole),
-            pl.BlockSpec((1, model // parts, wide), lambda i, k: (i, k, 0)),
-            pl.BlockSpec((2 * head_dim, model), lambda i, k: (i, 0)),
-            pl.BlockSpec((1, head_dim), whole),
-            pl.BlockSpec((1, head_dim), whole),
-            pl.BlockSpec((1, model), whole),
-        ],
-        out_specs=(
-            pl.BlockSpec((1, tokens, wide), lambda i, k: (i, 0, 0)),
-            pl.BlockSpec((2, tokens, tokens), lambda i, k: (i, 0, 0)),
-            pl.BlockSpec((tokens, model), whole),
-            pl.BlockSpec((local, model), whole),
-            pl.BlockSpec((local, model), whole),
-        ),
+        in_specs=[smem, smem, vmem, vmem, hbm, hbm, vmem, vmem, vmem],
+        out_specs=(vmem,) * 5,
         scratch_shapes=[
             pltpu.VMEM((tokens, model), BF16),
-            pltpu.VMEM((tokens, tokens), F32),
-            pltpu.VMEM((tokens, wide), F32),
+            pltpu.VMEM(weight.shape, BF16),
+            pltpu.VMEM(out_weight.shape, BF16),
+            pltpu.SemaphoreType.DMA((3 * pairs,)),
         ],
         compiler_params=params(46),
         cost_estimate=pl.CostEstimate(
-            flops=2 * tokens * model * pairs * (wide + 2 * head_dim),
-            bytes_accessed=2 * model * pairs * (wide + 2 * head_dim),
+            flops=2 * tokens * (weight.size + out_weight.size),
+            bytes_accessed=2 * (weight.size + out_weight.size),
             transcendentals=0,
         ),
         name="attention_forward",
     )(neighbours, tile_slot, own, other, weight, out_weight, query_gain, key_gain, gate)
 
 
+def input_grad_parts(weight_ref, buffer, first, block):
+    return [
+        (
+            weight_ref.at[:, pl.ds(first + start, block)],
+            buffer.at[:, pl.ds(start, block)],
+        )
+        for start in range(0, buffer.shape[1], block)
+    ]
+
+
+def input_grad_blocks(copies, grad_ref, buffer, own_ref, first, block, kept_ref, sent_ref):
+    local = own_ref.shape[0]
+    for start in range(0, buffer.shape[1], block):
+        copies.wait()
+        part = slice(start, start + block)
+        total = dot_nt(grad_ref[0], buffer[0, part, :])
+        for pair in range(1, grad_ref.shape[0]):
+            total += dot_nt(grad_ref[pair], buffer[pair, part, :])
+        own = own_ref[:, first + start : first + start + block].astype(F32)
+        kept_ref[:, part] = (own + total[:local]).astype(BF16)
+        sent_ref[:, part] = total[local:].astype(BF16)
+
+
 def backward_kernel(
+    block,
     own_ref,
     other_ref,
     out_weight_ref,
+    weight_ref,
     projected_ref,
     probs_ref,
     attention_ref,
@@ -441,122 +500,130 @@
     gate_ref,
     grad_ref,
     gate_grad_ref,
+    kept_ref,
+    sent_ref,
     scaled_ref,
+    attended_grad_ref,
+    out_weight_buffer,
+    weight_buffer,
+    semaphores,
 ):
-    step = pl.program_id(0)
     local = own_ref.shape[0]
     width = query_gain_ref.shape[1]
-    heads = probs_ref.shape[0]
-    columns = attention_ref.shape[1]
-
-    @pl.when(step == 0)
-    def _():
-        gate = gate_ref[...]
-        scaled_ref[:local, :] = (own_ref[...].astype(F32) * gate).astype(BF16)
-        scaled_ref[local:, :] = (other_ref[...].astype(F32) * gate).astype(BF16)
-
-    part = pl.ds(pl.multiple_of(step * columns, columns), columns)
+    pairs = grad_ref.shape[0]
+    order = []
+    for pair in range(pairs):
+        place = pl.ds(pair * 2 * width, 2 * width)
+        order.append((out_weight_ref.at[place], out_weight_buffer.at[place]))
+    order += input_grad_parts(weight_ref, weight_buffer, 0, block)
+    copies = Copies(order, semaphores, 4)
+
+    gate = gate_ref[...]
+    own, other = own_ref[...].astype(F32), other_ref[...].astype(F32)
+    scaled_ref[:local, :] = (own * gate).astype(BF16)
+    scaled_ref[local:, :] = (other * gate).astype(BF16)
     gate_grad_ref[...] = jnp.sum(
-        own_ref[:, part].astype(F32) * attention_ref[:local, :], axis=0, keepdims=True
-    ) + jnp.sum(other_ref[:, part].astype(F32) * attention_ref[local:, :], axis=0, keepdims=True)
-
-    attended_grad = dot_nt(scaled_ref[...], out_weight_ref[...]).astype(BF16)
-    scale_factor = 1.0 / math.sqrt(width)
-    for head in range(heads):
+        own * attention_ref[:local, :] + other * attention_ref[local:, :], axis=0, keepdims=True
+    )
+
+    def attended_grad(pair):
+        part = slice(pair * 2 * width, (pair + 1) * 2 * width)
+        product = dot_nt(scaled_ref[...], out_weight_buffer[part, :])
+        attended_grad_ref[pair] = product.astype(BF16)
+
+    def attend_backward(pair, head):
         left = head * 3 * width
-        query = projected_ref[0, :, left : left + width]
-        key = projected_ref[0, :, left + width : left + 2 * width]
-        value = projected_ref[0, :, left + 2 * width : left + 3 * width].astype(BF16)
-        query_inverse = lax.rsqrt(jnp.mean(query * query, axis=-1, keepdims=True) + EPSILON)
-        key_inverse = lax.rsqrt(jnp.mean(key * key, axis=-1, keepdims=True) + EPSILON)
-        query_unit = query * query_inverse
-        key_unit = key * key_inverse
-        queries = (query_unit * query_gain_ref[...]).astype(BF16)
-        keys = (key_unit * key_gain_ref[...]).astype(BF16)
-        grad = attended_grad[:, head * width : (head + 1) * width]
-        probs = probs_ref[head]
+        query_part = slice(left, left + width)
+        key_part = slice(left + width, left + 2 * width)
+        value_part = slice(left + 2 * width, left + 3 * width)
+        query_gain, key_gain = query_gain_ref[...], key_gain_ref[...]
+        query_unit, query_inverse, queries = normed(projected_ref[pair, :, query_part], query_gain)
+        key_unit, key_inverse, keys = normed(projected_ref[pair, :, key_part], key_gain)
+        value = projected_ref[pair, :, value_part].astype(BF16)
+        grad = attended_grad_ref[pair, :, head * width : (head + 1) * width]
+        probs = probs_ref[2 * pair + head]
         probs_wide = probs.astype(F32)
-        value_grad = dot_tn(probs, grad)
+        grad_ref[pair, :, value_part] = dot_tn(probs, grad).astype(BF16)
         prob_grad = dot_nt(grad, value)
         row_delta = jnp.sum(probs_wide * prob_grad, axis=-1, keepdims=True)
+        scale_factor = 1.0 / math.sqrt(width)
         score_grad = (probs_wide * (prob_grad - row_delta) * scale_factor).astype(BF16)
-        query_scaled = dot_nn(score_grad, keys) * query_gain_ref[...]
-        key_scaled = dot_tn(score_grad, queries) * key_gain_ref[...]
+        query_scaled = dot_nn(score_grad, keys) * query_gain
+        key_scaled = dot_tn(score_grad, queries) * key_gain
         query_mean = jnp.mean(query_scaled * query_unit, axis=-1, keepdims=True)
         key_mean = jnp.mean(key_scaled * key_unit, axis=-1, keepdims=True)
-        grad_ref[0, :, left : left + width] = (
+        grad_ref[pair, :, query_part] = (
             (query_scaled - query_unit * query_mean) * query_inverse
         ).astype(BF16)
-        grad_ref[0, :, left + width : left + 2 * width] = (
-            (key_scaled - key_unit * key_mean) * key_inverse
-        ).astype(BF16)
-        grad_ref[0, :, left + 2 * width : left + 3 * width] = value_grad.astype(BF16)
-
-
-def backward(own, other, out_weight, projected, probs, attention, query_gain, key_gain, gate):
+        grad_ref[pair, :, key_part] = ((key_scaled - key_unit * key_mean) * key_inverse).astype(BF16)
+
+    copies.wait()
+    attended_grad(0)
+    for pair in range(pairs):
+        if pair + 1 < pairs:
+            copies.wait()
+            attended_grad(pair + 1)
+        for head in range(2):
+            attend_backward(pair, head)
+    input_grad_blocks(copies, grad_ref, weight_buffer, own_ref, 0, block, kept_ref, sent_ref)
+
+
+def backward(
+    own, other, out_weight, weight, projected, probs, attention, query_gain, key_gain, gate, columns
+):
     local, model = own.shape
     pairs, tokens, wide = projected.shape
     head_dim = query_gain.shape[1]
-    whole = lambda i: (0, 0)
+    block = 256
+    vmem = pl.BlockSpec(memory_space=pltpu.VMEM)
+    hbm = pl.BlockSpec(memory_space=pl.ANY)
     return pl.pallas_call(
-        backward_kernel,
-        grid=(pairs,),
+        functools.partial(backward_kernel, block),
         out_shape=(
             jax.ShapeDtypeStruct((pairs, tokens, wide), BF16),
             jax.ShapeDtypeStruct((1, model), F32),
+            jax.ShapeDtypeStruct((local, columns), BF16),
+            jax.ShapeDtypeStruct((local, columns), BF16),
         ),
-        in_specs=[
-            pl.BlockSpec((local, model), whole),
-            pl.BlockSpec((local, model), whole),
-            pl.BlockSpec((2 * head_dim, model), lambda i: (i, 0)),
-            pl.BlockSpec((1, tokens, wide), lambda i: (i, 0, 0)),
-            pl.BlockSpec((2, tokens, tokens), lambda i: (i, 0, 0)),
-            pl.BlockSpec((tokens, model // pairs), lambda i: (0, i)),
-            pl.BlockSpec((1, head_dim), whole),
-            pl.BlockSpec((1, head_dim), whole),
-            pl.BlockSpec((1, model), whole),
+        in_specs=[vmem, vmem, hbm, hbm] + [vmem] * 6,
+        out_specs=(vmem,) * 4,
+        scratch_shapes=[
+            pltpu.VMEM((tokens, model), BF16),
+            pltpu.VMEM((pairs, tokens, 2 * head_dim), BF16),
+            pltpu.VMEM(out_weight.shape, BF16),
+            pltpu.VMEM((pairs, columns, wide), BF16),
+            pltpu.SemaphoreType.DMA((pairs + columns // block,)),
         ],
-        out_specs=(
-            pl.BlockSpec((1, tokens, wide), lambda i: (i, 0, 0)),
-            pl.BlockSpec((1, model // pairs), lambda i: (0, i)),
-        ),
-        scratch_shapes=[pltpu.VMEM((tokens, model), BF16)],
         compiler_params=params(46),
         cost_estimate=pl.CostEstimate(
-            flops=2 * tokens * model * pairs * 2 * head_dim,
-            bytes_accessed=2 * model * pairs * 2 * head_dim,
+            flops=2 * tokens * (out_weight.size + pairs * columns * wide),
+            bytes_accessed=2 * (out_weight.size + pairs * columns * wide),
             transcendentals=0,
         ),
         name="attention_backward",
-    )(own, other, out_weight, projected, probs, attention, query_gain, key_gain, gate)
-
-
-def input_grad_kernel(grad_ref, weight_ref, own_ref, kept_ref, sent_ref):
-    local = own_ref.shape[0]
-    total = dot_nt(grad_ref[0], weight_ref[0])
-    for pair in range(1, grad_ref.shape[0]):
-        total += dot_nt(grad_ref[pair], weight_ref[pair])
-    kept_ref[...] = (own_ref[...].astype(F32) + total[:local]).astype(BF16)
-    sent_ref[...] = total[local:].astype(BF16)
-
-
-def input_grad_part(grad, weight, own, part, parts, block):
+    )(own, other, out_weight, weight, projected, probs, attention, query_gain, key_gain, gate)
+
+
+def input_grad_kernel(first, block, grad_ref, weight_ref, own_ref, kept_ref, sent_ref, buffer, sems):
+    copies = Copies(input_grad_parts(weight_ref, buffer, first, block), sems, 4)
+    input_grad_blocks(copies, grad_ref, buffer, own_ref, first, block, kept_ref, sent_ref)
+
+
+def input_grad_part(grad, weight, own, first, columns):
     local, model = own.shape
     pairs, tokens, wide = grad.shape
-    columns = model // parts
-    first = part * columns // block
+    block = 256
     out = jax.ShapeDtypeStruct((local, columns), BF16)
-    out_spec = pl.BlockSpec((local, block), lambda i: (0, i))
+    vmem = pl.BlockSpec(memory_space=pltpu.VMEM)
     return pl.pallas_call(
-        input_grad_kernel,
-        grid=(columns // block,),
+        functools.partial(input_grad_kernel, first, block),
         out_shape=(out, out),
-        in_specs=[
-            pl.BlockSpec((pairs, tokens, wide), lambda i: (0, 0, 0)),
-            pl.BlockSpec((pairs, block, wide), lambda i: (0, i + first, 0)),
-            pl.BlockSpec((local, block), lambda i: (0, i + first)),
+        in_specs=[vmem, pl.BlockSpec(memory_space=pl.ANY), vmem],
+        out_specs=(vmem, vmem),
+        scratch_shapes=[
+            pltpu.VMEM((pairs, columns, wide), BF16),
+            pltpu.SemaphoreType.DMA((columns // block,)),
         ],
-        out_specs=(out_spec, out_spec),
         compiler_params=params(46),
         cost_estimate=pl.CostEstimate(
             flops=2 * tokens * columns * pairs * wide,
@@ -593,7 +660,7 @@
     out_local = out_weight[0]
     model = stream.shape[1]
     other_stream = routed(stream, 1, 0)
-    weight = regroup(qkv_weight[0], 128)
+    weight = regroup(qkv_weight[0], 128, 6)
     weight, upstream_after = lax.optimization_barrier((weight, upstream))
     other_upstream = routed(upstream_after, 1, 0)
     projected, probs, attention, kept, sent = forward(
@@ -609,19 +676,21 @@
     )
     kept = routed(kept, 0, 1)
     sent = routed(sent, 1, 1)
-    grad, gate_share = backward(
+    columns = model // 2
+    grad, gate_share, first, second = backward(
         upstream,
         other_upstream,
         out_local,
+        weight,
         projected,
         probs,
         attention,
         query_gain,
         key_gain,
         gate_scale,
+        columns,
     )
     other_gate = routed(gate_share, 1, 0)
-    first, second = input_grad_part(grad, weight, upstream, 0, 2, 256)
     pieces = [(routed(first, 0, -1), routed(second, 1, -1))]
     segment_output = (kept.astype(F32) + sent.astype(F32)).astype(BF16)
     half = model // lax.axis_size("seq")
@@ -629,7 +698,7 @@
         gate_share + other_gate, lax.axis_index("seq") * half, half, 1
     )
     grad, segment_output, gate_total = lax.optimization_barrier((grad, segment_output, gate_total))
-    first, second = input_grad_part(grad, weight, upstream, 1, 2, 256)
+    first, second = input_grad_part(grad, weight, upstream, columns, model - columns)
     pieces.append((routed(first, 0, -1), routed(second, 1, -1)))
     input_grad = jnp.concatenate(
         [(a.astype(F32) + b.astype(F32)).astype(BF16) for a, b in pieces], axis=1

time: 86.6 us -> 66.4 us (0.77)
  Pallas kernels: 66.2 us -> 46 us
    pallas_call x5 -> x4, Pallas kernels: 66.2 us -> 46 us  [the longest x1 14.2 us: regroup(): pl.pallas_call(functools.partial(regroup_kernel, rows, ahead), out_shape=...]
  transfers between devices with their start and end apart: 9 -> 9, of which waited for: 2 -> 3; matrix products, arithmetic and copies ran while one was open for 2% -> 2% of each run, Pallas kernels for 77% -> 70%
where the time goes in v5:
time: 66.4 us; the launch traced here: 65.8 us
  Pallas kernels  46 us (69%)
  starting transfers between devices  10.1 us (15%)
  waiting for transfers between devices  6.57 us (10%)
  other arithmetic  2.31 us (3%)
  between operations  0.77 us (1%)
    pallas_call x1, Pallas kernels, regroup(): pl.pallas_call(functools.partial(regroup_kernel, rows, ahead), out_shape=...  14.2 us
    pallas_call x1, Pallas kernels, backward(): pl.pallas_call(functools.partial(backward_kernel, block), out_shape=(jax....  12.8 us
    pallas_call x1, Pallas kernels, forward(): pl.pallas_call(forward_kernel, out_shape=(jax.ShapeDtypeStruct((pairs, to...  11.6 us
    ppermute x9, starting transfers between devices, routed(): return lax.ppermute(block, ('seq', 'pipe'), route)  10.1 us
    pallas_call x1, Pallas kernels, input_grad_part(): pl.pallas_call(functools.partial(input_grad_kernel, first, block), out_sh...  7.37 us
    ppermute x9, waiting for transfers between devices, routed(): return lax.ppermute(block, ('seq', 'pipe'), route)  6.57 us
  transfers between devices with their start and end apart: 9, of which 3 were waited for; matrix products, arithmetic and copies ran while one was open for 2% of the time, Pallas kernels for 70%

profile of v5, /device:TPU:1, one launch (start us, length us, event | category | flops | bytes accessed | tf_op | source)
XLA Modules:
  0.0 65.8 jit_solution(5539483282754301424)
XLA Ops:
  0.6 2.1 %collective-permute-start.1 = (bf16[64,3072]{1,0:T(8,128)(2,1)}, bf16[64,3072]{1,0:T(8,128)(2,1)S(1)}, u32[]{:S(2)}, u32[]{:S(2)}) collective-permute-start(bf16[64,3072]{1,0:T(8,128)(2,1)} %bitcast.10), channel_id=1, source_target_pairs={{0,16},{4,20},{8,24},{12,28},{16,0},{20,4},{24,8},{28,12},{1,17},{... | collective-permute-start | bytes 1179656 | tf_op jit(solution)/shard_map/ppermute | solution.py:644
  2.8 0.0 copy-start.4
  2.8 0.0 copy-start.5
  2.8 0.0 copy-start.6
  2.8 14.2 %regroup.1.weight_ref = bf16[4,3072,768]{2,1,0:T(8,128)(2,1)} custom-call(bf16[3072,8,384]{2,1,0:T(8,128)(2,1)} %bitcast.14), custom_call_target="tpu_custom_call" | custom-call | bytes 37748736 | tf_op jit(solution)/shard_map/regroup/pallas_call | solution.py:289
  16.9 0.0 copy-done
  16.9 0.1 collective-permute-start
  17.0 0.0 collective-permute-done.1.other_ref
  17.0 0.0 copy-done.1
  17.0 0.0 copy-done.2
  17.1 0.0 copy-done.3
  17.1 11.6 %attention_forward.1 = (f32[4,128,768]{2,1,0:T(8,128)S(1)}, bf16[8,128,128]{2,1,0:T(8,128)(2,1)S(1)}, f32[128,3072]{1,0:T(8,128)S(1)}, bf16[64,3072]{1,0:T(8,128)(2,1)S(1)}, bf16[64,3072]{1,0:T(8,128)(2,1)S(1)}) custom-call(s32[2,27]{1,0:T(2,128)S(1)} %copy-done.5, s32[2]{0:T(128)S(1)} %copy-done.6, bf16[64,3072]{1,0:T(8,128)(2,1)S(1)} %bitcast.11, ...), custom_call_target="tpu_custom_call" | custom-call | flops 3221225472 | bytes 25165824 | tf_op jit(solution)/shard_map/attention_forward/pallas_call | solution.py:439
  28.7 2.6 %collective-permute-start.2 = (bf16[64,3072]{1,0:T(8,128)(2,1)S(1)}, bf16[64,3072]{1,0:T(8,128)(2,1)S(1)}, u32[]{:S(2)}, u32[]{:S(2)}) collective-permute-start(bf16[64,3072]{1,0:T(8,128)(2,1)S(1)} %get-tuple-element.25), channel_id=1, source_target_pairs={{0,4},{4,8},{8,12},{12,0},{16,20},{20,24},{24,28},{28,16},{1,5},{5... | collective-permute-start | bytes 1179656 | tf_op jit(solution)/shard_map/ppermute | solution.py:644
  31.3 1.0 %collective-permute-start.3 = (bf16[64,3072]{1,0:T(8,128)(2,1)S(1)}, bf16[64,3072]{1,0:T(8,128)(2,1)S(1)}, u32[]{:S(2)}, u32[]{:S(2)}) collective-permute-start(bf16[64,3072]{1,0:T(8,128)(2,1)S(1)} %get-tuple-element.26), channel_id=1, source_target_pairs={{0,20},{4,24},{8,28},{12,16},{16,4},{20,8},{24,12},{28,0},{1,21},{... | collective-permute-start | bytes 1179656 | tf_op jit(solution)/shard_map/ppermute | solution.py:644
  32.3 0.0 collective-permute-done.other_ref
  32.3 12.8 %attention_backward.1 = (bf16[4,128,768]{2,1,0:T(8,128)(2,1)S(1)}, f32[1,3072]{1,0:T(1,128)S(1)}, bf16[64,1536]{1,0:T(8,128)(2,1)S(1)}, bf16[64,1536]{1,0:T(8,128)(2,1)S(1)}) custom-call(bf16[64,3072]{1,0:T(8,128)(2,1)S(1)} %bitcast.8, bf16[64,3072]{1,0:T(8,128)(2,1)S(1)} %collective-permute-done.other_ref, bf16[1024,3072]{1,0:T(8,128)(2,1)} %bitcast.13, ...), custom_call_target="tpu_custom_call" | custom-call | flops 2013265920 | bytes 15728640 | tf_op jit(solution)/shard_map/attention_backward/pallas_call | solution.py:580
  45.2 0.3 collective-permute-start.4
  45.5 0.9 %collective-permute-start.5 = (bf16[64,1536]{1,0:T(8,128)(2,1)S(1)}, bf16[64,1536]{1,0:T(8,128)(2,1)S(1)}, u32[]{:S(2)}, u32[]{:S(2)}) collective-permute-start(bf16[64,1536]{1,0:T(8,128)(2,1)S(1)} %get-tuple-element.29), channel_id=1, source_target_pairs={{0,12},{4,0},{8,4},{12,8},{16,28},{20,16},{24,20},{28,24},{1,13},{... | collective-permute-start | bytes 589832 | tf_op jit(solution)/shard_map/ppermute | solution.py:644
  46.4 1.1 %collective-permute-start.6 = (bf16[64,1536]{1,0:T(8,128)(2,1)S(1)}, bf16[64,1536]{1,0:T(8,128)(2,1)S(1)}, u32[]{:S(2)}, u32[]{:S(2)}) collective-permute-start(bf16[64,1536]{1,0:T(8,128)(2,1)S(1)} %get-tuple-element.30), channel_id=1, source_target_pairs={{0,28},{4,16},{8,20},{12,24},{16,12},{20,0},{24,4},{28,8},{1,29},{... | collective-permute-start | bytes 589832 | tf_op jit(solution)/shard_map/ppermute | solution.py:644
  47.5 0.3 collective-permute-done.4
  47.8 0.6 dynamic-slice_add_fusion
  48.4 0.0 collective-permute-done.2
  48.4 0.0 collective-permute-done.3
  48.4 0.8 %add_convert_fusion = bf16[64,3072]{1,0:T(8,128)(2,1)} fusion(bf16[64,3072]{1,0:T(8,128)(2,1)S(1)} %collective-permute-done.3, bf16[64,3072]{1,0:T(8,128)(2,1)S(1)} %collective-permute-done.2), kind=kLoop, calls=%fused_computation | loop fusion | flops 786432 | bytes 1179648 | tf_op jit(solution)/shard_map/convert_element_type | solution.py:695
  49.3 7.4 %input_grad.1 = (bf16[64,1536]{1,0:T(8,128)(2,1)S(1)}, bf16[64,1536]{1,0:T(8,128)(2,1)S(1)}) custom-call(bf16[4,128,768]{2,1,0:T(8,128)(2,1)S(1)} %get-tuple-element.31.grad_ref, bf16[4,3072,768]{2,1,0:T(8,128)(2,1)} %regroup.1.weight_ref, bf16[64,3072]{1,0:T(8,128)(2,1)S(1)} %bitcast.9), custom_call_target="tpu_custom_call" | custom-call | flops 1207959552 | bytes 9437184 | tf_op jit(solution)/shard_map/input_grad/pallas_call | solution.py:618
  56.6 1.9 %collective-permute-start.7 = (bf16[64,1536]{1,0:T(8,128)(2,1)S(1)}, bf16[64,1536]{1,0:T(8,128)(2,1)S(1)}, u32[]{:S(2)}, u32[]{:S(2)}) collective-permute-start(bf16[64,1536]{1,0:T(8,128)(2,1)S(1)} %get-tuple-element.32), channel_id=1, source_target_pairs={{0,12},{4,0},{8,4},{12,8},{16,28},{20,16},{24,20},{28,24},{1,13},{... | collective-permute-start | bytes 589832 | tf_op jit(solution)/shard_map/ppermute | solution.py:644
  58.6 0.1 collective-permute-start.8
  58.7 0.0 collective-permute-done.5
  58.7 0.0 collective-permute-done.6
  58.7 3.5 %collective-permute-done.7 = bf16[64,1536]{1,0:T(8,128)(2,1)S(1)} collective-permute-done((bf16[64,1536]{1,0:T(8,128)(2,1)S(1)}, bf16[64,1536]{1,0:T(8,128)(2,1)S(1)}, u32[]{:S(2)}, u32[]{:S(2)}) %collective-permute-start.7) | collective-permute-done | bytes 196640 | tf_op jit(solution)/shard_map/ppermute | solution.py:644
  62.2 2.8 %collective-permute-done.8 = bf16[64,1536]{1,0:T(8,128)(2,1)S(1)} collective-permute-done((bf16[64,1536]{1,0:T(8,128)(2,1)S(1)}, bf16[64,1536]{1,0:T(8,128)(2,1)S(1)}, u32[]{:S(2)}, u32[]{:S(2)}) %collective-permute-start.8) | collective-permute-done | bytes 196640 | tf_op jit(solution)/shard_map/ppermute | solution.py:644
  65.0 0.8 %maximum_bitcast_fusion = bf16[1,64,3072]{2,1,0:T(8,128)(2,1)} fusion(bf16[64,1536]{1,0:T(8,128)(2,1)S(1)} %add_convert_fusion.1, bf16[64,1536]{1,0:T(8,128)(2,1)S(1)} %add_convert_fusion.2), kind=kLoop, calls=%fused_computation.1 | loop fusion | flops 786432 | bytes 786432 | tf_op jit(solution)/shard_map/broadcast_in_dim | solution.py:706
  (9 shorter events, 0.1 us)
Async XLA Ops:
  0.6 16.4 %collective-permute-start.1 = (bf16[64,3072]{1,0:T(8,128)(2,1)}, bf16[64,3072]{1,0:T(8,128)(2,1)S(1)}, u32[]{:S(2)}, u32[]{:S(2)}) collective-permute-start(bf16[64,3072]{1,0:T(8,128)(2,1)} %bitcast.10), channel_id=1, source_target_pairs={{0,16},{4,20},{8,24},{12,28},{16,0},{20,4},{24,8},{28,12},{1,17},{... | collective-permute-start | bytes 1179656 | tf_op jit(solution)/shard_map/ppermute | solution.py:644
  2.7 14.2 %copy-start = (bf16[1,64,3072]{2,1,0:T(8,128)(2,1)S(1)}, bf16[1,64,3072]{2,1,0:T(8,128)(2,1)}, u32[]{:S(2)}) copy-start(bf16[1,64,3072]{2,1,0:T(8,128)(2,1)} %param.10) | copy-start | bytes 1179652
  2.7 14.3 %copy-start.1 = (bf16[1,64,3072]{2,1,0:T(8,128)(2,1)S(1)}, bf16[1,64,3072]{2,1,0:T(8,128)(2,1)}, u32[]{:S(2)}) copy-start(bf16[1,64,3072]{2,1,0:T(8,128)(2,1)} %param.9) | copy-start | bytes 1179652
  2.7 14.3 %copy-start.2 = (f32[1,3072]{1,0:T(1,128)S(1)}, f32[1,3072]{1,0:T(1,128)}, u32[]{:S(2)}) copy-start(f32[1,3072]{1,0:T(1,128)} %gate_ref.3) | copy-start | bytes 36868
  2.7 14.3 %copy-start.3 = (f32[1,128]{1,0:T(1,128)S(1)}, f32[1,128]{1,0:T(1,128)}, u32[]{:S(2)}) copy-start(f32[1,128]{1,0:T(1,128)} %query_gain_ref.3) | copy-start | bytes 1540
  2.8 14.3 %copy-start.4 = (f32[1,128]{1,0:T(1,128)S(1)}, f32[1,128]{1,0:T(1,128)}, u32[]{:S(2)}) copy-start(f32[1,128]{1,0:T(1,128)} %key_gain_ref.3) | copy-start | bytes 1540
  2.8 14.3 %copy-start.5 = (s32[2,27]{1,0:T(2,128)S(1)}, s32[2,27]{1,0:T(2,128)}, u32[]{:S(2)}) copy-start(s32[2,27]{1,0:T(2,128)} %neighbours_ref.1) | copy-start | bytes 652
  2.8 14.3 %copy-start.6 = (s32[2]{0:T(128)S(1)}, s32[2]{0:T(128)}, u32[]{:S(2)}) copy-start(s32[2]{0:T(128)} %tile_slot_ref.1) | copy-start | bytes 28
  16.9 15.4 %collective-permute-start = (bf16[64,3072]{1,0:T(8,128)(2,1)S(1)}, bf16[64,3072]{1,0:T(8,128)(2,1)S(1)}, u32[]{:S(2)}, u32[]{:S(2)}) collective-permute-start(bf16[64,3072]{1,0:T(8,128)(2,1)S(1)} %bitcast.7), channel_id=1, source_target_pairs={{0,16},{4,20},{8,24},{12,28},{16,0},{20,4},{24,8},{28,12},{1,17},{... | collective-permute-start | bytes 1179656 | tf_op jit(solution)/shard_map/ppermute | solution.py:644
  28.7 19.7 %collective-permute-start.2 = (bf16[64,3072]{1,0:T(8,128)(2,1)S(1)}, bf16[64,3072]{1,0:T(8,128)(2,1)S(1)}, u32[]{:S(2)}, u32[]{:S(2)}) collective-permute-start(bf16[64,3072]{1,0:T(8,128)(2,1)S(1)} %get-tuple-element.25), channel_id=1, source_target_pairs={{0,4},{4,8},{8,12},{12,0},{16,20},{20,24},{24,28},{28,16},{1,5},{5... | collective-permute-start | bytes 1179656 | tf_op jit(solution)/shard_map/ppermute | solution.py:644
  31.3 17.1 %collective-permute-start.3 = (bf16[64,3072]{1,0:T(8,128)(2,1)S(1)}, bf16[64,3072]{1,0:T(8,128)(2,1)S(1)}, u32[]{:S(2)}, u32[]{:S(2)}) collective-permute-start(bf16[64,3072]{1,0:T(8,128)(2,1)S(1)} %get-tuple-element.26), channel_id=1, source_target_pairs={{0,20},{4,24},{8,28},{12,16},{16,4},{20,8},{24,12},{28,0},{1,21},{... | collective-permute-start | bytes 1179656 | tf_op jit(solution)/shard_map/ppermute | solution.py:644
  45.2 2.6 %collective-permute-start.4 = (f32[1,3072]{1,0:T(1,128)S(1)}, f32[1,3072]{1,0:T(1,128)S(1)}, u32[]{:S(2)}, u32[]{:S(2)}) collective-permute-start(f32[1,3072]{1,0:T(1,128)S(1)} %get-tuple-element.27), channel_id=1, source_target_pairs={{0,16},{4,20},{8,24},{12,28},{16,0},{20,4},{24,8},{28,12},{1,17},{... | collective-permute-start | bytes 36872 | tf_op jit(solution)/shard_map/ppermute | solution.py:644
  45.5 13.2 %collective-permute-start.5 = (bf16[64,1536]{1,0:T(8,128)(2,1)S(1)}, bf16[64,1536]{1,0:T(8,128)(2,1)S(1)}, u32[]{:S(2)}, u32[]{:S(2)}) collective-permute-start(bf16[64,1536]{1,0:T(8,128)(2,1)S(1)} %get-tuple-element.29), channel_id=1, source_target_pairs={{0,12},{4,0},{8,4},{12,8},{16,28},{20,16},{24,20},{28,24},{1,13},{... | collective-permute-start | bytes 589832 | tf_op jit(solution)/shard_map/ppermute | solution.py:644
  46.4 12.3 %collective-permute-start.6 = (bf16[64,1536]{1,0:T(8,128)(2,1)S(1)}, bf16[64,1536]{1,0:T(8,128)(2,1)S(1)}, u32[]{:S(2)}, u32[]{:S(2)}) collective-permute-start(bf16[64,1536]{1,0:T(8,128)(2,1)S(1)} %get-tuple-element.30), channel_id=1, source_target_pairs={{0,28},{4,16},{8,20},{12,24},{16,12},{20,0},{24,4},{28,8},{1,29},{... | collective-permute-start | bytes 589832 | tf_op jit(solution)/shard_map/ppermute | solution.py:644
  56.6 5.6 %collective-permute-start.7 = (bf16[64,1536]{1,0:T(8,128)(2,1)S(1)}, bf16[64,1536]{1,0:T(8,128)(2,1)S(1)}, u32[]{:S(2)}, u32[]{:S(2)}) collective-permute-start(bf16[64,1536]{1,0:T(8,128)(2,1)S(1)} %get-tuple-element.32), channel_id=1, source_target_pairs={{0,12},{4,0},{8,4},{12,8},{16,28},{20,16},{24,20},{28,24},{1,13},{... | collective-permute-start | bytes 589832 | tf_op jit(solution)/shard_map/ppermute | solution.py:644
  58.6 6.4 %collective-permute-start.8 = (bf16[64,1536]{1,0:T(8,128)(2,1)S(1)}, bf16[64,1536]{1,0:T(8,128)(2,1)S(1)}, u32[]{:S(2)}, u32[]{:S(2)}) collective-permute-start(bf16[64,1536]{1,0:T(8,128)(2,1)S(1)} %get-tuple-element.33), channel_id=1, source_target_pairs={{0,28},{4,16},{8,20},{12,24},{16,12},{20,0},{24,4},{28,8},{1,29},{... | collective-permute-start | bytes 589832 | tf_op jit(solution)/shard_map/ppermute | solution.py:644

commit v6 on v5

--- a/solution.py
+++ b/solution.py
@@ -13,6 +13,7 @@
 F32 = jnp.float32
 BF16 = jnp.bfloat16
 MIB = 1024 * 1024
+GROUP = 4
 
 
 def passed_along(block, axis, distance):
@@ -274,8 +275,8 @@
 
         by_head = jnp.swapaxes(read_ref[part(step)], 0, 1)
         for head in range(heads):
-            left = (head % 2) * width
-            written_ref[head // 2, part(step), left : left + width] = by_head[head]
+            left = (head % GROUP) * width
+            written_ref[head // GROUP, part(step), left : left + width] = by_head[head]
         write(step).start()
 
     @pl.loop(0, steps)
@@ -285,7 +286,7 @@
 
 def regroup(weight, rows, ahead):
     depth, heads, width = weight.shape
-    out = (heads // 2, depth, 2 * width)
+    out = (heads // GROUP, depth, GROUP * width)
     return pl.pallas_call(
         functools.partial(regroup_kernel, rows, ahead),
         out_shape=jax.ShapeDtypeStruct(out, weight.dtype),
@@ -350,23 +351,24 @@
     local, model = own_ref.shape
     tokens = 2 * local
     width = query_gain_ref.shape[1]
-    pairs = weight_ref.shape[0]
-    halves = 2
-    half = model // halves
-
-    def weight_part(pair, index):
-        place = (pair, pl.ds(index * half, half))
+    groups = weight_ref.shape[0]
+    parts = 4
+    depth = model // parts
+    rows = GROUP * width
+
+    def weight_part(group, index):
+        place = (group, pl.ds(index * depth, depth))
         return weight_ref.at[place], weight_buffer.at[place]
 
-    def out_weight_part(pair):
-        place = pl.ds(pair * 2 * width, 2 * width)
+    def out_weight_part(group):
+        place = pl.ds(group * rows, rows)
         return out_weight_ref.at[place], out_weight_buffer.at[place]
 
-    order = [weight_part(0, 0), weight_part(0, 1)]
-    for pair in range(1, pairs):
-        order += [weight_part(pair, 0), weight_part(pair, 1), out_weight_part(pair - 1)]
-    order.append(out_weight_part(pairs - 1))
-    copies = Copies(order, semaphores, 3)
+    order = []
+    for group in range(groups):
+        order += [weight_part(group, index) for index in range(parts)]
+    order += [out_weight_part(group) for group in range(groups)]
+    copies = Copies(order, semaphores, 4)
 
     tokens_ref[:local, :] = own_ref[...]
     tokens_ref[local:, :] = other_ref[...]
@@ -382,56 +384,59 @@
             table = jnp.where((row_slot == r) & (column_slot == c), allowed[r][c], table)
     bias = jnp.where(table > 0, 0.0, -jnp.inf).astype(F32)
 
-    def project(pair):
+    def project(group):
         total = None
-        for index in range(halves):
-            part = slice(index * half, (index + 1) * half)
-            product = dot_nn(tokens_ref[:, part], weight_buffer[pair, part, :])
+        for index in range(parts):
+            copies.wait()
+            part = slice(index * depth, (index + 1) * depth)
+            product = dot_nn(tokens_ref[:, part], weight_buffer[group, part, :])
             total = product if total is None else total + product
-        projected_ref[pair] = total
-
-    def attend(pair):
+        projected_ref[group] = total
+
+    def attend(group):
         attended = []
-        for head in range(2):
+        for head in range(GROUP):
             left = head * 3 * width
-            _, _, queries = normed(projected_ref[pair, :, left : left + width], query_gain_ref[...])
+            _, _, queries = normed(projected_ref[group, :, left : left + width], query_gain_ref[...])
             left += width
-            _, _, keys = normed(projected_ref[pair, :, left : left + width], key_gain_ref[...])
+            _, _, keys = normed(projected_ref[group, :, left : left + width], key_gain_ref[...])
             left += width
-            value = projected_ref[pair, :, left : left + width].astype(BF16)
+            value = projected_ref[group, :, left : left + width].astype(BF16)
             scores = dot_nt(queries, keys) * (1.0 / math.sqrt(width)) + bias
             row_max = jnp.max(scores, axis=-1, keepdims=True)
             weights = jnp.exp(scores - row_max)
             probs = (weights / jnp.sum(weights, axis=-1, keepdims=True)).astype(BF16)
-            probs_ref[2 * pair + head] = probs
+            probs_ref[GROUP * group + head] = probs
             attended.append(dot_nn(probs, value).astype(BF16))
         return jnp.concatenate(attended, axis=1)
 
-    copies.wait(halves)
+    def share(group, attended):
+        return dot_nn(attended, out_weight_buffer[group * rows : (group + 1) * rows, :])
+
     project(0)
-    for pair in range(pairs):
-        if pair + 1 < pairs:
-            copies.wait(halves + 1)
-            project(pair + 1)
+    attended = attend(0)
+    for group in range(1, groups):
+        project(group)
+        copies.wait()
+        following = attend(group)
+        if group == 1:
+            attention_ref[...] = share(0, attended)
         else:
-            copies.wait()
-        part = slice(pair * 2 * width, (pair + 1) * 2 * width)
-        share = dot_nn(attend(pair), out_weight_buffer[part, :])
-        if pair == 0:
-            attention_ref[...] = share
-        elif pair + 1 < pairs:
-            attention_ref[...] += share
-        else:
-            total = attention_ref[...] + share
-            attention_ref[...] = total
-            gate = gate_ref[...]
-            kept_ref[...] = (own_ref[...].astype(F32) + gate * total[:local]).astype(BF16)
-            sent_ref[...] = (gate * total[local:]).astype(BF16)
+            attention_ref[...] += share(group - 1, attended)
+        attended = following
+    copies.wait()
+    total = share(groups - 1, attended)
+    if groups > 1:
+        total += attention_ref[...]
+    attention_ref[...] = total
+    gate = gate_ref[...]
+    kept_ref[...] = (own_ref[...].astype(F32) + gate * total[:local]).astype(BF16)
+    sent_ref[...] = (gate * total[local:]).astype(BF16)
 
 
 def forward(neighbours, tile_slot, own, other, weight, out_weight, query_gain, key_gain, gate):
     local, model = own.shape
-    pairs, _, wide = weight.shape
+    groups, _, wide = weight.shape
     tokens = 2 * local
     smem = pl.BlockSpec(memory_space=pltpu.SMEM)
     vmem = pl.BlockSpec(memory_space=pltpu.VMEM)
@@ -439,8 +444,8 @@
     return pl.pallas_call(
         forward_kernel,
         out_shape=(
-            jax.ShapeDtypeStruct((pairs, tokens, wide), F32),
-            jax.ShapeDtypeStruct((2 * pairs, tokens, tokens), BF16),
+            jax.ShapeDtypeStruct((groups, tokens, wide), F32),
+            jax.ShapeDtypeStruct((GROUP * groups, tokens, tokens), BF16),
             jax.ShapeDtypeStruct((tokens, model), F32),
             jax.ShapeDtypeStruct((local, model), BF16),
             jax.ShapeDtypeStruct((local, model), BF16),
@@ -451,7 +456,7 @@
             pltpu.VMEM((tokens, model), BF16),
             pltpu.VMEM(weight.shape, BF16),
             pltpu.VMEM(out_weight.shape, BF16),
-            pltpu.SemaphoreType.DMA((3 * pairs,)),
+            pltpu.SemaphoreType.DMA((5 * groups,)),
         ],
         compiler_params=params(46),
         cost_estimate=pl.CostEstimate(
@@ -510,10 +515,11 @@
 ):
     local = own_ref.shape[0]
     width = query_gain_ref.shape[1]
-    pairs = grad_ref.shape[0]
+    groups = grad_ref.shape[0]
+    rows = GROUP * width
     order = []
-    for pair in range(pairs):
-        place = pl.ds(pair * 2 * width, 2 * width)
+    for start in range(0, groups * rows, rows // 2):
+        place = pl.ds(start, rows // 2)
         order.append((out_weight_ref.at[place], out_weight_buffer.at[place]))
     order += input_grad_parts(weight_ref, weight_buffer, 0, block)
     copies = Copies(order, semaphores, 4)
@@ -526,24 +532,25 @@
         own * attention_ref[:local, :] + other * attention_ref[local:, :], axis=0, keepdims=True
     )
 
-    def attended_grad(pair):
-        part = slice(pair * 2 * width, (pair + 1) * 2 * width)
+    def attended_grad(group):
+        copies.wait(2)
+        part = slice(group * rows, (group + 1) * rows)
         product = dot_nt(scaled_ref[...], out_weight_buffer[part, :])
-        attended_grad_ref[pair] = product.astype(BF16)
-
-    def attend_backward(pair, head):
+        attended_grad_ref[group] = product.astype(BF16)
+
+    def attend_backward(group, head):
         left = head * 3 * width
         query_part = slice(left, left + width)
         key_part = slice(left + width, left + 2 * width)
         value_part = slice(left + 2 * width, left + 3 * width)
         query_gain, key_gain = query_gain_ref[...], key_gain_ref[...]
-        query_unit, query_inverse, queries = normed(projected_ref[pair, :, query_part], query_gain)
-        key_unit, key_inverse, keys = normed(projected_ref[pair, :, key_part], key_gain)
-        value = projected_ref[pair, :, value_part].astype(BF16)
-        grad = attended_grad_ref[pair, :, head * width : (head + 1) * width]
-        probs = probs_ref[2 * pair + head]
+        query_unit, query_inverse, queries = normed(projected_ref[group, :, query_part], query_gain)
+        key_unit, key_inverse, keys = normed(projected_ref[group, :, key_part], key_gain)
+        value = projected_ref[group, :, value_part].astype(BF16)
+        grad = attended_grad_ref[group, :, head * width : (head + 1) * width]
+        probs = probs_ref[GROUP * group + head]
         probs_wide = probs.astype(F32)
-        grad_ref[pair, :, value_part] = dot_tn(probs, grad).astype(BF16)
+        grad_ref[group, :, value_part] = dot_tn(probs, grad).astype(BF16)
         prob_grad = dot_nt(grad, value)
         row_delta = jnp.sum(probs_wide * prob_grad, axis=-1, keepdims=True)
         scale_factor = 1.0 / math.sqrt(width)
@@ -552,19 +559,17 @@
         key_scaled = dot_tn(score_grad, queries) * key_gain
         query_mean = jnp.mean(query_scaled * query_unit, axis=-1, keepdims=True)
         key_mean = jnp.mean(key_scaled * key_unit, axis=-1, keepdims=True)
-        grad_ref[pair, :, query_part] = (
+        grad_ref[group, :, query_part] = (
             (query_scaled - query_unit * query_mean) * query_inverse
         ).astype(BF16)
-        grad_ref[pair, :, key_part] = ((key_scaled - key_unit * key_mean) * key_inverse).astype(BF16)
-
-    copies.wait()
+        grad_ref[group, :, key_part] = ((key_scaled - key_unit * key_mean) * key_inverse).astype(BF16)
+
     attended_grad(0)
-    for pair in range(pairs):
-        if pair + 1 < pairs:
-            copies.wait()
-            attended_grad(pair + 1)
-        for head in range(2):
-            attend_backward(pair, head)
+    for group in range(groups):
+        if group + 1 < groups:
+            attended_grad(group + 1)
+        for head in range(GROUP):
+            attend_backward(group, head)
     input_grad_blocks(copies, grad_ref, weight_buffer, own_ref, 0, block, kept_ref, sent_ref)
 
 
@@ -572,15 +577,15 @@
     own, other, out_weight, weight, projected, probs, attention, query_gain, key_gain, gate, columns
 ):
     local, model = own.shape
-    pairs, tokens, wide = projected.shape
+    groups, tokens, wide = projected.shape
     head_dim = query_gain.shape[1]
-    block = 256
+    block = 512
     vmem = pl.BlockSpec(memory_space=pltpu.VMEM)
     hbm = pl.BlockSpec(memory_space=pl.ANY)
     return pl.pallas_call(
         functools.partial(backward_kernel, block),
         out_shape=(
-            jax.ShapeDtypeStruct((pairs, tokens, wide), BF16),
+            jax.ShapeDtypeStruct((groups, tokens, wide), BF16),
             jax.ShapeDtypeStruct((1, model), F32),
             jax.ShapeDtypeStruct((local, columns), BF16),
             jax.ShapeDtypeStruct((local, columns), BF16),
@@ -589,15 +594,15 @@
         out_specs=(vmem,) * 4,
         scratch_shapes=[
             pltpu.VMEM((tokens, model), BF16),
-            pltpu.VMEM((pairs, tokens, 2 * head_dim), BF16),
+            pltpu.VMEM((groups, tokens, GROUP * head_dim), BF16),
             pltpu.VMEM(out_weight.shape, BF16),
-            pltpu.VMEM((pairs, columns, wide), BF16),
-            pltpu.SemaphoreType.DMA((pairs + columns // block,)),
+            pltpu.VMEM((groups, columns, wide), BF16),
+            pltpu.SemaphoreType.DMA((2 * groups + columns // block,)),
         ],
         compiler_params=params(46),
         cost_estimate=pl.CostEstimate(
-            flops=2 * tokens * (out_weight.size + pairs * columns * wide),
-            bytes_accessed=2 * (out_weight.size + pairs * columns * wide),
+            flops=2 * tokens * (out_weight.size + groups * columns * wide),
+            bytes_accessed=2 * (out_weight.size + groups * columns * wide),
             transcendentals=0,
         ),
         name="attention_backward",
@@ -612,7 +617,7 @@
 def input_grad_part(grad, weight, own, first, columns):
     local, model = own.shape
     pairs, tokens, wide = grad.shape
-    block = 256
+    block = 512
     out = jax.ShapeDtypeStruct((local, columns), BF16)
     vmem = pl.BlockSpec(memory_space=pltpu.VMEM)
     return pl.pallas_call(
@@ -692,14 +697,17 @@
     )
     other_gate = routed(gate_share, 1, 0)
     pieces = [(routed(first, 0, -1), routed(second, 1, -1))]
+    grad, kept, sent = lax.optimization_barrier((grad, kept, sent))
+    first, second = input_grad_part(grad, weight, upstream, columns, model - columns)
+    first, second, kept, sent, gate_share, other_gate = lax.optimization_barrier(
+        (first, second, kept, sent, gate_share, other_gate)
+    )
+    pieces.append((routed(first, 0, -1), routed(second, 1, -1)))
     segment_output = (kept.astype(F32) + sent.astype(F32)).astype(BF16)
     half = model // lax.axis_size("seq")
     gate_total = lax.dynamic_slice_in_dim(
         gate_share + other_gate, lax.axis_index("seq") * half, half, 1
     )
-    grad, segment_output, gate_total = lax.optimization_barrier((grad, segment_output, gate_total))
-    first, second = input_grad_part(grad, weight, upstream, columns, model - columns)
-    pieces.append((routed(first, 0, -1), routed(second, 1, -1)))
     input_grad = jnp.concatenate(
         [(a.astype(F32) + b.astype(F32)).astype(BF16) for a, b in pieces], axis=1
     )
@@ -726,7 +734,7 @@
 
     def body(*args):
         one_tile_each = args[0].shape[1] == TILE and args[8].shape[0] == 2
-        if mesh.shape["seq"] == 2 and one_tile_each and args[2].shape[2] % 2 == 0:
+        if mesh.shape["seq"] == 2 and one_tile_each and args[2].shape[2] % GROUP == 0:
             return pair_body(*args)
         return general_body(*args)
 

time: 66.4 us -> 69.3 us (1.044)
  waiting for transfers between devices: 6.57 us -> 16.4 us
  Pallas kernels: 46 us -> 39.9 us
    ppermute x9, waiting for transfers between devices: 6.57 us -> 16.4 us  [routed(): return lax.ppermute(block, ('seq', 'pipe'), route)]
    pallas_call x1, Pallas kernels: 12.8 us -> 10.1 us  [backward(): pl.pallas_call(functools.partial(backward_kernel, block), out_shape=(jax....]
    pallas_call x1, Pallas kernels: 7.37 us -> 5.3 us  [input_grad_part(): pl.pallas_call(functools.partial(input_grad_kernel, first, block), out_sh...]
    pallas_call x1, Pallas kernels: 11.6 us -> 10.4 us  [forward(): pl.pallas_call(forward_kernel, out_shape=(jax.ShapeDtypeStruct((groups, t...]
    convert_element_type x1 -> x0, other arithmetic: 0.84 us -> none  [pair_body(): segment_output = (kept.astype(F32) + sent.astype(F32)).astype(BF16)]
    broadcast_in_dim x1 -> x2, other arithmetic: 0.77 us -> 1.61 us  [pair_body(): return (segment_output[None], input_grad[None], gate_total)]
  transfers between devices with their start and end apart: 9 -> 9, of which waited for: 3 -> 6; matrix products, arithmetic and copies ran while one was open for 2% -> 2% of each run, Pallas kernels for 70% -> 43%
where the time goes in v6:
time: 69.3 us; the launch traced here: 69.2 us
  Pallas kernels  39.9 us (58%)
  waiting for transfers between devices  16.4 us (24%)
  starting transfers between devices  9.78 us (14%)
  other arithmetic  2.31 us (3%)
  between operations  0.79 us (1%)
    ppermute x9, waiting for transfers between devices, routed(): return lax.ppermute(block, ('seq', 'pipe'), route)  16.4 us
    pallas_call x1, Pallas kernels, regroup(): pl.pallas_call(functools.partial(regroup_kernel, rows, ahead), out_shape=...  14.2 us
    pallas_call x1, Pallas kernels, forward(): pl.pallas_call(forward_kernel, out_shape=(jax.ShapeDtypeStruct((groups, t...  10.4 us
    pallas_call x1, Pallas kernels, backward(): pl.pallas_call(functools.partial(backward_kernel, block), out_shape=(jax....  10.1 us
    ppermute x9, starting transfers between devices, routed(): return lax.ppermute(block, ('seq', 'pipe'), route)  9.78 us
    pallas_call x1, Pallas kernels, input_grad_part(): pl.pallas_call(functools.partial(input_grad_kernel, first, block), out_sh...  5.3 us
    broadcast_in_dim x2, other arithmetic, pair_body(): return (segment_output[None], input_grad[None], gate_total)  1.61 us
  transfers between devices with their start and end apart: 9, of which 6 were waited for; matrix products, arithmetic and copies ran while one was open for 2% of the time, Pallas kernels for 43%

profile of v6, /device:TPU:1, one launch (start us, length us, event | category | flops | bytes accessed | tf_op | source)
XLA Modules:
  0.0 69.2 jit_solution(13177687445266294160)
XLA Ops:
  0.6 2.1 %collective-permute-start.1 = (bf16[64,3072]{1,0:T(8,128)(2,1)}, bf16[64,3072]{1,0:T(8,128)(2,1)S(1)}, u32[]{:S(2)}, u32[]{:S(2)}) collective-permute-start(bf16[64,3072]{1,0:T(8,128)(2,1)} %bitcast.11), channel_id=1, source_target_pairs={{0,16},{4,20},{8,24},{12,28},{16,0},{20,4},{24,8},{28,12},{1,17},{... | collective-permute-start | bytes 1179656 | tf_op jit(solution)/shard_map/ppermute | solution.py:649
  2.8 0.0 copy-start.4
  2.8 0.0 copy-start.5
  2.8 0.0 copy-start.6
  2.8 14.2 %regroup.1.weight_ref = bf16[2,3072,1536]{2,1,0:T(8,128)(2,1)} custom-call(bf16[3072,8,384]{2,1,0:T(8,128)(2,1)} %bitcast.15), custom_call_target="tpu_custom_call" | custom-call | bytes 37748736 | tf_op jit(solution)/shard_map/regroup/pallas_call | solution.py:290
  16.9 0.0 copy-done
  17.0 0.1 collective-permute-start
  17.0 0.0 collective-permute-done.1.other_ref
  17.0 0.0 copy-done.1
  17.1 0.0 copy-done.2
  17.1 0.0 copy-done.3
  17.1 10.4 %attention_forward.1 = (f32[2,128,1536]{2,1,0:T(8,128)S(1)}, bf16[8,128,128]{2,1,0:T(8,128)(2,1)S(1)}, f32[128,3072]{1,0:T(8,128)S(1)}, bf16[64,3072]{1,0:T(8,128)(2,1)S(1)}, bf16[64,3072]{1,0:T(8,128)(2,1)S(1)}) custom-call(s32[2,27]{1,0:T(2,128)S(1)} %copy-done.5, s32[2]{0:T(128)S(1)} %copy-done.6, bf16[64,3072]{1,0:T(8,128)(2,1)S(1)} %bitcast.12, ...), custom_call_target="tpu_custom_call" | custom-call | flops 3221225472 | bytes 25165824 | tf_op jit(solution)/shard_map/attention_forward/pallas_call | solution.py:444
  27.5 0.0 collective-permute-done.other_ref
  27.5 10.1 %attention_backward.1 = (bf16[2,128,1536]{2,1,0:T(8,128)(2,1)S(1)}, f32[1,3072]{1,0:T(1,128)S(1)}, bf16[64,1536]{1,0:T(8,128)(2,1)S(1)}, bf16[64,1536]{1,0:T(8,128)(2,1)S(1)}) custom-call(bf16[64,3072]{1,0:T(8,128)(2,1)S(1)} %bitcast.9, bf16[64,3072]{1,0:T(8,128)(2,1)S(1)} %collective-permute-done.other_ref, bf16[1024,3072]{1,0:T(8,128)(2,1)} %bitcast.14, ...), custom_call_target="tpu_custom_call" | custom-call | flops 2013265920 | bytes 15728640 | tf_op jit(solution)/shard_map/attention_backward/pallas_call | solution.py:585
  37.6 1.1 %collective-permute-start.5 = (bf16[64,1536]{1,0:T(8,128)(2,1)S(1)}, bf16[64,1536]{1,0:T(8,128)(2,1)S(1)}, u32[]{:S(2)}, u32[]{:S(2)}) collective-permute-start(bf16[64,1536]{1,0:T(8,128)(2,1)S(1)} %get-tuple-element.41), channel_id=1, source_target_pairs={{0,12},{4,0},{8,4},{12,8},{16,28},{20,16},{24,20},{28,24},{1,13},{... | collective-permute-start | bytes 589832 | tf_op jit(solution)/shard_map/ppermute | solution.py:649
  38.7 1.9 %collective-permute-start.6 = (bf16[64,1536]{1,0:T(8,128)(2,1)S(1)}, bf16[64,1536]{1,0:T(8,128)(2,1)S(1)}, u32[]{:S(2)}, u32[]{:S(2)}) collective-permute-start(bf16[64,1536]{1,0:T(8,128)(2,1)S(1)} %get-tuple-element.42), channel_id=1, source_target_pairs={{0,28},{4,16},{8,20},{12,24},{16,12},{20,0},{24,4},{28,8},{1,29},{... | collective-permute-start | bytes 589832 | tf_op jit(solution)/shard_map/ppermute | solution.py:649
  40.6 1.2 %collective-permute-start.2 = (bf16[64,3072]{1,0:T(8,128)(2,1)S(1)}, bf16[64,3072]{1,0:T(8,128)(2,1)S(1)}, u32[]{:S(2)}, u32[]{:S(2)}) collective-permute-start(bf16[64,3072]{1,0:T(8,128)(2,1)S(1)} %get-tuple-element.31), channel_id=1, source_target_pairs={{0,4},{4,8},{8,12},{12,0},{16,20},{20,24},{24,28},{28,16},{1,5},{5... | collective-permute-start | bytes 1179656 | tf_op jit(solution)/shard_map/ppermute | solution.py:649
  41.8 0.1 collective-permute-start.3
  41.9 1.2 %collective-permute-start.4 = (f32[1,3072]{1,0:T(1,128)S(1)}, f32[1,3072]{1,0:T(1,128)S(1)}, u32[]{:S(2)}, u32[]{:S(2)}) collective-permute-start(f32[1,3072]{1,0:T(1,128)S(1)} %get-tuple-element.45), channel_id=1, source_target_pairs={{0,16},{4,20},{8,24},{12,28},{16,0},{20,4},{24,8},{28,12},{1,17},{... | collective-permute-start | bytes 36872 | tf_op jit(solution)/shard_map/ppermute | solution.py:649
  43.1 2.3 %collective-permute-done.5 = bf16[64,1536]{1,0:T(8,128)(2,1)S(1)} collective-permute-done((bf16[64,1536]{1,0:T(8,128)(2,1)S(1)}, bf16[64,1536]{1,0:T(8,128)(2,1)S(1)}, u32[]{:S(2)}, u32[]{:S(2)}) %collective-permute-start.5) | collective-permute-done | bytes 196640 | tf_op jit(solution)/shard_map/ppermute | solution.py:649
  45.4 1.7 %collective-permute-done.6 = bf16[64,1536]{1,0:T(8,128)(2,1)S(1)} collective-permute-done((bf16[64,1536]{1,0:T(8,128)(2,1)S(1)}, bf16[64,1536]{1,0:T(8,128)(2,1)S(1)}, u32[]{:S(2)}, u32[]{:S(2)}) %collective-permute-start.6) | collective-permute-done | bytes 196640 | tf_op jit(solution)/shard_map/ppermute | solution.py:649
  47.1 5.7 %collective-permute-done.2 = bf16[64,3072]{1,0:T(8,128)(2,1)S(1)} collective-permute-done((bf16[64,3072]{1,0:T(8,128)(2,1)S(1)}, bf16[64,3072]{1,0:T(8,128)(2,1)S(1)}, u32[]{:S(2)}, u32[]{:S(2)}) %collective-permute-start.2) | collective-permute-done | bytes 393248 | tf_op jit(solution)/shard_map/ppermute | solution.py:649
  52.8 2.1 %collective-permute-done.3 = bf16[64,3072]{1,0:T(8,128)(2,1)S(1)} collective-permute-done((bf16[64,3072]{1,0:T(8,128)(2,1)S(1)}, bf16[64,3072]{1,0:T(8,128)(2,1)S(1)}, u32[]{:S(2)}, u32[]{:S(2)}) %collective-permute-start.3) | collective-permute-done | bytes 393248 | tf_op jit(solution)/shard_map/ppermute | solution.py:649
  54.9 5.3 %input_grad.1 = (bf16[64,1536]{1,0:T(8,128)(2,1)S(1)}, bf16[64,1536]{1,0:T(8,128)(2,1)S(1)}) custom-call(bf16[2,128,1536]{2,1,0:T(8,128)(2,1)S(1)} %get-tuple-element.33.grad_ref, bf16[2,3072,1536]{2,1,0:T(8,128)(2,1)} %regroup.1.weight_ref, bf16[64,3072]{1,0:T(8,128)(2,1)S(1)} %bitcast.10), custom_call_target="tpu_custom_call" | custom-call | flops 1207959552 | bytes 9437184 | tf_op jit(solution)/shard_map/input_grad/pallas_call | solution.py:623
  60.2 0.0 collective-permute-done.4
  60.2 0.7 %collective-permute-start.7 = (bf16[64,1536]{1,0:T(8,128)(2,1)S(1)}, bf16[64,1536]{1,0:T(8,128)(2,1)S(1)}, u32[]{:S(2)}, u32[]{:S(2)}) collective-permute-start(bf16[64,1536]{1,0:T(8,128)(2,1)S(1)} %get-tuple-element.43), channel_id=1, source_target_pairs={{0,12},{4,0},{8,4},{12,8},{16,28},{20,16},{24,20},{28,24},{1,13},{... | collective-permute-start | bytes 589832 | tf_op jit(solution)/shard_map/ppermute | solution.py:649
  61.0 1.4 %collective-permute-start.8 = (bf16[64,1536]{1,0:T(8,128)(2,1)S(1)}, bf16[64,1536]{1,0:T(8,128)(2,1)S(1)}, u32[]{:S(2)}, u32[]{:S(2)}) collective-permute-start(bf16[64,1536]{1,0:T(8,128)(2,1)S(1)} %get-tuple-element.44), channel_id=1, source_target_pairs={{0,28},{4,16},{8,20},{12,24},{16,12},{20,0},{24,4},{28,8},{1,29},{... | collective-permute-start | bytes 589832 | tf_op jit(solution)/shard_map/ppermute | solution.py:649
  62.3 0.8 %fusion = bf16[1,64,3072]{2,1,0:T(8,128)(2,1)} fusion(bf16[64,3072]{1,0:T(8,128)(2,1)S(1)} %collective-permute-done.3, bf16[64,3072]{1,0:T(8,128)(2,1)S(1)} %collective-permute-done.2), kind=kLoop, calls=%fused_computation.1 | loop fusion | flops 786432 | bytes 1179648 | tf_op jit(solution)/shard_map/broadcast_in_dim | solution.py:714
  63.2 0.6 dynamic-slice_add_fusion
  63.8 2.5 %collective-permute-done.7 = bf16[64,1536]{1,0:T(8,128)(2,1)S(1)} collective-permute-done((bf16[64,1536]{1,0:T(8,128)(2,1)S(1)}, bf16[64,1536]{1,0:T(8,128)(2,1)S(1)}, u32[]{:S(2)}, u32[]{:S(2)}) %collective-permute-start.7) | collective-permute-done | bytes 196640 | tf_op jit(solution)/shard_map/ppermute | solution.py:649
  66.2 2.1 %collective-permute-done.8 = bf16[64,1536]{1,0:T(8,128)(2,1)S(1)} collective-permute-done((bf16[64,1536]{1,0:T(8,128)(2,1)S(1)}, bf16[64,1536]{1,0:T(8,128)(2,1)S(1)}, u32[]{:S(2)}, u32[]{:S(2)}) %collective-permute-start.8) | collective-permute-done | bytes 196640 | tf_op jit(solution)/shard_map/ppermute | solution.py:649
  68.4 0.8 %maximum_bitcast_fusion = bf16[1,64,3072]{2,1,0:T(8,128)(2,1)} fusion(bf16[64,1536]{1,0:T(8,128)(2,1)S(1)} %add_convert_fusion.1, bf16[64,1536]{1,0:T(8,128)(2,1)S(1)} %add_convert_fusion.2), kind=kLoop, calls=%fused_computation.2 | loop fusion | flops 786432 | bytes 786432 | tf_op jit(solution)/shard_map/broadcast_in_dim | solution.py:714
  (9 shorter events, 0.1 us)
Async XLA Ops:
  0.6 16.4 %collective-permute-start.1 = (bf16[64,3072]{1,0:T(8,128)(2,1)}, bf16[64,3072]{1,0:T(8,128)(2,1)S(1)}, u32[]{:S(2)}, u32[]{:S(2)}) collective-permute-start(bf16[64,3072]{1,0:T(8,128)(2,1)} %bitcast.11), channel_id=1, source_target_pairs={{0,16},{4,20},{8,24},{12,28},{16,0},{20,4},{24,8},{28,12},{1,17},{... | collective-permute-start | bytes 1179656 | tf_op jit(solution)/shard_map/ppermute | solution.py:649
  2.7 14.2 %copy-start = (bf16[1,64,3072]{2,1,0:T(8,128)(2,1)S(1)}, bf16[1,64,3072]{2,1,0:T(8,128)(2,1)}, u32[]{:S(2)}) copy-start(bf16[1,64,3072]{2,1,0:T(8,128)(2,1)} %param.10) | copy-start | bytes 1179652
  2.7 14.3 %copy-start.1 = (bf16[1,64,3072]{2,1,0:T(8,128)(2,1)S(1)}, bf16[1,64,3072]{2,1,0:T(8,128)(2,1)}, u32[]{:S(2)}) copy-start(bf16[1,64,3072]{2,1,0:T(8,128)(2,1)} %param.9) | copy-start | bytes 1179652
  2.7 14.3 %copy-start.2 = (f32[1,3072]{1,0:T(1,128)S(1)}, f32[1,3072]{1,0:T(1,128)}, u32[]{:S(2)}) copy-start(f32[1,3072]{1,0:T(1,128)} %gate_ref.3) | copy-start | bytes 36868
  2.7 14.3 %copy-start.3 = (f32[1,128]{1,0:T(1,128)S(1)}, f32[1,128]{1,0:T(1,128)}, u32[]{:S(2)}) copy-start(f32[1,128]{1,0:T(1,128)} %query_gain_ref.3) | copy-start | bytes 1540
  2.8 14.3 %copy-start.4 = (f32[1,128]{1,0:T(1,128)S(1)}, f32[1,128]{1,0:T(1,128)}, u32[]{:S(2)}) copy-start(f32[1,128]{1,0:T(1,128)} %key_gain_ref.3) | copy-start | bytes 1540
  2.8 14.3 %copy-start.5 = (s32[2,27]{1,0:T(2,128)S(1)}, s32[2,27]{1,0:T(2,128)}, u32[]{:S(2)}) copy-start(s32[2,27]{1,0:T(2,128)} %neighbours_ref.1) | copy-start | bytes 652
  2.8 14.3 %copy-start.6 = (s32[2]{0:T(128)S(1)}, s32[2]{0:T(128)}, u32[]{:S(2)}) copy-start(s32[2]{0:T(128)} %tile_slot_ref.1) | copy-start | bytes 28
  17.0 10.5 %collective-permute-start = (bf16[64,3072]{1,0:T(8,128)(2,1)S(1)}, bf16[64,3072]{1,0:T(8,128)(2,1)S(1)}, u32[]{:S(2)}, u32[]{:S(2)}) collective-permute-start(bf16[64,3072]{1,0:T(8,128)(2,1)S(1)} %bitcast.8), channel_id=1, source_target_pairs={{0,16},{4,20},{8,24},{12,28},{16,0},{20,4},{24,8},{28,12},{1,17},{... | collective-permute-start | bytes 1179656 | tf_op jit(solution)/shard_map/ppermute | solution.py:649
  37.6 7.8 %collective-permute-start.5 = (bf16[64,1536]{1,0:T(8,128)(2,1)S(1)}, bf16[64,1536]{1,0:T(8,128)(2,1)S(1)}, u32[]{:S(2)}, u32[]{:S(2)}) collective-permute-start(bf16[64,1536]{1,0:T(8,128)(2,1)S(1)} %get-tuple-element.41), channel_id=1, source_target_pairs={{0,12},{4,0},{8,4},{12,8},{16,28},{20,16},{24,20},{28,24},{1,13},{... | collective-permute-start | bytes 589832 | tf_op jit(solution)/shard_map/ppermute | solution.py:649
  38.7 8.4 %collective-permute-start.6 = (bf16[64,1536]{1,0:T(8,128)(2,1)S(1)}, bf16[64,1536]{1,0:T(8,128)(2,1)S(1)}, u32[]{:S(2)}, u32[]{:S(2)}) collective-permute-start(bf16[64,1536]{1,0:T(8,128)(2,1)S(1)} %get-tuple-element.42), channel_id=1, source_target_pairs={{0,28},{4,16},{8,20},{12,24},{16,12},{20,0},{24,4},{28,8},{1,29},{... | collective-permute-start | bytes 589832 | tf_op jit(solution)/shard_map/ppermute | solution.py:649
  40.6 12.2 %collective-permute-start.2 = (bf16[64,3072]{1,0:T(8,128)(2,1)S(1)}, bf16[64,3072]{1,0:T(8,128)(2,1)S(1)}, u32[]{:S(2)}, u32[]{:S(2)}) collective-permute-start(bf16[64,3072]{1,0:T(8,128)(2,1)S(1)} %get-tuple-element.31), channel_id=1, source_target_pairs={{0,4},{4,8},{8,12},{12,0},{16,20},{20,24},{24,28},{28,16},{1,5},{5... | collective-permute-start | bytes 1179656 | tf_op jit(solution)/shard_map/ppermute | solution.py:649
  41.8 13.1 %collective-permute-start.3 = (bf16[64,3072]{1,0:T(8,128)(2,1)S(1)}, bf16[64,3072]{1,0:T(8,128)(2,1)S(1)}, u32[]{:S(2)}, u32[]{:S(2)}) collective-permute-start(bf16[64,3072]{1,0:T(8,128)(2,1)S(1)} %get-tuple-element.32), channel_id=1, source_target_pairs={{0,20},{4,24},{8,28},{12,16},{16,4},{20,8},{24,12},{28,0},{1,21},{... | collective-permute-start | bytes 1179656 | tf_op jit(solution)/shard_map/ppermute | solution.py:649
  41.9 18.4 %collective-permute-start.4 = (f32[1,3072]{1,0:T(1,128)S(1)}, f32[1,3072]{1,0:T(1,128)S(1)}, u32[]{:S(2)}, u32[]{:S(2)}) collective-permute-start(f32[1,3072]{1,0:T(1,128)S(1)} %get-tuple-element.45), channel_id=1, source_target_pairs={{0,16},{4,20},{8,24},{12,28},{16,0},{20,4},{24,8},{28,12},{1,17},{... | collective-permute-start | bytes 36872 | tf_op jit(solution)/shard_map/ppermute | solution.py:649
  60.2 6.0 %collective-permute-start.7 = (bf16[64,1536]{1,0:T(8,128)(2,1)S(1)}, bf16[64,1536]{1,0:T(8,128)(2,1)S(1)}, u32[]{:S(2)}, u32[]{:S(2)}) collective-permute-start(bf16[64,1536]{1,0:T(8,128)(2,1)S(1)} %get-tuple-element.43), channel_id=1, source_target_pairs={{0,12},{4,0},{8,4},{12,8},{16,28},{20,16},{24,20},{28,24},{1,13},{... | collective-permute-start | bytes 589832 | tf_op jit(solution)/shard_map/ppermute | solution.py:649
  61.0 7.4 %collective-permute-start.8 = (bf16[64,1536]{1,0:T(8,128)(2,1)S(1)}, bf16[64,1536]{1,0:T(8,128)(2,1)S(1)}, u32[]{:S(2)}, u32[]{:S(2)}) collective-permute-start(bf16[64,1536]{1,0:T(8,128)(2,1)S(1)} %get-tuple-element.44), channel_id=1, source_target_pairs={{0,28},{4,16},{8,20},{12,24},{16,12},{20,0},{24,4},{28,8},{1,29},{... | collective-permute-start | bytes 589832 | tf_op jit(solution)/shard_map/ppermute | solution.py:649

commit v7 on v6

--- a/solution.py
+++ b/solution.py
@@ -245,65 +245,54 @@
             self.waited += 1
 
 
-def regroup_kernel(rows, ahead, weight_ref, out_ref, read_ref, written_ref, reads, writes):
+def regroup_kernel(weight_ref, out_ref, read_ref, reads):
     depth, heads, width = weight_ref.shape
+    slots, rows = read_ref.shape[:2]
     steps = depth // rows
 
     def part(step):
         return pl.ds(pl.multiple_of(step * rows, rows), rows)
 
-    def read(step):
+    def read(step, slot):
         return pltpu.make_async_copy(
-            weight_ref.at[part(step)], read_ref.at[part(step)], reads.at[step]
+            weight_ref.at[part(step)], read_ref.at[slot], reads.at[slot]
         )
 
-    def write(step):
-        return pltpu.make_async_copy(
-            written_ref.at[:, part(step)], out_ref.at[:, part(step)], writes.at[step]
-        )
-
-    for step in range(ahead):
-        read(step).start()
+    for slot in range(slots):
+        read(slot, slot).start()
 
     @pl.loop(0, steps)
     def _(step):
-        read(step).wait()
-
-        @pl.when(step + ahead < steps)
-        def _():
-            read(step + ahead).start()
-
-        by_head = jnp.swapaxes(read_ref[part(step)], 0, 1)
+        slot = lax.rem(step, slots)
+        read(step, slot).wait()
+        by_head = jnp.swapaxes(read_ref[slot], 0, 1)
         for head in range(heads):
             left = (head % GROUP) * width
-            written_ref[head // GROUP, part(step), left : left + width] = by_head[head]
-        write(step).start()
-
-    @pl.loop(0, steps)
-    def _(step):
-        write(step).wait()
-
-
-def regroup(weight, rows, ahead):
+            out_ref[head // GROUP, part(step), left : left + width] = by_head[head]
+
+        @pl.when(step + slots < steps)
+        def _():
+            read(step + slots, slot).start()
+
+
+def regroup(weight, rows, slots):
     depth, heads, width = weight.shape
     out = (heads // GROUP, depth, GROUP * width)
     return pl.pallas_call(
-        functools.partial(regroup_kernel, rows, ahead),
-        out_shape=jax.ShapeDtypeStruct(out, weight.dtype),
+        regroup_kernel,
+        out_shape=pltpu.VMEM(out, weight.dtype),
         in_specs=[pl.BlockSpec(memory_space=pl.ANY)],
-        out_specs=pl.BlockSpec(memory_space=pl.ANY),
+        out_specs=pl.BlockSpec(memory_space=pltpu.VMEM),
         scratch_shapes=[
-            pltpu.VMEM(weight.shape, weight.dtype),
-            pltpu.VMEM(out, weight.dtype),
-            pltpu.SemaphoreType.DMA((depth // rows,)),
-            pltpu.SemaphoreType.DMA((depth // rows,)),
+            pltpu.VMEM((slots, rows, heads, width), weight.dtype),
+            pltpu.SemaphoreType.DMA((slots,)),
         ],
-        compiler_params=params(46),
+        compiler_params=params(12),
         cost_estimate=pl.CostEstimate(
             flops=0, bytes_accessed=4 * depth * heads * width, transcendentals=0
         ),
         name="regroup",
-    )(weight)
+    )(pltpu.with_memory_space_constraint(weight, pltpu.HBM))
 
 
 def listed_slots(neighbours_ref, tile_slot_ref):
@@ -343,32 +332,21 @@
     attention_ref,
     kept_ref,
     sent_ref,
+    out_weight_buffer,
     tokens_ref,
-    weight_buffer,
-    out_weight_buffer,
     semaphores,
 ):
     local, model = own_ref.shape
     tokens = 2 * local
     width = query_gain_ref.shape[1]
     groups = weight_ref.shape[0]
-    parts = 4
-    depth = model // parts
     rows = GROUP * width
-
-    def weight_part(group, index):
-        place = (group, pl.ds(index * depth, depth))
-        return weight_ref.at[place], weight_buffer.at[place]
 
     def out_weight_part(group):
         place = pl.ds(group * rows, rows)
         return out_weight_ref.at[place], out_weight_buffer.at[place]
 
-    order = []
-    for group in range(groups):
-        order += [weight_part(group, index) for index in range(parts)]
-    order += [out_weight_part(group) for group in range(groups)]
-    copies = Copies(order, semaphores, 4)
+    copies = Copies([out_weight_part(group) for group in range(groups)], semaphores, groups)
 
     tokens_ref[:local, :] = own_ref[...]
     tokens_ref[local:, :] = other_ref[...]
@@ -385,13 +363,7 @@
     bias = jnp.where(table > 0, 0.0, -jnp.inf).astype(F32)
 
     def project(group):
-        total = None
-        for index in range(parts):
-            copies.wait()
-            part = slice(index * depth, (index + 1) * depth)
-            product = dot_nn(tokens_ref[:, part], weight_buffer[group, part, :])
-            total = product if total is None else total + product
-        projected_ref[group] = total
+        projected_ref[group] = dot_nn(tokens_ref[...], weight_ref[group])
 
     def attend(group):
         attended = []
@@ -438,6 +410,8 @@
     local, model = own.shape
     groups, _, wide = weight.shape
     tokens = 2 * local
+    weight = pltpu.with_memory_space_constraint(weight, pltpu.VMEM)
+    out_weight = pltpu.with_memory_space_constraint(out_weight, pltpu.HBM)
     smem = pl.BlockSpec(memory_space=pltpu.SMEM)
     vmem = pl.BlockSpec(memory_space=pltpu.VMEM)
     hbm = pl.BlockSpec(memory_space=pl.ANY)
@@ -449,16 +423,15 @@
             jax.ShapeDtypeStruct((tokens, model), F32),
             jax.ShapeDtypeStruct((local, model), BF16),
             jax.ShapeDtypeStruct((local, model), BF16),
+            pltpu.VMEM(out_weight.shape, BF16),
         ),
-        in_specs=[smem, smem, vmem, vmem, hbm, hbm, vmem, vmem, vmem],
-        out_specs=(vmem,) * 5,
+        in_specs=[smem, smem, vmem, vmem, vmem, hbm, vmem, vmem, vmem],
+        out_specs=(vmem,) * 6,
         scratch_shapes=[
             pltpu.VMEM((tokens, model), BF16),
-            pltpu.VMEM(weight.shape, BF16),
-            pltpu.VMEM(out_weight.shape, BF16),
-            pltpu.SemaphoreType.DMA((5 * groups,)),
+            pltpu.SemaphoreType.DMA((groups,)),
         ],
-        compiler_params=params(46),
+        compiler_params=params(12),
         cost_estimate=pl.CostEstimate(
             flops=2 * tokens * (weight.size + out_weight.size),
             bytes_accessed=2 * (weight.size + out_weight.size),
@@ -468,31 +441,20 @@
     )(neighbours, tile_slot, own, other, weight, out_weight, query_gain, key_gain, gate)
 
 
-def input_grad_parts(weight_ref, buffer, first, block):
-    return [
-        (
-            weight_ref.at[:, pl.ds(first + start, block)],
-            buffer.at[:, pl.ds(start, block)],
-        )
-        for start in range(0, buffer.shape[1], block)
-    ]
-
-
-def input_grad_blocks(copies, grad_ref, buffer, own_ref, first, block, kept_ref, sent_ref):
-    local = own_ref.shape[0]
-    for start in range(0, buffer.shape[1], block):
-        copies.wait()
+def input_grad_blocks(grad_ref, weight_ref, own_ref, first, kept_ref, sent_ref):
+    local, columns = kept_ref.shape
+    block = math.gcd(columns, 512)
+    for start in range(0, columns, block):
+        rows = slice(first + start, first + start + block)
+        total = dot_nt(grad_ref[0], weight_ref[0, rows, :])
+        for group in range(1, grad_ref.shape[0]):
+            total += dot_nt(grad_ref[group], weight_ref[group, rows, :])
         part = slice(start, start + block)
-        total = dot_nt(grad_ref[0], buffer[0, part, :])
-        for pair in range(1, grad_ref.shape[0]):
-            total += dot_nt(grad_ref[pair], buffer[pair, part, :])
-        own = own_ref[:, first + start : first + start + block].astype(F32)
-        kept_ref[:, part] = (own + total[:local]).astype(BF16)
+        kept_ref[:, part] = (own_ref[:, rows].astype(F32) + total[:local]).astype(BF16)
         sent_ref[:, part] = total[local:].astype(BF16)
 
 
 def backward_kernel(
-    block,
     own_ref,
     other_ref,
     out_weight_ref,
@@ -504,25 +466,18 @@
     key_gain_ref,
     gate_ref,
     grad_ref,
-    gate_grad_ref,
+    gate_kept_ref,
+    gate_sent_ref,
     kept_ref,
     sent_ref,
     scaled_ref,
     attended_grad_ref,
-    out_weight_buffer,
-    weight_buffer,
-    semaphores,
+    gate_grad_ref,
 ):
     local = own_ref.shape[0]
     width = query_gain_ref.shape[1]
     groups = grad_ref.shape[0]
     rows = GROUP * width
-    order = []
-    for start in range(0, groups * rows, rows // 2):
-        place = pl.ds(start, rows // 2)
-        order.append((out_weight_ref.at[place], out_weight_buffer.at[place]))
-    order += input_grad_parts(weight_ref, weight_buffer, 0, block)
-    copies = Copies(order, semaphores, 4)
 
     gate = gate_ref[...]
     own, other = own_ref[...].astype(F32), other_ref[...].astype(F32)
@@ -531,11 +486,14 @@
     gate_grad_ref[...] = jnp.sum(
         own * attention_ref[:local, :] + other * attention_ref[local:, :], axis=0, keepdims=True
     )
+    half = gate_kept_ref.shape[1]
+    mine = lax.axis_index("seq")
+    gate_kept_ref[...] = gate_grad_ref[:, pl.ds(pl.multiple_of(mine * half, half), half)]
+    gate_sent_ref[...] = gate_grad_ref[:, pl.ds(pl.multiple_of((1 - mine) * half, half), half)]
 
     def attended_grad(group):
-        copies.wait(2)
         part = slice(group * rows, (group + 1) * rows)
-        product = dot_nt(scaled_ref[...], out_weight_buffer[part, :])
+        product = dot_nt(scaled_ref[...], out_weight_ref[part, :])
         attended_grad_ref[group] = product.astype(BF16)
 
     def attend_backward(group, head):
@@ -570,7 +528,7 @@
             attended_grad(group + 1)
         for head in range(GROUP):
             attend_backward(group, head)
-    input_grad_blocks(copies, grad_ref, weight_buffer, own_ref, 0, block, kept_ref, sent_ref)
+    input_grad_blocks(grad_ref, weight_ref, own_ref, 0, kept_ref, sent_ref)
 
 
 def backward(
@@ -579,27 +537,26 @@
     local, model = own.shape
     groups, tokens, wide = projected.shape
     head_dim = query_gain.shape[1]
-    block = 512
+    out_weight = pltpu.with_memory_space_constraint(out_weight, pltpu.VMEM)
+    weight = pltpu.with_memory_space_constraint(weight, pltpu.VMEM)
     vmem = pl.BlockSpec(memory_space=pltpu.VMEM)
-    hbm = pl.BlockSpec(memory_space=pl.ANY)
     return pl.pallas_call(
-        functools.partial(backward_kernel, block),
+        backward_kernel,
         out_shape=(
             jax.ShapeDtypeStruct((groups, tokens, wide), BF16),
-            jax.ShapeDtypeStruct((1, model), F32),
+            jax.ShapeDtypeStruct((1, model // 2), F32),
+            jax.ShapeDtypeStruct((1, model // 2), F32),
             jax.ShapeDtypeStruct((local, columns), BF16),
             jax.ShapeDtypeStruct((local, columns), BF16),
         ),
-        in_specs=[vmem, vmem, hbm, hbm] + [vmem] * 6,
-        out_specs=(vmem,) * 4,
+        in_specs=[vmem] * 10,
+        out_specs=(vmem,) * 5,
         scratch_shapes=[
             pltpu.VMEM((tokens, model), BF16),
             pltpu.VMEM((groups, tokens, GROUP * head_dim), BF16),
-            pltpu.VMEM(out_weight.shape, BF16),
-            pltpu.VMEM((groups, columns, wide), BF16),
-            pltpu.SemaphoreType.DMA((2 * groups + columns // block,)),
+            pltpu.VMEM((1, model), F32),
         ],
-        compiler_params=params(46),
+        compiler_params=params(12),
         cost_estimate=pl.CostEstimate(
             flops=2 * tokens * (out_weight.size + groups * columns * wide),
             bytes_accessed=2 * (out_weight.size + groups * columns * wide),
@@ -609,34 +566,28 @@
     )(own, other, out_weight, weight, projected, probs, attention, query_gain, key_gain, gate)
 
 
-def input_grad_kernel(first, block, grad_ref, weight_ref, own_ref, kept_ref, sent_ref, buffer, sems):
-    copies = Copies(input_grad_parts(weight_ref, buffer, first, block), sems, 4)
-    input_grad_blocks(copies, grad_ref, buffer, own_ref, first, block, kept_ref, sent_ref)
+def input_grad_kernel(first, grad_ref, weight_ref, own_ref, kept_ref, sent_ref):
+    input_grad_blocks(grad_ref, weight_ref, own_ref, first, kept_ref, sent_ref)
 
 
 def input_grad_part(grad, weight, own, first, columns):
     local, model = own.shape
-    pairs, tokens, wide = grad.shape
-    block = 512
+    groups, tokens, wide = grad.shape
     out = jax.ShapeDtypeStruct((local, columns), BF16)
     vmem = pl.BlockSpec(memory_space=pltpu.VMEM)
     return pl.pallas_call(
-        functools.partial(input_grad_kernel, first, block),
+        functools.partial(input_grad_kernel, first),
         out_shape=(out, out),
-        in_specs=[vmem, pl.BlockSpec(memory_space=pl.ANY), vmem],
+        in_specs=[vmem, vmem, vmem],
         out_specs=(vmem, vmem),
-        scratch_shapes=[
-            pltpu.VMEM((pairs, columns, wide), BF16),
-            pltpu.SemaphoreType.DMA((columns // block,)),
-        ],
-        compiler_params=params(46),
+        compiler_params=params(8),
         cost_estimate=pl.CostEstimate(
-            flops=2 * tokens * columns * pairs * wide,
-            bytes_accessed=2 * columns * pairs * wide,
+            flops=2 * tokens * columns * groups * wide,
+            bytes_accessed=2 * columns * groups * wide,
             transcendentals=0,
         ),
         name="input_grad",
-    )(grad, weight, own)
+    )(grad, pltpu.with_memory_space_constraint(weight, pltpu.VMEM), own)
 
 
 def routed(block, seq_step, pipe_step):
@@ -665,10 +616,10 @@
     out_local = out_weight[0]
     model = stream.shape[1]
     other_stream = routed(stream, 1, 0)
-    weight = regroup(qkv_weight[0], 128, 6)
-    weight, upstream_after = lax.optimization_barrier((weight, upstream))
-    other_upstream = routed(upstream_after, 1, 0)
-    projected, probs, attention, kept, sent = forward(
+    weight = regroup(qkv_weight[0], 128, 8)
+    weight, upstream = lax.optimization_barrier((weight, upstream))
+    other_upstream = routed(upstream, 1, 0)
+    projected, probs, attention, kept, sent, out_local = forward(
         neighbours,
         tile_slot,
         stream,
@@ -682,7 +633,7 @@
     kept = routed(kept, 0, 1)
     sent = routed(sent, 1, 1)
     columns = model // 2
-    grad, gate_share, first, second = backward(
+    grad, gate_kept, gate_sent, first, second = backward(
         upstream,
         other_upstream,
         out_local,
@@ -695,23 +646,19 @@
         gate_scale,
         columns,
     )
-    other_gate = routed(gate_share, 1, 0)
-    pieces = [(routed(first, 0, -1), routed(second, 1, -1))]
-    grad, kept, sent = lax.optimization_barrier((grad, kept, sent))
-    first, second = input_grad_part(grad, weight, upstream, columns, model - columns)
-    first, second, kept, sent, gate_share, other_gate = lax.optimization_barrier(
-        (first, second, kept, sent, gate_share, other_gate)
-    )
-    pieces.append((routed(first, 0, -1), routed(second, 1, -1)))
+    grad, first, second, kept, sent = lax.optimization_barrier((grad, first, second, kept, sent))
+    gate_sent = routed(gate_sent, 1, 0)
+    early = (routed(first, 0, -1), routed(second, 1, -1))
+    late = input_grad_part(grad, weight, upstream, columns, model - columns)
+    late, early, kept, sent, gate_sent = lax.optimization_barrier(
+        (late, early, kept, sent, gate_sent)
+    )
+    pieces = [early, (routed(late[0], 0, -1), routed(late[1], 1, -1))]
     segment_output = (kept.astype(F32) + sent.astype(F32)).astype(BF16)
-    half = model // lax.axis_size("seq")
-    gate_total = lax.dynamic_slice_in_dim(
-        gate_share + other_gate, lax.axis_index("seq") * half, half, 1
-    )
     input_grad = jnp.concatenate(
         [(a.astype(F32) + b.astype(F32)).astype(BF16) for a, b in pieces], axis=1
     )
-    return (segment_output[None], input_grad[None], gate_total)
+    return (segment_output[None], input_grad[None], gate_kept + gate_sent)
 
 
 def solution(mesh):

time: 69.3 us -> 50 us (0.72)
  Pallas kernels: 39.9 us -> 24.1 us
  waiting for transfers between devices: 16.4 us -> 11.6 us
  starting transfers between devices: 9.78 us -> 11.1 us
    pallas_call x3, Pallas kernels: 29.5 us -> 17.6 us  [the longest x1 7.33 us: backward(): pl.pallas_call(backward_kernel, out_shape=(jax.ShapeDtypeStruct((groups,...]
    ppermute x9, waiting for transfers between devices: 16.4 us -> 11.6 us  [routed(): return lax.ppermute(block, ('seq', 'pipe'), route)]
    pallas_call x1, Pallas kernels: 10.4 us -> 6.48 us  [forward(): pl.pallas_call(forward_kernel, out_shape=(jax.ShapeDtypeStruct((groups, t...]
    ppermute x9, starting transfers between devices: 9.78 us -> 11.1 us  [routed(): return lax.ppermute(block, ('seq', 'pipe'), route)]
  transfers between devices with their start and end apart: 9 -> 9, of which waited for: 6 -> 6; matrix products, arithmetic and copies ran while one was open for 2% -> 3% of each run, Pallas kernels for 43% -> 48%
where the time goes in v7:
time: 50 us; the launch traced here: 49.8 us
  Pallas kernels  24.1 us (48%)
  waiting for transfers between devices  11.6 us (23%)
  starting transfers between devices  11.1 us (22%)
  other arithmetic  2.31 us (5%)
  between operations  0.75 us (2%)
    ppermute x9, waiting for transfers between devices, routed(): return lax.ppermute(block, ('seq', 'pipe'), route)  11.6 us
    ppermute x9, starting transfers between devices, routed(): return lax.ppermute(block, ('seq', 'pipe'), route)  11.1 us
    pallas_call x1, Pallas kernels, backward(): pl.pallas_call(backward_kernel, out_shape=(jax.ShapeDtypeStruct((groups,...  7.33 us
    pallas_call x1, Pallas kernels, regroup(): pl.pallas_call(regroup_kernel, out_shape=pltpu.VMEM(out, weight.dtype), i...  7.17 us
    pallas_call x1, Pallas kernels, forward(): pl.pallas_call(forward_kernel, out_shape=(jax.ShapeDtypeStruct((groups, t...  6.48 us
    pallas_call x1, Pallas kernels, input_grad_part(): pl.pallas_call(functools.partial(input_grad_kernel, first), out_shape=(ou...  3.09 us
    broadcast_in_dim x2, other arithmetic, pair_body(): return (segment_output[None], input_grad[None], gate_kept + gate_sent)  1.61 us
  transfers between devices with their start and end apart: 9, of which 6 were waited for; matrix products, arithmetic and copies ran while one was open for 3% of the time, Pallas kernels for 48%

profile of v7, /device:TPU:1, one launch (start us, length us, event | category | flops | bytes accessed | tf_op | source)
XLA Modules:
  0.0 49.8 jit_solution(14639849406555589750)
XLA Ops:
  0.6 2.1 %collective-permute-start.1 = (bf16[64,3072]{1,0:T(8,128)(2,1)}, bf16[64,3072]{1,0:T(8,128)(2,1)S(1)}, u32[]{:S(2)}, u32[]{:S(2)}) collective-permute-start(bf16[64,3072]{1,0:T(8,128)(2,1)} %bitcast.11), channel_id=1, source_target_pairs={{0,16},{4,20},{8,24},{12,28},{16,0},{20,4},{24,8},{28,12},{1,17},{... | collective-permute-start | bytes 1179656 | tf_op jit(solution)/shard_map/ppermute | solution.py:600
  2.8 0.0 copy-start.4
  2.8 0.0 copy-start.5
  2.8 0.0 copy-start.6
  2.8 7.2 %regroup.1.weight_ref = bf16[2,3072,1536]{2,1,0:T(8,128)(2,1)S(1)} custom-call(bf16[3072,8,384]{2,1,0:T(8,128)(2,1)} %bitcast.13), custom_call_target="tpu_custom_call" | custom-call | bytes 37748736 | tf_op jit(solution)/shard_map/regroup/pallas_call | solution.py:281
  10.0 0.0 copy-done
  10.0 0.1 collective-permute-start
  10.1 1.7 %collective-permute-done.1.other_ref = bf16[64,3072]{1,0:T(8,128)(2,1)S(1)} collective-permute-done((bf16[64,3072]{1,0:T(8,128)(2,1)}, bf16[64,3072]{1,0:T(8,128)(2,1)S(1)}, u32[]{:S(2)}, u32[]{:S(2)}) %collective-permute-start.1) | collective-permute-done | bytes 393248 | tf_op jit(solution)/shard_map/ppermute | solution.py:600
  11.8 0.0 copy-done.1
  11.8 0.0 copy-done.2
  11.8 0.0 copy-done.3
  11.8 6.5 %attention_forward.1 = (f32[2,128,1536]{2,1,0:T(8,128)S(1)}, bf16[8,128,128]{2,1,0:T(8,128)(2,1)S(1)}, f32[128,3072]{1,0:T(8,128)S(1)}, bf16[64,3072]{1,0:T(8,12...) custom-call(s32[2,27]{1,0:T(2,128)S(1)} %copy-done.5, s32[2]{0:T(128)S(1)} %copy-done.6, ...), custom_call_target="tpu_custom_call" | custom-call | flops 3221225472 | bytes 25165824 | tf_op jit(solution)/shard_map/attention_forward/pallas_call | solution.py:418
  18.3 2.8 %collective-permute-start.2 = (bf16[64,3072]{1,0:T(8,128)(2,1)S(1)}, bf16[64,3072]{1,0:T(8,128)(2,1)S(1)}, u32[]{:S(2)}, u32[]{:S(2)}) collective-permute-start(bf16[64,3072]{1,0:T(8,128)(2,1)S(1)} %get-tuple-element.39), channel_id=1, source_target_pairs={{0,4},{4,8},{8,12},{12,0},{16,20},{20,24},{24,28},{28,16},{1,5},{5... | collective-permute-start | bytes 1179656 | tf_op jit(solution)/shard_map/ppermute | solution.py:600
  21.1 1.9 %collective-permute-start.3 = (bf16[64,3072]{1,0:T(8,128)(2,1)S(1)}, bf16[64,3072]{1,0:T(8,128)(2,1)S(1)}, u32[]{:S(2)}, u32[]{:S(2)}) collective-permute-start(bf16[64,3072]{1,0:T(8,128)(2,1)S(1)} %get-tuple-element.40), channel_id=1, source_target_pairs={{0,20},{4,24},{8,28},{12,16},{16,4},{20,8},{24,12},{28,0},{1,21},{... | collective-permute-start | bytes 1179656 | tf_op jit(solution)/shard_map/ppermute | solution.py:600
  23.0 0.0 collective-permute-done.other_ref
  23.0 7.3 %attention_backward.1 = (bf16[2,128,1536]{2,1,0:T(8,128)(2,1)S(1)}, f32[1,1536]{1,0:T(1,128)S(1)}, f32[1,1536]{1,0:T(1,128)S(1)}, bf16[64,1536]{1,0:T(8,128)(2,1)S(1)}, bf16[64,1536]{1,0:T(8,128)(2,1)S(1)}) custom-call(bf16[64,3072]{1,0:T(8,128)(2,1)S(1)} %bitcast.9, bf16[64,3072]{1,0:T(8,128)(2,1)S(1)} %collective-permute-done.other_ref, ...), custom_call_target="tpu_custom_call" | custom-call | flops 2013265920 | bytes 15728640 | tf_op jit(solution)/shard_map/attention_backward/pallas_call | solution.py:543
  30.3 0.0 collective-permute-done.2
  30.3 2.4 %collective-permute-done.3 = bf16[64,3072]{1,0:T(8,128)(2,1)S(1)} collective-permute-done((bf16[64,3072]{1,0:T(8,128)(2,1)S(1)}, bf16[64,3072]{1,0:T(8,128)(2,1)S(1)}, u32[]{:S(2)}, u32[]{:S(2)}) %collective-permute-start.3) | collective-permute-done | bytes 393248 | tf_op jit(solution)/shard_map/ppermute | solution.py:600
  32.8 0.6 %collective-permute-start.4 = (bf16[64,1536]{1,0:T(8,128)(2,1)S(1)}, bf16[64,1536]{1,0:T(8,128)(2,1)S(1)}, u32[]{:S(2)}, u32[]{:S(2)}) collective-permute-start(bf16[64,1536]{1,0:T(8,128)(2,1)S(1)} %get-tuple-element.44), channel_id=1, source_target_pairs={{0,12},{4,0},{8,4},{12,8},{16,28},{20,16},{24,20},{28,24},{1,13},{... | collective-permute-start | bytes 589832 | tf_op jit(solution)/shard_map/ppermute | solution.py:600
  33.3 1.4 %collective-permute-start.5 = (bf16[64,1536]{1,0:T(8,128)(2,1)S(1)}, bf16[64,1536]{1,0:T(8,128)(2,1)S(1)}, u32[]{:S(2)}, u32[]{:S(2)}) collective-permute-start(bf16[64,1536]{1,0:T(8,128)(2,1)S(1)} %get-tuple-element.45), channel_id=1, source_target_pairs={{0,28},{4,16},{8,20},{12,24},{16,12},{20,0},{24,4},{28,8},{1,29},{... | collective-permute-start | bytes 589832 | tf_op jit(solution)/shard_map/ppermute | solution.py:600
  34.8 0.2 collective-permute-start.6
  35.0 3.1 %input_grad.1 = (bf16[64,1536]{1,0:T(8,128)(2,1)S(1)}, bf16[64,1536]{1,0:T(8,128)(2,1)S(1)}) custom-call(bf16[2,128,1536]{2,1,0:T(8,128)(2,1)S(1)} %get-tuple-element.41.grad_ref, bf16[2,3072,1536]{2,1,0:T(8,128)(2,1)S(1)} %regroup.1.weight_ref, bf16[64,3072]{1,0:T(8,128)(2,1)S(1)} %bitcast.10), custom_call_target="tpu_custom_call" | custom-call | flops 1207959552 | bytes 9437184 | tf_op jit(solution)/shard_map/input_grad/pallas_call | solution.py:578
  38.1 1.2 %collective-permute-done.6 = f32[1,1536]{1,0:T(1,128)S(1)} collective-permute-done((f32[1,1536]{1,0:T(1,128)S(1)}, f32[1,1536]{1,0:T(1,128)S(1)}, u32[]{:S(2)}, u32[]{:S(2)}) %collective-permute-start.6) | collective-permute-done | bytes 6176 | tf_op jit(solution)/shard_map/ppermute | solution.py:600
  39.2 0.0 collective-permute-done.4
  39.2 1.7 %collective-permute-done.5 = bf16[64,1536]{1,0:T(8,128)(2,1)S(1)} collective-permute-done((bf16[64,1536]{1,0:T(8,128)(2,1)S(1)}, bf16[64,1536]{1,0:T(8,128)(2,1)S(1)}, u32[]{:S(2)}, u32[]{:S(2)}) %collective-permute-start.5) | collective-permute-done | bytes 196640 | tf_op jit(solution)/shard_map/ppermute | solution.py:600
  40.9 0.1 collective-permute-start.7
  41.0 1.9 %collective-permute-start.8 = (bf16[64,1536]{1,0:T(8,128)(2,1)S(1)}, bf16[64,1536]{1,0:T(8,128)(2,1)S(1)}, u32[]{:S(2)}, u32[]{:S(2)}) collective-permute-start(bf16[64,1536]{1,0:T(8,128)(2,1)S(1)} %get-tuple-element.54), channel_id=1, source_target_pairs={{0,28},{4,16},{8,20},{12,24},{16,12},{20,0},{24,4},{28,8},{1,29},{... | collective-permute-start | bytes 589832 | tf_op jit(solution)/shard_map/ppermute | solution.py:600
  42.9 0.8 %fusion = bf16[1,64,3072]{2,1,0:T(8,128)(2,1)} fusion(bf16[64,3072]{1,0:T(8,128)(2,1)S(1)} %collective-permute-done.3, bf16[64,3072]{1,0:T(8,128)(2,1)S(1)} %collective-permute-done.2), kind=kLoop, calls=%fused_computation.1 | loop fusion | flops 786432 | bytes 1179648 | tf_op jit(solution)/shard_map/broadcast_in_dim | solution.py:661
  43.8 0.6 %add.15 = f32[1,1536]{1,0:T(1,128)} add(f32[1,1536]{1,0:T(1,128)S(1)} %get-tuple-element.55, f32[1,1536]{1,0:T(1,128)S(1)} %collective-permute-done.6) | non-fusion elementwise | flops 1536 | bytes 18432 | tf_op jit(solution)/shard_map/add | solution.py:661
  44.4 3.0 %collective-permute-done.7 = bf16[64,1536]{1,0:T(8,128)(2,1)S(1)} collective-permute-done((bf16[64,1536]{1,0:T(8,128)(2,1)S(1)}, bf16[64,1536]{1,0:T(8,128)(2,1)S(1)}, u32[]{:S(2)}, u32[]{:S(2)}) %collective-permute-start.7) | collective-permute-done | bytes 196640 | tf_op jit(solution)/shard_map/ppermute | solution.py:600
  47.4 1.6 %collective-permute-done.8 = bf16[64,1536]{1,0:T(8,128)(2,1)S(1)} collective-permute-done((bf16[64,1536]{1,0:T(8,128)(2,1)S(1)}, bf16[64,1536]{1,0:T(8,128)(2,1)S(1)}, u32[]{:S(2)}, u32[]{:S(2)}) %collective-permute-start.8) | collective-permute-done | bytes 196640 | tf_op jit(solution)/shard_map/ppermute | solution.py:600
  49.1 0.8 %maximum_bitcast_fusion = bf16[1,64,3072]{2,1,0:T(8,128)(2,1)} fusion(bf16[64,1536]{1,0:T(8,128)(2,1)S(1)} %add_convert_fusion.1, bf16[64,1536]{1,0:T(8,128)(2,1)S(1)} %add_convert_fusion.2), kind=kLoop, calls=%fused_computation.2 | loop fusion | flops 786432 | bytes 786432 | tf_op jit(solution)/shard_map/broadcast_in_dim | solution.py:661
  (9 shorter events, 0.1 us)
Async XLA Ops:
  0.6 11.2 %collective-permute-start.1 = (bf16[64,3072]{1,0:T(8,128)(2,1)}, bf16[64,3072]{1,0:T(8,128)(2,1)S(1)}, u32[]{:S(2)}, u32[]{:S(2)}) collective-permute-start(bf16[64,3072]{1,0:T(8,128)(2,1)} %bitcast.11), channel_id=1, source_target_pairs={{0,16},{4,20},{8,24},{12,28},{16,0},{20,4},{24,8},{28,12},{1,17},{... | collective-permute-start | bytes 1179656 | tf_op jit(solution)/shard_map/ppermute | solution.py:600
  2.7 7.2 %copy-start = (bf16[1,64,3072]{2,1,0:T(8,128)(2,1)S(1)}, bf16[1,64,3072]{2,1,0:T(8,128)(2,1)}, u32[]{:S(2)}) copy-start(bf16[1,64,3072]{2,1,0:T(8,128)(2,1)} %param.10) | copy-start | bytes 1179652
  2.7 9.1 %copy-start.1 = (bf16[1,64,3072]{2,1,0:T(8,128)(2,1)S(1)}, bf16[1,64,3072]{2,1,0:T(8,128)(2,1)}, u32[]{:S(2)}) copy-start(bf16[1,64,3072]{2,1,0:T(8,128)(2,1)} %param.9) | copy-start | bytes 1179652
  2.7 9.1 %copy-start.2 = (f32[1,3072]{1,0:T(1,128)S(1)}, f32[1,3072]{1,0:T(1,128)}, u32[]{:S(2)}) copy-start(f32[1,3072]{1,0:T(1,128)} %gate_ref.3) | copy-start | bytes 36868
  2.7 9.1 %copy-start.3 = (f32[1,128]{1,0:T(1,128)S(1)}, f32[1,128]{1,0:T(1,128)}, u32[]{:S(2)}) copy-start(f32[1,128]{1,0:T(1,128)} %query_gain_ref.3) | copy-start | bytes 1540
  2.8 9.1 %copy-start.4 = (f32[1,128]{1,0:T(1,128)S(1)}, f32[1,128]{1,0:T(1,128)}, u32[]{:S(2)}) copy-start(f32[1,128]{1,0:T(1,128)} %key_gain_ref.3) | copy-start | bytes 1540
  2.8 9.1 %copy-start.5 = (s32[2,27]{1,0:T(2,128)S(1)}, s32[2,27]{1,0:T(2,128)}, u32[]{:S(2)}) copy-start(s32[2,27]{1,0:T(2,128)} %neighbours_ref.1) | copy-start | bytes 652
  2.8 9.1 %copy-start.6 = (s32[2]{0:T(128)S(1)}, s32[2]{0:T(128)}, u32[]{:S(2)}) copy-start(s32[2]{0:T(128)} %tile_slot_ref.1) | copy-start | bytes 28
  10.0 13.0 %collective-permute-start = (bf16[64,3072]{1,0:T(8,128)(2,1)S(1)}, bf16[64,3072]{1,0:T(8,128)(2,1)S(1)}, u32[]{:S(2)}, u32[]{:S(2)}) collective-permute-start(bf16[64,3072]{1,0:T(8,128)(2,1)S(1)} %bitcast.8), channel_id=1, source_target_pairs={{0,16},{4,20},{8,24},{12,28},{16,0},{20,4},{24,8},{28,12},{1,17},{... | collective-permute-start | bytes 1179656 | tf_op jit(solution)/shard_map/ppermute | solution.py:600
  18.3 12.0 %collective-permute-start.2 = (bf16[64,3072]{1,0:T(8,128)(2,1)S(1)}, bf16[64,3072]{1,0:T(8,128)(2,1)S(1)}, u32[]{:S(2)}, u32[]{:S(2)}) collective-permute-start(bf16[64,3072]{1,0:T(8,128)(2,1)S(1)} %get-tuple-element.39), channel_id=1, source_target_pairs={{0,4},{4,8},{8,12},{12,0},{16,20},{20,24},{24,28},{28,16},{1,5},{5... | collective-permute-start | bytes 1179656 | tf_op jit(solution)/shard_map/ppermute | solution.py:600
  21.1 11.6 %collective-permute-start.3 = (bf16[64,3072]{1,0:T(8,128)(2,1)S(1)}, bf16[64,3072]{1,0:T(8,128)(2,1)S(1)}, u32[]{:S(2)}, u32[]{:S(2)}) collective-permute-start(bf16[64,3072]{1,0:T(8,128)(2,1)S(1)} %get-tuple-element.40), channel_id=1, source_target_pairs={{0,20},{4,24},{8,28},{12,16},{16,4},{20,8},{24,12},{28,0},{1,21},{... | collective-permute-start | bytes 1179656 | tf_op jit(solution)/shard_map/ppermute | solution.py:600
  32.8 6.5 %collective-permute-start.4 = (bf16[64,1536]{1,0:T(8,128)(2,1)S(1)}, bf16[64,1536]{1,0:T(8,128)(2,1)S(1)}, u32[]{:S(2)}, u32[]{:S(2)}) collective-permute-start(bf16[64,1536]{1,0:T(8,128)(2,1)S(1)} %get-tuple-element.44), channel_id=1, source_target_pairs={{0,12},{4,0},{8,4},{12,8},{16,28},{20,16},{24,20},{28,24},{1,13},{... | collective-permute-start | bytes 589832 | tf_op jit(solution)/shard_map/ppermute | solution.py:600
  33.3 7.6 %collective-permute-start.5 = (bf16[64,1536]{1,0:T(8,128)(2,1)S(1)}, bf16[64,1536]{1,0:T(8,128)(2,1)S(1)}, u32[]{:S(2)}, u32[]{:S(2)}) collective-permute-start(bf16[64,1536]{1,0:T(8,128)(2,1)S(1)} %get-tuple-element.45), channel_id=1, source_target_pairs={{0,28},{4,16},{8,20},{12,24},{16,12},{20,0},{24,4},{28,8},{1,29},{... | collective-permute-start | bytes 589832 | tf_op jit(solution)/shard_map/ppermute | solution.py:600
  34.8 4.5 %collective-permute-start.6 = (f32[1,1536]{1,0:T(1,128)S(1)}, f32[1,1536]{1,0:T(1,128)S(1)}, u32[]{:S(2)}, u32[]{:S(2)}) collective-permute-start(f32[1,1536]{1,0:T(1,128)S(1)} %get-tuple-element.48), channel_id=1, source_target_pairs={{0,16},{4,20},{8,24},{12,28},{16,0},{20,4},{24,8},{28,12},{1,17},{... | collective-permute-start | bytes 18440 | tf_op jit(solution)/shard_map/ppermute | solution.py:600
  40.9 6.5 %collective-permute-start.7 = (bf16[64,1536]{1,0:T(8,128)(2,1)S(1)}, bf16[64,1536]{1,0:T(8,128)(2,1)S(1)}, u32[]{:S(2)}, u32[]{:S(2)}) collective-permute-start(bf16[64,1536]{1,0:T(8,128)(2,1)S(1)} %get-tuple-element.53), channel_id=1, source_target_pairs={{0,12},{4,0},{8,4},{12,8},{16,28},{20,16},{24,20},{28,24},{1,13},{... | collective-permute-start | bytes 589832 | tf_op jit(solution)/shard_map/ppermute | solution.py:600
  41.0 8.0 %collective-permute-start.8 = (bf16[64,1536]{1,0:T(8,128)(2,1)S(1)}, bf16[64,1536]{1,0:T(8,128)(2,1)S(1)}, u32[]{:S(2)}, u32[]{:S(2)}) collective-permute-start(bf16[64,1536]{1,0:T(8,128)(2,1)S(1)} %get-tuple-element.54), channel_id=1, source_target_pairs={{0,28},{4,16},{8,20},{12,24},{16,12},{20,0},{24,4},{28,8},{1,29},{... | collective-permute-start | bytes 589832 | tf_op jit(solution)/shard_map/ppermute | solution.py:600

commit v8 on v7

--- a/solution.py
+++ b/solution.py
@@ -441,16 +441,15 @@
     )(neighbours, tile_slot, own, other, weight, out_weight, query_gain, key_gain, gate)
 
 
-def input_grad_blocks(grad_ref, weight_ref, own_ref, first, kept_ref, sent_ref):
-    local, columns = kept_ref.shape
-    block = math.gcd(columns, 512)
-    for start in range(0, columns, block):
-        rows = slice(first + start, first + start + block)
-        total = dot_nt(grad_ref[0], weight_ref[0, rows, :])
+def input_grad(grad_ref, weight_ref, own_ref, kept_ref, sent_ref):
+    local, model = own_ref.shape
+    block = 512
+    for start in range(0, model, block):
+        part = slice(start, start + block)
+        total = dot_nt(grad_ref[0], weight_ref[0, part, :])
         for group in range(1, grad_ref.shape[0]):
-            total += dot_nt(grad_ref[group], weight_ref[group, rows, :])
-        part = slice(start, start + block)
-        kept_ref[:, part] = (own_ref[:, rows].astype(F32) + total[:local]).astype(BF16)
+            total += dot_nt(grad_ref[group], weight_ref[group, part, :])
+        kept_ref[:, part] = (own_ref[:, part].astype(F32) + total[:local]).astype(BF16)
         sent_ref[:, part] = total[local:].astype(BF16)
 
 
@@ -465,11 +464,11 @@
     query_gain_ref,
     key_gain_ref,
     gate_ref,
-    grad_ref,
     gate_kept_ref,
     gate_sent_ref,
     kept_ref,
     sent_ref,
+    grad_ref,
     scaled_ref,
     attended_grad_ref,
     gate_grad_ref,
@@ -528,11 +527,11 @@
             attended_grad(group + 1)
         for head in range(GROUP):
             attend_backward(group, head)
-    input_grad_blocks(grad_ref, weight_ref, own_ref, 0, kept_ref, sent_ref)
+    input_grad(grad_ref, weight_ref, own_ref, kept_ref, sent_ref)
 
 
 def backward(
-    own, other, out_weight, weight, projected, probs, attention, query_gain, key_gain, gate, columns
+    own, other, out_weight, weight, projected, probs, attention, query_gain, key_gain, gate
 ):
     local, model = own.shape
     groups, tokens, wide = projected.shape
@@ -543,51 +542,27 @@
     return pl.pallas_call(
         backward_kernel,
         out_shape=(
-            jax.ShapeDtypeStruct((groups, tokens, wide), BF16),
             jax.ShapeDtypeStruct((1, model // 2), F32),
             jax.ShapeDtypeStruct((1, model // 2), F32),
-            jax.ShapeDtypeStruct((local, columns), BF16),
-            jax.ShapeDtypeStruct((local, columns), BF16),
+            jax.ShapeDtypeStruct((local, model), BF16),
+            jax.ShapeDtypeStruct((local, model), BF16),
         ),
         in_specs=[vmem] * 10,
-        out_specs=(vmem,) * 5,
+        out_specs=(vmem,) * 4,
         scratch_shapes=[
+            pltpu.VMEM((groups, tokens, wide), BF16),
             pltpu.VMEM((tokens, model), BF16),
             pltpu.VMEM((groups, tokens, GROUP * head_dim), BF16),
             pltpu.VMEM((1, model), F32),
         ],
         compiler_params=params(12),
         cost_estimate=pl.CostEstimate(
-            flops=2 * tokens * (out_weight.size + groups * columns * wide),
-            bytes_accessed=2 * (out_weight.size + groups * columns * wide),
+            flops=2 * tokens * (out_weight.size + weight.size),
+            bytes_accessed=2 * (out_weight.size + weight.size),
             transcendentals=0,
         ),
         name="attention_backward",
     )(own, other, out_weight, weight, projected, probs, attention, query_gain, key_gain, gate)
-
-
-def input_grad_kernel(first, grad_ref, weight_ref, own_ref, kept_ref, sent_ref):
-    input_grad_blocks(grad_ref, weight_ref, own_ref, first, kept_ref, sent_ref)
-
-
-def input_grad_part(grad, weight, own, first, columns):
-    local, model = own.shape
-    groups, tokens, wide = grad.shape
-    out = jax.ShapeDtypeStruct((local, columns), BF16)
-    vmem = pl.BlockSpec(memory_space=pltpu.VMEM)
-    return pl.pallas_call(
-        functools.partial(input_grad_kernel, first),
-        out_shape=(out, out),
-        in_specs=[vmem, vmem, vmem],
-        out_specs=(vmem, vmem),
-        compiler_params=params(8),
-        cost_estimate=pl.CostEstimate(
-            flops=2 * tokens * columns * groups * wide,
-            bytes_accessed=2 * columns * groups * wide,
-            transcendentals=0,
-        ),
-        name="input_grad",
-    )(grad, pltpu.with_memory_space_constraint(weight, pltpu.VMEM), own)
 
 
 def routed(block, seq_step, pipe_step):
@@ -614,7 +589,6 @@
     stream = segment_input[0]
     upstream = output_grad[0]
     out_local = out_weight[0]
-    model = stream.shape[1]
     other_stream = routed(stream, 1, 0)
     weight = regroup(qkv_weight[0], 128, 8)
     weight, upstream = lax.optimization_barrier((weight, upstream))
@@ -632,8 +606,7 @@
     )
     kept = routed(kept, 0, 1)
     sent = routed(sent, 1, 1)
-    columns = model // 2
-    grad, gate_kept, gate_sent, first, second = backward(
+    gate_kept, gate_sent, grad_kept, grad_sent = backward(
         upstream,
         other_upstream,
         out_local,
@@ -644,20 +617,13 @@
         query_gain,
         key_gain,
         gate_scale,
-        columns,
-    )
-    grad, first, second, kept, sent = lax.optimization_barrier((grad, first, second, kept, sent))
+    )
+    grad_kept, grad_sent, kept, sent = lax.optimization_barrier((grad_kept, grad_sent, kept, sent))
+    grad_sent = routed(grad_sent, 1, -1)
+    grad_kept = routed(grad_kept, 0, -1)
     gate_sent = routed(gate_sent, 1, 0)
-    early = (routed(first, 0, -1), routed(second, 1, -1))
-    late = input_grad_part(grad, weight, upstream, columns, model - columns)
-    late, early, kept, sent, gate_sent = lax.optimization_barrier(
-        (late, early, kept, sent, gate_sent)
-    )
-    pieces = [early, (routed(late[0], 0, -1), routed(late[1], 1, -1))]
     segment_output = (kept.astype(F32) + sent.astype(F32)).astype(BF16)
-    input_grad = jnp.concatenate(
-        [(a.astype(F32) + b.astype(F32)).astype(BF16) for a, b in pieces], axis=1
-    )
+    input_grad = (grad_kept.astype(F32) + grad_sent.astype(F32)).astype(BF16)
     return (segment_output[None], input_grad[None], gate_kept + gate_sent)
 
 

time: 50 us -> 49.7 us (level)
  waiting for transfers between devices: 11.6 us -> 14 us
  starting transfers between devices: 11.1 us -> 8.91 us
  Pallas kernels: 24.1 us -> 23.6 us
    ppermute x9 -> x7, waiting for transfers between devices: 11.6 us -> 14 us  [routed(): return lax.ppermute(block, ('seq', 'pipe'), route)]
    ppermute x9 -> x7, starting transfers between devices: 11.1 us -> 8.91 us  [routed(): return lax.ppermute(block, ('seq', 'pipe'), route)]
    pallas_call x2 -> x1, Pallas kernels: 10.4 us -> 9.99 us  [backward(): pl.pallas_call(backward_kernel, out_shape=(jax.ShapeDtypeStruct((1, model...]
  transfers between devices with their start and end apart: 9 -> 7, of which waited for: 6 -> 4; matrix products, arithmetic and copies ran while one was open for 3% -> 3% of each run, Pallas kernels for 48% -> 48%
where the time goes in v8:
time: 49.7 us; the launch traced here: 49.6 us
  Pallas kernels  23.6 us (47%)
  waiting for transfers between devices  14 us (28%)
  starting transfers between devices  8.91 us (18%)
  other arithmetic  2.28 us (5%)
  between operations  0.73 us (1%)
    ppermute x7, waiting for transfers between devices, routed(): return lax.ppermute(block, ('seq', 'pipe'), route)  14 us
    pallas_call x1, Pallas kernels, backward(): pl.pallas_call(backward_kernel, out_shape=(jax.ShapeDtypeStruct((1, model...  9.99 us
    ppermute x7, starting transfers between devices, routed(): return lax.ppermute(block, ('seq', 'pipe'), route)  8.91 us
    pallas_call x1, Pallas kernels, regroup(): pl.pallas_call(regroup_kernel, out_shape=pltpu.VMEM(out, weight.dtype), i...  7.17 us
    pallas_call x1, Pallas kernels, forward(): pl.pallas_call(forward_kernel, out_shape=(jax.ShapeDtypeStruct((groups, t...  6.46 us
    broadcast_in_dim x2, other arithmetic, pair_body(): return (segment_output[None], input_grad[None], gate_kept + gate_sent)  1.68 us
  transfers between devices with their start and end apart: 7, of which 4 were waited for; matrix products, arithmetic and copies ran while one was open for 3% of the time, Pallas kernels for 48%

profile of v8, /device:TPU:1, one launch (start us, length us, event | category | flops | bytes accessed | tf_op | source)
XLA Modules:
  0.0 49.6 jit_solution(2275923010582937927)
XLA Ops:
  0.6 2.1 %collective-permute-start.1 = (bf16[64,3072]{1,0:T(8,128)(2,1)}, bf16[64,3072]{1,0:T(8,128)(2,1)S(1)}, u32[]{:S(2)}, u32[]{:S(2)}) collective-permute-start(bf16[64,3072]{1,0:T(8,128)(2,1)} %bitcast.10), channel_id=1, source_target_pairs={{0,16},{4,20},{8,24},{12,28},{16,0},{20,4},{24,8},{28,12},{1,17},{... | collective-permute-start | bytes 1179656 | tf_op jit(solution)/shard_map/ppermute | solution.py:575
  2.7 0.0 copy-start
  2.7 0.0 copy-start.1
  2.8 0.0 copy-start.4
  2.8 0.0 copy-start.5
  2.8 0.0 copy-start.6
  2.8 7.2 %regroup.1.weight_ref = bf16[2,3072,1536]{2,1,0:T(8,128)(2,1)S(1)} custom-call(bf16[3072,8,384]{2,1,0:T(8,128)(2,1)} %bitcast.12), custom_call_target="tpu_custom_call" | custom-call | bytes 37748736 | tf_op jit(solution)/shard_map/regroup/pallas_call | solution.py:281
  10.0 0.0 copy-done
  10.0 0.1 collective-permute-start
  10.1 1.7 %collective-permute-done.1.other_ref = bf16[64,3072]{1,0:T(8,128)(2,1)S(1)} collective-permute-done((bf16[64,3072]{1,0:T(8,128)(2,1)}, bf16[64,3072]{1,0:T(8,128)(2,1)S(1)}, u32[]{:S(2)}, u32[]{:S(2)}) %collective-permute-start.1) | collective-permute-done | bytes 393248 | tf_op jit(solution)/shard_map/ppermute | solution.py:575
  11.8 0.0 copy-done.1
  11.8 0.0 copy-done.2
  11.8 0.0 copy-done.3
  11.8 0.0 copy-done.4
  11.8 0.0 copy-done.5
  11.8 0.0 copy-done.6
  11.8 6.5 %attention_forward.1 = (f32[2,128,1536]{2,1,0:T(8,128)S(1)}, bf16[8,128,128]{2,1,0:T(8,128)(2,1)S(1)}, f32[128,3072]{1,0:T(8,128)S(1)}, bf16[64,3072]{1,0:T(8,12...) custom-call(s32[2,27]{1,0:T(2,128)S(1)} %copy-done.5, s32[2]{0:T(128)S(1)} %copy-done.6, ...), custom_call_target="tpu_custom_call" | custom-call | flops 3221225472 | bytes 25165824 | tf_op jit(solution)/shard_map/attention_forward/pallas_call | solution.py:418
  18.3 2.8 %collective-permute-start.2 = (bf16[64,3072]{1,0:T(8,128)(2,1)S(1)}, bf16[64,3072]{1,0:T(8,128)(2,1)S(1)}, u32[]{:S(2)}, u32[]{:S(2)}) collective-permute-start(bf16[64,3072]{1,0:T(8,128)(2,1)S(1)} %get-tuple-element.27), channel_id=1, source_target_pairs={{0,4},{4,8},{8,12},{12,0},{16,20},{20,24},{24,28},{28,16},{1,5},{5... | collective-permute-start | bytes 1179656 | tf_op jit(solution)/shard_map/ppermute | solution.py:575
  21.1 1.9 %collective-permute-start.3 = (bf16[64,3072]{1,0:T(8,128)(2,1)S(1)}, bf16[64,3072]{1,0:T(8,128)(2,1)S(1)}, u32[]{:S(2)}, u32[]{:S(2)}) collective-permute-start(bf16[64,3072]{1,0:T(8,128)(2,1)S(1)} %get-tuple-element.28), channel_id=1, source_target_pairs={{0,20},{4,24},{8,28},{12,16},{16,4},{20,8},{24,12},{28,0},{1,21},{... | collective-permute-start | bytes 1179656 | tf_op jit(solution)/shard_map/ppermute | solution.py:575
  23.0 0.0 collective-permute-done.other_ref
  23.0 10.0 %attention_backward.1 = (f32[1,1536]{1,0:T(1,128)S(1)}, f32[1,1536]{1,0:T(1,128)S(1)}, bf16[64,3072]{1,0:T(8,128)(2,1)S(1)}, bf16[64,3072]{1,0:T(8,128)(2,1)S(1)}) custom-call(bf16[64,3072]{1,0:T(8,128)(2,1)S(1)} %bitcast.9, bf16[64,3072]{1,0:T(8,128)(2,1)S(1)} %collective-permute-done.other_ref, bf16[1024,3072]{1,0:T(8,128)(2,1)S(1)} %get-tuple-element.21.out_weight_ref, ...), custom_call_target="tpu_custom_call" | custom-call | flops 3221225472 | bytes 25165824 | tf_op jit(solution)/shard_map/attention_backward/pallas_call | solution.py:542
  33.0 0.3 collective-permute-start.6
  33.3 2.3 %collective-permute-done.6 = f32[1,1536]{1,0:T(1,128)S(1)} collective-permute-done((f32[1,1536]{1,0:T(1,128)S(1)}, f32[1,1536]{1,0:T(1,128)S(1)}, u32[]{:S(2)}, u32[]{:S(2)}) %collective-permute-start.6) | collective-permute-done | bytes 6176 | tf_op jit(solution)/shard_map/ppermute | solution.py:575
  35.5 0.6 %add.11 = f32[1,1536]{1,0:T(1,128)} add(f32[1,1536]{1,0:T(1,128)S(1)} %get-tuple-element.33, f32[1,1536]{1,0:T(1,128)S(1)} %collective-permute-done.6) | non-fusion elementwise | flops 1536 | bytes 18432 | tf_op jit(solution)/shard_map/add | solution.py:627
  36.1 0.0 collective-permute-done.2
  36.1 0.0 collective-permute-done.3
  36.1 1.8 %collective-permute-start.4 = (bf16[64,3072]{1,0:T(8,128)(2,1)S(1)}, bf16[64,3072]{1,0:T(8,128)(2,1)S(1)}, u32[]{:S(2)}, u32[]{:S(2)}) collective-permute-start(bf16[64,3072]{1,0:T(8,128)(2,1)S(1)} %get-tuple-element.31), channel_id=1, source_target_pairs={{0,12},{4,0},{8,4},{12,8},{16,28},{20,16},{24,20},{28,24},{1,13},{... | collective-permute-start | bytes 1179656 | tf_op jit(solution)/shard_map/ppermute | solution.py:575
  37.9 0.0 collective-permute-start.5
  37.9 0.8 %fusion = bf16[1,64,3072]{2,1,0:T(8,128)(2,1)} fusion(bf16[64,3072]{1,0:T(8,128)(2,1)S(1)} %collective-permute-done.3, bf16[64,3072]{1,0:T(8,128)(2,1)S(1)} %collective-permute-done.2), kind=kLoop, calls=%fused_computation.2 | loop fusion | flops 786432 | bytes 1179648 | tf_op jit(solution)/shard_map/broadcast_in_dim | solution.py:627
  38.7 6.9 %collective-permute-done.4 = bf16[64,3072]{1,0:T(8,128)(2,1)S(1)} collective-permute-done((bf16[64,3072]{1,0:T(8,128)(2,1)S(1)}, bf16[64,3072]{1,0:T(8,128)(2,1)S(1)}, u32[]{:S(2)}, u32[]{:S(2)}) %collective-permute-start.4) | collective-permute-done | bytes 393248 | tf_op jit(solution)/shard_map/ppermute | solution.py:575
  45.6 3.1 %collective-permute-done.5 = bf16[64,3072]{1,0:T(8,128)(2,1)S(1)} collective-permute-done((bf16[64,3072]{1,0:T(8,128)(2,1)S(1)}, bf16[64,3072]{1,0:T(8,128)(2,1)S(1)}, u32[]{:S(2)}, u32[]{:S(2)}) %collective-permute-start.5) | collective-permute-done | bytes 393248 | tf_op jit(solution)/shard_map/ppermute | solution.py:575
  48.7 0.8 %fusion.1 = bf16[1,64,3072]{2,1,0:T(8,128)(2,1)} fusion(bf16[64,3072]{1,0:T(8,128)(2,1)S(1)} %collective-permute-done.5, bf16[64,3072]{1,0:T(8,128)(2,1)S(1)} %collective-permute-done.4), kind=kLoop, calls=%fused_computation.3 | loop fusion | flops 786432 | bytes 1179648 | tf_op jit(solution)/shard_map/broadcast_in_dim | solution.py:627
  (2 shorter events, 0.0 us)
Async XLA Ops:
  0.6 11.2 %collective-permute-start.1 = (bf16[64,3072]{1,0:T(8,128)(2,1)}, bf16[64,3072]{1,0:T(8,128)(2,1)S(1)}, u32[]{:S(2)}, u32[]{:S(2)}) collective-permute-start(bf16[64,3072]{1,0:T(8,128)(2,1)} %bitcast.10), channel_id=1, source_target_pairs={{0,16},{4,20},{8,24},{12,28},{16,0},{20,4},{24,8},{28,12},{1,17},{... | collective-permute-start | bytes 1179656 | tf_op jit(solution)/shard_map/ppermute | solution.py:575
  2.7 7.2 %copy-start = (bf16[1,64,3072]{2,1,0:T(8,128)(2,1)S(1)}, bf16[1,64,3072]{2,1,0:T(8,128)(2,1)}, u32[]{:S(2)}) copy-start(bf16[1,64,3072]{2,1,0:T(8,128)(2,1)} %param.10) | copy-start | bytes 1179652
  2.7 9.1 %copy-start.1 = (bf16[1,64,3072]{2,1,0:T(8,128)(2,1)S(1)}, bf16[1,64,3072]{2,1,0:T(8,128)(2,1)}, u32[]{:S(2)}) copy-start(bf16[1,64,3072]{2,1,0:T(8,128)(2,1)} %param.9) | copy-start | bytes 1179652
  2.7 9.1 %copy-start.2 = (f32[1,3072]{1,0:T(1,128)S(1)}, f32[1,3072]{1,0:T(1,128)}, u32[]{:S(2)}) copy-start(f32[1,3072]{1,0:T(1,128)} %gate_ref.3) | copy-start | bytes 36868
  2.7 9.1 %copy-start.3 = (f32[1,128]{1,0:T(1,128)S(1)}, f32[1,128]{1,0:T(1,128)}, u32[]{:S(2)}) copy-start(f32[1,128]{1,0:T(1,128)} %query_gain_ref.3) | copy-start | bytes 1540
  2.8 9.1 %copy-start.4 = (f32[1,128]{1,0:T(1,128)S(1)}, f32[1,128]{1,0:T(1,128)}, u32[]{:S(2)}) copy-start(f32[1,128]{1,0:T(1,128)} %key_gain_ref.3) | copy-start | bytes 1540
  2.8 9.1 %copy-start.5 = (s32[2,27]{1,0:T(2,128)S(1)}, s32[2,27]{1,0:T(2,128)}, u32[]{:S(2)}) copy-start(s32[2,27]{1,0:T(2,128)} %neighbours_ref.1) | copy-start | bytes 652
  2.8 9.1 %copy-start.6 = (s32[2]{0:T(128)S(1)}, s32[2]{0:T(128)}, u32[]{:S(2)}) copy-start(s32[2]{0:T(128)} %tile_slot_ref.1) | copy-start | bytes 28
  10.0 13.0 %collective-permute-start = (bf16[64,3072]{1,0:T(8,128)(2,1)S(1)}, bf16[64,3072]{1,0:T(8,128)(2,1)S(1)}, u32[]{:S(2)}, u32[]{:S(2)}) collective-permute-start(bf16[64,3072]{1,0:T(8,128)(2,1)S(1)} %bitcast.8), channel_id=1, source_target_pairs={{0,16},{4,20},{8,24},{12,28},{16,0},{20,4},{24,8},{28,12},{1,17},{... | collective-permute-start | bytes 1179656 | tf_op jit(solution)/shard_map/ppermute | solution.py:575
  18.3 17.8 %collective-permute-start.2 = (bf16[64,3072]{1,0:T(8,128)(2,1)S(1)}, bf16[64,3072]{1,0:T(8,128)(2,1)S(1)}, u32[]{:S(2)}, u32[]{:S(2)}) collective-permute-start(bf16[64,3072]{1,0:T(8,128)(2,1)S(1)} %get-tuple-element.27), channel_id=1, source_target_pairs={{0,4},{4,8},{8,12},{12,0},{16,20},{20,24},{24,28},{28,16},{1,5},{5... | collective-permute-start | bytes 1179656 | tf_op jit(solution)/shard_map/ppermute | solution.py:575
  21.1 15.0 %collective-permute-start.3 = (bf16[64,3072]{1,0:T(8,128)(2,1)S(1)}, bf16[64,3072]{1,0:T(8,128)(2,1)S(1)}, u32[]{:S(2)}, u32[]{:S(2)}) collective-permute-start(bf16[64,3072]{1,0:T(8,128)(2,1)S(1)} %get-tuple-element.28), channel_id=1, source_target_pairs={{0,20},{4,24},{8,28},{12,16},{16,4},{20,8},{24,12},{28,0},{1,21},{... | collective-permute-start | bytes 1179656 | tf_op jit(solution)/shard_map/ppermute | solution.py:575
  33.0 2.5 %collective-permute-start.6 = (f32[1,1536]{1,0:T(1,128)S(1)}, f32[1,1536]{1,0:T(1,128)S(1)}, u32[]{:S(2)}, u32[]{:S(2)}) collective-permute-start(f32[1,1536]{1,0:T(1,128)S(1)} %get-tuple-element.34), channel_id=1, source_target_pairs={{0,16},{4,20},{8,24},{12,28},{16,0},{20,4},{24,8},{28,12},{1,17},{... | collective-permute-start | bytes 18440 | tf_op jit(solution)/shard_map/ppermute | solution.py:575
  36.1 9.5 %collective-permute-start.4 = (bf16[64,3072]{1,0:T(8,128)(2,1)S(1)}, bf16[64,3072]{1,0:T(8,128)(2,1)S(1)}, u32[]{:S(2)}, u32[]{:S(2)}) collective-permute-start(bf16[64,3072]{1,0:T(8,128)(2,1)S(1)} %get-tuple-element.31), channel_id=1, source_target_pairs={{0,12},{4,0},{8,4},{12,8},{16,28},{20,16},{24,20},{28,24},{1,13},{... | collective-permute-start | bytes 1179656 | tf_op jit(solution)/shard_map/ppermute | solution.py:575
  37.9 10.9 %collective-permute-start.5 = (bf16[64,3072]{1,0:T(8,128)(2,1)S(1)}, bf16[64,3072]{1,0:T(8,128)(2,1)S(1)}, u32[]{:S(2)}, u32[]{:S(2)}) collective-permute-start(bf16[64,3072]{1,0:T(8,128)(2,1)S(1)} %get-tuple-element.32), channel_id=1, source_target_pairs={{0,28},{4,16},{8,20},{12,24},{16,12},{20,0},{24,4},{28,8},{1,29},{... | collective-permute-start | bytes 1179656 | tf_op jit(solution)/shard_map/ppermute | solution.py:575

commit v9 on v8

--- a/solution.py
+++ b/solution.py
@@ -446,9 +446,10 @@
     block = 512
     for start in range(0, model, block):
         part = slice(start, start + block)
-        total = dot_nt(grad_ref[0], weight_ref[0, part, :])
+        total = dot_nt(weight_ref[0, part, :], grad_ref[0])
         for group in range(1, grad_ref.shape[0]):
-            total += dot_nt(grad_ref[group], weight_ref[group, part, :])
+            total += dot_nt(weight_ref[group, part, :], grad_ref[group])
+        total = total.T
         kept_ref[:, part] = (own_ref[:, part].astype(F32) + total[:local]).astype(BF16)
         sent_ref[:, part] = total[local:].astype(BF16)
 
@@ -621,8 +622,9 @@
     grad_kept, grad_sent, kept, sent = lax.optimization_barrier((grad_kept, grad_sent, kept, sent))
     grad_sent = routed(grad_sent, 1, -1)
     grad_kept = routed(grad_kept, 0, -1)
+    segment_output = (kept.astype(F32) + sent.astype(F32)).astype(BF16)
+    segment_output, gate_sent = lax.optimization_barrier((segment_output, gate_sent))
     gate_sent = routed(gate_sent, 1, 0)
-    segment_output = (kept.astype(F32) + sent.astype(F32)).astype(BF16)
     input_grad = (grad_kept.astype(F32) + grad_sent.astype(F32)).astype(BF16)
     return (segment_output[None], input_grad[None], gate_kept + gate_sent)
 

time: 49.7 us -> 46.7 us (0.940); the launches traced: 49.6 us -> 45.9 us
  waiting for transfers between devices: 14 us -> 10.6 us
    ppermute x7, waiting for transfers between devices: 14 us -> 10.6 us  [routed(): return lax.ppermute(block, ('seq', 'pipe'), route)]
    convert_element_type x0 -> x1, other arithmetic: none -> 0.84 us  [pair_body(): segment_output = (kept.astype(F32) + sent.astype(F32)).astype(BF16)]
    broadcast_in_dim x2 -> x1, other arithmetic: 1.68 us -> 0.84 us  [pair_body(): return (segment_output[None], input_grad[None], gate_kept + gate_sent)]
  transfers between devices with their start and end apart: 7 -> 7, of which waited for: 4 -> 4; matrix products, arithmetic and copies ran while one was open for 3% -> 3% of each run, Pallas kernels for 48% -> 51%
where the time goes in v9:
time: 46.7 us; the launch traced here: 45.9 us
  Pallas kernels  23.3 us (50%)
  waiting for transfers between devices  10.6 us (23%)
  starting transfers between devices  9.08 us (19%)
  other arithmetic  2.28 us (5%)
  between operations  0.73 us (2%)
    ppermute x7, waiting for transfers between devices, routed(): return lax.ppermute(block, ('seq', 'pipe'), route)  10.6 us
    pallas_call x1, Pallas kernels, backward(): pl.pallas_call(backward_kernel, out_shape=(jax.ShapeDtypeStruct((1, model...  9.63 us
    ppermute x7, starting transfers between devices, routed(): return lax.ppermute(block, ('seq', 'pipe'), route)  9.08 us
    pallas_call x1, Pallas kernels, regroup(): pl.pallas_call(regroup_kernel, out_shape=pltpu.VMEM(out, weight.dtype), i...  7.17 us
    pallas_call x1, Pallas kernels, forward(): pl.pallas_call(forward_kernel, out_shape=(jax.ShapeDtypeStruct((groups, t...  6.46 us
  transfers between devices with their start and end apart: 7, of which 4 were waited for; matrix products, arithmetic and copies ran while one was open for 3% of the time, Pallas kernels for 51%

profile of v9, /device:TPU:1, one launch (start us, length us, event | category | flops | bytes accessed | tf_op | source)
XLA Modules:
  0.0 45.9 jit_solution(3326686320493216012)
XLA Ops:
  0.6 2.1 %collective-permute-start.1 = (bf16[64,3072]{1,0:T(8,128)(2,1)}, bf16[64,3072]{1,0:T(8,128)(2,1)S(1)}, u32[]{:S(2)}, u32[]{:S(2)}) collective-permute-start(bf16[64,3072]{1,0:T(8,128)(2,1)} %bitcast.9), channel_id=1, source_target_pairs={{0,16},{4,20},{8,24},{12,28},{16,0},{20,4},{24,8},{28,12},{1,17},{... | collective-permute-start | bytes 1179656 | tf_op jit(solution)/shard_map/ppermute | solution.py:576
  2.7 0.0 copy-start
  2.7 0.0 copy-start.1
  2.8 0.0 copy-start.4
  2.8 0.0 copy-start.5
  2.8 0.0 copy-start.6
  2.8 7.2 %regroup.1.weight_ref = bf16[2,3072,1536]{2,1,0:T(8,128)(2,1)S(1)} custom-call(bf16[3072,8,384]{2,1,0:T(8,128)(2,1)} %bitcast.11), custom_call_target="tpu_custom_call" | custom-call | bytes 37748736 | tf_op jit(solution)/shard_map/regroup/pallas_call | solution.py:281
  10.0 0.0 copy-done
  10.0 0.1 collective-permute-start
  10.1 1.7 %collective-permute-done.1.other_ref = bf16[64,3072]{1,0:T(8,128)(2,1)S(1)} collective-permute-done((bf16[64,3072]{1,0:T(8,128)(2,1)}, bf16[64,3072]{1,0:T(8,128)(2,1)S(1)}, u32[]{:S(2)}, u32[]{:S(2)}) %collective-permute-start.1) | collective-permute-done | bytes 393248 | tf_op jit(solution)/shard_map/ppermute | solution.py:576
  11.8 0.0 copy-done.1
  11.8 0.0 copy-done.2
  11.8 0.0 copy-done.3
  11.8 0.0 copy-done.4
  11.8 0.0 copy-done.5
  11.8 0.0 copy-done.6
  11.8 6.5 %attention_forward.1 = (f32[2,128,1536]{2,1,0:T(8,128)S(1)}, bf16[8,128,128]{2,1,0:T(8,128)(2,1)S(1)}, f32[128,3072]{1,0:T(8,128)S(1)}, bf16[64,3072]{1,0:T(8,12...) custom-call(s32[2,27]{1,0:T(2,128)S(1)} %copy-done.5, s32[2]{0:T(128)S(1)} %copy-done.6, ...), custom_call_target="tpu_custom_call" | custom-call | flops 3221225472 | bytes 25165824 | tf_op jit(solution)/shard_map/attention_forward/pallas_call | solution.py:418
  18.3 2.8 %collective-permute-start.2 = (bf16[64,3072]{1,0:T(8,128)(2,1)S(1)}, bf16[64,3072]{1,0:T(8,128)(2,1)S(1)}, u32[]{:S(2)}, u32[]{:S(2)}) collective-permute-start(bf16[64,3072]{1,0:T(8,128)(2,1)S(1)} %get-tuple-element.29), channel_id=1, source_target_pairs={{0,4},{4,8},{8,12},{12,0},{16,20},{20,24},{24,28},{28,16},{1,5},{5... | collective-permute-start | bytes 1179656 | tf_op jit(solution)/shard_map/ppermute | solution.py:576
  21.1 1.9 %collective-permute-start.3 = (bf16[64,3072]{1,0:T(8,128)(2,1)S(1)}, bf16[64,3072]{1,0:T(8,128)(2,1)S(1)}, u32[]{:S(2)}, u32[]{:S(2)}) collective-permute-start(bf16[64,3072]{1,0:T(8,128)(2,1)S(1)} %get-tuple-element.30), channel_id=1, source_target_pairs={{0,20},{4,24},{8,28},{12,16},{16,4},{20,8},{24,12},{28,0},{1,21},{... | collective-permute-start | bytes 1179656 | tf_op jit(solution)/shard_map/ppermute | solution.py:576
  23.0 0.0 collective-permute-done.other_ref
  23.0 9.6 %attention_backward.1 = (f32[1,1536]{1,0:T(1,128)S(1)}, f32[1,1536]{1,0:T(1,128)S(1)}, bf16[64,3072]{1,0:T(8,128)(2,1)S(1)}, bf16[64,3072]{1,0:T(8,128)(2,1)S(1)}) custom-call(bf16[64,3072]{1,0:T(8,128)(2,1)S(1)} %bitcast.8, bf16[64,3072]{1,0:T(8,128)(2,1)S(1)} %collective-permute-done.other_ref, bf16[1024,3072]{1,0:T(8,128)(2,1)S(1)} %get-tuple-element.23.out_weight_ref, ...), custom_call_target="tpu_custom_call" | custom-call | flops 3221225472 | bytes 25165824 | tf_op jit(solution)/shard_map/attention_backward/pallas_call | solution.py:543
  32.6 0.0 collective-permute-done.2
  32.6 0.1 collective-permute-done.3
  32.7 0.6 %collective-permute-start.4 = (bf16[64,3072]{1,0:T(8,128)(2,1)S(1)}, bf16[64,3072]{1,0:T(8,128)(2,1)S(1)}, u32[]{:S(2)}, u32[]{:S(2)}) collective-permute-start(bf16[64,3072]{1,0:T(8,128)(2,1)S(1)} %get-tuple-element.35), channel_id=1, source_target_pairs={{0,12},{4,0},{8,4},{12,8},{16,28},{20,16},{24,20},{28,24},{1,13},{... | collective-permute-start | bytes 1179656 | tf_op jit(solution)/shard_map/ppermute | solution.py:576
  33.3 1.4 %collective-permute-start.5 = (bf16[64,3072]{1,0:T(8,128)(2,1)S(1)}, bf16[64,3072]{1,0:T(8,128)(2,1)S(1)}, u32[]{:S(2)}, u32[]{:S(2)}) collective-permute-start(bf16[64,3072]{1,0:T(8,128)(2,1)S(1)} %get-tuple-element.36), channel_id=1, source_target_pairs={{0,28},{4,16},{8,20},{12,24},{16,12},{20,0},{24,4},{28,8},{1,29},{... | collective-permute-start | bytes 1179656 | tf_op jit(solution)/shard_map/ppermute | solution.py:576
  34.7 0.8 %add_convert_fusion.1 = bf16[64,3072]{1,0:T(8,128)(2,1)} fusion(bf16[64,3072]{1,0:T(8,128)(2,1)S(1)} %collective-permute-done.3, bf16[64,3072]{1,0:T(8,128)(2,1)S(1)} %collective-permute-done.2), kind=kLoop, calls=%fused_computation.1 | loop fusion | flops 786432 | bytes 1179648 | tf_op jit(solution)/shard_map/convert_element_type | solution.py:625
  35.6 0.2 collective-permute-start.6
  35.8 7.6 %collective-permute-done.6 = f32[1,1536]{1,0:T(1,128)S(1)} collective-permute-done((f32[1,1536]{1,0:T(1,128)S(1)}, f32[1,1536]{1,0:T(1,128)S(1)}, u32[]{:S(2)}, u32[]{:S(2)}) %collective-permute-start.6) | collective-permute-done | bytes 6176 | tf_op jit(solution)/shard_map/ppermute | solution.py:576
  43.4 0.6 %add.11 = f32[1,1536]{1,0:T(1,128)} add(f32[1,1536]{1,0:T(1,128)S(1)} %get-tuple-element.37, f32[1,1536]{1,0:T(1,128)S(1)} %collective-permute-done.6) | non-fusion elementwise | flops 1536 | bytes 18432 | tf_op jit(solution)/shard_map/add | solution.py:629
  44.0 0.0 collective-permute-done.4
  44.0 1.1 %collective-permute-done.5 = bf16[64,3072]{1,0:T(8,128)(2,1)S(1)} collective-permute-done((bf16[64,3072]{1,0:T(8,128)(2,1)S(1)}, bf16[64,3072]{1,0:T(8,128)(2,1)S(1)}, u32[]{:S(2)}, u32[]{:S(2)}) %collective-permute-start.5) | collective-permute-done | bytes 393248 | tf_op jit(solution)/shard_map/ppermute | solution.py:576
  45.1 0.8 %fusion = bf16[1,64,3072]{2,1,0:T(8,128)(2,1)} fusion(bf16[64,3072]{1,0:T(8,128)(2,1)S(1)} %collective-permute-done.5, bf16[64,3072]{1,0:T(8,128)(2,1)S(1)} %collective-permute-done.4), kind=kLoop, calls=%fused_computation.2 | loop fusion | flops 786432 | bytes 1179648 | tf_op jit(solution)/shard_map/broadcast_in_dim | solution.py:629
  (2 shorter events, 0.0 us)
Async XLA Ops:
  0.6 11.2 %collective-permute-start.1 = (bf16[64,3072]{1,0:T(8,128)(2,1)}, bf16[64,3072]{1,0:T(8,128)(2,1)S(1)}, u32[]{:S(2)}, u32[]{:S(2)}) collective-permute-start(bf16[64,3072]{1,0:T(8,128)(2,1)} %bitcast.9), channel_id=1, source_target_pairs={{0,16},{4,20},{8,24},{12,28},{16,0},{20,4},{24,8},{28,12},{1,17},{... | collective-permute-start | bytes 1179656 | tf_op jit(solution)/shard_map/ppermute | solution.py:576
  2.7 7.2 %copy-start = (bf16[1,64,3072]{2,1,0:T(8,128)(2,1)S(1)}, bf16[1,64,3072]{2,1,0:T(8,128)(2,1)}, u32[]{:S(2)}) copy-start(bf16[1,64,3072]{2,1,0:T(8,128)(2,1)} %param.10) | copy-start | bytes 1179652
  2.7 9.1 %copy-start.1 = (bf16[1,64,3072]{2,1,0:T(8,128)(2,1)S(1)}, bf16[1,64,3072]{2,1,0:T(8,128)(2,1)}, u32[]{:S(2)}) copy-start(bf16[1,64,3072]{2,1,0:T(8,128)(2,1)} %param.9) | copy-start | bytes 1179652
  2.7 9.1 %copy-start.2 = (f32[1,3072]{1,0:T(1,128)S(1)}, f32[1,3072]{1,0:T(1,128)}, u32[]{:S(2)}) copy-start(f32[1,3072]{1,0:T(1,128)} %gate_ref.3) | copy-start | bytes 36868
  2.7 9.1 %copy-start.3 = (f32[1,128]{1,0:T(1,128)S(1)}, f32[1,128]{1,0:T(1,128)}, u32[]{:S(2)}) copy-start(f32[1,128]{1,0:T(1,128)} %query_gain_ref.3) | copy-start | bytes 1540
  2.8 9.1 %copy-start.4 = (f32[1,128]{1,0:T(1,128)S(1)}, f32[1,128]{1,0:T(1,128)}, u32[]{:S(2)}) copy-start(f32[1,128]{1,0:T(1,128)} %key_gain_ref.3) | copy-start | bytes 1540
  2.8 9.1 %copy-start.5 = (s32[2,27]{1,0:T(2,128)S(1)}, s32[2,27]{1,0:T(2,128)}, u32[]{:S(2)}) copy-start(s32[2,27]{1,0:T(2,128)} %neighbours_ref.1) | copy-start | bytes 652
  2.8 9.1 %copy-start.6 = (s32[2]{0:T(128)S(1)}, s32[2]{0:T(128)}, u32[]{:S(2)}) copy-start(s32[2]{0:T(128)} %tile_slot_ref.1) | copy-start | bytes 28
  10.0 13.0 %collective-permute-start = (bf16[64,3072]{1,0:T(8,128)(2,1)S(1)}, bf16[64,3072]{1,0:T(8,128)(2,1)S(1)}, u32[]{:S(2)}, u32[]{:S(2)}) collective-permute-start(bf16[64,3072]{1,0:T(8,128)(2,1)S(1)} %bitcast.7), channel_id=1, source_target_pairs={{0,16},{4,20},{8,24},{12,28},{16,0},{20,4},{24,8},{28,12},{1,17},{... | collective-permute-start | bytes 1179656 | tf_op jit(solution)/shard_map/ppermute | solution.py:576
  18.3 14.3 %collective-permute-start.2 = (bf16[64,3072]{1,0:T(8,128)(2,1)S(1)}, bf16[64,3072]{1,0:T(8,128)(2,1)S(1)}, u32[]{:S(2)}, u32[]{:S(2)}) collective-permute-start(bf16[64,3072]{1,0:T(8,128)(2,1)S(1)} %get-tuple-element.29), channel_id=1, source_target_pairs={{0,4},{4,8},{8,12},{12,0},{16,20},{20,24},{24,28},{28,16},{1,5},{5... | collective-permute-start | bytes 1179656 | tf_op jit(solution)/shard_map/ppermute | solution.py:576
  21.1 11.6 %collective-permute-start.3 = (bf16[64,3072]{1,0:T(8,128)(2,1)S(1)}, bf16[64,3072]{1,0:T(8,128)(2,1)S(1)}, u32[]{:S(2)}, u32[]{:S(2)}) collective-permute-start(bf16[64,3072]{1,0:T(8,128)(2,1)S(1)} %get-tuple-element.30), channel_id=1, source_target_pairs={{0,20},{4,24},{8,28},{12,16},{16,4},{20,8},{24,12},{28,0},{1,21},{... | collective-permute-start | bytes 1179656 | tf_op jit(solution)/shard_map/ppermute | solution.py:576
  32.7 11.3 %collective-permute-start.4 = (bf16[64,3072]{1,0:T(8,128)(2,1)S(1)}, bf16[64,3072]{1,0:T(8,128)(2,1)S(1)}, u32[]{:S(2)}, u32[]{:S(2)}) collective-permute-start(bf16[64,3072]{1,0:T(8,128)(2,1)S(1)} %get-tuple-element.35), channel_id=1, source_target_pairs={{0,12},{4,0},{8,4},{12,8},{16,28},{20,16},{24,20},{28,24},{1,13},{... | collective-permute-start | bytes 1179656 | tf_op jit(solution)/shard_map/ppermute | solution.py:576
  33.3 11.8 %collective-permute-start.5 = (bf16[64,3072]{1,0:T(8,128)(2,1)S(1)}, bf16[64,3072]{1,0:T(8,128)(2,1)S(1)}, u32[]{:S(2)}, u32[]{:S(2)}) collective-permute-start(bf16[64,3072]{1,0:T(8,128)(2,1)S(1)} %get-tuple-element.36), channel_id=1, source_target_pairs={{0,28},{4,16},{8,20},{12,24},{16,12},{20,0},{24,4},{28,8},{1,29},{... | collective-permute-start | bytes 1179656 | tf_op jit(solution)/shard_map/ppermute | solution.py:576
  35.6 7.9 %collective-permute-start.6 = (f32[1,1536]{1,0:T(1,128)S(1)}, f32[1,1536]{1,0:T(1,128)S(1)}, u32[]{:S(2)}, u32[]{:S(2)}) collective-permute-start(f32[1,1536]{1,0:T(1,128)S(1)} %get-tuple-element.38), channel_id=1, source_target_pairs={{0,16},{4,20},{8,24},{12,28},{16,0},{20,4},{24,8},{28,12},{1,17},{... | collective-permute-start | bytes 18440 | tf_op jit(solution)/shard_map/ppermute | solution.py:576

commit v10 on v9

--- a/solution.py
+++ b/solution.py
@@ -619,13 +619,13 @@
         key_gain,
         gate_scale,
     )
-    grad_kept, grad_sent, kept, sent = lax.optimization_barrier((grad_kept, grad_sent, kept, sent))
     grad_sent = routed(grad_sent, 1, -1)
     grad_kept = routed(grad_kept, 0, -1)
     segment_output = (kept.astype(F32) + sent.astype(F32)).astype(BF16)
     segment_output, gate_sent = lax.optimization_barrier((segment_output, gate_sent))
     gate_sent = routed(gate_sent, 1, 0)
     input_grad = (grad_kept.astype(F32) + grad_sent.astype(F32)).astype(BF16)
+    input_grad, gate_sent = lax.optimization_barrier((input_grad, gate_sent))
     return (segment_output[None], input_grad[None], gate_kept + gate_sent)
 
 

time: 46.7 us -> 45.9 us (0.983); the launches traced: 45.9 us -> 45.7 us
    convert_element_type x0 -> x1, other arithmetic: none -> 0.85 us  [pair_body(): input_grad = (grad_kept.astype(F32) + grad_sent.astype(F32)).astype(BF16)]
    broadcast_in_dim x1 -> x0, other arithmetic: 0.84 us -> none  [pair_body(): return (segment_output[None], input_grad[None], gate_kept + gate_sent)]
  transfers between devices with their start and end apart: 7 -> 7, of which waited for: 4 -> 3; matrix products, arithmetic and copies ran while one was open for 3% -> 4% of each run, Pallas kernels for 51% -> 51%
where the time goes in v10:
time: 45.9 us; the launch traced here: 45.7 us
  Pallas kernels  23.3 us (51%)
  waiting for transfers between devices  10.6 us (23%)
  starting transfers between devices  8.77 us (19%)
  other arithmetic  2.29 us (5%)
  between operations  0.73 us (2%)
    ppermute x7, waiting for transfers between devices, routed(): return lax.ppermute(block, ('seq', 'pipe'), route)  10.6 us
    pallas_call x1, Pallas kernels, backward(): pl.pallas_call(backward_kernel, out_shape=(jax.ShapeDtypeStruct((1, model...  9.63 us
    ppermute x7, starting transfers between devices, routed(): return lax.ppermute(block, ('seq', 'pipe'), route)  8.77 us
    pallas_call x1, Pallas kernels, regroup(): pl.pallas_call(regroup_kernel, out_shape=pltpu.VMEM(out, weight.dtype), i...  7.17 us
    pallas_call x1, Pallas kernels, forward(): pl.pallas_call(forward_kernel, out_shape=(jax.ShapeDtypeStruct((groups, t...  6.46 us
  transfers between devices with their start and end apart: 7, of which 3 were waited for; matrix products, arithmetic and copies ran while one was open for 4% of the time, Pallas kernels for 51%

profile of v10, /device:TPU:1, one launch (start us, length us, event | category | flops | bytes accessed | tf_op | source)
XLA Modules:
  0.0 45.7 jit_solution(5223154332153343954)
XLA Ops:
  0.6 2.1 %collective-permute-start = (bf16[64,3072]{1,0:T(8,128)(2,1)}, bf16[64,3072]{1,0:T(8,128)(2,1)S(1)}, u32[]{:S(2)}, u32[]{:S(2)}) collective-permute-start(bf16[64,3072]{1,0:T(8,128)(2,1)} %bitcast.8), channel_id=1, source_target_pairs={{0,16},{4,20},{8,24},{12,28},{16,0},{20,4},{24,8},{28,12},{1,17},{... | collective-permute-start | bytes 1179656 | tf_op jit(solution)/shard_map/ppermute | solution.py:576
  2.7 0.0 copy-start
  2.7 0.0 copy-start.1
  2.8 0.0 copy-start.4
  2.8 0.0 copy-start.5
  2.8 0.0 copy-start.6
  2.8 7.2 %regroup.1.weight_ref = bf16[2,3072,1536]{2,1,0:T(8,128)(2,1)S(1)} custom-call(bf16[3072,8,384]{2,1,0:T(8,128)(2,1)} %bitcast.10), custom_call_target="tpu_custom_call" | custom-call | bytes 37748736 | tf_op jit(solution)/shard_map/regroup/pallas_call | solution.py:281
  10.0 0.0 copy-done
  10.0 0.1 collective-permute-start.3
  10.1 1.7 %collective-permute-done.other_ref = bf16[64,3072]{1,0:T(8,128)(2,1)S(1)} collective-permute-done((bf16[64,3072]{1,0:T(8,128)(2,1)}, bf16[64,3072]{1,0:T(8,128)(2,1)S(1)}, u32[]{:S(2)}, u32[]{:S(2)}) %collective-permute-start) | collective-permute-done | bytes 393248 | tf_op jit(solution)/shard_map/ppermute | solution.py:576
  11.8 0.0 copy-done.1
  11.8 0.0 copy-done.2
  11.8 0.0 copy-done.3
  11.8 0.0 copy-done.4
  11.8 0.0 copy-done.5
  11.8 0.0 copy-done.6
  11.8 6.5 %attention_forward.1 = (f32[2,128,1536]{2,1,0:T(8,128)S(1)}, bf16[8,128,128]{2,1,0:T(8,128)(2,1)S(1)}, f32[128,3072]{1,0:T(8,128)S(1)}, bf16[64,3072]{1,0:T(8,12...) custom-call(s32[2,27]{1,0:T(2,128)S(1)} %copy-done.5, s32[2]{0:T(128)S(1)} %copy-done.6, ...), custom_call_target="tpu_custom_call" | custom-call | flops 3221225472 | bytes 25165824 | tf_op jit(solution)/shard_map/attention_forward/pallas_call | solution.py:418
  18.3 4.6 %collective-permute-start.2 = (bf16[64,3072]{1,0:T(8,128)(2,1)S(1)}, bf16[64,3072]{1,0:T(8,128)(2,1)S(1)}, u32[]{:S(2)}, u32[]{:S(2)}) collective-permute-start(bf16[64,3072]{1,0:T(8,128)(2,1)S(1)} %get-tuple-element.21), channel_id=1, source_target_pairs={{0,20},{4,24},{8,28},{12,16},{16,4},{20,8},{24,12},{28,0},{1,21},{... | collective-permute-start | bytes 1179656 | tf_op jit(solution)/shard_map/ppermute | solution.py:576
  22.9 0.0 collective-permute-start.1
  22.9 0.0 collective-permute-done.3.other_ref
  22.9 9.6 %attention_backward.1 = (f32[1,1536]{1,0:T(1,128)S(1)}, f32[1,1536]{1,0:T(1,128)S(1)}, bf16[64,3072]{1,0:T(8,128)(2,1)S(1)}, bf16[64,3072]{1,0:T(8,128)(2,1)S(1)}) custom-call(bf16[64,3072]{1,0:T(8,128)(2,1)S(1)} %bitcast.7, bf16[64,3072]{1,0:T(8,128)(2,1)S(1)} %collective-permute-done.3.other_ref, bf16[1024,3072]{1,0:T(8,128)(2,1)S(1)} %get-tuple-element.23.out_weight_ref, ...), custom_call_target="tpu_custom_call" | custom-call | flops 3221225472 | bytes 25165824 | tf_op jit(solution)/shard_map/attention_backward/pallas_call | solution.py:543
  32.5 0.1 collective-permute-start.5
  32.6 0.8 %collective-permute-start.4 = (bf16[64,3072]{1,0:T(8,128)(2,1)S(1)}, bf16[64,3072]{1,0:T(8,128)(2,1)S(1)}, u32[]{:S(2)}, u32[]{:S(2)}) collective-permute-start(bf16[64,3072]{1,0:T(8,128)(2,1)S(1)} %get-tuple-element.29), channel_id=1, source_target_pairs={{0,12},{4,0},{8,4},{12,8},{16,28},{20,16},{24,20},{28,24},{1,13},{... | collective-permute-start | bytes 1179656 | tf_op jit(solution)/shard_map/ppermute | solution.py:576
  33.4 0.0 collective-permute-done.2
  33.4 0.0 collective-permute-done.1
  33.4 0.8 %add_convert_fusion.1 = bf16[64,3072]{1,0:T(8,128)(2,1)} fusion(bf16[64,3072]{1,0:T(8,128)(2,1)S(1)} %collective-permute-done.2, bf16[64,3072]{1,0:T(8,128)(2,1)S(1)} %collective-permute-done.1), kind=kLoop, calls=%fused_computation.1 | loop fusion | flops 786432 | bytes 1179648 | tf_op jit(solution)/shard_map/convert_element_type | solution.py:624
  34.3 1.1 %collective-permute-start.6 = (f32[1,1536]{1,0:T(1,128)S(1)}, f32[1,1536]{1,0:T(1,128)S(1)}, u32[]{:S(2)}, u32[]{:S(2)}) collective-permute-start(f32[1,1536]{1,0:T(1,128)S(1)} %get-tuple-element.31), channel_id=1, source_target_pairs={{0,16},{4,20},{8,24},{12,28},{16,0},{20,4},{24,8},{28,12},{1,17},{... | collective-permute-start | bytes 18440 | tf_op jit(solution)/shard_map/ppermute | solution.py:576
  35.4 8.7 %collective-permute-done.5 = bf16[64,3072]{1,0:T(8,128)(2,1)S(1)} collective-permute-done((bf16[64,3072]{1,0:T(8,128)(2,1)S(1)}, bf16[64,3072]{1,0:T(8,128)(2,1)S(1)}, u32[]{:S(2)}, u32[]{:S(2)}) %collective-permute-start.5) | collective-permute-done | bytes 393248 | tf_op jit(solution)/shard_map/ppermute | solution.py:576
  44.1 0.2 collective-permute-done.4
  44.3 0.8 %add_convert_fusion = bf16[64,3072]{1,0:T(8,128)(2,1)} fusion(bf16[64,3072]{1,0:T(8,128)(2,1)S(1)} %collective-permute-done.5, bf16[64,3072]{1,0:T(8,128)(2,1)S(1)} %collective-permute-done.4), kind=kLoop, calls=%fused_computation | loop fusion | flops 786432 | bytes 1179648 | tf_op jit(solution)/shard_map/convert_element_type | solution.py:627
  45.1 0.0 collective-permute-done.6
  45.1 0.6 %add.11 = f32[1,1536]{1,0:T(1,128)} add(f32[1,1536]{1,0:T(1,128)S(1)} %get-tuple-element.33, f32[1,1536]{1,0:T(1,128)S(1)} %collective-permute-done.6) | non-fusion elementwise | flops 1536 | bytes 18432 | tf_op jit(solution)/shard_map/add | solution.py:629
  (2 shorter events, 0.0 us)
Async XLA Ops:
  0.6 11.2 %collective-permute-start = (bf16[64,3072]{1,0:T(8,128)(2,1)}, bf16[64,3072]{1,0:T(8,128)(2,1)S(1)}, u32[]{:S(2)}, u32[]{:S(2)}) collective-permute-start(bf16[64,3072]{1,0:T(8,128)(2,1)} %bitcast.8), channel_id=1, source_target_pairs={{0,16},{4,20},{8,24},{12,28},{16,0},{20,4},{24,8},{28,12},{1,17},{... | collective-permute-start | bytes 1179656 | tf_op jit(solution)/shard_map/ppermute | solution.py:576
  2.7 7.2 %copy-start = (bf16[1,64,3072]{2,1,0:T(8,128)(2,1)S(1)}, bf16[1,64,3072]{2,1,0:T(8,128)(2,1)}, u32[]{:S(2)}) copy-start(bf16[1,64,3072]{2,1,0:T(8,128)(2,1)} %param.10) | copy-start | bytes 1179652
  2.7 9.1 %copy-start.1 = (bf16[1,64,3072]{2,1,0:T(8,128)(2,1)S(1)}, bf16[1,64,3072]{2,1,0:T(8,128)(2,1)}, u32[]{:S(2)}) copy-start(bf16[1,64,3072]{2,1,0:T(8,128)(2,1)} %param.9) | copy-start | bytes 1179652
  2.7 9.1 %copy-start.2 = (f32[1,3072]{1,0:T(1,128)S(1)}, f32[1,3072]{1,0:T(1,128)}, u32[]{:S(2)}) copy-start(f32[1,3072]{1,0:T(1,128)} %gate_ref.3) | copy-start | bytes 36868
  2.7 9.1 %copy-start.3 = (f32[1,128]{1,0:T(1,128)S(1)}, f32[1,128]{1,0:T(1,128)}, u32[]{:S(2)}) copy-start(f32[1,128]{1,0:T(1,128)} %query_gain_ref.3) | copy-start | bytes 1540
  2.8 9.1 %copy-start.4 = (f32[1,128]{1,0:T(1,128)S(1)}, f32[1,128]{1,0:T(1,128)}, u32[]{:S(2)}) copy-start(f32[1,128]{1,0:T(1,128)} %key_gain_ref.3) | copy-start | bytes 1540
  2.8 9.1 %copy-start.5 = (s32[2,27]{1,0:T(2,128)S(1)}, s32[2,27]{1,0:T(2,128)}, u32[]{:S(2)}) copy-start(s32[2,27]{1,0:T(2,128)} %neighbours_ref.1) | copy-start | bytes 652
  2.8 9.1 %copy-start.6 = (s32[2]{0:T(128)S(1)}, s32[2]{0:T(128)}, u32[]{:S(2)}) copy-start(s32[2]{0:T(128)} %tile_slot_ref.1) | copy-start | bytes 28
  10.0 12.9 %collective-permute-start.3 = (bf16[64,3072]{1,0:T(8,128)(2,1)S(1)}, bf16[64,3072]{1,0:T(8,128)(2,1)S(1)}, u32[]{:S(2)}, u32[]{:S(2)}) collective-permute-start(bf16[64,3072]{1,0:T(8,128)(2,1)S(1)} %bitcast.6), channel_id=1, source_target_pairs={{0,16},{4,20},{8,24},{12,28},{16,0},{20,4},{24,8},{28,12},{1,17},{... | collective-permute-start | bytes 1179656 | tf_op jit(solution)/shard_map/ppermute | solution.py:576
  18.3 15.1 %collective-permute-start.2 = (bf16[64,3072]{1,0:T(8,128)(2,1)S(1)}, bf16[64,3072]{1,0:T(8,128)(2,1)S(1)}, u32[]{:S(2)}, u32[]{:S(2)}) collective-permute-start(bf16[64,3072]{1,0:T(8,128)(2,1)S(1)} %get-tuple-element.21), channel_id=1, source_target_pairs={{0,20},{4,24},{8,28},{12,16},{16,4},{20,8},{24,12},{28,0},{1,21},{... | collective-permute-start | bytes 1179656 | tf_op jit(solution)/shard_map/ppermute | solution.py:576
  22.9 10.5 %collective-permute-start.1 = (bf16[64,3072]{1,0:T(8,128)(2,1)S(1)}, bf16[64,3072]{1,0:T(8,128)(2,1)S(1)}, u32[]{:S(2)}, u32[]{:S(2)}) collective-permute-start(bf16[64,3072]{1,0:T(8,128)(2,1)S(1)} %get-tuple-element.20), channel_id=1, source_target_pairs={{0,4},{4,8},{8,12},{12,0},{16,20},{20,24},{24,28},{28,16},{1,5},{5... | collective-permute-start | bytes 1179656 | tf_op jit(solution)/shard_map/ppermute | solution.py:576
  32.5 11.5 %collective-permute-start.5 = (bf16[64,3072]{1,0:T(8,128)(2,1)S(1)}, bf16[64,3072]{1,0:T(8,128)(2,1)S(1)}, u32[]{:S(2)}, u32[]{:S(2)}) collective-permute-start(bf16[64,3072]{1,0:T(8,128)(2,1)S(1)} %get-tuple-element.30), channel_id=1, source_target_pairs={{0,28},{4,16},{8,20},{12,24},{16,12},{20,0},{24,4},{28,8},{1,29},{... | collective-permute-start | bytes 1179656 | tf_op jit(solution)/shard_map/ppermute | solution.py:576
  32.6 11.6 %collective-permute-start.4 = (bf16[64,3072]{1,0:T(8,128)(2,1)S(1)}, bf16[64,3072]{1,0:T(8,128)(2,1)S(1)}, u32[]{:S(2)}, u32[]{:S(2)}) collective-permute-start(bf16[64,3072]{1,0:T(8,128)(2,1)S(1)} %get-tuple-element.29), channel_id=1, source_target_pairs={{0,12},{4,0},{8,4},{12,8},{16,28},{20,16},{24,20},{28,24},{1,13},{... | collective-permute-start | bytes 1179656 | tf_op jit(solution)/shard_map/ppermute | solution.py:576
  34.3 10.9 %collective-permute-start.6 = (f32[1,1536]{1,0:T(1,128)S(1)}, f32[1,1536]{1,0:T(1,128)S(1)}, u32[]{:S(2)}, u32[]{:S(2)}) collective-permute-start(f32[1,1536]{1,0:T(1,128)S(1)} %get-tuple-element.31), channel_id=1, source_target_pairs={{0,16},{4,20},{8,24},{12,28},{16,0},{20,4},{24,8},{28,12},{1,17},{... | collective-permute-start | bytes 18440 | tf_op jit(solution)/shard_map/ppermute | solution.py:576

commit v11 on v10

--- a/solution.py
+++ b/solution.py
@@ -441,19 +441,6 @@
     )(neighbours, tile_slot, own, other, weight, out_weight, query_gain, key_gain, gate)
 
 
-def input_grad(grad_ref, weight_ref, own_ref, kept_ref, sent_ref):
-    local, model = own_ref.shape
-    block = 512
-    for start in range(0, model, block):
-        part = slice(start, start + block)
-        total = dot_nt(weight_ref[0, part, :], grad_ref[0])
-        for group in range(1, grad_ref.shape[0]):
-            total += dot_nt(weight_ref[group, part, :], grad_ref[group])
-        total = total.T
-        kept_ref[:, part] = (own_ref[:, part].astype(F32) + total[:local]).astype(BF16)
-        sent_ref[:, part] = total[local:].astype(BF16)
-
-
 def backward_kernel(
     own_ref,
     other_ref,
@@ -473,23 +460,17 @@
     scaled_ref,
     attended_grad_ref,
     gate_grad_ref,
+    partial_ref,
 ):
     local = own_ref.shape[0]
     width = query_gain_ref.shape[1]
     groups = grad_ref.shape[0]
     rows = GROUP * width
 
+    model = own_ref.shape[1]
     gate = gate_ref[...]
-    own, other = own_ref[...].astype(F32), other_ref[...].astype(F32)
-    scaled_ref[:local, :] = (own * gate).astype(BF16)
-    scaled_ref[local:, :] = (other * gate).astype(BF16)
-    gate_grad_ref[...] = jnp.sum(
-        own * attention_ref[:local, :] + other * attention_ref[local:, :], axis=0, keepdims=True
-    )
-    half = gate_kept_ref.shape[1]
-    mine = lax.axis_index("seq")
-    gate_kept_ref[...] = gate_grad_ref[:, pl.ds(pl.multiple_of(mine * half, half), half)]
-    gate_sent_ref[...] = gate_grad_ref[:, pl.ds(pl.multiple_of((1 - mine) * half, half), half)]
+    scaled_ref[:local, :] = (own_ref[...].astype(F32) * gate).astype(BF16)
+    scaled_ref[local:, :] = (other_ref[...].astype(F32) * gate).astype(BF16)
 
     def attended_grad(group):
         part = slice(group * rows, (group + 1) * rows)
@@ -522,13 +503,39 @@
         ).astype(BF16)
         grad_ref[group, :, key_part] = ((key_scaled - key_unit * key_mean) * key_inverse).astype(BF16)
 
+    def input_grad(group, part):
+        return dot_nt(grad_ref[group], weight_ref[group, part, :])
+
+    block = 512
+    blocks = [slice(start, start + block) for start in range(0, model, block)]
     attended_grad(0)
     for group in range(groups):
         if group + 1 < groups:
             attended_grad(group + 1)
         for head in range(GROUP):
             attend_backward(group, head)
-    input_grad(grad_ref, weight_ref, own_ref, kept_ref, sent_ref)
+            if group > 0:
+                for part in blocks[head::GROUP]:
+                    product = input_grad(group - 1, part)
+                    if group > 1:
+                        product += partial_ref[:, part]
+                    partial_ref[:, part] = product
+    for part in blocks:
+        total = input_grad(groups - 1, part)
+        if groups > 1:
+            total += partial_ref[:, part]
+        own, other = own_ref[:, part].astype(F32), other_ref[:, part].astype(F32)
+        kept_ref[:, part] = (own + total[:local]).astype(BF16)
+        sent_ref[:, part] = total[local:].astype(BF16)
+        gate_grad_ref[:, part] = jnp.sum(
+            own * attention_ref[:local, part] + other * attention_ref[local:, part],
+            axis=0,
+            keepdims=True,
+        )
+    half = gate_kept_ref.shape[1]
+    mine = lax.axis_index("seq")
+    gate_kept_ref[...] = gate_grad_ref[:, pl.ds(pl.multiple_of(mine * half, half), half)]
+    gate_sent_ref[...] = gate_grad_ref[:, pl.ds(pl.multiple_of((1 - mine) * half, half), half)]
 
 
 def backward(
@@ -555,6 +562,7 @@
             pltpu.VMEM((tokens, model), BF16),
             pltpu.VMEM((groups, tokens, GROUP * head_dim), BF16),
             pltpu.VMEM((1, model), F32),
+            pltpu.VMEM((tokens, model), F32),
         ],
         compiler_params=params(12),
         cost_estimate=pl.CostEstimate(
@@ -564,6 +572,26 @@
         ),
         name="attention_backward",
     )(own, other, out_weight, weight, projected, probs, attention, query_gain, key_gain, gate)
+
+
+def sums_kernel(kept_ref, sent_ref, gate_kept_ref, gate_sent_ref, grad_ref, gate_ref):
+    grad_ref[...] = (kept_ref[...].astype(F32) + sent_ref[...].astype(F32)).astype(BF16)
+    gate_ref[...] = gate_kept_ref[...] + gate_sent_ref[...]
+
+
+def sums(kept, sent, gate_kept, gate_sent):
+    vmem = pl.BlockSpec(memory_space=pltpu.VMEM)
+    return pl.pallas_call(
+        sums_kernel,
+        out_shape=(
+            jax.ShapeDtypeStruct(kept.shape, BF16),
+            jax.ShapeDtypeStruct(gate_kept.shape, F32),
+        ),
+        in_specs=[vmem] * 4,
+        out_specs=(vmem, vmem),
+        compiler_params=params(8),
+        name="sums",
+    )(kept, sent, gate_kept, gate_sent)
 
 
 def routed(block, seq_step, pipe_step):
@@ -624,9 +652,8 @@
     segment_output = (kept.astype(F32) + sent.astype(F32)).astype(BF16)
     segment_output, gate_sent = lax.optimization_barrier((segment_output, gate_sent))
     gate_sent = routed(gate_sent, 1, 0)
-    input_grad = (grad_kept.astype(F32) + grad_sent.astype(F32)).astype(BF16)
-    input_grad, gate_sent = lax.optimization_barrier((input_grad, gate_sent))
-    return (segment_output[None], input_grad[None], gate_kept + gate_sent)
+    input_grad, gate_grad = sums(grad_sent, grad_kept, gate_kept, gate_sent)
+    return (segment_output[None], input_grad[None], gate_grad)
 
 
 def solution(mesh):

time: 45.9 us -> 45.8 us (level)
  other arithmetic: 2.29 us -> 0.84 us
  Pallas kernels: 23.3 us -> 24.3 us
    convert_element_type x1 -> x0, other arithmetic: 0.85 us -> none  [pair_body(): input_grad = (grad_kept.astype(F32) + grad_sent.astype(F32)).astype(BF16)]
    pallas_call x0 -> x1, Pallas kernels: none -> 0.84 us  [sums(): pl.pallas_call(sums_kernel, out_shape=(jax.ShapeDtypeStruct(kept.shape, B...]
    add x1 -> x0, other arithmetic: 0.6 us -> none  [pair_body(): return (segment_output[None], input_grad[None], gate_kept + gate_sent)]
  transfers between devices with their start and end apart: 7 -> 7, of which waited for: 3 -> 3; matrix products, arithmetic and copies ran while one was open for 4% -> 2% of each run, Pallas kernels for 51% -> 52%
where the time goes in v11:
time: 45.8 us; the launch traced here: 45.3 us
  Pallas kernels  24.3 us (53%)
  waiting for transfers between devices  10.6 us (23%)
  starting transfers between devices  8.77 us (19%)
  other arithmetic  0.84 us (2%)
  between operations  0.73 us (2%)
    ppermute x7, waiting for transfers between devices, routed(): return lax.ppermute(block, ('seq', 'pipe'), route)  10.6 us
    pallas_call x1, Pallas kernels, backward(): pl.pallas_call(backward_kernel, out_shape=(jax.ShapeDtypeStruct((1, model...  9.8 us
    ppermute x7, starting transfers between devices, routed(): return lax.ppermute(block, ('seq', 'pipe'), route)  8.77 us
    pallas_call x1, Pallas kernels, regroup(): pl.pallas_call(regroup_kernel, out_shape=pltpu.VMEM(out, weight.dtype), i...  7.17 us
    pallas_call x1, Pallas kernels, forward(): pl.pallas_call(forward_kernel, out_shape=(jax.ShapeDtypeStruct((groups, t...  6.46 us
  transfers between devices with their start and end apart: 7, of which 3 were waited for; matrix products, arithmetic and copies ran while one was open for 2% of the time, Pallas kernels for 52%

profile of v11, /device:TPU:1, one launch (start us, length us, event | category | flops | bytes accessed | tf_op | source)
XLA Modules:
  0.0 45.3 jit_solution(16034872974406700762)
XLA Ops:
  0.6 2.1 %collective-permute-start = (bf16[64,3072]{1,0:T(8,128)(2,1)}, bf16[64,3072]{1,0:T(8,128)(2,1)S(1)}, u32[]{:S(2)}, u32[]{:S(2)}) collective-permute-start(bf16[64,3072]{1,0:T(8,128)(2,1)} %bitcast.8), channel_id=1, source_target_pairs={{0,16},{4,20},{8,24},{12,28},{16,0},{20,4},{24,8},{28,12},{1,17},{... | collective-permute-start | bytes 1179656 | tf_op jit(solution)/shard_map/ppermute | solution.py:604
  2.7 0.0 copy-start
  2.7 0.0 copy-start.1
  2.7 0.0 copy-start.2
  2.8 0.0 copy-start.4
  2.8 0.0 copy-start.5
  2.8 0.0 copy-start.6
  2.8 7.2 %regroup.1.weight_ref = bf16[2,3072,1536]{2,1,0:T(8,128)(2,1)S(1)} custom-call(bf16[3072,8,384]{2,1,0:T(8,128)(2,1)} %bitcast.10), custom_call_target="tpu_custom_call" | custom-call | bytes 37748736 | tf_op jit(solution)/shard_map/regroup/pallas_call | solution.py:281
  10.0 0.0 copy-done
  10.0 0.1 collective-permute-start.3
  10.1 1.7 %collective-permute-done.other_ref = bf16[64,3072]{1,0:T(8,128)(2,1)S(1)} collective-permute-done((bf16[64,3072]{1,0:T(8,128)(2,1)}, bf16[64,3072]{1,0:T(8,128)(2,1)S(1)}, u32[]{:S(2)}, u32[]{:S(2)}) %collective-permute-start) | collective-permute-done | bytes 393248 | tf_op jit(solution)/shard_map/ppermute | solution.py:604
  11.8 0.0 copy-done.1
  11.8 0.0 copy-done.2
  11.8 0.0 copy-done.3
  11.8 0.0 copy-done.4
  11.8 0.0 copy-done.5
  11.8 0.0 copy-done.6
  11.8 6.5 %attention_forward.1 = (f32[2,128,1536]{2,1,0:T(8,128)S(1)}, bf16[8,128,128]{2,1,0:T(8,128)(2,1)S(1)}, f32[128,3072]{1,0:T(8,128)S(1)}, bf16[64,3072]{1,0:T(8,12...) custom-call(s32[2,27]{1,0:T(2,128)S(1)} %copy-done.5, s32[2]{0:T(128)S(1)} %copy-done.6, ...), custom_call_target="tpu_custom_call" | custom-call | flops 3221225472 | bytes 25165824 | tf_op jit(solution)/shard_map/attention_forward/pallas_call | solution.py:418
  18.3 4.6 %collective-permute-start.2 = (bf16[64,3072]{1,0:T(8,128)(2,1)S(1)}, bf16[64,3072]{1,0:T(8,128)(2,1)S(1)}, u32[]{:S(2)}, u32[]{:S(2)}) collective-permute-start(bf16[64,3072]{1,0:T(8,128)(2,1)S(1)} %get-tuple-element.21), channel_id=1, source_target_pairs={{0,20},{4,24},{8,28},{12,16},{16,4},{20,8},{24,12},{28,0},{1,21},{... | collective-permute-start | bytes 1179656 | tf_op jit(solution)/shard_map/ppermute | solution.py:604
  22.9 0.0 collective-permute-start.1
  22.9 0.0 collective-permute-done.3.other_ref
  22.9 9.8 %attention_backward.1 = (f32[1,1536]{1,0:T(1,128)S(1)}, f32[1,1536]{1,0:T(1,128)S(1)}, bf16[64,3072]{1,0:T(8,128)(2,1)S(1)}, bf16[64,3072]{1,0:T(8,128)(2,1)S(1)}) custom-call(bf16[64,3072]{1,0:T(8,128)(2,1)S(1)} %bitcast.7, bf16[64,3072]{1,0:T(8,128)(2,1)S(1)} %collective-permute-done.3.other_ref, bf16[1024,3072]{1,0:T(8,128)(2,1)S(1)} %get-tuple-element.23.out_weight_ref, ...), custom_call_target="tpu_custom_call" | custom-call | flops 3221225472 | bytes 25165824 | tf_op jit(solution)/shard_map/attention_backward/pallas_call | solution.py:550
  32.7 0.1 collective-permute-start.4
  32.8 0.8 %collective-permute-start.5 = (bf16[64,3072]{1,0:T(8,128)(2,1)S(1)}, bf16[64,3072]{1,0:T(8,128)(2,1)S(1)}, u32[]{:S(2)}, u32[]{:S(2)}) collective-permute-start(bf16[64,3072]{1,0:T(8,128)(2,1)S(1)} %get-tuple-element.30), channel_id=1, source_target_pairs={{0,12},{4,0},{8,4},{12,8},{16,28},{20,16},{24,20},{28,24},{1,13},{... | collective-permute-start | bytes 1179656 | tf_op jit(solution)/shard_map/ppermute | solution.py:604
  33.6 0.0 collective-permute-done.2
  33.6 0.0 collective-permute-done.1
  33.6 0.8 %add_convert_fusion = bf16[64,3072]{1,0:T(8,128)(2,1)} fusion(bf16[64,3072]{1,0:T(8,128)(2,1)S(1)} %collective-permute-done.2, bf16[64,3072]{1,0:T(8,128)(2,1)S(1)} %collective-permute-done.1), kind=kLoop, calls=%fused_computation | loop fusion | flops 786432 | bytes 1179648 | tf_op jit(solution)/shard_map/convert_element_type | solution.py:652
  34.4 1.1 %collective-permute-start.6 = (f32[1,1536]{1,0:T(1,128)S(1)}, f32[1,1536]{1,0:T(1,128)S(1)}, u32[]{:S(2)}, u32[]{:S(2)}) collective-permute-start(f32[1,1536]{1,0:T(1,128)S(1)} %get-tuple-element.32), channel_id=1, source_target_pairs={{0,16},{4,20},{8,24},{12,28},{16,0},{20,4},{24,8},{28,12},{1,17},{... | collective-permute-start | bytes 18440 | tf_op jit(solution)/shard_map/ppermute | solution.py:604
  35.5 8.7 %collective-permute-done.4.kept_ref = bf16[64,3072]{1,0:T(8,128)(2,1)S(1)} collective-permute-done((bf16[64,3072]{1,0:T(8,128)(2,1)S(1)}, bf16[64,3072]{1,0:T(8,128)(2,1)S(1)}, u32[]{:S(2)}, u32[]{:S(2)}) %collective-permute-start.4) | collective-permute-done | bytes 393248 | tf_op jit(solution)/shard_map/ppermute | solution.py:604
  44.2 0.2 collective-permute-done.5.sent_ref
  44.4 0.0 collective-permute-done.6.gate_sent_ref
  44.4 0.8 %sums.1 = (bf16[64,3072]{1,0:T(8,128)(2,1)}, f32[1,1536]{1,0:T(1,128)}) custom-call(bf16[64,3072]{1,0:T(8,128)(2,1)S(1)} %collective-permute-done.4.kept_ref, bf16[64,3072]{1,0:T(8,128)(2,1)S(1)} %collective-permute-done.5.sent_ref, f32[1,1536]{1,0:T(1,128)S(1)} %get-tuple-element.31.gate_kept_ref, f32[1,1536]{1,0:T(1,128)S(1)} %collective-permute-done.6.gate_sent_ref), custom_call_target="tpu_custom_call" | custom-call | tf_op jit(solution)/shard_map/sums/pallas_call | solution.py:584
  (1 shorter events, 0.0 us)
Async XLA Ops:
  0.6 11.2 %collective-permute-start = (bf16[64,3072]{1,0:T(8,128)(2,1)}, bf16[64,3072]{1,0:T(8,128)(2,1)S(1)}, u32[]{:S(2)}, u32[]{:S(2)}) collective-permute-start(bf16[64,3072]{1,0:T(8,128)(2,1)} %bitcast.8), channel_id=1, source_target_pairs={{0,16},{4,20},{8,24},{12,28},{16,0},{20,4},{24,8},{28,12},{1,17},{... | collective-permute-start | bytes 1179656 | tf_op jit(solution)/shard_map/ppermute | solution.py:604
  2.7 7.2 %copy-start = (bf16[1,64,3072]{2,1,0:T(8,128)(2,1)S(1)}, bf16[1,64,3072]{2,1,0:T(8,128)(2,1)}, u32[]{:S(2)}) copy-start(bf16[1,64,3072]{2,1,0:T(8,128)(2,1)} %param.10) | copy-start | bytes 1179652
  2.7 9.1 %copy-start.1 = (bf16[1,64,3072]{2,1,0:T(8,128)(2,1)S(1)}, bf16[1,64,3072]{2,1,0:T(8,128)(2,1)}, u32[]{:S(2)}) copy-start(bf16[1,64,3072]{2,1,0:T(8,128)(2,1)} %param.9) | copy-start | bytes 1179652
  2.7 9.1 %copy-start.2 = (f32[1,3072]{1,0:T(1,128)S(1)}, f32[1,3072]{1,0:T(1,128)}, u32[]{:S(2)}) copy-start(f32[1,3072]{1,0:T(1,128)} %gate_ref.3) | copy-start | bytes 36868
  2.7 9.1 %copy-start.3 = (f32[1,128]{1,0:T(1,128)S(1)}, f32[1,128]{1,0:T(1,128)}, u32[]{:S(2)}) copy-start(f32[1,128]{1,0:T(1,128)} %query_gain_ref.3) | copy-start | bytes 1540
  2.8 9.1 %copy-start.4 = (f32[1,128]{1,0:T(1,128)S(1)}, f32[1,128]{1,0:T(1,128)}, u32[]{:S(2)}) copy-start(f32[1,128]{1,0:T(1,128)} %key_gain_ref.3) | copy-start | bytes 1540
  2.8 9.1 %copy-start.5 = (s32[2,27]{1,0:T(2,128)S(1)}, s32[2,27]{1,0:T(2,128)}, u32[]{:S(2)}) copy-start(s32[2,27]{1,0:T(2,128)} %neighbours_ref.1) | copy-start | bytes 652
  2.8 9.1 %copy-start.6 = (s32[2]{0:T(128)S(1)}, s32[2]{0:T(128)}, u32[]{:S(2)}) copy-start(s32[2]{0:T(128)} %tile_slot_ref.1) | copy-start | bytes 28
  10.0 12.9 %collective-permute-start.3 = (bf16[64,3072]{1,0:T(8,128)(2,1)S(1)}, bf16[64,3072]{1,0:T(8,128)(2,1)S(1)}, u32[]{:S(2)}, u32[]{:S(2)}) collective-permute-start(bf16[64,3072]{1,0:T(8,128)(2,1)S(1)} %bitcast.6), channel_id=1, source_target_pairs={{0,16},{4,20},{8,24},{12,28},{16,0},{20,4},{24,8},{28,12},{1,17},{... | collective-permute-start | bytes 1179656 | tf_op jit(solution)/shard_map/ppermute | solution.py:604
  18.3 15.3 %collective-permute-start.2 = (bf16[64,3072]{1,0:T(8,128)(2,1)S(1)}, bf16[64,3072]{1,0:T(8,128)(2,1)S(1)}, u32[]{:S(2)}, u32[]{:S(2)}) collective-permute-start(bf16[64,3072]{1,0:T(8,128)(2,1)S(1)} %get-tuple-element.21), channel_id=1, source_target_pairs={{0,20},{4,24},{8,28},{12,16},{16,4},{20,8},{24,12},{28,0},{1,21},{... | collective-permute-start | bytes 1179656 | tf_op jit(solution)/shard_map/ppermute | solution.py:604
  22.9 10.7 %collective-permute-start.1 = (bf16[64,3072]{1,0:T(8,128)(2,1)S(1)}, bf16[64,3072]{1,0:T(8,128)(2,1)S(1)}, u32[]{:S(2)}, u32[]{:S(2)}) collective-permute-start(bf16[64,3072]{1,0:T(8,128)(2,1)S(1)} %get-tuple-element.20), channel_id=1, source_target_pairs={{0,4},{4,8},{8,12},{12,0},{16,20},{20,24},{24,28},{28,16},{1,5},{5... | collective-permute-start | bytes 1179656 | tf_op jit(solution)/shard_map/ppermute | solution.py:604
  32.7 11.5 %collective-permute-start.4 = (bf16[64,3072]{1,0:T(8,128)(2,1)S(1)}, bf16[64,3072]{1,0:T(8,128)(2,1)S(1)}, u32[]{:S(2)}, u32[]{:S(2)}) collective-permute-start(bf16[64,3072]{1,0:T(8,128)(2,1)S(1)} %get-tuple-element.29), channel_id=1, source_target_pairs={{0,28},{4,16},{8,20},{12,24},{16,12},{20,0},{24,4},{28,8},{1,29},{... | collective-permute-start | bytes 1179656 | tf_op jit(solution)/shard_map/ppermute | solution.py:604
  32.8 11.7 %collective-permute-start.5 = (bf16[64,3072]{1,0:T(8,128)(2,1)S(1)}, bf16[64,3072]{1,0:T(8,128)(2,1)S(1)}, u32[]{:S(2)}, u32[]{:S(2)}) collective-permute-start(bf16[64,3072]{1,0:T(8,128)(2,1)S(1)} %get-tuple-element.30), channel_id=1, source_target_pairs={{0,12},{4,0},{8,4},{12,8},{16,28},{20,16},{24,20},{28,24},{1,13},{... | collective-permute-start | bytes 1179656 | tf_op jit(solution)/shard_map/ppermute | solution.py:604
  34.4 10.0 %collective-permute-start.6 = (f32[1,1536]{1,0:T(1,128)S(1)}, f32[1,1536]{1,0:T(1,128)S(1)}, u32[]{:S(2)}, u32[]{:S(2)}) collective-permute-start(f32[1,1536]{1,0:T(1,128)S(1)} %get-tuple-element.32), channel_id=1, source_target_pairs={{0,16},{4,20},{8,24},{12,28},{16,0},{20,4},{24,8},{28,12},{1,17},{... | collective-permute-start | bytes 18440 | tf_op jit(solution)/shard_map/ppermute | solution.py:604

commit v12 on v11

--- a/solution.py
+++ b/solution.py
@@ -441,26 +441,37 @@
     )(neighbours, tile_slot, own, other, weight, out_weight, query_gain, key_gain, gate)
 
 
+SIDE = 256
+
+
+def tiled_products(accumulators, depth, columns, left, right, store):
+    turn = 0
+    for start in range(0, columns, 2 * SIDE):
+        pair = accumulators[2 * turn : 2 * turn + 2]
+        for step in range(depth // SIDE):
+            for unit in range(2):
+                tile = right(start + unit * SIDE, step)
+                pltpu.matmul_push_rhs(tile, step % 2, unit, transpose=True)
+            rows = left(step)
+            for unit in range(2):
+                pltpu.matmul_acc_lhs(pair[unit], rows, load_staged_rhs=step % 2)
+        for unit in range(2):
+            store(slice(start + unit * SIDE, start + (unit + 1) * SIDE), pltpu.matmul_pop(pair[unit]))
+        turn = 1 - turn
+
+
 def backward_kernel(
     own_ref,
     other_ref,
     out_weight_ref,
-    weight_ref,
     projected_ref,
     probs_ref,
-    attention_ref,
     query_gain_ref,
     key_gain_ref,
     gate_ref,
-    gate_kept_ref,
-    gate_sent_ref,
-    kept_ref,
-    sent_ref,
     grad_ref,
     scaled_ref,
     attended_grad_ref,
-    gate_grad_ref,
-    partial_ref,
 ):
     local = own_ref.shape[0]
     width = query_gain_ref.shape[1]
@@ -503,27 +514,64 @@
         ).astype(BF16)
         grad_ref[group, :, key_part] = ((key_scaled - key_unit * key_mean) * key_inverse).astype(BF16)
 
-    def input_grad(group, part):
-        return dot_nt(grad_ref[group], weight_ref[group, part, :])
-
-    block = 512
-    blocks = [slice(start, start + block) for start in range(0, model, block)]
     attended_grad(0)
     for group in range(groups):
         if group + 1 < groups:
             attended_grad(group + 1)
         for head in range(GROUP):
             attend_backward(group, head)
-            if group > 0:
-                for part in blocks[head::GROUP]:
-                    product = input_grad(group - 1, part)
-                    if group > 1:
-                        product += partial_ref[:, part]
-                    partial_ref[:, part] = product
-    for part in blocks:
-        total = input_grad(groups - 1, part)
-        if groups > 1:
-            total += partial_ref[:, part]
+
+
+def backward(own, other, out_weight, projected, probs, query_gain, key_gain, gate):
+    local, model = own.shape
+    groups, tokens, wide = projected.shape
+    head_dim = query_gain.shape[1]
+    out_weight = pltpu.with_memory_space_constraint(out_weight, pltpu.VMEM)
+    vmem = pl.BlockSpec(memory_space=pltpu.VMEM)
+    return pl.pallas_call(
+        backward_kernel,
+        out_shape=jax.ShapeDtypeStruct((groups, tokens, wide), BF16),
+        in_specs=[vmem] * 8,
+        out_specs=vmem,
+        scratch_shapes=[
+            pltpu.VMEM((tokens, model), BF16),
+            pltpu.VMEM((groups, tokens, GROUP * head_dim), BF16),
+        ],
+        compiler_params=params(12),
+        cost_estimate=pl.CostEstimate(
+            flops=2 * tokens * out_weight.size,
+            bytes_accessed=2 * out_weight.size,
+            transcendentals=0,
+        ),
+        name="attention_backward",
+    )(own, other, out_weight, projected, probs, query_gain, key_gain, gate)
+
+
+def input_grad_kernel(
+    grad_ref,
+    weight_ref,
+    own_ref,
+    other_ref,
+    attention_ref,
+    gate_kept_ref,
+    gate_sent_ref,
+    kept_ref,
+    sent_ref,
+    gate_grad_ref,
+):
+    local, model = own_ref.shape
+    groups, tokens, wide = grad_ref.shape
+    steps = wide // SIDE
+
+    def left(step):
+        first = step % steps * SIDE
+        return grad_ref[step // steps, :, first : first + SIDE]
+
+    def right(row, step):
+        first = step % steps * SIDE
+        return weight_ref[step // steps, row : row + SIDE, first : first + SIDE]
+
+    def store(part, total):
         own, other = own_ref[:, part].astype(F32), other_ref[:, part].astype(F32)
         kept_ref[:, part] = (own + total[:local]).astype(BF16)
         sent_ref[:, part] = total[local:].astype(BF16)
@@ -532,46 +580,37 @@
             axis=0,
             keepdims=True,
         )
+
+    def products(*accumulators):
+        tiled_products(accumulators, groups * wide, model, left, right, store)
+
+    pl.run_scoped(
+        products, *[pltpu.ACC(unit)((tokens, SIDE), F32) for _ in range(2) for unit in range(2)]
+    )
     half = gate_kept_ref.shape[1]
     mine = lax.axis_index("seq")
     gate_kept_ref[...] = gate_grad_ref[:, pl.ds(pl.multiple_of(mine * half, half), half)]
     gate_sent_ref[...] = gate_grad_ref[:, pl.ds(pl.multiple_of((1 - mine) * half, half), half)]
 
 
-def backward(
-    own, other, out_weight, weight, projected, probs, attention, query_gain, key_gain, gate
-):
+def input_grad(grad, weight, own, other, attention):
     local, model = own.shape
-    groups, tokens, wide = projected.shape
-    head_dim = query_gain.shape[1]
-    out_weight = pltpu.with_memory_space_constraint(out_weight, pltpu.VMEM)
     weight = pltpu.with_memory_space_constraint(weight, pltpu.VMEM)
     vmem = pl.BlockSpec(memory_space=pltpu.VMEM)
     return pl.pallas_call(
-        backward_kernel,
+        input_grad_kernel,
         out_shape=(
             jax.ShapeDtypeStruct((1, model // 2), F32),
             jax.ShapeDtypeStruct((1, model // 2), F32),
             jax.ShapeDtypeStruct((local, model), BF16),
             jax.ShapeDtypeStruct((local, model), BF16),
         ),
-        in_specs=[vmem] * 10,
+        in_specs=[vmem] * 5,
         out_specs=(vmem,) * 4,
-        scratch_shapes=[
-            pltpu.VMEM((groups, tokens, wide), BF16),
-            pltpu.VMEM((tokens, model), BF16),
-            pltpu.VMEM((groups, tokens, GROUP * head_dim), BF16),
-            pltpu.VMEM((1, model), F32),
-            pltpu.VMEM((tokens, model), F32),
-        ],
-        compiler_params=params(12),
-        cost_estimate=pl.CostEstimate(
-            flops=2 * tokens * (out_weight.size + weight.size),
-            bytes_accessed=2 * (out_weight.size + weight.size),
-            transcendentals=0,
-        ),
-        name="attention_backward",
-    )(own, other, out_weight, weight, projected, probs, attention, query_gain, key_gain, gate)
+        scratch_shapes=[pltpu.VMEM((1, model), F32)],
+        compiler_params=params(8),
+        name="input_grad",
+    )(grad, weight, own, other, attention)
 
 
 def sums_kernel(kept_ref, sent_ref, gate_kept_ref, gate_sent_ref, grad_ref, gate_ref):
@@ -635,25 +674,19 @@
     )
     kept = routed(kept, 0, 1)
     sent = routed(sent, 1, 1)
-    gate_kept, gate_sent, grad_kept, grad_sent = backward(
-        upstream,
-        other_upstream,
-        out_local,
-        weight,
-        projected,
-        probs,
-        attention,
-        query_gain,
-        key_gain,
-        gate_scale,
+    grad = backward(
+        upstream, other_upstream, out_local, projected, probs, query_gain, key_gain, gate_scale
+    )
+    gate_kept, gate_sent, grad_kept, grad_sent = input_grad(
+        grad, weight, upstream, other_upstream, attention
     )
     grad_sent = routed(grad_sent, 1, -1)
     grad_kept = routed(grad_kept, 0, -1)
     segment_output = (kept.astype(F32) + sent.astype(F32)).astype(BF16)
     segment_output, gate_sent = lax.optimization_barrier((segment_output, gate_sent))
     gate_sent = routed(gate_sent, 1, 0)
-    input_grad, gate_grad = sums(grad_sent, grad_kept, gate_kept, gate_sent)
-    return (segment_output[None], input_grad[None], gate_grad)
+    token_grad, gate_grad = sums(grad_sent, grad_kept, gate_kept, gate_sent)
+    return (segment_output[None], token_grad[None], gate_grad)
 
 
 def solution(mesh):

time: 45.8 us -> 46.5 us (1.015)
  Pallas kernels: 24.3 us -> 25.1 us
    pallas_call x1 -> x2, Pallas kernels: 9.8 us -> 10.6 us  [the longest x1 5.96 us: input_grad(): pl.pallas_call(input_grad_kernel, out_shape=(jax.ShapeDtypeStruct((1, mod...]
  transfers between devices with their start and end apart: 7 -> 7, of which waited for: 3 -> 3; matrix products, arithmetic and copies ran while one was open for 2% -> 2% of each run, Pallas kernels for 52% -> 53%
where the time goes in v12:
time: 46.5 us; the launch traced here: 46.1 us
  Pallas kernels  25.1 us (54%)
  waiting for transfers between devices  10.6 us (23%)
  starting transfers between devices  8.76 us (19%)
  other arithmetic  0.84 us (2%)
  between operations  0.74 us (2%)
    ppermute x7, waiting for transfers between devices, routed(): return lax.ppermute(block, ('seq', 'pipe'), route)  10.6 us
    ppermute x7, starting transfers between devices, routed(): return lax.ppermute(block, ('seq', 'pipe'), route)  8.76 us
    pallas_call x1, Pallas kernels, regroup(): pl.pallas_call(regroup_kernel, out_shape=pltpu.VMEM(out, weight.dtype), i...  7.17 us
    pallas_call x1, Pallas kernels, forward(): pl.pallas_call(forward_kernel, out_shape=(jax.ShapeDtypeStruct((groups, t...  6.47 us
    pallas_call x1, Pallas kernels, input_grad(): pl.pallas_call(input_grad_kernel, out_shape=(jax.ShapeDtypeStruct((1, mod...  5.96 us
    pallas_call x1, Pallas kernels, backward(): pl.pallas_call(backward_kernel, out_shape=jax.ShapeDtypeStruct((groups, t...  4.61 us
  transfers between devices with their start and end apart: 7, of which 3 were waited for; matrix products, arithmetic and copies ran while one was open for 2% of the time, Pallas kernels for 53%

profile of v12, /device:TPU:1, one launch (start us, length us, event | category | flops | bytes accessed | tf_op | source)
XLA Modules:
  0.0 46.1 jit_solution(9605860638373730693)
XLA Ops:
  0.6 2.1 %collective-permute-start = (bf16[64,3072]{1,0:T(8,128)(2,1)}, bf16[64,3072]{1,0:T(8,128)(2,1)S(1)}, u32[]{:S(2)}, u32[]{:S(2)}) collective-permute-start(bf16[64,3072]{1,0:T(8,128)(2,1)} %bitcast.9), channel_id=1, source_target_pairs={{0,16},{4,20},{8,24},{12,28},{16,0},{20,4},{24,8},{28,12},{1,17},{... | collective-permute-start | bytes 1179656 | tf_op jit(solution)/shard_map/ppermute | solution.py:643
  2.7 0.0 copy-start
  2.7 0.0 copy-start.1
  2.8 0.0 copy-start.4
  2.8 0.0 copy-start.5
  2.8 0.0 copy-start.6
  2.8 7.2 %regroup.1.weight_ref = bf16[2,3072,1536]{2,1,0:T(8,128)(2,1)S(1)} custom-call(bf16[3072,8,384]{2,1,0:T(8,128)(2,1)} %bitcast.11), custom_call_target="tpu_custom_call" | custom-call | bytes 37748736 | tf_op jit(solution)/shard_map/regroup/pallas_call | solution.py:281
  10.0 0.0 copy-done
  10.0 0.1 collective-permute-start.3
  10.1 1.7 %collective-permute-done.other_ref = bf16[64,3072]{1,0:T(8,128)(2,1)S(1)} collective-permute-done((bf16[64,3072]{1,0:T(8,128)(2,1)}, bf16[64,3072]{1,0:T(8,128)(2,1)S(1)}, u32[]{:S(2)}, u32[]{:S(2)}) %collective-permute-start) | collective-permute-done | bytes 393248 | tf_op jit(solution)/shard_map/ppermute | solution.py:643
  11.8 0.0 copy-done.1
  11.8 0.0 copy-done.2
  11.8 0.0 copy-done.3
  11.8 0.0 copy-done.4
  11.8 0.0 copy-done.5
  11.8 0.0 copy-done.6
  11.8 6.5 %attention_forward.1 = (f32[2,128,1536]{2,1,0:T(8,128)S(1)}, bf16[8,128,128]{2,1,0:T(8,128)(2,1)S(1)}, f32[128,3072]{1,0:T(8,128)S(1)}, bf16[64,3072]{1,0:T(8,12...) custom-call(s32[2,27]{1,0:T(2,128)S(1)} %copy-done.5, s32[2]{0:T(128)S(1)} %copy-done.6, ...), custom_call_target="tpu_custom_call" | custom-call | flops 3221225472 | bytes 25165824 | tf_op jit(solution)/shard_map/attention_forward/pallas_call | solution.py:418
  18.3 4.6 %collective-permute-start.2 = (bf16[64,3072]{1,0:T(8,128)(2,1)S(1)}, bf16[64,3072]{1,0:T(8,128)(2,1)S(1)}, u32[]{:S(2)}, u32[]{:S(2)}) collective-permute-start(bf16[64,3072]{1,0:T(8,128)(2,1)S(1)} %get-tuple-element.21), channel_id=1, source_target_pairs={{0,20},{4,24},{8,28},{12,16},{16,4},{20,8},{24,12},{28,0},{1,21},{... | collective-permute-start | bytes 1179656 | tf_op jit(solution)/shard_map/ppermute | solution.py:643
  22.9 0.0 collective-permute-start.1
  22.9 0.0 collective-permute-done.3.other_ref
  22.9 4.6 %attention_backward.1.grad_ref = bf16[2,128,1536]{2,1,0:T(8,128)(2,1)S(1)} custom-call(bf16[64,3072]{1,0:T(8,128)(2,1)S(1)} %bitcast.7, bf16[64,3072]{1,0:T(8,128)(2,1)S(1)} %collective-permute-done.3.other_ref, bf16[1024,3072]{1,0:T(8,128)(2,1)S(1)} %get-tuple-element.23.out_weight_ref, f32[2,128,1536]{2,1,0:T(8,128)S(1)} %get-tuple-element.24.projected_ref, ...), custom_call_target="tpu_custom_call" | custom-call | flops 805306368 | bytes 6291456 | tf_op jit(solution)/shard_map/attention_backward/pallas_call | solution.py:531
  27.5 6.0 %input_grad.1 = (f32[1,1536]{1,0:T(1,128)S(1)}, f32[1,1536]{1,0:T(1,128)S(1)}, bf16[64,3072]{1,0:T(8,128)(2,1)S(1)}, bf16[64,3072]{1,0:T(8,128)(2,1)S(1)}) custom-call(bf16[2,128,1536]{2,1,0:T(8,128)(2,1)S(1)} %attention_backward.1.grad_ref, bf16[2,3072,1536]{2,1,0:T(8,128)(2,1)S(1)} %regroup.1.weight_ref, bf16[64,3072]{1,0:T(8,128)(2,1)S(1)} %bitcast.8, ...), custom_call_target="tpu_custom_call" | custom-call | tf_op jit(solution)/shard_map/input_grad/pallas_call | solution.py:600
  33.5 0.1 collective-permute-start.4
  33.6 0.8 %collective-permute-start.5 = (bf16[64,3072]{1,0:T(8,128)(2,1)S(1)}, bf16[64,3072]{1,0:T(8,128)(2,1)S(1)}, u32[]{:S(2)}, u32[]{:S(2)}) collective-permute-start(bf16[64,3072]{1,0:T(8,128)(2,1)S(1)} %get-tuple-element.30), channel_id=1, source_target_pairs={{0,12},{4,0},{8,4},{12,8},{16,28},{20,16},{24,20},{28,24},{1,13},{... | collective-permute-start | bytes 1179656 | tf_op jit(solution)/shard_map/ppermute | solution.py:643
  34.3 0.0 collective-permute-done.2
  34.4 0.0 collective-permute-done.1
  34.4 0.8 %add_convert_fusion = bf16[64,3072]{1,0:T(8,128)(2,1)} fusion(bf16[64,3072]{1,0:T(8,128)(2,1)S(1)} %collective-permute-done.2, bf16[64,3072]{1,0:T(8,128)(2,1)S(1)} %collective-permute-done.1), kind=kLoop, calls=%fused_computation | loop fusion | flops 786432 | bytes 1179648 | tf_op jit(solution)/shard_map/convert_element_type | solution.py:685
  35.2 1.1 %collective-permute-start.6 = (f32[1,1536]{1,0:T(1,128)S(1)}, f32[1,1536]{1,0:T(1,128)S(1)}, u32[]{:S(2)}, u32[]{:S(2)}) collective-permute-start(f32[1,1536]{1,0:T(1,128)S(1)} %get-tuple-element.32), channel_id=1, source_target_pairs={{0,16},{4,20},{8,24},{12,28},{16,0},{20,4},{24,8},{28,12},{1,17},{... | collective-permute-start | bytes 18440 | tf_op jit(solution)/shard_map/ppermute | solution.py:643
  36.3 8.7 %collective-permute-done.4.kept_ref = bf16[64,3072]{1,0:T(8,128)(2,1)S(1)} collective-permute-done((bf16[64,3072]{1,0:T(8,128)(2,1)S(1)}, bf16[64,3072]{1,0:T(8,128)(2,1)S(1)}, u32[]{:S(2)}, u32[]{:S(2)}) %collective-permute-start.4) | collective-permute-done | bytes 393248 | tf_op jit(solution)/shard_map/ppermute | solution.py:643
  45.0 0.2 collective-permute-done.5.sent_ref
  45.2 0.0 collective-permute-done.6.gate_sent_ref
  45.2 0.8 %sums.1 = (bf16[64,3072]{1,0:T(8,128)(2,1)}, f32[1,1536]{1,0:T(1,128)}) custom-call(bf16[64,3072]{1,0:T(8,128)(2,1)S(1)} %collective-permute-done.4.kept_ref, bf16[64,3072]{1,0:T(8,128)(2,1)S(1)} %collective-permute-done.5.sent_ref, f32[1,1536]{1,0:T(1,128)S(1)} %get-tuple-element.31.gate_kept_ref, f32[1,1536]{1,0:T(1,128)S(1)} %collective-permute-done.6.gate_sent_ref), custom_call_target="tpu_custom_call" | custom-call | tf_op jit(solution)/shard_map/sums/pallas_call | solution.py:623
  (2 shorter events, 0.0 us)
Async XLA Ops:
  0.6 11.2 %collective-permute-start = (bf16[64,3072]{1,0:T(8,128)(2,1)}, bf16[64,3072]{1,0:T(8,128)(2,1)S(1)}, u32[]{:S(2)}, u32[]{:S(2)}) collective-permute-start(bf16[64,3072]{1,0:T(8,128)(2,1)} %bitcast.9), channel_id=1, source_target_pairs={{0,16},{4,20},{8,24},{12,28},{16,0},{20,4},{24,8},{28,12},{1,17},{... | collective-permute-start | bytes 1179656 | tf_op jit(solution)/shard_map/ppermute | solution.py:643
  2.7 7.2 %copy-start = (bf16[1,64,3072]{2,1,0:T(8,128)(2,1)S(1)}, bf16[1,64,3072]{2,1,0:T(8,128)(2,1)}, u32[]{:S(2)}) copy-start(bf16[1,64,3072]{2,1,0:T(8,128)(2,1)} %param.10) | copy-start | bytes 1179652
  2.7 9.1 %copy-start.1 = (bf16[1,64,3072]{2,1,0:T(8,128)(2,1)S(1)}, bf16[1,64,3072]{2,1,0:T(8,128)(2,1)}, u32[]{:S(2)}) copy-start(bf16[1,64,3072]{2,1,0:T(8,128)(2,1)} %param.9) | copy-start | bytes 1179652
  2.7 9.1 %copy-start.2 = (f32[1,3072]{1,0:T(1,128)S(1)}, f32[1,3072]{1,0:T(1,128)}, u32[]{:S(2)}) copy-start(f32[1,3072]{1,0:T(1,128)} %gate_ref.3) | copy-start | bytes 36868
  2.7 9.1 %copy-start.3 = (f32[1,128]{1,0:T(1,128)S(1)}, f32[1,128]{1,0:T(1,128)}, u32[]{:S(2)}) copy-start(f32[1,128]{1,0:T(1,128)} %query_gain_ref.3) | copy-start | bytes 1540
  2.8 9.1 %copy-start.4 = (f32[1,128]{1,0:T(1,128)S(1)}, f32[1,128]{1,0:T(1,128)}, u32[]{:S(2)}) copy-start(f32[1,128]{1,0:T(1,128)} %key_gain_ref.3) | copy-start | bytes 1540
  2.8 9.1 %copy-start.5 = (s32[2,27]{1,0:T(2,128)S(1)}, s32[2,27]{1,0:T(2,128)}, u32[]{:S(2)}) copy-start(s32[2,27]{1,0:T(2,128)} %neighbours_ref.1) | copy-start | bytes 652
  2.8 9.1 %copy-start.6 = (s32[2]{0:T(128)S(1)}, s32[2]{0:T(128)}, u32[]{:S(2)}) copy-start(s32[2]{0:T(128)} %tile_slot_ref.1) | copy-start | bytes 28
  10.0 13.0 %collective-permute-start.3 = (bf16[64,3072]{1,0:T(8,128)(2,1)S(1)}, bf16[64,3072]{1,0:T(8,128)(2,1)S(1)}, u32[]{:S(2)}, u32[]{:S(2)}) collective-permute-start(bf16[64,3072]{1,0:T(8,128)(2,1)S(1)} %bitcast.6), channel_id=1, source_target_pairs={{0,16},{4,20},{8,24},{12,28},{16,0},{20,4},{24,8},{28,12},{1,17},{... | collective-permute-start | bytes 1179656 | tf_op jit(solution)/shard_map/ppermute | solution.py:643
  18.3 16.0 %collective-permute-start.2 = (bf16[64,3072]{1,0:T(8,128)(2,1)S(1)}, bf16[64,3072]{1,0:T(8,128)(2,1)S(1)}, u32[]{:S(2)}, u32[]{:S(2)}) collective-permute-start(bf16[64,3072]{1,0:T(8,128)(2,1)S(1)} %get-tuple-element.21), channel_id=1, source_target_pairs={{0,20},{4,24},{8,28},{12,16},{16,4},{20,8},{24,12},{28,0},{1,21},{... | collective-permute-start | bytes 1179656 | tf_op jit(solution)/shard_map/ppermute | solution.py:643
  22.9 11.4 %collective-permute-start.1 = (bf16[64,3072]{1,0:T(8,128)(2,1)S(1)}, bf16[64,3072]{1,0:T(8,128)(2,1)S(1)}, u32[]{:S(2)}, u32[]{:S(2)}) collective-permute-start(bf16[64,3072]{1,0:T(8,128)(2,1)S(1)} %get-tuple-element.20), channel_id=1, source_target_pairs={{0,4},{4,8},{8,12},{12,0},{16,20},{20,24},{24,28},{28,16},{1,5},{5... | collective-permute-start | bytes 1179656 | tf_op jit(solution)/shard_map/ppermute | solution.py:643
  33.5 11.5 %collective-permute-start.4 = (bf16[64,3072]{1,0:T(8,128)(2,1)S(1)}, bf16[64,3072]{1,0:T(8,128)(2,1)S(1)}, u32[]{:S(2)}, u32[]{:S(2)}) collective-permute-start(bf16[64,3072]{1,0:T(8,128)(2,1)S(1)} %get-tuple-element.29), channel_id=1, source_target_pairs={{0,28},{4,16},{8,20},{12,24},{16,12},{20,0},{24,4},{28,8},{1,29},{... | collective-permute-start | bytes 1179656 | tf_op jit(solution)/shard_map/ppermute | solution.py:643
  33.6 11.6 %collective-permute-start.5 = (bf16[64,3072]{1,0:T(8,128)(2,1)S(1)}, bf16[64,3072]{1,0:T(8,128)(2,1)S(1)}, u32[]{:S(2)}, u32[]{:S(2)}) collective-permute-start(bf16[64,3072]{1,0:T(8,128)(2,1)S(1)} %get-tuple-element.30), channel_id=1, source_target_pairs={{0,12},{4,0},{8,4},{12,8},{16,28},{20,16},{24,20},{28,24},{1,13},{... | collective-permute-start | bytes 1179656 | tf_op jit(solution)/shard_map/ppermute | solution.py:643
  35.2 10.0 %collective-permute-start.6 = (f32[1,1536]{1,0:T(1,128)S(1)}, f32[1,1536]{1,0:T(1,128)S(1)}, u32[]{:S(2)}, u32[]{:S(2)}) collective-permute-start(f32[1,1536]{1,0:T(1,128)S(1)} %get-tuple-element.32), channel_id=1, source_target_pairs={{0,16},{4,20},{8,24},{12,28},{16,0},{20,4},{24,8},{28,12},{1,17},{... | collective-permute-start | bytes 18440 | tf_op jit(solution)/shard_map/ppermute | solution.py:643

commit v13 on v10

--- a/solution.py
+++ b/solution.py
@@ -566,6 +566,26 @@
     )(own, other, out_weight, weight, projected, probs, attention, query_gain, key_gain, gate)
 
 
+def sums_kernel(sent_ref, kept_ref, gate_kept_ref, gate_sent_ref, grad_ref, gate_ref):
+    grad_ref[...] = (kept_ref[...].astype(F32) + sent_ref[...].astype(F32)).astype(BF16)
+    gate_ref[...] = gate_kept_ref[...] + gate_sent_ref[...]
+
+
+def sums(sent, kept, gate_kept, gate_sent):
+    vmem = pl.BlockSpec(memory_space=pltpu.VMEM)
+    return pl.pallas_call(
+        sums_kernel,
+        out_shape=(
+            jax.ShapeDtypeStruct(kept.shape, BF16),
+            jax.ShapeDtypeStruct(gate_kept.shape, F32),
+        ),
+        in_specs=[vmem] * 4,
+        out_specs=(vmem, vmem),
+        compiler_params=params(8),
+        name="sums",
+    )(sent, kept, gate_kept, gate_sent)
+
+
 def routed(block, seq_step, pipe_step):
     seq_size, pipe_size = lax.axis_size("seq"), lax.axis_size("pipe")
     route = []
@@ -592,7 +612,6 @@
     out_local = out_weight[0]
     other_stream = routed(stream, 1, 0)
     weight = regroup(qkv_weight[0], 128, 8)
-    weight, upstream = lax.optimization_barrier((weight, upstream))
     other_upstream = routed(upstream, 1, 0)
     projected, probs, attention, kept, sent, out_local = forward(
         neighbours,
@@ -624,9 +643,8 @@
     segment_output = (kept.astype(F32) + sent.astype(F32)).astype(BF16)
     segment_output, gate_sent = lax.optimization_barrier((segment_output, gate_sent))
     gate_sent = routed(gate_sent, 1, 0)
-    input_grad = (grad_kept.astype(F32) + grad_sent.astype(F32)).astype(BF16)
-    input_grad, gate_sent = lax.optimization_barrier((input_grad, gate_sent))
-    return (segment_output[None], input_grad[None], gate_kept + gate_sent)
+    token_grad, gate_grad = sums(grad_sent, grad_kept, gate_kept, gate_sent)
+    return (segment_output[None], token_grad[None], gate_grad)
 
 
 def solution(mesh):

time: 45.9 us -> 45.8 us (level)
  other arithmetic: 2.29 us -> 0.84 us
  Pallas kernels: 23.3 us -> 24 us
  waiting for transfers between devices: 10.6 us -> 11.2 us
    convert_element_type x1 -> x0, other arithmetic: 0.85 us -> none  [pair_body(): input_grad = (grad_kept.astype(F32) + grad_sent.astype(F32)).astype(BF16)]
    pallas_call x0 -> x1, Pallas kernels: none -> 0.84 us  [sums(): pl.pallas_call(sums_kernel, out_shape=(jax.ShapeDtypeStruct(kept.shape, B...]
    add x1 -> x0, other arithmetic: 0.6 us -> none  [pair_body(): return (segment_output[None], input_grad[None], gate_kept + gate_sent)]
    ppermute x7, waiting for transfers between devices: 10.6 us -> 11.2 us  [routed(): return lax.ppermute(block, ('seq', 'pipe'), route)]
  transfers between devices with their start and end apart: 7 -> 7, of which waited for: 3 -> 3; matrix products, arithmetic and copies ran while one was open for 4% -> 2% of each run, Pallas kernels for 51% -> 51%
where the time goes in v13:
time: 45.8 us; the launch traced here: 45.6 us
  Pallas kernels  24 us (52%)
  waiting for transfers between devices  11.2 us (24%)
  starting transfers between devices  8.82 us (19%)
  other arithmetic  0.84 us (2%)
  between operations  0.72 us (2%)
    ppermute x7, waiting for transfers between devices, routed(): return lax.ppermute(block, ('seq', 'pipe'), route)  11.2 us
    pallas_call x1, Pallas kernels, backward(): pl.pallas_call(backward_kernel, out_shape=(jax.ShapeDtypeStruct((1, model...  9.64 us
    ppermute x7, starting transfers between devices, routed(): return lax.ppermute(block, ('seq', 'pipe'), route)  8.82 us
    pallas_call x1, Pallas kernels, regroup(): pl.pallas_call(regroup_kernel, out_shape=pltpu.VMEM(out, weight.dtype), i...  7.07 us
    pallas_call x1, Pallas kernels, forward(): pl.pallas_call(forward_kernel, out_shape=(jax.ShapeDtypeStruct((groups, t...  6.45 us
  transfers between devices with their start and end apart: 7, of which 3 were waited for; matrix products, arithmetic and copies ran while one was open for 2% of the time, Pallas kernels for 51%

profile of v13, /device:TPU:1, one launch (start us, length us, event | category | flops | bytes accessed | tf_op | source)
XLA Modules:
  0.0 45.6 jit_solution(17866246093231857140)
XLA Ops:
  0.6 2.1 %collective-permute-start = (bf16[64,3072]{1,0:T(8,128)(2,1)}, bf16[64,3072]{1,0:T(8,128)(2,1)S(1)}, u32[]{:S(2)}, u32[]{:S(2)}) collective-permute-start(bf16[64,3072]{1,0:T(8,128)(2,1)} %bitcast.8), channel_id=1, source_target_pairs={{0,16},{4,20},{8,24},{12,28},{16,0},{20,4},{24,8},{28,12},{1,17},{... | collective-permute-start | bytes 1179656 | tf_op jit(solution)/shard_map/ppermute | solution.py:596
  2.7 0.1 collective-permute-start.3
  2.8 0.0 copy-start.1
  2.8 0.0 copy-start.2
  2.8 0.0 copy-start.3
  2.8 0.0 copy-start.5
  2.8 0.0 copy-start.6
  2.8 7.1 %regroup.1.weight_ref = bf16[2,3072,1536]{2,1,0:T(8,128)(2,1)S(1)} custom-call(bf16[3072,8,384]{2,1,0:T(8,128)(2,1)} %bitcast.10), custom_call_target="tpu_custom_call" | custom-call | bytes 37748736 | tf_op jit(solution)/shard_map/regroup/pallas_call | solution.py:281
  9.9 1.9 %collective-permute-done.other_ref = bf16[64,3072]{1,0:T(8,128)(2,1)S(1)} collective-permute-done((bf16[64,3072]{1,0:T(8,128)(2,1)}, bf16[64,3072]{1,0:T(8,128)(2,1)S(1)}, u32[]{:S(2)}, u32[]{:S(2)}) %collective-permute-start) | collective-permute-done | bytes 393248 | tf_op jit(solution)/shard_map/ppermute | solution.py:596
  11.8 0.0 copy-done.1
  11.8 0.0 copy-done.2
  11.8 0.0 copy-done.3
  11.8 0.0 copy-done.4
  11.8 0.0 copy-done.5
  11.8 0.0 copy-done.6
  11.8 0.0 copy-start
  11.8 6.5 %attention_forward.1 = (f32[2,128,1536]{2,1,0:T(8,128)S(1)}, bf16[8,128,128]{2,1,0:T(8,128)(2,1)S(1)}, f32[128,3072]{1,0:T(8,128)S(1)}, bf16[64,3072]{1,0:T(8,12...) custom-call(s32[2,27]{1,0:T(2,128)S(1)} %copy-done.5, s32[2]{0:T(128)S(1)} %copy-done.6, ...), custom_call_target="tpu_custom_call" | custom-call | flops 3221225472 | bytes 25165824 | tf_op jit(solution)/shard_map/attention_forward/pallas_call | solution.py:418
  18.3 4.7 %collective-permute-start.2 = (bf16[64,3072]{1,0:T(8,128)(2,1)S(1)}, bf16[64,3072]{1,0:T(8,128)(2,1)S(1)}, u32[]{:S(2)}, u32[]{:S(2)}) collective-permute-start(bf16[64,3072]{1,0:T(8,128)(2,1)S(1)} %get-tuple-element.18), channel_id=1, source_target_pairs={{0,20},{4,24},{8,28},{12,16},{16,4},{20,8},{24,12},{28,0},{1,21},{... | collective-permute-start | bytes 1179656 | tf_op jit(solution)/shard_map/ppermute | solution.py:596
  23.0 0.0 collective-permute-start.1
  23.0 0.0 collective-permute-done.3.other_ref
  23.0 0.0 copy-done
  23.0 9.6 %attention_backward.1 = (f32[1,1536]{1,0:T(1,128)S(1)}, f32[1,1536]{1,0:T(1,128)S(1)}, bf16[64,3072]{1,0:T(8,128)(2,1)S(1)}, bf16[64,3072]{1,0:T(8,128)(2,1)S(1)}) custom-call(bf16[64,3072]{1,0:T(8,128)(2,1)S(1)} %bitcast.7, bf16[64,3072]{1,0:T(8,128)(2,1)S(1)} %collective-permute-done.3.other_ref, bf16[1024,3072]{1,0:T(8,128)(2,1)S(1)} %get-tuple-element.19.out_weight_ref, ...), custom_call_target="tpu_custom_call" | custom-call | flops 3221225472 | bytes 25165824 | tf_op jit(solution)/shard_map/attention_backward/pallas_call | solution.py:543
  32.7 0.7 %collective-permute-start.4 = (bf16[64,3072]{1,0:T(8,128)(2,1)S(1)}, bf16[64,3072]{1,0:T(8,128)(2,1)S(1)}, u32[]{:S(2)}, u32[]{:S(2)}) collective-permute-start(bf16[64,3072]{1,0:T(8,128)(2,1)S(1)} %get-tuple-element.25), channel_id=1, source_target_pairs={{0,28},{4,16},{8,20},{12,24},{16,12},{20,0},{24,4},{28,8},{1,29},{... | collective-permute-start | bytes 1179656 | tf_op jit(solution)/shard_map/ppermute | solution.py:596
  33.4 0.0 collective-permute-start.5
  33.4 0.0 collective-permute-done.2
  33.4 0.0 collective-permute-done.1
  33.4 0.8 %add_convert_fusion = bf16[64,3072]{1,0:T(8,128)(2,1)} fusion(bf16[64,3072]{1,0:T(8,128)(2,1)S(1)} %collective-permute-done.2, bf16[64,3072]{1,0:T(8,128)(2,1)S(1)} %collective-permute-done.1), kind=kLoop, calls=%fused_computation | loop fusion | flops 786432 | bytes 1179648 | tf_op jit(solution)/shard_map/convert_element_type | solution.py:643
  34.3 1.2 %collective-permute-start.6 = (f32[1,1536]{1,0:T(1,128)S(1)}, f32[1,1536]{1,0:T(1,128)S(1)}, u32[]{:S(2)}, u32[]{:S(2)}) collective-permute-start(f32[1,1536]{1,0:T(1,128)S(1)} %get-tuple-element.28), channel_id=1, source_target_pairs={{0,16},{4,20},{8,24},{12,28},{16,0},{20,4},{24,8},{28,12},{1,17},{... | collective-permute-start | bytes 18440 | tf_op jit(solution)/shard_map/ppermute | solution.py:596
  35.4 8.6 %collective-permute-done.4.sent_ref = bf16[64,3072]{1,0:T(8,128)(2,1)S(1)} collective-permute-done((bf16[64,3072]{1,0:T(8,128)(2,1)S(1)}, bf16[64,3072]{1,0:T(8,128)(2,1)S(1)}, u32[]{:S(2)}, u32[]{:S(2)}) %collective-permute-start.4) | collective-permute-done | bytes 393248 | tf_op jit(solution)/shard_map/ppermute | solution.py:596
  44.1 0.7 %collective-permute-done.5.kept_ref = bf16[64,3072]{1,0:T(8,128)(2,1)S(1)} collective-permute-done((bf16[64,3072]{1,0:T(8,128)(2,1)S(1)}, bf16[64,3072]{1,0:T(8,128)(2,1)S(1)}, u32[]{:S(2)}, u32[]{:S(2)}) %collective-permute-start.5) | collective-permute-done | bytes 393248 | tf_op jit(solution)/shard_map/ppermute | solution.py:596
  44.8 0.0 collective-permute-done.6.gate_sent_ref
  44.8 0.8 %sums.1 = (bf16[64,3072]{1,0:T(8,128)(2,1)}, f32[1,1536]{1,0:T(1,128)}) custom-call(bf16[64,3072]{1,0:T(8,128)(2,1)S(1)} %collective-permute-done.4.sent_ref, bf16[64,3072]{1,0:T(8,128)(2,1)S(1)} %collective-permute-done.5.kept_ref, f32[1,1536]{1,0:T(1,128)S(1)} %get-tuple-element.27.gate_kept_ref, f32[1,1536]{1,0:T(1,128)S(1)} %collective-permute-done.6.gate_sent_ref), custom_call_target="tpu_custom_call" | custom-call | tf_op jit(solution)/shard_map/sums/pallas_call | solution.py:576
  (1 shorter events, 0.0 us)
Async XLA Ops:
  0.6 11.2 %collective-permute-start = (bf16[64,3072]{1,0:T(8,128)(2,1)}, bf16[64,3072]{1,0:T(8,128)(2,1)S(1)}, u32[]{:S(2)}, u32[]{:S(2)}) collective-permute-start(bf16[64,3072]{1,0:T(8,128)(2,1)} %bitcast.8), channel_id=1, source_target_pairs={{0,16},{4,20},{8,24},{12,28},{16,0},{20,4},{24,8},{28,12},{1,17},{... | collective-permute-start | bytes 1179656 | tf_op jit(solution)/shard_map/ppermute | solution.py:596
  2.7 20.3 %collective-permute-start.3 = (bf16[64,3072]{1,0:T(8,128)(2,1)}, bf16[64,3072]{1,0:T(8,128)(2,1)S(1)}, u32[]{:S(2)}, u32[]{:S(2)}) collective-permute-start(bf16[64,3072]{1,0:T(8,128)(2,1)} %bitcast.6), channel_id=1, source_target_pairs={{0,16},{4,20},{8,24},{12,28},{16,0},{20,4},{24,8},{28,12},{1,17},{... | collective-permute-start | bytes 1179656 | tf_op jit(solution)/shard_map/ppermute | solution.py:596
  2.8 9.0 %copy-start.1 = (bf16[1,64,3072]{2,1,0:T(8,128)(2,1)S(1)}, bf16[1,64,3072]{2,1,0:T(8,128)(2,1)}, u32[]{:S(2)}) copy-start(bf16[1,64,3072]{2,1,0:T(8,128)(2,1)} %param.9) | copy-start | bytes 1179652
  2.8 9.0 %copy-start.2 = (f32[1,3072]{1,0:T(1,128)S(1)}, f32[1,3072]{1,0:T(1,128)}, u32[]{:S(2)}) copy-start(f32[1,3072]{1,0:T(1,128)} %gate_ref.3) | copy-start | bytes 36868
  2.8 9.0 %copy-start.3 = (f32[1,128]{1,0:T(1,128)S(1)}, f32[1,128]{1,0:T(1,128)}, u32[]{:S(2)}) copy-start(f32[1,128]{1,0:T(1,128)} %query_gain_ref.3) | copy-start | bytes 1540
  2.8 9.0 %copy-start.4 = (f32[1,128]{1,0:T(1,128)S(1)}, f32[1,128]{1,0:T(1,128)}, u32[]{:S(2)}) copy-start(f32[1,128]{1,0:T(1,128)} %key_gain_ref.3) | copy-start | bytes 1540
  2.8 9.0 %copy-start.5 = (s32[2,27]{1,0:T(2,128)S(1)}, s32[2,27]{1,0:T(2,128)}, u32[]{:S(2)}) copy-start(s32[2,27]{1,0:T(2,128)} %neighbours_ref.1) | copy-start | bytes 652
  2.8 9.0 %copy-start.6 = (s32[2]{0:T(128)S(1)}, s32[2]{0:T(128)}, u32[]{:S(2)}) copy-start(s32[2]{0:T(128)} %tile_slot_ref.1) | copy-start | bytes 28
  11.8 11.2 %copy-start = (bf16[1,64,3072]{2,1,0:T(8,128)(2,1)S(1)}, bf16[1,64,3072]{2,1,0:T(8,128)(2,1)}, u32[]{:S(2)}) copy-start(bf16[1,64,3072]{2,1,0:T(8,128)(2,1)} %param.10) | copy-start | bytes 1179652
  18.3 15.1 %collective-permute-start.2 = (bf16[64,3072]{1,0:T(8,128)(2,1)S(1)}, bf16[64,3072]{1,0:T(8,128)(2,1)S(1)}, u32[]{:S(2)}, u32[]{:S(2)}) collective-permute-start(bf16[64,3072]{1,0:T(8,128)(2,1)S(1)} %get-tuple-element.18), channel_id=1, source_target_pairs={{0,20},{4,24},{8,28},{12,16},{16,4},{20,8},{24,12},{28,0},{1,21},{... | collective-permute-start | bytes 1179656 | tf_op jit(solution)/shard_map/ppermute | solution.py:596
  23.0 10.4 %collective-permute-start.1 = (bf16[64,3072]{1,0:T(8,128)(2,1)S(1)}, bf16[64,3072]{1,0:T(8,128)(2,1)S(1)}, u32[]{:S(2)}, u32[]{:S(2)}) collective-permute-start(bf16[64,3072]{1,0:T(8,128)(2,1)S(1)} %get-tuple-element.17), channel_id=1, source_target_pairs={{0,4},{4,8},{8,12},{12,0},{16,20},{20,24},{24,28},{28,16},{1,5},{5... | collective-permute-start | bytes 1179656 | tf_op jit(solution)/shard_map/ppermute | solution.py:596
  32.7 11.4 %collective-permute-start.4 = (bf16[64,3072]{1,0:T(8,128)(2,1)S(1)}, bf16[64,3072]{1,0:T(8,128)(2,1)S(1)}, u32[]{:S(2)}, u32[]{:S(2)}) collective-permute-start(bf16[64,3072]{1,0:T(8,128)(2,1)S(1)} %get-tuple-element.25), channel_id=1, source_target_pairs={{0,28},{4,16},{8,20},{12,24},{16,12},{20,0},{24,4},{28,8},{1,29},{... | collective-permute-start | bytes 1179656 | tf_op jit(solution)/shard_map/ppermute | solution.py:596
  33.4 11.4 %collective-permute-start.5 = (bf16[64,3072]{1,0:T(8,128)(2,1)S(1)}, bf16[64,3072]{1,0:T(8,128)(2,1)S(1)}, u32[]{:S(2)}, u32[]{:S(2)}) collective-permute-start(bf16[64,3072]{1,0:T(8,128)(2,1)S(1)} %get-tuple-element.26), channel_id=1, source_target_pairs={{0,12},{4,0},{8,4},{12,8},{16,28},{20,16},{24,20},{28,24},{1,13},{... | collective-permute-start | bytes 1179656 | tf_op jit(solution)/shard_map/ppermute | solution.py:596
  34.3 10.5 %collective-permute-start.6 = (f32[1,1536]{1,0:T(1,128)S(1)}, f32[1,1536]{1,0:T(1,128)S(1)}, u32[]{:S(2)}, u32[]{:S(2)}) collective-permute-start(f32[1,1536]{1,0:T(1,128)S(1)} %get-tuple-element.28), channel_id=1, source_target_pairs={{0,16},{4,20},{8,24},{12,28},{16,0},{20,4},{24,8},{28,12},{1,17},{... | collective-permute-start | bytes 18440 | tf_op jit(solution)/shard_map/ppermute | solution.py:596

commit v14 on v13

--- a/solution.py
+++ b/solution.py
@@ -245,7 +245,7 @@
             self.waited += 1
 
 
-def regroup_kernel(weight_ref, out_ref, read_ref, reads):
+def regroup_kernel(weight_ref, out_ref, turned_ref, read_ref, reads):
     depth, heads, width = weight_ref.shape
     slots, rows = read_ref.shape[:2]
     steps = depth // rows
@@ -269,6 +269,8 @@
         for head in range(heads):
             left = (head % GROUP) * width
             out_ref[head // GROUP, part(step), left : left + width] = by_head[head]
+            if head >= heads - GROUP:
+                turned_ref[left : left + width, part(step)] = by_head[head].T
 
         @pl.when(step + slots < steps)
         def _():
@@ -280,14 +282,17 @@
     out = (heads // GROUP, depth, GROUP * width)
     return pl.pallas_call(
         regroup_kernel,
-        out_shape=pltpu.VMEM(out, weight.dtype),
+        out_shape=(
+            pltpu.VMEM(out, weight.dtype),
+            pltpu.VMEM((out[2], out[1]), weight.dtype),
+        ),
         in_specs=[pl.BlockSpec(memory_space=pl.ANY)],
-        out_specs=pl.BlockSpec(memory_space=pltpu.VMEM),
+        out_specs=(pl.BlockSpec(memory_space=pltpu.VMEM),) * 2,
         scratch_shapes=[
             pltpu.VMEM((slots, rows, heads, width), weight.dtype),
             pltpu.SemaphoreType.DMA((slots,)),
         ],
-        compiler_params=params(12),
+        compiler_params=params(9),
         cost_estimate=pl.CostEstimate(
             flops=0, bytes_accessed=4 * depth * heads * width, transcendentals=0
         ),
@@ -431,7 +436,7 @@
             pltpu.VMEM((tokens, model), BF16),
             pltpu.SemaphoreType.DMA((groups,)),
         ],
-        compiler_params=params(12),
+        compiler_params=params(8),
         cost_estimate=pl.CostEstimate(
             flops=2 * tokens * (weight.size + out_weight.size),
             bytes_accessed=2 * (weight.size + out_weight.size),
@@ -441,15 +446,15 @@
     )(neighbours, tile_slot, own, other, weight, out_weight, query_gain, key_gain, gate)
 
 
-def input_grad(grad_ref, weight_ref, own_ref, kept_ref, sent_ref):
+def input_grad(grad_ref, weight_ref, turned_ref, own_ref, kept_ref, sent_ref):
     local, model = own_ref.shape
+    last = grad_ref.shape[0] - 1
     block = 512
     for start in range(0, model, block):
         part = slice(start, start + block)
-        total = dot_nt(weight_ref[0, part, :], grad_ref[0])
-        for group in range(1, grad_ref.shape[0]):
-            total += dot_nt(weight_ref[group, part, :], grad_ref[group])
-        total = total.T
+        total = dot_nn(grad_ref[last], turned_ref[:, part])
+        for group in range(last):
+            total += dot_nt(weight_ref[group, part, :], grad_ref[group]).T
         kept_ref[:, part] = (own_ref[:, part].astype(F32) + total[:local]).astype(BF16)
         sent_ref[:, part] = total[local:].astype(BF16)
 
@@ -459,6 +464,7 @@
     other_ref,
     out_weight_ref,
     weight_ref,
+    turned_ref,
     projected_ref,
     probs_ref,
     attention_ref,
@@ -528,17 +534,28 @@
             attended_grad(group + 1)
         for head in range(GROUP):
             attend_backward(group, head)
-    input_grad(grad_ref, weight_ref, own_ref, kept_ref, sent_ref)
+    input_grad(grad_ref, weight_ref, turned_ref, own_ref, kept_ref, sent_ref)
 
 
 def backward(
-    own, other, out_weight, weight, projected, probs, attention, query_gain, key_gain, gate
+    own,
+    other,
+    out_weight,
+    weight,
+    turned,
+    projected,
+    probs,
+    attention,
+    query_gain,
+    key_gain,
+    gate,
 ):
     local, model = own.shape
     groups, tokens, wide = projected.shape
     head_dim = query_gain.shape[1]
     out_weight = pltpu.with_memory_space_constraint(out_weight, pltpu.VMEM)
     weight = pltpu.with_memory_space_constraint(weight, pltpu.VMEM)
+    turned = pltpu.with_memory_space_constraint(turned, pltpu.VMEM)
     vmem = pl.BlockSpec(memory_space=pltpu.VMEM)
     return pl.pallas_call(
         backward_kernel,
@@ -548,7 +565,7 @@
             jax.ShapeDtypeStruct((local, model), BF16),
             jax.ShapeDtypeStruct((local, model), BF16),
         ),
-        in_specs=[vmem] * 10,
+        in_specs=[vmem] * 11,
         out_specs=(vmem,) * 4,
         scratch_shapes=[
             pltpu.VMEM((groups, tokens, wide), BF16),
@@ -556,14 +573,26 @@
             pltpu.VMEM((groups, tokens, GROUP * head_dim), BF16),
             pltpu.VMEM((1, model), F32),
         ],
-        compiler_params=params(12),
+        compiler_params=params(8),
         cost_estimate=pl.CostEstimate(
             flops=2 * tokens * (out_weight.size + weight.size),
             bytes_accessed=2 * (out_weight.size + weight.size),
             transcendentals=0,
         ),
         name="attention_backward",
-    )(own, other, out_weight, weight, projected, probs, attention, query_gain, key_gain, gate)
+    )(
+        own,
+        other,
+        out_weight,
+        weight,
+        turned,
+        projected,
+        probs,
+        attention,
+        query_gain,
+        key_gain,
+        gate,
+    )
 
 
 def sums_kernel(sent_ref, kept_ref, gate_kept_ref, gate_sent_ref, grad_ref, gate_ref):
@@ -611,7 +640,7 @@
     upstream = output_grad[0]
     out_local = out_weight[0]
     other_stream = routed(stream, 1, 0)
-    weight = regroup(qkv_weight[0], 128, 8)
+    weight, turned_weight = regroup(qkv_weight[0], 128, 6)
     other_upstream = routed(upstream, 1, 0)
     projected, probs, attention, kept, sent, out_local = forward(
         neighbours,
@@ -631,6 +660,7 @@
         other_upstream,
         out_local,
         weight,
+        turned_weight,
         projected,
         probs,
         attention,

time: 45.8 us -> 44.8 us (0.978)
  waiting for transfers between devices: 11.2 us -> 9.85 us
    pallas_call x1, Pallas kernels: 7.07 us -> 8.46 us  [regroup(): pl.pallas_call(regroup_kernel, out_shape=(pltpu.VMEM(out, weight.dtype),...]
    ppermute x7, waiting for transfers between devices: 11.2 us -> 9.85 us  [routed(): return lax.ppermute(block, ('seq', 'pipe'), route)]
    pallas_call x1, Pallas kernels: 9.64 us -> 8.59 us  [backward(): pl.pallas_call(backward_kernel, out_shape=(jax.ShapeDtypeStruct((1, model...]
  transfers between devices with their start and end apart: 7 -> 7, of which waited for: 3 -> 3; matrix products, arithmetic and copies ran while one was open for 2% -> 2% of each run, Pallas kernels for 51% -> 53%
where the time goes in v14:
time: 44.8 us; the launch traced here: 44.6 us
  Pallas kernels  24.4 us (54%)
  waiting for transfers between devices  9.85 us (22%)
  starting transfers between devices  8.82 us (20%)
  other arithmetic  0.84 us (2%)
  between operations  0.72 us (2%)
    ppermute x7, waiting for transfers between devices, routed(): return lax.ppermute(block, ('seq', 'pipe'), route)  9.85 us
    ppermute x7, starting transfers between devices, routed(): return lax.ppermute(block, ('seq', 'pipe'), route)  8.82 us
    pallas_call x1, Pallas kernels, backward(): pl.pallas_call(backward_kernel, out_shape=(jax.ShapeDtypeStruct((1, model...  8.59 us
    pallas_call x1, Pallas kernels, regroup(): pl.pallas_call(regroup_kernel, out_shape=(pltpu.VMEM(out, weight.dtype),...  8.46 us
    pallas_call x1, Pallas kernels, forward(): pl.pallas_call(forward_kernel, out_shape=(jax.ShapeDtypeStruct((groups, t...  6.47 us
  transfers between devices with their start and end apart: 7, of which 3 were waited for; matrix products, arithmetic and copies ran while one was open for 2% of the time, Pallas kernels for 53%

profile of v14, /device:TPU:1, one launch (start us, length us, event | category | flops | bytes accessed | tf_op | source)
XLA Modules:
  0.0 44.6 jit_solution(3295055159545220405)
XLA Ops:
  0.6 2.1 %collective-permute-start = (bf16[64,3072]{1,0:T(8,128)(2,1)}, bf16[64,3072]{1,0:T(8,128)(2,1)S(1)}, u32[]{:S(2)}, u32[]{:S(2)}) collective-permute-start(bf16[64,3072]{1,0:T(8,128)(2,1)} %bitcast.8), channel_id=1, source_target_pairs={{0,16},{4,20},{8,24},{12,28},{16,0},{20,4},{24,8},{28,12},{1,17},{... | collective-permute-start | bytes 1179656 | tf_op jit(solution)/shard_map/ppermute | solution.py:625
  2.7 0.1 collective-permute-start.3
  2.8 0.0 copy-start.1
  2.8 0.0 copy-start.3
  2.8 0.0 copy-start.4
  2.8 0.0 copy-start.5
  2.8 0.0 copy-start.6
  2.8 8.5 %regroup.1 = (bf16[2,3072,1536]{2,1,0:T(8,128)(2,1)S(1)}, bf16[1536,3072]{1,0:T(8,128)(2,1)S(1)}) custom-call(bf16[3072,8,384]{2,1,0:T(8,128)(2,1)} %bitcast.10), custom_call_target="tpu_custom_call" | custom-call | bytes 37748736 | tf_op jit(solution)/shard_map/regroup/pallas_call | solution.py:283
  11.3 0.5 %collective-permute-done.other_ref = bf16[64,3072]{1,0:T(8,128)(2,1)S(1)} collective-permute-done((bf16[64,3072]{1,0:T(8,128)(2,1)}, bf16[64,3072]{1,0:T(8,128)(2,1)S(1)}, u32[]{:S(2)}, u32[]{:S(2)}) %collective-permute-start) | collective-permute-done | bytes 393248 | tf_op jit(solution)/shard_map/ppermute | solution.py:625
  11.8 0.0 copy-done.1
  11.8 0.0 copy-done.2
  11.8 0.0 copy-done.3
  11.8 0.0 copy-done.4
  11.8 0.0 copy-done.5
  11.8 0.0 copy-done.6
  11.8 0.0 copy-start
  11.8 6.5 %attention_forward.1 = (f32[2,128,1536]{2,1,0:T(8,128)S(1)}, bf16[8,128,128]{2,1,0:T(8,128)(2,1)S(1)}, f32[128,3072]{1,0:T(8,128)S(1)}, bf16[64,3072]{1,0:T(8,12...) custom-call(s32[2,27]{1,0:T(2,128)S(1)} %copy-done.5, s32[2]{0:T(128)S(1)} %copy-done.6, ...), custom_call_target="tpu_custom_call" | custom-call | flops 3221225472 | bytes 25165824 | tf_op jit(solution)/shard_map/attention_forward/pallas_call | solution.py:423
  18.3 4.7 %collective-permute-start.2 = (bf16[64,3072]{1,0:T(8,128)(2,1)S(1)}, bf16[64,3072]{1,0:T(8,128)(2,1)S(1)}, u32[]{:S(2)}, u32[]{:S(2)}) collective-permute-start(bf16[64,3072]{1,0:T(8,128)(2,1)S(1)} %get-tuple-element.21), channel_id=1, source_target_pairs={{0,20},{4,24},{8,28},{12,16},{16,4},{20,8},{24,12},{28,0},{1,21},{... | collective-permute-start | bytes 1179656 | tf_op jit(solution)/shard_map/ppermute | solution.py:625
  23.0 0.0 collective-permute-start.1
  23.0 0.0 collective-permute-done.3.other_ref
  23.1 0.0 copy-done
  23.1 8.6 %attention_backward.1 = (f32[1,1536]{1,0:T(1,128)S(1)}, f32[1,1536]{1,0:T(1,128)S(1)}, bf16[64,3072]{1,0:T(8,128)(2,1)S(1)}, bf16[64,3072]{1,0:T(8,128)(2,1)S(1)}) custom-call(bf16[64,3072]{1,0:T(8,128)(2,1)S(1)} %bitcast.7, bf16[64,3072]{1,0:T(8,128)(2,1)S(1)} %collective-permute-done.3.other_ref, bf16[1024,3072]{1,0:T(8,128)(2,1)S(1)} %get-tuple-element.22.out_weight_ref, ...), custom_call_target="tpu_custom_call" | custom-call | flops 3221225472 | bytes 25165824 | tf_op jit(solution)/shard_map/attention_backward/pallas_call | solution.py:560
  31.7 0.7 %collective-permute-start.4 = (bf16[64,3072]{1,0:T(8,128)(2,1)S(1)}, bf16[64,3072]{1,0:T(8,128)(2,1)S(1)}, u32[]{:S(2)}, u32[]{:S(2)}) collective-permute-start(bf16[64,3072]{1,0:T(8,128)(2,1)S(1)} %get-tuple-element.29), channel_id=1, source_target_pairs={{0,28},{4,16},{8,20},{12,24},{16,12},{20,0},{24,4},{28,8},{1,29},{... | collective-permute-start | bytes 1179656 | tf_op jit(solution)/shard_map/ppermute | solution.py:625
  32.4 0.0 collective-permute-start.5
  32.4 0.0 collective-permute-done.2
  32.4 0.0 collective-permute-done.1
  32.4 0.8 %add_convert_fusion = bf16[64,3072]{1,0:T(8,128)(2,1)} fusion(bf16[64,3072]{1,0:T(8,128)(2,1)S(1)} %collective-permute-done.2, bf16[64,3072]{1,0:T(8,128)(2,1)S(1)} %collective-permute-done.1), kind=kLoop, calls=%fused_computation | loop fusion | flops 786432 | bytes 1179648 | tf_op jit(solution)/shard_map/convert_element_type | solution.py:673
  33.2 1.2 %collective-permute-start.6 = (f32[1,1536]{1,0:T(1,128)S(1)}, f32[1,1536]{1,0:T(1,128)S(1)}, u32[]{:S(2)}, u32[]{:S(2)}) collective-permute-start(f32[1,1536]{1,0:T(1,128)S(1)} %get-tuple-element.32), channel_id=1, source_target_pairs={{0,16},{4,20},{8,24},{12,28},{16,0},{20,4},{24,8},{28,12},{1,17},{... | collective-permute-start | bytes 18440 | tf_op jit(solution)/shard_map/ppermute | solution.py:625
  34.4 8.6 %collective-permute-done.4.sent_ref = bf16[64,3072]{1,0:T(8,128)(2,1)S(1)} collective-permute-done((bf16[64,3072]{1,0:T(8,128)(2,1)S(1)}, bf16[64,3072]{1,0:T(8,128)(2,1)S(1)}, u32[]{:S(2)}, u32[]{:S(2)}) %collective-permute-start.4) | collective-permute-done | bytes 393248 | tf_op jit(solution)/shard_map/ppermute | solution.py:625
  43.0 0.7 %collective-permute-done.5.kept_ref = bf16[64,3072]{1,0:T(8,128)(2,1)S(1)} collective-permute-done((bf16[64,3072]{1,0:T(8,128)(2,1)S(1)}, bf16[64,3072]{1,0:T(8,128)(2,1)S(1)}, u32[]{:S(2)}, u32[]{:S(2)}) %collective-permute-start.5) | collective-permute-done | bytes 393248 | tf_op jit(solution)/shard_map/ppermute | solution.py:625
  43.8 0.0 collective-permute-done.6.gate_sent_ref
  43.8 0.8 %sums.1 = (bf16[64,3072]{1,0:T(8,128)(2,1)}, f32[1,1536]{1,0:T(1,128)}) custom-call(bf16[64,3072]{1,0:T(8,128)(2,1)S(1)} %collective-permute-done.4.sent_ref, bf16[64,3072]{1,0:T(8,128)(2,1)S(1)} %collective-permute-done.5.kept_ref, f32[1,1536]{1,0:T(1,128)S(1)} %get-tuple-element.31.gate_kept_ref, f32[1,1536]{1,0:T(1,128)S(1)} %collective-permute-done.6.gate_sent_ref), custom_call_target="tpu_custom_call" | custom-call | tf_op jit(solution)/shard_map/sums/pallas_call | solution.py:605
  (1 shorter events, 0.0 us)
Async XLA Ops:
  0.6 11.2 %collective-permute-start = (bf16[64,3072]{1,0:T(8,128)(2,1)}, bf16[64,3072]{1,0:T(8,128)(2,1)S(1)}, u32[]{:S(2)}, u32[]{:S(2)}) collective-permute-start(bf16[64,3072]{1,0:T(8,128)(2,1)} %bitcast.8), channel_id=1, source_target_pairs={{0,16},{4,20},{8,24},{12,28},{16,0},{20,4},{24,8},{28,12},{1,17},{... | collective-permute-start | bytes 1179656 | tf_op jit(solution)/shard_map/ppermute | solution.py:625
  2.7 20.3 %collective-permute-start.3 = (bf16[64,3072]{1,0:T(8,128)(2,1)}, bf16[64,3072]{1,0:T(8,128)(2,1)S(1)}, u32[]{:S(2)}, u32[]{:S(2)}) collective-permute-start(bf16[64,3072]{1,0:T(8,128)(2,1)} %bitcast.6), channel_id=1, source_target_pairs={{0,16},{4,20},{8,24},{12,28},{16,0},{20,4},{24,8},{28,12},{1,17},{... | collective-permute-start | bytes 1179656 | tf_op jit(solution)/shard_map/ppermute | solution.py:625
  2.8 9.0 %copy-start.1 = (bf16[1,64,3072]{2,1,0:T(8,128)(2,1)S(1)}, bf16[1,64,3072]{2,1,0:T(8,128)(2,1)}, u32[]{:S(2)}) copy-start(bf16[1,64,3072]{2,1,0:T(8,128)(2,1)} %param.9) | copy-start | bytes 1179652
  2.8 9.0 %copy-start.2 = (f32[1,3072]{1,0:T(1,128)S(1)}, f32[1,3072]{1,0:T(1,128)}, u32[]{:S(2)}) copy-start(f32[1,3072]{1,0:T(1,128)} %gate_ref.3) | copy-start | bytes 36868
  2.8 9.0 %copy-start.3 = (f32[1,128]{1,0:T(1,128)S(1)}, f32[1,128]{1,0:T(1,128)}, u32[]{:S(2)}) copy-start(f32[1,128]{1,0:T(1,128)} %query_gain_ref.3) | copy-start | bytes 1540
  2.8 9.0 %copy-start.4 = (f32[1,128]{1,0:T(1,128)S(1)}, f32[1,128]{1,0:T(1,128)}, u32[]{:S(2)}) copy-start(f32[1,128]{1,0:T(1,128)} %key_gain_ref.3) | copy-start | bytes 1540
  2.8 9.0 %copy-start.5 = (s32[2,27]{1,0:T(2,128)S(1)}, s32[2,27]{1,0:T(2,128)}, u32[]{:S(2)}) copy-start(s32[2,27]{1,0:T(2,128)} %neighbours_ref.1) | copy-start | bytes 652
  2.8 9.0 %copy-start.6 = (s32[2]{0:T(128)S(1)}, s32[2]{0:T(128)}, u32[]{:S(2)}) copy-start(s32[2]{0:T(128)} %tile_slot_ref.1) | copy-start | bytes 28
  11.8 11.2 %copy-start = (bf16[1,64,3072]{2,1,0:T(8,128)(2,1)S(1)}, bf16[1,64,3072]{2,1,0:T(8,128)(2,1)}, u32[]{:S(2)}) copy-start(bf16[1,64,3072]{2,1,0:T(8,128)(2,1)} %param.10) | copy-start | bytes 1179652
  18.3 14.1 %collective-permute-start.2 = (bf16[64,3072]{1,0:T(8,128)(2,1)S(1)}, bf16[64,3072]{1,0:T(8,128)(2,1)S(1)}, u32[]{:S(2)}, u32[]{:S(2)}) collective-permute-start(bf16[64,3072]{1,0:T(8,128)(2,1)S(1)} %get-tuple-element.21), channel_id=1, source_target_pairs={{0,20},{4,24},{8,28},{12,16},{16,4},{20,8},{24,12},{28,0},{1,21},{... | collective-permute-start | bytes 1179656 | tf_op jit(solution)/shard_map/ppermute | solution.py:625
  23.0 9.4 %collective-permute-start.1 = (bf16[64,3072]{1,0:T(8,128)(2,1)S(1)}, bf16[64,3072]{1,0:T(8,128)(2,1)S(1)}, u32[]{:S(2)}, u32[]{:S(2)}) collective-permute-start(bf16[64,3072]{1,0:T(8,128)(2,1)S(1)} %get-tuple-element.20), channel_id=1, source_target_pairs={{0,4},{4,8},{8,12},{12,0},{16,20},{20,24},{24,28},{28,16},{1,5},{5... | collective-permute-start | bytes 1179656 | tf_op jit(solution)/shard_map/ppermute | solution.py:625
  31.7 11.4 %collective-permute-start.4 = (bf16[64,3072]{1,0:T(8,128)(2,1)S(1)}, bf16[64,3072]{1,0:T(8,128)(2,1)S(1)}, u32[]{:S(2)}, u32[]{:S(2)}) collective-permute-start(bf16[64,3072]{1,0:T(8,128)(2,1)S(1)} %get-tuple-element.29), channel_id=1, source_target_pairs={{0,28},{4,16},{8,20},{12,24},{16,12},{20,0},{24,4},{28,8},{1,29},{... | collective-permute-start | bytes 1179656 | tf_op jit(solution)/shard_map/ppermute | solution.py:625
  32.4 11.4 %collective-permute-start.5 = (bf16[64,3072]{1,0:T(8,128)(2,1)S(1)}, bf16[64,3072]{1,0:T(8,128)(2,1)S(1)}, u32[]{:S(2)}, u32[]{:S(2)}) collective-permute-start(bf16[64,3072]{1,0:T(8,128)(2,1)S(1)} %get-tuple-element.30), channel_id=1, source_target_pairs={{0,12},{4,0},{8,4},{12,8},{16,28},{20,16},{24,20},{28,24},{1,13},{... | collective-permute-start | bytes 1179656 | tf_op jit(solution)/shard_map/ppermute | solution.py:625
  33.2 10.5 %collective-permute-start.6 = (f32[1,1536]{1,0:T(1,128)S(1)}, f32[1,1536]{1,0:T(1,128)S(1)}, u32[]{:S(2)}, u32[]{:S(2)}) collective-permute-start(f32[1,1536]{1,0:T(1,128)S(1)} %get-tuple-element.32), channel_id=1, source_target_pairs={{0,16},{4,20},{8,24},{12,28},{16,0},{20,4},{24,8},{28,12},{1,17},{... | collective-permute-start | bytes 18440 | tf_op jit(solution)/shard_map/ppermute | solution.py:625

commit v15 on v14

--- a/solution.py
+++ b/solution.py
@@ -14,6 +14,7 @@
 BF16 = jnp.bfloat16
 MIB = 1024 * 1024
 GROUP = 4
+TURNED = 6
 
 
 def passed_along(block, axis, distance):
@@ -269,22 +270,23 @@
         for head in range(heads):
             left = (head % GROUP) * width
             out_ref[head // GROUP, part(step), left : left + width] = by_head[head]
-            if head >= heads - GROUP:
-                turned_ref[left : left + width, part(step)] = by_head[head].T
+            above = (head + 1) * width - (heads * width - turned_ref.shape[0])
+            if above > 0:
+                turned_ref[above - width : above, part(step)] = by_head[head].T
 
         @pl.when(step + slots < steps)
         def _():
             read(step + slots, slot).start()
 
 
-def regroup(weight, rows, slots):
+def regroup(weight, rows, slots, turned):
     depth, heads, width = weight.shape
     out = (heads // GROUP, depth, GROUP * width)
     return pl.pallas_call(
         regroup_kernel,
         out_shape=(
             pltpu.VMEM(out, weight.dtype),
-            pltpu.VMEM((out[2], out[1]), weight.dtype),
+            pltpu.VMEM((turned * width, depth), weight.dtype),
         ),
         in_specs=[pl.BlockSpec(memory_space=pl.ANY)],
         out_specs=(pl.BlockSpec(memory_space=pltpu.VMEM),) * 2,
@@ -292,7 +294,7 @@
             pltpu.VMEM((slots, rows, heads, width), weight.dtype),
             pltpu.SemaphoreType.DMA((slots,)),
         ],
-        compiler_params=params(9),
+        compiler_params=params(6),
         cost_estimate=pl.CostEstimate(
             flops=0, bytes_accessed=4 * depth * heads * width, transcendentals=0
         ),
@@ -333,6 +335,7 @@
     key_gain_ref,
     gate_ref,
     projected_ref,
+    inverse_ref,
     probs_ref,
     attention_ref,
     kept_ref,
@@ -374,10 +377,16 @@
         attended = []
         for head in range(GROUP):
             left = head * 3 * width
-            _, _, queries = normed(projected_ref[group, :, left : left + width], query_gain_ref[...])
-            left += width
-            _, _, keys = normed(projected_ref[group, :, left : left + width], key_gain_ref[...])
-            left += width
+            operands = []
+            for index, gain_ref in enumerate((query_gain_ref, key_gain_ref)):
+                part = slice(left, left + width)
+                unit, inverse, operand = normed(projected_ref[group, :, part], gain_ref[...])
+                projected_ref[group, :, part] = unit
+                place = 2 * head + index
+                inverse_ref[group, :, place : place + 1] = inverse
+                operands.append(operand)
+                left += width
+            queries, keys = operands
             value = projected_ref[group, :, left : left + width].astype(BF16)
             scores = dot_nt(queries, keys) * (1.0 / math.sqrt(width)) + bias
             row_max = jnp.max(scores, axis=-1, keepdims=True)
@@ -424,6 +433,7 @@
         forward_kernel,
         out_shape=(
             jax.ShapeDtypeStruct((groups, tokens, wide), F32),
+            jax.ShapeDtypeStruct((groups, tokens, 2 * GROUP), F32),
             jax.ShapeDtypeStruct((GROUP * groups, tokens, tokens), BF16),
             jax.ShapeDtypeStruct((tokens, model), F32),
             jax.ShapeDtypeStruct((local, model), BF16),
@@ -431,12 +441,12 @@
             pltpu.VMEM(out_weight.shape, BF16),
         ),
         in_specs=[smem, smem, vmem, vmem, vmem, hbm, vmem, vmem, vmem],
-        out_specs=(vmem,) * 6,
+        out_specs=(vmem,) * 7,
         scratch_shapes=[
             pltpu.VMEM((tokens, model), BF16),
             pltpu.SemaphoreType.DMA((groups,)),
         ],
-        compiler_params=params(8),
+        compiler_params=params(6),
         cost_estimate=pl.CostEstimate(
             flops=2 * tokens * (weight.size + out_weight.size),
             bytes_accessed=2 * (weight.size + out_weight.size),
@@ -448,13 +458,22 @@
 
 def input_grad(grad_ref, weight_ref, turned_ref, own_ref, kept_ref, sent_ref):
     local, model = own_ref.shape
-    last = grad_ref.shape[0] - 1
+    groups, _, wide = grad_ref.shape
+    streamed = groups * wide - turned_ref.shape[0]
     block = 512
     for start in range(0, model, block):
         part = slice(start, start + block)
-        total = dot_nn(grad_ref[last], turned_ref[:, part])
-        for group in range(last):
-            total += dot_nt(weight_ref[group, part, :], grad_ref[group]).T
+        total = None
+        for group in range(groups):
+            first = group * wide
+            cut = min(max(streamed - first, 0), wide)
+            if cut < wide:
+                rows = slice(first + cut - streamed, first + wide - streamed)
+                product = dot_nn(grad_ref[group, :, cut:], turned_ref[rows, part])
+                total = product if total is None else total + product
+            if cut > 0:
+                product = dot_nt(weight_ref[group, part, :cut], grad_ref[group, :, :cut]).T
+                total = product if total is None else total + product
         kept_ref[:, part] = (own_ref[:, part].astype(F32) + total[:local]).astype(BF16)
         sent_ref[:, part] = total[local:].astype(BF16)
 
@@ -466,6 +485,7 @@
     weight_ref,
     turned_ref,
     projected_ref,
+    inverse_ref,
     probs_ref,
     attention_ref,
     query_gain_ref,
@@ -508,8 +528,11 @@
         key_part = slice(left + width, left + 2 * width)
         value_part = slice(left + 2 * width, left + 3 * width)
         query_gain, key_gain = query_gain_ref[...], key_gain_ref[...]
-        query_unit, query_inverse, queries = normed(projected_ref[group, :, query_part], query_gain)
-        key_unit, key_inverse, keys = normed(projected_ref[group, :, key_part], key_gain)
+        query_unit, key_unit = projected_ref[group, :, query_part], projected_ref[group, :, key_part]
+        query_inverse = inverse_ref[group, :, 2 * head : 2 * head + 1]
+        key_inverse = inverse_ref[group, :, 2 * head + 1 : 2 * head + 2]
+        queries = (query_unit * query_gain).astype(BF16)
+        keys = (key_unit * key_gain).astype(BF16)
         value = projected_ref[group, :, value_part].astype(BF16)
         grad = attended_grad_ref[group, :, head * width : (head + 1) * width]
         probs = probs_ref[GROUP * group + head]
@@ -544,6 +567,7 @@
     weight,
     turned,
     projected,
+    inverse,
     probs,
     attention,
     query_gain,
@@ -565,7 +589,7 @@
             jax.ShapeDtypeStruct((local, model), BF16),
             jax.ShapeDtypeStruct((local, model), BF16),
         ),
-        in_specs=[vmem] * 11,
+        in_specs=[vmem] * 12,
         out_specs=(vmem,) * 4,
         scratch_shapes=[
             pltpu.VMEM((groups, tokens, wide), BF16),
@@ -573,7 +597,7 @@
             pltpu.VMEM((groups, tokens, GROUP * head_dim), BF16),
             pltpu.VMEM((1, model), F32),
         ],
-        compiler_params=params(8),
+        compiler_params=params(6),
         cost_estimate=pl.CostEstimate(
             flops=2 * tokens * (out_weight.size + weight.size),
             bytes_accessed=2 * (out_weight.size + weight.size),
@@ -587,6 +611,7 @@
         weight,
         turned,
         projected,
+        inverse,
         probs,
         attention,
         query_gain,
@@ -640,9 +665,9 @@
     upstream = output_grad[0]
     out_local = out_weight[0]
     other_stream = routed(stream, 1, 0)
-    weight, turned_weight = regroup(qkv_weight[0], 128, 6)
+    weight, turned_weight = regroup(qkv_weight[0], 128, 4, TURNED)
     other_upstream = routed(upstream, 1, 0)
-    projected, probs, attention, kept, sent, out_local = forward(
+    projected, inverse, probs, attention, kept, sent, out_local = forward(
         neighbours,
         tile_slot,
         stream,
@@ -662,6 +687,7 @@
         weight,
         turned_weight,
         projected,
+        inverse,
         probs,
         attention,
         query_gain,

time: 44.8 us -> 44.6 us (level)
  Pallas kernels: 24.4 us -> 25.3 us
  starting transfers between devices: 8.82 us -> 8.15 us
  waiting for transfers between devices: 9.85 us -> 9.38 us
    pallas_call x1, Pallas kernels: 8.46 us -> 9.55 us  [regroup(): pl.pallas_call(regroup_kernel, out_shape=(pltpu.VMEM(out, weight.dtype),...]
    ppermute x7, starting transfers between devices: 8.82 us -> 8.15 us  [routed(): return lax.ppermute(block, ('seq', 'pipe'), route)]
    ppermute x7, waiting for transfers between devices: 9.85 us -> 9.38 us  [routed(): return lax.ppermute(block, ('seq', 'pipe'), route)]
  transfers between devices with their start and end apart: 7 -> 7, of which waited for: 3 -> 2; matrix products, arithmetic and copies ran while one was open for 2% -> 2% of each run, Pallas kernels for 53% -> 55%
where the time goes in v15:
time: 44.6 us; the launch traced here: 44.5 us
  Pallas kernels  25.3 us (57%)
  waiting for transfers between devices  9.38 us (21%)
  starting transfers between devices  8.15 us (18%)
  other arithmetic  0.84 us (2%)
  between operations  0.75 us (2%)
    pallas_call x1, Pallas kernels, regroup(): pl.pallas_call(regroup_kernel, out_shape=(pltpu.VMEM(out, weight.dtype),...  9.55 us
    ppermute x7, waiting for transfers between devices, routed(): return lax.ppermute(block, ('seq', 'pipe'), route)  9.38 us
    pallas_call x1, Pallas kernels, backward(): pl.pallas_call(backward_kernel, out_shape=(jax.ShapeDtypeStruct((1, model...  8.46 us
    ppermute x7, starting transfers between devices, routed(): return lax.ppermute(block, ('seq', 'pipe'), route)  8.15 us
    pallas_call x1, Pallas kernels, forward(): pl.pallas_call(forward_kernel, out_shape=(jax.ShapeDtypeStruct((groups, t...  6.44 us
  transfers between devices with their start and end apart: 7, of which 2 were waited for; matrix products, arithmetic and copies ran while one was open for 2% of the time, Pallas kernels for 55%

profile of v15, /device:TPU:1, one launch (start us, length us, event | category | flops | bytes accessed | tf_op | source)
XLA Modules:
  0.0 44.5 jit_solution(4594933851021785747)
XLA Ops:
  0.6 2.1 %collective-permute-start = (bf16[64,3072]{1,0:T(8,128)(2,1)}, bf16[64,3072]{1,0:T(8,128)(2,1)S(1)}, u32[]{:S(2)}, u32[]{:S(2)}) collective-permute-start(bf16[64,3072]{1,0:T(8,128)(2,1)} %bitcast.8), channel_id=1, source_target_pairs={{0,16},{4,20},{8,24},{12,28},{16,0},{20,4},{24,8},{28,12},{1,17},{... | collective-permute-start | bytes 1179656 | tf_op jit(solution)/shard_map/ppermute | solution.py:650
  2.7 0.1 collective-permute-start.3
  2.8 0.0 copy-start.1
  2.8 0.0 copy-start.2
  2.8 0.0 copy-start.3
  2.8 0.0 copy-start.5
  2.8 0.0 copy-start.6
  2.8 9.6 %regroup.1 = (bf16[2,3072,1536]{2,1,0:T(8,128)(2,1)S(1)}, bf16[2304,3072]{1,0:T(8,128)(2,1)S(1)}) custom-call(bf16[3072,8,384]{2,1,0:T(8,128)(2,1)} %bitcast.10), custom_call_target="tpu_custom_call" | custom-call | bytes 37748736 | tf_op jit(solution)/shard_map/regroup/pallas_call | solution.py:285
  12.4 0.0 collective-permute-done.other_ref
  12.4 0.0 copy-done.1
  12.4 0.0 copy-done.2
  12.4 0.0 copy-done.3
  12.5 0.0 copy-done.4
  12.5 0.0 copy-done.5
  12.5 0.0 copy-done.6
  12.5 0.0 copy-start
  12.5 6.4 %attention_forward.1 = (f32[2,128,1536]{2,1,0:T(8,128)S(1)}, f32[2,128,8]{2,1,0:T(8,128)S(1)}, bf16[8,128,128]{2,1,0:T(8,128)(2,1)S(1)}, f32[128,3072]{1,0:T(8,1...) custom-call(s32[2,27]{1,0:T(2,128)S(1)} %copy-done.5, ...), custom_call_target="tpu_custom_call" | custom-call | flops 3221225472 | bytes 25165824 | tf_op jit(solution)/shard_map/attention_forward/pallas_call | solution.py:432
  18.9 4.1 %collective-permute-start.2 = (bf16[64,3072]{1,0:T(8,128)(2,1)S(1)}, bf16[64,3072]{1,0:T(8,128)(2,1)S(1)}, u32[]{:S(2)}, u32[]{:S(2)}) collective-permute-start(bf16[64,3072]{1,0:T(8,128)(2,1)S(1)} %get-tuple-element.22), channel_id=1, source_target_pairs={{0,20},{4,24},{8,28},{12,16},{16,4},{20,8},{24,12},{28,0},{1,21},{... | collective-permute-start | bytes 1179656 | tf_op jit(solution)/shard_map/ppermute | solution.py:650
  23.0 0.0 collective-permute-start.1
  23.0 0.0 collective-permute-done.3.other_ref
  23.0 0.0 copy-done
  23.0 8.5 %attention_backward.1 = (f32[1,1536]{1,0:T(1,128)S(1)}, f32[1,1536]{1,0:T(1,128)S(1)}, bf16[64,3072]{1,0:T(8,128)(2,1)S(1)}, bf16[64,3072]{1,0:T(8,128)(2,1)S(1)}) custom-call(bf16[64,3072]{1,0:T(8,128)(2,1)S(1)} %bitcast.7, bf16[64,3072]{1,0:T(8,128)(2,1)S(1)} %collective-permute-done.3.other_ref, bf16[1024,3072]{1,0:T(8,128)(2,1)S(1)} %get-tuple-element.23.out_weight_ref, ...), custom_call_target="tpu_custom_call" | custom-call | flops 3221225472 | bytes 25165824 | tf_op jit(solution)/shard_map/attention_backward/pallas_call | solution.py:584
  31.5 0.7 %collective-permute-start.4 = (bf16[64,3072]{1,0:T(8,128)(2,1)S(1)}, bf16[64,3072]{1,0:T(8,128)(2,1)S(1)}, u32[]{:S(2)}, u32[]{:S(2)}) collective-permute-start(bf16[64,3072]{1,0:T(8,128)(2,1)S(1)} %get-tuple-element.31), channel_id=1, source_target_pairs={{0,28},{4,16},{8,20},{12,24},{16,12},{20,0},{24,4},{28,8},{1,29},{... | collective-permute-start | bytes 1179656 | tf_op jit(solution)/shard_map/ppermute | solution.py:650
  32.2 0.0 collective-permute-start.5
  32.2 0.0 collective-permute-done.2
  32.2 0.0 collective-permute-done.1
  32.2 0.8 %add_convert_fusion = bf16[64,3072]{1,0:T(8,128)(2,1)} fusion(bf16[64,3072]{1,0:T(8,128)(2,1)S(1)} %collective-permute-done.2, bf16[64,3072]{1,0:T(8,128)(2,1)S(1)} %collective-permute-done.1), kind=kLoop, calls=%fused_computation | loop fusion | flops 786432 | bytes 1179648 | tf_op jit(solution)/shard_map/convert_element_type | solution.py:699
  33.1 1.2 %collective-permute-start.6 = (f32[1,1536]{1,0:T(1,128)S(1)}, f32[1,1536]{1,0:T(1,128)S(1)}, u32[]{:S(2)}, u32[]{:S(2)}) collective-permute-start(f32[1,1536]{1,0:T(1,128)S(1)} %get-tuple-element.34), channel_id=1, source_target_pairs={{0,16},{4,20},{8,24},{12,28},{16,0},{20,4},{24,8},{28,12},{1,17},{... | collective-permute-start | bytes 18440 | tf_op jit(solution)/shard_map/ppermute | solution.py:650
  34.2 8.6 %collective-permute-done.4.sent_ref = bf16[64,3072]{1,0:T(8,128)(2,1)S(1)} collective-permute-done((bf16[64,3072]{1,0:T(8,128)(2,1)S(1)}, bf16[64,3072]{1,0:T(8,128)(2,1)S(1)}, u32[]{:S(2)}, u32[]{:S(2)}) %collective-permute-start.4) | collective-permute-done | bytes 393248 | tf_op jit(solution)/shard_map/ppermute | solution.py:650
  42.9 0.7 %collective-permute-done.5.kept_ref = bf16[64,3072]{1,0:T(8,128)(2,1)S(1)} collective-permute-done((bf16[64,3072]{1,0:T(8,128)(2,1)S(1)}, bf16[64,3072]{1,0:T(8,128)(2,1)S(1)}, u32[]{:S(2)}, u32[]{:S(2)}) %collective-permute-start.5) | collective-permute-done | bytes 393248 | tf_op jit(solution)/shard_map/ppermute | solution.py:650
  43.6 0.0 collective-permute-done.6.gate_sent_ref
  43.6 0.8 %sums.1 = (bf16[64,3072]{1,0:T(8,128)(2,1)}, f32[1,1536]{1,0:T(1,128)}) custom-call(bf16[64,3072]{1,0:T(8,128)(2,1)S(1)} %collective-permute-done.4.sent_ref, bf16[64,3072]{1,0:T(8,128)(2,1)S(1)} %collective-permute-done.5.kept_ref, f32[1,1536]{1,0:T(1,128)S(1)} %get-tuple-element.33.gate_kept_ref, f32[1,1536]{1,0:T(1,128)S(1)} %collective-permute-done.6.gate_sent_ref), custom_call_target="tpu_custom_call" | custom-call | tf_op jit(solution)/shard_map/sums/pallas_call | solution.py:630
  (1 shorter events, 0.0 us)
Async XLA Ops:
  0.6 11.8 %collective-permute-start = (bf16[64,3072]{1,0:T(8,128)(2,1)}, bf16[64,3072]{1,0:T(8,128)(2,1)S(1)}, u32[]{:S(2)}, u32[]{:S(2)}) collective-permute-start(bf16[64,3072]{1,0:T(8,128)(2,1)} %bitcast.8), channel_id=1, source_target_pairs={{0,16},{4,20},{8,24},{12,28},{16,0},{20,4},{24,8},{28,12},{1,17},{... | collective-permute-start | bytes 1179656 | tf_op jit(solution)/shard_map/ppermute | solution.py:650
  2.7 20.3 %collective-permute-start.3 = (bf16[64,3072]{1,0:T(8,128)(2,1)}, bf16[64,3072]{1,0:T(8,128)(2,1)S(1)}, u32[]{:S(2)}, u32[]{:S(2)}) collective-permute-start(bf16[64,3072]{1,0:T(8,128)(2,1)} %bitcast.6), channel_id=1, source_target_pairs={{0,16},{4,20},{8,24},{12,28},{16,0},{20,4},{24,8},{28,12},{1,17},{... | collective-permute-start | bytes 1179656 | tf_op jit(solution)/shard_map/ppermute | solution.py:650
  2.8 9.6 %copy-start.1 = (bf16[1,64,3072]{2,1,0:T(8,128)(2,1)S(1)}, bf16[1,64,3072]{2,1,0:T(8,128)(2,1)}, u32[]{:S(2)}) copy-start(bf16[1,64,3072]{2,1,0:T(8,128)(2,1)} %param.9) | copy-start | bytes 1179652
  2.8 9.6 %copy-start.2 = (f32[1,3072]{1,0:T(1,128)S(1)}, f32[1,3072]{1,0:T(1,128)}, u32[]{:S(2)}) copy-start(f32[1,3072]{1,0:T(1,128)} %gate_ref.3) | copy-start | bytes 36868
  2.8 9.6 %copy-start.3 = (f32[1,128]{1,0:T(1,128)S(1)}, f32[1,128]{1,0:T(1,128)}, u32[]{:S(2)}) copy-start(f32[1,128]{1,0:T(1,128)} %query_gain_ref.3) | copy-start | bytes 1540
  2.8 9.6 %copy-start.4 = (f32[1,128]{1,0:T(1,128)S(1)}, f32[1,128]{1,0:T(1,128)}, u32[]{:S(2)}) copy-start(f32[1,128]{1,0:T(1,128)} %key_gain_ref.3) | copy-start | bytes 1540
  2.8 9.6 %copy-start.5 = (s32[2,27]{1,0:T(2,128)S(1)}, s32[2,27]{1,0:T(2,128)}, u32[]{:S(2)}) copy-start(s32[2,27]{1,0:T(2,128)} %neighbours_ref.1) | copy-start | bytes 652
  2.8 9.6 %copy-start.6 = (s32[2]{0:T(128)S(1)}, s32[2]{0:T(128)}, u32[]{:S(2)}) copy-start(s32[2]{0:T(128)} %tile_slot_ref.1) | copy-start | bytes 28
  12.5 10.5 %copy-start = (bf16[1,64,3072]{2,1,0:T(8,128)(2,1)S(1)}, bf16[1,64,3072]{2,1,0:T(8,128)(2,1)}, u32[]{:S(2)}) copy-start(bf16[1,64,3072]{2,1,0:T(8,128)(2,1)} %param.10) | copy-start | bytes 1179652
  18.9 13.3 %collective-permute-start.2 = (bf16[64,3072]{1,0:T(8,128)(2,1)S(1)}, bf16[64,3072]{1,0:T(8,128)(2,1)S(1)}, u32[]{:S(2)}, u32[]{:S(2)}) collective-permute-start(bf16[64,3072]{1,0:T(8,128)(2,1)S(1)} %get-tuple-element.22), channel_id=1, source_target_pairs={{0,20},{4,24},{8,28},{12,16},{16,4},{20,8},{24,12},{28,0},{1,21},{... | collective-permute-start | bytes 1179656 | tf_op jit(solution)/shard_map/ppermute | solution.py:650
  23.0 9.2 %collective-permute-start.1 = (bf16[64,3072]{1,0:T(8,128)(2,1)S(1)}, bf16[64,3072]{1,0:T(8,128)(2,1)S(1)}, u32[]{:S(2)}, u32[]{:S(2)}) collective-permute-start(bf16[64,3072]{1,0:T(8,128)(2,1)S(1)} %get-tuple-element.21), channel_id=1, source_target_pairs={{0,4},{4,8},{8,12},{12,0},{16,20},{20,24},{24,28},{28,16},{1,5},{5... | collective-permute-start | bytes 1179656 | tf_op jit(solution)/shard_map/ppermute | solution.py:650
  31.5 11.4 %collective-permute-start.4 = (bf16[64,3072]{1,0:T(8,128)(2,1)S(1)}, bf16[64,3072]{1,0:T(8,128)(2,1)S(1)}, u32[]{:S(2)}, u32[]{:S(2)}) collective-permute-start(bf16[64,3072]{1,0:T(8,128)(2,1)S(1)} %get-tuple-element.31), channel_id=1, source_target_pairs={{0,28},{4,16},{8,20},{12,24},{16,12},{20,0},{24,4},{28,8},{1,29},{... | collective-permute-start | bytes 1179656 | tf_op jit(solution)/shard_map/ppermute | solution.py:650
  32.2 11.4 %collective-permute-start.5 = (bf16[64,3072]{1,0:T(8,128)(2,1)S(1)}, bf16[64,3072]{1,0:T(8,128)(2,1)S(1)}, u32[]{:S(2)}, u32[]{:S(2)}) collective-permute-start(bf16[64,3072]{1,0:T(8,128)(2,1)S(1)} %get-tuple-element.32), channel_id=1, source_target_pairs={{0,12},{4,0},{8,4},{12,8},{16,28},{20,16},{24,20},{28,24},{1,13},{... | collective-permute-start | bytes 1179656 | tf_op jit(solution)/shard_map/ppermute | solution.py:650
  33.1 10.5 %collective-permute-start.6 = (f32[1,1536]{1,0:T(1,128)S(1)}, f32[1,1536]{1,0:T(1,128)S(1)}, u32[]{:S(2)}, u32[]{:S(2)}) collective-permute-start(f32[1,1536]{1,0:T(1,128)S(1)} %get-tuple-element.34), channel_id=1, source_target_pairs={{0,16},{4,20},{8,24},{12,28},{16,0},{20,4},{24,8},{28,12},{1,17},{... | collective-permute-start | bytes 18440 | tf_op jit(solution)/shard_map/ppermute | solution.py:650

commit v16 on v15

--- a/solution.py
+++ b/solution.py
@@ -374,26 +374,28 @@
         projected_ref[group] = dot_nn(tokens_ref[...], weight_ref[group])
 
     def attend(group):
+        heads = range(GROUP)
+        operands = []
+        for place in range(2 * GROUP):
+            gain_ref = (query_gain_ref, key_gain_ref)[place % 2]
+            left = (3 * (place // 2) + place % 2) * width
+            part = slice(left, left + width)
+            unit, inverse, operand = normed(projected_ref[group, :, part], gain_ref[...])
+            projected_ref[group, :, part] = unit
+            inverse_ref[group, :, place : place + 1] = inverse
+            operands.append(operand)
+        scale_factor = 1.0 / math.sqrt(width)
+        scores = [dot_nt(operands[2 * h], operands[2 * h + 1]) * scale_factor + bias for h in heads]
+        tops = [jnp.max(scores[h], axis=-1, keepdims=True) for h in heads]
+        weights = [jnp.exp(scores[h] - tops[h]) for h in heads]
+        sums = [jnp.sum(weights[h], axis=-1, keepdims=True) for h in heads]
+        probs = [(weights[h] / sums[h]).astype(BF16) for h in heads]
         attended = []
-        for head in range(GROUP):
-            left = head * 3 * width
-            operands = []
-            for index, gain_ref in enumerate((query_gain_ref, key_gain_ref)):
-                part = slice(left, left + width)
-                unit, inverse, operand = normed(projected_ref[group, :, part], gain_ref[...])
-                projected_ref[group, :, part] = unit
-                place = 2 * head + index
-                inverse_ref[group, :, place : place + 1] = inverse
-                operands.append(operand)
-                left += width
-            queries, keys = operands
+        for h in heads:
+            probs_ref[GROUP * group + h] = probs[h]
+            left = (3 * h + 2) * width
             value = projected_ref[group, :, left : left + width].astype(BF16)
-            scores = dot_nt(queries, keys) * (1.0 / math.sqrt(width)) + bias
-            row_max = jnp.max(scores, axis=-1, keepdims=True)
-            weights = jnp.exp(scores - row_max)
-            probs = (weights / jnp.sum(weights, axis=-1, keepdims=True)).astype(BF16)
-            probs_ref[GROUP * group + head] = probs
-            attended.append(dot_nn(probs, value).astype(BF16))
+            attended.append(dot_nn(probs[h], value).astype(BF16))
         return jnp.concatenate(attended, axis=1)
 
     def share(group, attended):
@@ -522,41 +524,54 @@
         product = dot_nt(scaled_ref[...], out_weight_ref[part, :])
         attended_grad_ref[group] = product.astype(BF16)
 
-    def attend_backward(group, head):
-        left = head * 3 * width
-        query_part = slice(left, left + width)
-        key_part = slice(left + width, left + 2 * width)
-        value_part = slice(left + 2 * width, left + 3 * width)
+    def attend_backward(group):
+        heads = range(GROUP)
         query_gain, key_gain = query_gain_ref[...], key_gain_ref[...]
-        query_unit, key_unit = projected_ref[group, :, query_part], projected_ref[group, :, key_part]
-        query_inverse = inverse_ref[group, :, 2 * head : 2 * head + 1]
-        key_inverse = inverse_ref[group, :, 2 * head + 1 : 2 * head + 2]
-        queries = (query_unit * query_gain).astype(BF16)
-        keys = (key_unit * key_gain).astype(BF16)
-        value = projected_ref[group, :, value_part].astype(BF16)
-        grad = attended_grad_ref[group, :, head * width : (head + 1) * width]
-        probs = probs_ref[GROUP * group + head]
-        probs_wide = probs.astype(F32)
-        grad_ref[group, :, value_part] = dot_tn(probs, grad).astype(BF16)
-        prob_grad = dot_nt(grad, value)
-        row_delta = jnp.sum(probs_wide * prob_grad, axis=-1, keepdims=True)
         scale_factor = 1.0 / math.sqrt(width)
-        score_grad = (probs_wide * (prob_grad - row_delta) * scale_factor).astype(BF16)
-        query_scaled = dot_nn(score_grad, keys) * query_gain
-        key_scaled = dot_tn(score_grad, queries) * key_gain
-        query_mean = jnp.mean(query_scaled * query_unit, axis=-1, keepdims=True)
-        key_mean = jnp.mean(key_scaled * key_unit, axis=-1, keepdims=True)
-        grad_ref[group, :, query_part] = (
-            (query_scaled - query_unit * query_mean) * query_inverse
-        ).astype(BF16)
-        grad_ref[group, :, key_part] = ((key_scaled - key_unit * key_mean) * key_inverse).astype(BF16)
+
+        def part(head, index):
+            left = (3 * head + index) * width
+            return slice(left, left + width)
+
+        def inverse(head, index):
+            return inverse_ref[group, :, 2 * head + index : 2 * head + index + 1]
+
+        grads = [attended_grad_ref[group, :, h * width : (h + 1) * width] for h in heads]
+        values = [projected_ref[group, :, part(h, 2)].astype(BF16) for h in heads]
+        prob_grads = [dot_nt(grads[h], values[h]) for h in heads]
+        for h in heads:
+            product = dot_tn(probs_ref[GROUP * group + h], grads[h])
+            grad_ref[group, :, part(h, 2)] = product.astype(BF16)
+        wide = [probs_ref[GROUP * group + h].astype(F32) for h in heads]
+        deltas = [jnp.sum(wide[h] * prob_grads[h], axis=-1, keepdims=True) for h in heads]
+        score_grads = [
+            (wide[h] * (prob_grads[h] - deltas[h]) * scale_factor).astype(BF16) for h in heads
+        ]
+        units = [[projected_ref[group, :, part(h, index)] for index in range(2)] for h in heads]
+        keys = [(units[h][1] * key_gain).astype(BF16) for h in heads]
+        queries = [(units[h][0] * query_gain).astype(BF16) for h in heads]
+        scaled = [
+            [
+                dot_nn(score_grads[h], keys[h]) * query_gain,
+                dot_tn(score_grads[h], queries[h]) * key_gain,
+            ]
+            for h in heads
+        ]
+        means = [
+            [jnp.mean(scaled[h][i] * units[h][i], axis=-1, keepdims=True) for i in range(2)]
+            for h in heads
+        ]
+        for h in heads:
+            for i in range(2):
+                grad_ref[group, :, part(h, i)] = (
+                    (scaled[h][i] - units[h][i] * means[h][i]) * inverse(h, i)
+                ).astype(BF16)
 
     attended_grad(0)
     for group in range(groups):
         if group + 1 < groups:
             attended_grad(group + 1)
-        for head in range(GROUP):
-            attend_backward(group, head)
+        attend_backward(group)
     input_grad(grad_ref, weight_ref, turned_ref, own_ref, kept_ref, sent_ref)
 
 

time: 44.6 us -> 41.9 us (0.939)
  Pallas kernels: 25.3 us -> 22.4 us
  waiting for transfers between devices: 9.38 us -> 10.2 us
  starting transfers between devices: 8.15 us -> 7.49 us
    pallas_call x1, Pallas kernels: 8.46 us -> 6.61 us  [backward(): pl.pallas_call(backward_kernel, out_shape=(jax.ShapeDtypeStruct((1, model...]
    pallas_call x1, Pallas kernels: 6.44 us -> 5.38 us  [forward(): pl.pallas_call(forward_kernel, out_shape=(jax.ShapeDtypeStruct((groups, t...]
    ppermute x7, waiting for transfers between devices: 9.38 us -> 10.2 us  [routed(): return lax.ppermute(block, ('seq', 'pipe'), route)]
    ppermute x7, starting transfers between devices: 8.15 us -> 7.49 us  [routed(): return lax.ppermute(block, ('seq', 'pipe'), route)]
  transfers between devices with their start and end apart: 7 -> 7, of which waited for: 2 -> 4; matrix products, arithmetic and copies ran while one was open for 2% -> 2% of each run, Pallas kernels for 55% -> 52%
where the time goes in v16:
time: 41.9 us; the launch traced here: 41.7 us
  Pallas kernels  22.4 us (53%)
  waiting for transfers between devices  10.2 us (24%)
  starting transfers between devices  7.49 us (18%)
  other arithmetic  0.84 us (2%)
  between operations  0.75 us (2%)
    ppermute x7, waiting for transfers between devices, routed(): return lax.ppermute(block, ('seq', 'pipe'), route)  10.2 us
    pallas_call x1, Pallas kernels, regroup(): pl.pallas_call(regroup_kernel, out_shape=(pltpu.VMEM(out, weight.dtype),...  9.55 us
    ppermute x7, starting transfers between devices, routed(): return lax.ppermute(block, ('seq', 'pipe'), route)  7.49 us
    pallas_call x1, Pallas kernels, backward(): pl.pallas_call(backward_kernel, out_shape=(jax.ShapeDtypeStruct((1, model...  6.61 us
    pallas_call x1, Pallas kernels, forward(): pl.pallas_call(forward_kernel, out_shape=(jax.ShapeDtypeStruct((groups, t...  5.38 us
    pallas_call x1, Pallas kernels, sums(): pl.pallas_call(sums_kernel, out_shape=(jax.ShapeDtypeStruct(kept.shape, B...  0.84 us
  transfers between devices with their start and end apart: 7, of which 4 were waited for; matrix products, arithmetic and copies ran while one was open for 2% of the time, Pallas kernels for 52%

profile of v16, /device:TPU:1, one launch (start us, length us, event | category | flops | bytes accessed | tf_op | source)
XLA Modules:
  0.0 41.7 jit_solution(16809555565788365787)
XLA Ops:
  0.6 2.1 %collective-permute-start = (bf16[64,3072]{1,0:T(8,128)(2,1)}, bf16[64,3072]{1,0:T(8,128)(2,1)S(1)}, u32[]{:S(2)}, u32[]{:S(2)}) collective-permute-start(bf16[64,3072]{1,0:T(8,128)(2,1)} %bitcast.8), channel_id=1, source_target_pairs={{0,16},{4,20},{8,24},{12,28},{16,0},{20,4},{24,8},{28,12},{1,17},{... | collective-permute-start | bytes 1179656 | tf_op jit(solution)/shard_map/ppermute | solution.py:665
  2.7 0.1 collective-permute-start.3
  2.8 0.0 copy-start.1
  2.8 0.0 copy-start.3
  2.8 0.0 copy-start.4
  2.8 0.0 copy-start.5
  2.8 0.0 copy-start.6
  2.8 9.6 %regroup.1 = (bf16[2,3072,1536]{2,1,0:T(8,128)(2,1)S(1)}, bf16[2304,3072]{1,0:T(8,128)(2,1)S(1)}) custom-call(bf16[3072,8,384]{2,1,0:T(8,128)(2,1)} %bitcast.10), custom_call_target="tpu_custom_call" | custom-call | bytes 37748736 | tf_op jit(solution)/shard_map/regroup/pallas_call | solution.py:285
  12.4 0.0 collective-permute-done.other_ref
  12.4 0.0 copy-done.1
  12.4 0.0 copy-done.2
  12.4 0.0 copy-done.3
  12.5 0.0 copy-done.4
  12.5 0.0 copy-done.5
  12.5 0.0 copy-done.6
  12.5 0.0 copy-start
  12.5 5.4 %attention_forward.1 = (f32[2,128,1536]{2,1,0:T(8,128)S(1)}, f32[2,128,8]{2,1,0:T(8,128)S(1)}, bf16[8,128,128]{2,1,0:T(8,128)(2,1)S(1)}, f32[128,3072]{1,0:T(8,1...) custom-call(s32[2,27]{1,0:T(2,128)S(1)} %copy-done.5, ...), custom_call_target="tpu_custom_call" | custom-call | flops 3221225472 | bytes 25165824 | tf_op jit(solution)/shard_map/attention_forward/pallas_call | solution.py:434
  17.9 4.1 %collective-permute-start.2 = (bf16[64,3072]{1,0:T(8,128)(2,1)S(1)}, bf16[64,3072]{1,0:T(8,128)(2,1)S(1)}, u32[]{:S(2)}, u32[]{:S(2)}) collective-permute-start(bf16[64,3072]{1,0:T(8,128)(2,1)S(1)} %get-tuple-element.22), channel_id=1, source_target_pairs={{0,20},{4,24},{8,28},{12,16},{16,4},{20,8},{24,12},{28,0},{1,21},{... | collective-permute-start | bytes 1179656 | tf_op jit(solution)/shard_map/ppermute | solution.py:665
  21.9 0.0 collective-permute-start.1
  22.0 0.0 collective-permute-done.3.other_ref
  22.0 0.0 copy-done
  22.0 6.6 %attention_backward.1 = (f32[1,1536]{1,0:T(1,128)S(1)}, f32[1,1536]{1,0:T(1,128)S(1)}, bf16[64,3072]{1,0:T(8,128)(2,1)S(1)}, bf16[64,3072]{1,0:T(8,128)(2,1)S(1)}) custom-call(bf16[64,3072]{1,0:T(8,128)(2,1)S(1)} %bitcast.7, bf16[64,3072]{1,0:T(8,128)(2,1)S(1)} %collective-permute-done.3.other_ref, bf16[1024,3072]{1,0:T(8,128)(2,1)S(1)} %get-tuple-element.23.out_weight_ref, ...), custom_call_target="tpu_custom_call" | custom-call | flops 3221225472 | bytes 25165824 | tf_op jit(solution)/shard_map/attention_backward/pallas_call | solution.py:599
  28.6 0.9 %collective-permute-start.4 = (bf16[64,3072]{1,0:T(8,128)(2,1)S(1)}, bf16[64,3072]{1,0:T(8,128)(2,1)S(1)}, u32[]{:S(2)}, u32[]{:S(2)}) collective-permute-start(bf16[64,3072]{1,0:T(8,128)(2,1)S(1)} %get-tuple-element.31), channel_id=1, source_target_pairs={{0,28},{4,16},{8,20},{12,24},{16,12},{20,0},{24,4},{28,8},{1,29},{... | collective-permute-start | bytes 1179656 | tf_op jit(solution)/shard_map/ppermute | solution.py:665
  29.4 0.0 collective-permute-start.5
  29.4 0.6 %collective-permute-done.2 = bf16[64,3072]{1,0:T(8,128)(2,1)S(1)} collective-permute-done((bf16[64,3072]{1,0:T(8,128)(2,1)S(1)}, bf16[64,3072]{1,0:T(8,128)(2,1)S(1)}, u32[]{:S(2)}, u32[]{:S(2)}) %collective-permute-start.2) | collective-permute-done | bytes 393248 | tf_op jit(solution)/shard_map/ppermute | solution.py:665
  30.1 0.8 %collective-permute-done.1 = bf16[64,3072]{1,0:T(8,128)(2,1)S(1)} collective-permute-done((bf16[64,3072]{1,0:T(8,128)(2,1)S(1)}, bf16[64,3072]{1,0:T(8,128)(2,1)S(1)}, u32[]{:S(2)}, u32[]{:S(2)}) %collective-permute-start.1) | collective-permute-done | bytes 393248 | tf_op jit(solution)/shard_map/ppermute | solution.py:665
  30.9 0.8 %add_convert_fusion = bf16[64,3072]{1,0:T(8,128)(2,1)} fusion(bf16[64,3072]{1,0:T(8,128)(2,1)S(1)} %collective-permute-done.2, bf16[64,3072]{1,0:T(8,128)(2,1)S(1)} %collective-permute-done.1), kind=kLoop, calls=%fused_computation | loop fusion | flops 786432 | bytes 1179648 | tf_op jit(solution)/shard_map/convert_element_type | solution.py:714
  31.7 0.4 collective-permute-start.6
  32.1 8.1 %collective-permute-done.4.sent_ref = bf16[64,3072]{1,0:T(8,128)(2,1)S(1)} collective-permute-done((bf16[64,3072]{1,0:T(8,128)(2,1)S(1)}, bf16[64,3072]{1,0:T(8,128)(2,1)S(1)}, u32[]{:S(2)}, u32[]{:S(2)}) %collective-permute-start.4) | collective-permute-done | bytes 393248 | tf_op jit(solution)/shard_map/ppermute | solution.py:665
  40.1 0.7 %collective-permute-done.5.kept_ref = bf16[64,3072]{1,0:T(8,128)(2,1)S(1)} collective-permute-done((bf16[64,3072]{1,0:T(8,128)(2,1)S(1)}, bf16[64,3072]{1,0:T(8,128)(2,1)S(1)}, u32[]{:S(2)}, u32[]{:S(2)}) %collective-permute-start.5) | collective-permute-done | bytes 393248 | tf_op jit(solution)/shard_map/ppermute | solution.py:665
  40.9 0.0 collective-permute-done.6.gate_sent_ref
  40.9 0.8 %sums.1 = (bf16[64,3072]{1,0:T(8,128)(2,1)}, f32[1,1536]{1,0:T(1,128)}) custom-call(bf16[64,3072]{1,0:T(8,128)(2,1)S(1)} %collective-permute-done.4.sent_ref, bf16[64,3072]{1,0:T(8,128)(2,1)S(1)} %collective-permute-done.5.kept_ref, f32[1,1536]{1,0:T(1,128)S(1)} %get-tuple-element.33.gate_kept_ref, f32[1,1536]{1,0:T(1,128)S(1)} %collective-permute-done.6.gate_sent_ref), custom_call_target="tpu_custom_call" | custom-call | tf_op jit(solution)/shard_map/sums/pallas_call | solution.py:645
  (1 shorter events, 0.0 us)
Async XLA Ops:
  0.6 11.8 %collective-permute-start = (bf16[64,3072]{1,0:T(8,128)(2,1)}, bf16[64,3072]{1,0:T(8,128)(2,1)S(1)}, u32[]{:S(2)}, u32[]{:S(2)}) collective-permute-start(bf16[64,3072]{1,0:T(8,128)(2,1)} %bitcast.8), channel_id=1, source_target_pairs={{0,16},{4,20},{8,24},{12,28},{16,0},{20,4},{24,8},{28,12},{1,17},{... | collective-permute-start | bytes 1179656 | tf_op jit(solution)/shard_map/ppermute | solution.py:665
  2.7 19.2 %collective-permute-start.3 = (bf16[64,3072]{1,0:T(8,128)(2,1)}, bf16[64,3072]{1,0:T(8,128)(2,1)S(1)}, u32[]{:S(2)}, u32[]{:S(2)}) collective-permute-start(bf16[64,3072]{1,0:T(8,128)(2,1)} %bitcast.6), channel_id=1, source_target_pairs={{0,16},{4,20},{8,24},{12,28},{16,0},{20,4},{24,8},{28,12},{1,17},{... | collective-permute-start | bytes 1179656 | tf_op jit(solution)/shard_map/ppermute | solution.py:665
  2.8 9.6 %copy-start.1 = (bf16[1,64,3072]{2,1,0:T(8,128)(2,1)S(1)}, bf16[1,64,3072]{2,1,0:T(8,128)(2,1)}, u32[]{:S(2)}) copy-start(bf16[1,64,3072]{2,1,0:T(8,128)(2,1)} %param.9) | copy-start | bytes 1179652
  2.8 9.6 %copy-start.2 = (f32[1,3072]{1,0:T(1,128)S(1)}, f32[1,3072]{1,0:T(1,128)}, u32[]{:S(2)}) copy-start(f32[1,3072]{1,0:T(1,128)} %gate_ref.3) | copy-start | bytes 36868
  2.8 9.6 %copy-start.3 = (f32[1,128]{1,0:T(1,128)S(1)}, f32[1,128]{1,0:T(1,128)}, u32[]{:S(2)}) copy-start(f32[1,128]{1,0:T(1,128)} %query_gain_ref.3) | copy-start | bytes 1540
  2.8 9.6 %copy-start.4 = (f32[1,128]{1,0:T(1,128)S(1)}, f32[1,128]{1,0:T(1,128)}, u32[]{:S(2)}) copy-start(f32[1,128]{1,0:T(1,128)} %key_gain_ref.3) | copy-start | bytes 1540
  2.8 9.6 %copy-start.5 = (s32[2,27]{1,0:T(2,128)S(1)}, s32[2,27]{1,0:T(2,128)}, u32[]{:S(2)}) copy-start(s32[2,27]{1,0:T(2,128)} %neighbours_ref.1) | copy-start | bytes 652
  2.8 9.6 %copy-start.6 = (s32[2]{0:T(128)S(1)}, s32[2]{0:T(128)}, u32[]{:S(2)}) copy-start(s32[2]{0:T(128)} %tile_slot_ref.1) | copy-start | bytes 28
  12.5 9.5 %copy-start = (bf16[1,64,3072]{2,1,0:T(8,128)(2,1)S(1)}, bf16[1,64,3072]{2,1,0:T(8,128)(2,1)}, u32[]{:S(2)}) copy-start(bf16[1,64,3072]{2,1,0:T(8,128)(2,1)} %param.10) | copy-start | bytes 1179652
  17.9 12.2 %collective-permute-start.2 = (bf16[64,3072]{1,0:T(8,128)(2,1)S(1)}, bf16[64,3072]{1,0:T(8,128)(2,1)S(1)}, u32[]{:S(2)}, u32[]{:S(2)}) collective-permute-start(bf16[64,3072]{1,0:T(8,128)(2,1)S(1)} %get-tuple-element.22), channel_id=1, source_target_pairs={{0,20},{4,24},{8,28},{12,16},{16,4},{20,8},{24,12},{28,0},{1,21},{... | collective-permute-start | bytes 1179656 | tf_op jit(solution)/shard_map/ppermute | solution.py:665
  21.9 8.9 %collective-permute-start.1 = (bf16[64,3072]{1,0:T(8,128)(2,1)S(1)}, bf16[64,3072]{1,0:T(8,128)(2,1)S(1)}, u32[]{:S(2)}, u32[]{:S(2)}) collective-permute-start(bf16[64,3072]{1,0:T(8,128)(2,1)S(1)} %get-tuple-element.21), channel_id=1, source_target_pairs={{0,4},{4,8},{8,12},{12,0},{16,20},{20,24},{24,28},{28,16},{1,5},{5... | collective-permute-start | bytes 1179656 | tf_op jit(solution)/shard_map/ppermute | solution.py:665
  28.6 11.6 %collective-permute-start.4 = (bf16[64,3072]{1,0:T(8,128)(2,1)S(1)}, bf16[64,3072]{1,0:T(8,128)(2,1)S(1)}, u32[]{:S(2)}, u32[]{:S(2)}) collective-permute-start(bf16[64,3072]{1,0:T(8,128)(2,1)S(1)} %get-tuple-element.31), channel_id=1, source_target_pairs={{0,28},{4,16},{8,20},{12,24},{16,12},{20,0},{24,4},{28,8},{1,29},{... | collective-permute-start | bytes 1179656 | tf_op jit(solution)/shard_map/ppermute | solution.py:665
  29.4 11.4 %collective-permute-start.5 = (bf16[64,3072]{1,0:T(8,128)(2,1)S(1)}, bf16[64,3072]{1,0:T(8,128)(2,1)S(1)}, u32[]{:S(2)}, u32[]{:S(2)}) collective-permute-start(bf16[64,3072]{1,0:T(8,128)(2,1)S(1)} %get-tuple-element.32), channel_id=1, source_target_pairs={{0,12},{4,0},{8,4},{12,8},{16,28},{20,16},{24,20},{28,24},{1,13},{... | collective-permute-start | bytes 1179656 | tf_op jit(solution)/shard_map/ppermute | solution.py:665
  31.7 9.2 %collective-permute-start.6 = (f32[1,1536]{1,0:T(1,128)S(1)}, f32[1,1536]{1,0:T(1,128)S(1)}, u32[]{:S(2)}, u32[]{:S(2)}) collective-permute-start(f32[1,1536]{1,0:T(1,128)S(1)} %get-tuple-element.34), channel_id=1, source_target_pairs={{0,16},{4,20},{8,24},{12,28},{16,0},{20,4},{24,8},{28,12},{1,17},{... | collective-permute-start | bytes 18440 | tf_op jit(solution)/shard_map/ppermute | solution.py:665

commit v17 on v16

--- a/solution.py
+++ b/solution.py
@@ -635,12 +635,12 @@
     )
 
 
-def sums_kernel(sent_ref, kept_ref, gate_kept_ref, gate_sent_ref, grad_ref, gate_ref):
+def sums_kernel(kept_ref, sent_ref, gate_kept_ref, gate_sent_ref, grad_ref, gate_ref):
     grad_ref[...] = (kept_ref[...].astype(F32) + sent_ref[...].astype(F32)).astype(BF16)
     gate_ref[...] = gate_kept_ref[...] + gate_sent_ref[...]
 
 
-def sums(sent, kept, gate_kept, gate_sent):
+def sums(kept, sent, gate_kept, gate_sent):
     vmem = pl.BlockSpec(memory_space=pltpu.VMEM)
     return pl.pallas_call(
         sums_kernel,
@@ -652,7 +652,7 @@
         out_specs=(vmem, vmem),
         compiler_params=params(8),
         name="sums",
-    )(sent, kept, gate_kept, gate_sent)
+    )(kept, sent, gate_kept, gate_sent)
 
 
 def routed(block, seq_step, pipe_step):
@@ -709,12 +709,12 @@
         key_gain,
         gate_scale,
     )
+    grad_kept = routed(grad_kept, 0, -1)
     grad_sent = routed(grad_sent, 1, -1)
-    grad_kept = routed(grad_kept, 0, -1)
     segment_output = (kept.astype(F32) + sent.astype(F32)).astype(BF16)
     segment_output, gate_sent = lax.optimization_barrier((segment_output, gate_sent))
     gate_sent = routed(gate_sent, 1, 0)
-    token_grad, gate_grad = sums(grad_sent, grad_kept, gate_kept, gate_sent)
+    token_grad, gate_grad = sums(grad_kept, grad_sent, gate_kept, gate_sent)
     return (segment_output[None], token_grad[None], gate_grad)
 
 

time: 41.9 us -> 42 us (level)
  no operation moved by 1% of the time
where the time goes in v17:
time: 42 us; the launch traced here: 41.8 us
  Pallas kernels  22.4 us (53%)
  waiting for transfers between devices  10.2 us (24%)
  starting transfers between devices  7.66 us (18%)
  other arithmetic  0.84 us (2%)
  between operations  0.75 us (2%)
    ppermute x7, waiting for transfers between devices, routed(): return lax.ppermute(block, ('seq', 'pipe'), route)  10.2 us
    pallas_call x1, Pallas kernels, regroup(): pl.pallas_call(regroup_kernel, out_shape=(pltpu.VMEM(out, weight.dtype),...  9.55 us
    ppermute x7, starting transfers between devices, routed(): return lax.ppermute(block, ('seq', 'pipe'), route)  7.66 us
    pallas_call x1, Pallas kernels, backward(): pl.pallas_call(backward_kernel, out_shape=(jax.ShapeDtypeStruct((1, model...  6.61 us
    pallas_call x1, Pallas kernels, forward(): pl.pallas_call(forward_kernel, out_shape=(jax.ShapeDtypeStruct((groups, t...  5.38 us
    pallas_call x1, Pallas kernels, sums(): pl.pallas_call(sums_kernel, out_shape=(jax.ShapeDtypeStruct(kept.shape, B...  0.84 us
  transfers between devices with their start and end apart: 7, of which 4 were waited for; matrix products, arithmetic and copies ran while one was open for 2% of the time, Pallas kernels for 52%

profile of v17, /device:TPU:1, one launch (start us, length us, event | category | flops | bytes accessed | tf_op | source)
XLA Modules:
  0.0 41.8 jit_solution(18097109782033963861)
XLA Ops:
  0.6 2.1 %collective-permute-start = (bf16[64,3072]{1,0:T(8,128)(2,1)}, bf16[64,3072]{1,0:T(8,128)(2,1)S(1)}, u32[]{:S(2)}, u32[]{:S(2)}) collective-permute-start(bf16[64,3072]{1,0:T(8,128)(2,1)} %bitcast.8), channel_id=1, source_target_pairs={{0,16},{4,20},{8,24},{12,28},{16,0},{20,4},{24,8},{28,12},{1,17},{... | collective-permute-start | bytes 1179656 | tf_op jit(solution)/shard_map/ppermute | solution.py:665
  2.7 0.1 collective-permute-start.3
  2.8 0.0 copy-start.1
  2.8 0.0 copy-start.2
  2.8 0.0 copy-start.3
  2.8 0.0 copy-start.5
  2.8 0.0 copy-start.6
  2.8 9.6 %regroup.1 = (bf16[2,3072,1536]{2,1,0:T(8,128)(2,1)S(1)}, bf16[2304,3072]{1,0:T(8,128)(2,1)S(1)}) custom-call(bf16[3072,8,384]{2,1,0:T(8,128)(2,1)} %bitcast.10), custom_call_target="tpu_custom_call" | custom-call | bytes 37748736 | tf_op jit(solution)/shard_map/regroup/pallas_call | solution.py:285
  12.4 0.0 collective-permute-done.other_ref
  12.4 0.0 copy-done.1
  12.4 0.0 copy-done.2
  12.4 0.0 copy-done.3
  12.5 0.0 copy-done.4
  12.5 0.0 copy-done.5
  12.5 0.0 copy-done.6
  12.5 0.0 copy-start
  12.5 5.4 %attention_forward.1 = (f32[2,128,1536]{2,1,0:T(8,128)S(1)}, f32[2,128,8]{2,1,0:T(8,128)S(1)}, bf16[8,128,128]{2,1,0:T(8,128)(2,1)S(1)}, f32[128,3072]{1,0:T(8,1...) custom-call(s32[2,27]{1,0:T(2,128)S(1)} %copy-done.5, ...), custom_call_target="tpu_custom_call" | custom-call | flops 3221225472 | bytes 25165824 | tf_op jit(solution)/shard_map/attention_forward/pallas_call | solution.py:434
  17.9 4.1 %collective-permute-start.2 = (bf16[64,3072]{1,0:T(8,128)(2,1)S(1)}, bf16[64,3072]{1,0:T(8,128)(2,1)S(1)}, u32[]{:S(2)}, u32[]{:S(2)}) collective-permute-start(bf16[64,3072]{1,0:T(8,128)(2,1)S(1)} %get-tuple-element.22), channel_id=1, source_target_pairs={{0,20},{4,24},{8,28},{12,16},{16,4},{20,8},{24,12},{28,0},{1,21},{... | collective-permute-start | bytes 1179656 | tf_op jit(solution)/shard_map/ppermute | solution.py:665
  21.9 0.0 collective-permute-start.1
  22.0 0.0 collective-permute-done.3.other_ref
  22.0 0.0 copy-done
  22.0 6.6 %attention_backward.1 = (f32[1,1536]{1,0:T(1,128)S(1)}, f32[1,1536]{1,0:T(1,128)S(1)}, bf16[64,3072]{1,0:T(8,128)(2,1)S(1)}, bf16[64,3072]{1,0:T(8,128)(2,1)S(1)}) custom-call(bf16[64,3072]{1,0:T(8,128)(2,1)S(1)} %bitcast.7, bf16[64,3072]{1,0:T(8,128)(2,1)S(1)} %collective-permute-done.3.other_ref, bf16[1024,3072]{1,0:T(8,128)(2,1)S(1)} %get-tuple-element.23.out_weight_ref, ...), custom_call_target="tpu_custom_call" | custom-call | flops 3221225472 | bytes 25165824 | tf_op jit(solution)/shard_map/attention_backward/pallas_call | solution.py:599
  28.6 0.5 %collective-permute-start.4 = (bf16[64,3072]{1,0:T(8,128)(2,1)S(1)}, bf16[64,3072]{1,0:T(8,128)(2,1)S(1)}, u32[]{:S(2)}, u32[]{:S(2)}) collective-permute-start(bf16[64,3072]{1,0:T(8,128)(2,1)S(1)} %get-tuple-element.31), channel_id=1, source_target_pairs={{0,12},{4,0},{8,4},{12,8},{16,28},{20,16},{24,20},{28,24},{1,13},{... | collective-permute-start | bytes 1179656 | tf_op jit(solution)/shard_map/ppermute | solution.py:665
  29.1 0.4 %collective-permute-start.5 = (bf16[64,3072]{1,0:T(8,128)(2,1)S(1)}, bf16[64,3072]{1,0:T(8,128)(2,1)S(1)}, u32[]{:S(2)}, u32[]{:S(2)}) collective-permute-start(bf16[64,3072]{1,0:T(8,128)(2,1)S(1)} %get-tuple-element.32), channel_id=1, source_target_pairs={{0,28},{4,16},{8,20},{12,24},{16,12},{20,0},{24,4},{28,8},{1,29},{... | collective-permute-start | bytes 1179656 | tf_op jit(solution)/shard_map/ppermute | solution.py:665
  29.5 0.5 %collective-permute-done.2 = bf16[64,3072]{1,0:T(8,128)(2,1)S(1)} collective-permute-done((bf16[64,3072]{1,0:T(8,128)(2,1)S(1)}, bf16[64,3072]{1,0:T(8,128)(2,1)S(1)}, u32[]{:S(2)}, u32[]{:S(2)}) %collective-permute-start.2) | collective-permute-done | bytes 393248 | tf_op jit(solution)/shard_map/ppermute | solution.py:665
  30.1 1.5 %collective-permute-done.1 = bf16[64,3072]{1,0:T(8,128)(2,1)S(1)} collective-permute-done((bf16[64,3072]{1,0:T(8,128)(2,1)S(1)}, bf16[64,3072]{1,0:T(8,128)(2,1)S(1)}, u32[]{:S(2)}, u32[]{:S(2)}) %collective-permute-start.1) | collective-permute-done | bytes 393248 | tf_op jit(solution)/shard_map/ppermute | solution.py:665
  31.6 0.8 %add_convert_fusion = bf16[64,3072]{1,0:T(8,128)(2,1)} fusion(bf16[64,3072]{1,0:T(8,128)(2,1)S(1)} %collective-permute-done.2, bf16[64,3072]{1,0:T(8,128)(2,1)S(1)} %collective-permute-done.1), kind=kLoop, calls=%fused_computation | loop fusion | flops 786432 | bytes 1179648 | tf_op jit(solution)/shard_map/convert_element_type | solution.py:714
  32.5 0.4 %collective-permute-start.6 = (f32[1,1536]{1,0:T(1,128)S(1)}, f32[1,1536]{1,0:T(1,128)S(1)}, u32[]{:S(2)}, u32[]{:S(2)}) collective-permute-start(f32[1,1536]{1,0:T(1,128)S(1)} %get-tuple-element.34), channel_id=1, source_target_pairs={{0,16},{4,20},{8,24},{12,28},{16,0},{20,4},{24,8},{28,12},{1,17},{... | collective-permute-start | bytes 18440 | tf_op jit(solution)/shard_map/ppermute | solution.py:665
  32.9 6.1 %collective-permute-done.4.kept_ref = bf16[64,3072]{1,0:T(8,128)(2,1)S(1)} collective-permute-done((bf16[64,3072]{1,0:T(8,128)(2,1)S(1)}, bf16[64,3072]{1,0:T(8,128)(2,1)S(1)}, u32[]{:S(2)}, u32[]{:S(2)}) %collective-permute-start.4) | collective-permute-done | bytes 393248 | tf_op jit(solution)/shard_map/ppermute | solution.py:665
  39.0 2.0 %collective-permute-done.5.sent_ref = bf16[64,3072]{1,0:T(8,128)(2,1)S(1)} collective-permute-done((bf16[64,3072]{1,0:T(8,128)(2,1)S(1)}, bf16[64,3072]{1,0:T(8,128)(2,1)S(1)}, u32[]{:S(2)}, u32[]{:S(2)}) %collective-permute-start.5) | collective-permute-done | bytes 393248 | tf_op jit(solution)/shard_map/ppermute | solution.py:665
  41.0 0.0 collective-permute-done.6.gate_sent_ref
  41.0 0.8 %sums.1 = (bf16[64,3072]{1,0:T(8,128)(2,1)}, f32[1,1536]{1,0:T(1,128)}) custom-call(bf16[64,3072]{1,0:T(8,128)(2,1)S(1)} %collective-permute-done.4.kept_ref, bf16[64,3072]{1,0:T(8,128)(2,1)S(1)} %collective-permute-done.5.sent_ref, f32[1,1536]{1,0:T(1,128)S(1)} %get-tuple-element.33.gate_kept_ref, f32[1,1536]{1,0:T(1,128)S(1)} %collective-permute-done.6.gate_sent_ref), custom_call_target="tpu_custom_call" | custom-call | tf_op jit(solution)/shard_map/sums/pallas_call | solution.py:645
  (1 shorter events, 0.0 us)
Async XLA Ops:
  0.6 11.8 %collective-permute-start = (bf16[64,3072]{1,0:T(8,128)(2,1)}, bf16[64,3072]{1,0:T(8,128)(2,1)S(1)}, u32[]{:S(2)}, u32[]{:S(2)}) collective-permute-start(bf16[64,3072]{1,0:T(8,128)(2,1)} %bitcast.8), channel_id=1, source_target_pairs={{0,16},{4,20},{8,24},{12,28},{16,0},{20,4},{24,8},{28,12},{1,17},{... | collective-permute-start | bytes 1179656 | tf_op jit(solution)/shard_map/ppermute | solution.py:665
  2.7 19.2 %collective-permute-start.3 = (bf16[64,3072]{1,0:T(8,128)(2,1)}, bf16[64,3072]{1,0:T(8,128)(2,1)S(1)}, u32[]{:S(2)}, u32[]{:S(2)}) collective-permute-start(bf16[64,3072]{1,0:T(8,128)(2,1)} %bitcast.6), channel_id=1, source_target_pairs={{0,16},{4,20},{8,24},{12,28},{16,0},{20,4},{24,8},{28,12},{1,17},{... | collective-permute-start | bytes 1179656 | tf_op jit(solution)/shard_map/ppermute | solution.py:665
  2.8 9.6 %copy-start.1 = (bf16[1,64,3072]{2,1,0:T(8,128)(2,1)S(1)}, bf16[1,64,3072]{2,1,0:T(8,128)(2,1)}, u32[]{:S(2)}) copy-start(bf16[1,64,3072]{2,1,0:T(8,128)(2,1)} %param.9) | copy-start | bytes 1179652
  2.8 9.6 %copy-start.2 = (f32[1,3072]{1,0:T(1,128)S(1)}, f32[1,3072]{1,0:T(1,128)}, u32[]{:S(2)}) copy-start(f32[1,3072]{1,0:T(1,128)} %gate_ref.3) | copy-start | bytes 36868
  2.8 9.6 %copy-start.3 = (f32[1,128]{1,0:T(1,128)S(1)}, f32[1,128]{1,0:T(1,128)}, u32[]{:S(2)}) copy-start(f32[1,128]{1,0:T(1,128)} %query_gain_ref.3) | copy-start | bytes 1540
  2.8 9.6 %copy-start.4 = (f32[1,128]{1,0:T(1,128)S(1)}, f32[1,128]{1,0:T(1,128)}, u32[]{:S(2)}) copy-start(f32[1,128]{1,0:T(1,128)} %key_gain_ref.3) | copy-start | bytes 1540
  2.8 9.6 %copy-start.5 = (s32[2,27]{1,0:T(2,128)S(1)}, s32[2,27]{1,0:T(2,128)}, u32[]{:S(2)}) copy-start(s32[2,27]{1,0:T(2,128)} %neighbours_ref.1) | copy-start | bytes 652
  2.8 9.6 %copy-start.6 = (s32[2]{0:T(128)S(1)}, s32[2]{0:T(128)}, u32[]{:S(2)}) copy-start(s32[2]{0:T(128)} %tile_slot_ref.1) | copy-start | bytes 28
  12.5 9.5 %copy-start = (bf16[1,64,3072]{2,1,0:T(8,128)(2,1)S(1)}, bf16[1,64,3072]{2,1,0:T(8,128)(2,1)}, u32[]{:S(2)}) copy-start(bf16[1,64,3072]{2,1,0:T(8,128)(2,1)} %param.10) | copy-start | bytes 1179652
  17.9 12.2 %collective-permute-start.2 = (bf16[64,3072]{1,0:T(8,128)(2,1)S(1)}, bf16[64,3072]{1,0:T(8,128)(2,1)S(1)}, u32[]{:S(2)}, u32[]{:S(2)}) collective-permute-start(bf16[64,3072]{1,0:T(8,128)(2,1)S(1)} %get-tuple-element.22), channel_id=1, source_target_pairs={{0,20},{4,24},{8,28},{12,16},{16,4},{20,8},{24,12},{28,0},{1,21},{... | collective-permute-start | bytes 1179656 | tf_op jit(solution)/shard_map/ppermute | solution.py:665
  21.9 9.7 %collective-permute-start.1 = (bf16[64,3072]{1,0:T(8,128)(2,1)S(1)}, bf16[64,3072]{1,0:T(8,128)(2,1)S(1)}, u32[]{:S(2)}, u32[]{:S(2)}) collective-permute-start(bf16[64,3072]{1,0:T(8,128)(2,1)S(1)} %get-tuple-element.21), channel_id=1, source_target_pairs={{0,4},{4,8},{8,12},{12,0},{16,20},{20,24},{24,28},{28,16},{1,5},{5... | collective-permute-start | bytes 1179656 | tf_op jit(solution)/shard_map/ppermute | solution.py:665
  28.6 10.4 %collective-permute-start.4 = (bf16[64,3072]{1,0:T(8,128)(2,1)S(1)}, bf16[64,3072]{1,0:T(8,128)(2,1)S(1)}, u32[]{:S(2)}, u32[]{:S(2)}) collective-permute-start(bf16[64,3072]{1,0:T(8,128)(2,1)S(1)} %get-tuple-element.31), channel_id=1, source_target_pairs={{0,12},{4,0},{8,4},{12,8},{16,28},{20,16},{24,20},{28,24},{1,13},{... | collective-permute-start | bytes 1179656 | tf_op jit(solution)/shard_map/ppermute | solution.py:665
  29.1 11.9 %collective-permute-start.5 = (bf16[64,3072]{1,0:T(8,128)(2,1)S(1)}, bf16[64,3072]{1,0:T(8,128)(2,1)S(1)}, u32[]{:S(2)}, u32[]{:S(2)}) collective-permute-start(bf16[64,3072]{1,0:T(8,128)(2,1)S(1)} %get-tuple-element.32), channel_id=1, source_target_pairs={{0,28},{4,16},{8,20},{12,24},{16,12},{20,0},{24,4},{28,8},{1,29},{... | collective-permute-start | bytes 1179656 | tf_op jit(solution)/shard_map/ppermute | solution.py:665
  32.5 8.5 %collective-permute-start.6 = (f32[1,1536]{1,0:T(1,128)S(1)}, f32[1,1536]{1,0:T(1,128)S(1)}, u32[]{:S(2)}, u32[]{:S(2)}) collective-permute-start(f32[1,1536]{1,0:T(1,128)S(1)} %get-tuple-element.34), channel_id=1, source_target_pairs={{0,16},{4,20},{8,24},{12,28},{16,0},{20,4},{24,8},{28,12},{1,17},{... | collective-permute-start | bytes 18440 | tf_op jit(solution)/shard_map/ppermute | solution.py:665

commit v18 on v17

--- a/solution.py
+++ b/solution.py
@@ -712,7 +712,6 @@
     grad_kept = routed(grad_kept, 0, -1)
     grad_sent = routed(grad_sent, 1, -1)
     segment_output = (kept.astype(F32) + sent.astype(F32)).astype(BF16)
-    segment_output, gate_sent = lax.optimization_barrier((segment_output, gate_sent))
     gate_sent = routed(gate_sent, 1, 0)
     token_grad, gate_grad = sums(grad_kept, grad_sent, gate_kept, gate_sent)
     return (segment_output[None], token_grad[None], gate_grad)

time: 42 us -> 42 us (level)
  waiting for transfers between devices: 10.2 us -> 9.56 us
  starting transfers between devices: 7.66 us -> 8.28 us
    convert_element_type x1 -> x0, other arithmetic: 0.84 us -> none  [pair_body(): segment_output = (kept.astype(F32) + sent.astype(F32)).astype(BF16)]
    broadcast_in_dim x0 -> x1, other arithmetic: none -> 0.84 us  [pair_body(): return (segment_output[None], token_grad[None], gate_grad)]
    ppermute x7, waiting for transfers between devices: 10.2 us -> 9.56 us  [routed(): return lax.ppermute(block, ('seq', 'pipe'), route)]
    ppermute x7, starting transfers between devices: 7.66 us -> 8.28 us  [routed(): return lax.ppermute(block, ('seq', 'pipe'), route)]
  transfers between devices with their start and end apart: 7 -> 7, of which waited for: 4 -> 3; matrix products, arithmetic and copies ran while one was open for 2% -> 2% of each run, Pallas kernels for 52% -> 52%
where the time goes in v18:
time: 42 us; the launch traced here: 41.8 us
  Pallas kernels  22.4 us (53%)
  waiting for transfers between devices  9.56 us (23%)
  starting transfers between devices  8.28 us (20%)
  other arithmetic  0.84 us (2%)
  between operations  0.75 us (2%)
    ppermute x7, waiting for transfers between devices, routed(): return lax.ppermute(block, ('seq', 'pipe'), route)  9.56 us
    pallas_call x1, Pallas kernels, regroup(): pl.pallas_call(regroup_kernel, out_shape=(pltpu.VMEM(out, weight.dtype),...  9.55 us
    ppermute x7, starting transfers between devices, routed(): return lax.ppermute(block, ('seq', 'pipe'), route)  8.28 us
    pallas_call x1, Pallas kernels, backward(): pl.pallas_call(backward_kernel, out_shape=(jax.ShapeDtypeStruct((1, model...  6.61 us
    pallas_call x1, Pallas kernels, forward(): pl.pallas_call(forward_kernel, out_shape=(jax.ShapeDtypeStruct((groups, t...  5.38 us
    pallas_call x1, Pallas kernels, sums(): pl.pallas_call(sums_kernel, out_shape=(jax.ShapeDtypeStruct(kept.shape, B...  0.84 us
  transfers between devices with their start and end apart: 7, of which 3 were waited for; matrix products, arithmetic and copies ran while one was open for 2% of the time, Pallas kernels for 52%

profile of v18, /device:TPU:1, one launch (start us, length us, event | category | flops | bytes accessed | tf_op | source)
XLA Modules:
  0.0 41.8 jit_solution(10448452981234562978)
XLA Ops:
  0.6 2.1 %collective-permute-start = (bf16[64,3072]{1,0:T(8,128)(2,1)}, bf16[64,3072]{1,0:T(8,128)(2,1)S(1)}, u32[]{:S(2)}, u32[]{:S(2)}) collective-permute-start(bf16[64,3072]{1,0:T(8,128)(2,1)} %bitcast.9), channel_id=1, source_target_pairs={{0,16},{4,20},{8,24},{12,28},{16,0},{20,4},{24,8},{28,12},{1,17},{... | collective-permute-start | bytes 1179656 | tf_op jit(solution)/shard_map/ppermute | solution.py:665
  2.7 0.1 collective-permute-start.3
  2.8 0.0 copy-start.1
  2.8 0.0 copy-start.2
  2.8 0.0 copy-start.3
  2.8 0.0 copy-start.5
  2.8 0.0 copy-start.6
  2.8 9.6 %regroup.1 = (bf16[2,3072,1536]{2,1,0:T(8,128)(2,1)S(1)}, bf16[2304,3072]{1,0:T(8,128)(2,1)S(1)}) custom-call(bf16[3072,8,384]{2,1,0:T(8,128)(2,1)} %bitcast.11), custom_call_target="tpu_custom_call" | custom-call | bytes 37748736 | tf_op jit(solution)/shard_map/regroup/pallas_call | solution.py:285
  12.4 0.0 collective-permute-done.other_ref
  12.4 0.0 copy-done.1
  12.4 0.0 copy-done.2
  12.4 0.0 copy-done.3
  12.5 0.0 copy-done.4
  12.5 0.0 copy-done.5
  12.5 0.0 copy-done.6
  12.5 0.0 copy-start
  12.5 5.4 %attention_forward.1 = (f32[2,128,1536]{2,1,0:T(8,128)S(1)}, f32[2,128,8]{2,1,0:T(8,128)S(1)}, bf16[8,128,128]{2,1,0:T(8,128)(2,1)S(1)}, f32[128,3072]{1,0:T(8,1...) custom-call(s32[2,27]{1,0:T(2,128)S(1)} %copy-done.5, ...), custom_call_target="tpu_custom_call" | custom-call | flops 3221225472 | bytes 25165824 | tf_op jit(solution)/shard_map/attention_forward/pallas_call | solution.py:434
  17.9 4.1 %collective-permute-start.2 = (bf16[64,3072]{1,0:T(8,128)(2,1)S(1)}, bf16[64,3072]{1,0:T(8,128)(2,1)S(1)}, u32[]{:S(2)}, u32[]{:S(2)}) collective-permute-start(bf16[64,3072]{1,0:T(8,128)(2,1)S(1)} %get-tuple-element.20), channel_id=1, source_target_pairs={{0,20},{4,24},{8,28},{12,16},{16,4},{20,8},{24,12},{28,0},{1,21},{... | collective-permute-start | bytes 1179656 | tf_op jit(solution)/shard_map/ppermute | solution.py:665
  21.9 0.0 collective-permute-start.1
  22.0 0.0 collective-permute-done.3.other_ref
  22.0 0.0 copy-done
  22.0 6.6 %attention_backward.1 = (f32[1,1536]{1,0:T(1,128)S(1)}, f32[1,1536]{1,0:T(1,128)S(1)}, bf16[64,3072]{1,0:T(8,128)(2,1)S(1)}, bf16[64,3072]{1,0:T(8,128)(2,1)S(1)}) custom-call(bf16[64,3072]{1,0:T(8,128)(2,1)S(1)} %bitcast.8, bf16[64,3072]{1,0:T(8,128)(2,1)S(1)} %collective-permute-done.3.other_ref, bf16[1024,3072]{1,0:T(8,128)(2,1)S(1)} %get-tuple-element.21.out_weight_ref, ...), custom_call_target="tpu_custom_call" | custom-call | flops 3221225472 | bytes 25165824 | tf_op jit(solution)/shard_map/attention_backward/pallas_call | solution.py:599
  28.6 0.5 %collective-permute-start.4 = (bf16[64,3072]{1,0:T(8,128)(2,1)S(1)}, bf16[64,3072]{1,0:T(8,128)(2,1)S(1)}, u32[]{:S(2)}, u32[]{:S(2)}) collective-permute-start(bf16[64,3072]{1,0:T(8,128)(2,1)S(1)} %get-tuple-element.27), channel_id=1, source_target_pairs={{0,12},{4,0},{8,4},{12,8},{16,28},{20,16},{24,20},{28,24},{1,13},{... | collective-permute-start | bytes 1179656 | tf_op jit(solution)/shard_map/ppermute | solution.py:665
  29.1 0.4 %collective-permute-start.5 = (bf16[64,3072]{1,0:T(8,128)(2,1)S(1)}, bf16[64,3072]{1,0:T(8,128)(2,1)S(1)}, u32[]{:S(2)}, u32[]{:S(2)}) collective-permute-start(bf16[64,3072]{1,0:T(8,128)(2,1)S(1)} %get-tuple-element.28), channel_id=1, source_target_pairs={{0,28},{4,16},{8,20},{12,24},{16,12},{20,0},{24,4},{28,8},{1,29},{... | collective-permute-start | bytes 1179656 | tf_op jit(solution)/shard_map/ppermute | solution.py:665
  29.5 1.1 %collective-permute-start.6 = (f32[1,1536]{1,0:T(1,128)S(1)}, f32[1,1536]{1,0:T(1,128)S(1)}, u32[]{:S(2)}, u32[]{:S(2)}) collective-permute-start(f32[1,1536]{1,0:T(1,128)S(1)} %get-tuple-element.30), channel_id=1, source_target_pairs={{0,16},{4,20},{8,24},{12,28},{16,0},{20,4},{24,8},{28,12},{1,17},{... | collective-permute-start | bytes 18440 | tf_op jit(solution)/shard_map/ppermute | solution.py:665
  30.6 0.0 collective-permute-done.2
  30.6 1.0 %collective-permute-done.1 = bf16[64,3072]{1,0:T(8,128)(2,1)S(1)} collective-permute-done((bf16[64,3072]{1,0:T(8,128)(2,1)S(1)}, bf16[64,3072]{1,0:T(8,128)(2,1)S(1)}, u32[]{:S(2)}, u32[]{:S(2)}) %collective-permute-start.1) | collective-permute-done | bytes 393248 | tf_op jit(solution)/shard_map/ppermute | solution.py:665
  31.6 0.8 %fusion = bf16[1,64,3072]{2,1,0:T(8,128)(2,1)} fusion(bf16[64,3072]{1,0:T(8,128)(2,1)S(1)} %collective-permute-done.2, bf16[64,3072]{1,0:T(8,128)(2,1)S(1)} %collective-permute-done.1), kind=kLoop, calls=%fused_computation.1 | loop fusion | flops 786432 | bytes 1179648 | tf_op jit(solution)/shard_map/broadcast_in_dim | solution.py:717
  32.5 7.1 %collective-permute-done.6.gate_sent_ref = f32[1,1536]{1,0:T(1,128)S(1)} collective-permute-done((f32[1,1536]{1,0:T(1,128)S(1)}, f32[1,1536]{1,0:T(1,128)S(1)}, u32[]{:S(2)}, u32[]{:S(2)}) %collective-permute-start.6) | collective-permute-done | bytes 6176 | tf_op jit(solution)/shard_map/ppermute | solution.py:665
  39.6 0.0 collective-permute-done.4.kept_ref
  39.6 1.4 %collective-permute-done.5.sent_ref = bf16[64,3072]{1,0:T(8,128)(2,1)S(1)} collective-permute-done((bf16[64,3072]{1,0:T(8,128)(2,1)S(1)}, bf16[64,3072]{1,0:T(8,128)(2,1)S(1)}, u32[]{:S(2)}, u32[]{:S(2)}) %collective-permute-start.5) | collective-permute-done | bytes 393248 | tf_op jit(solution)/shard_map/ppermute | solution.py:665
  41.0 0.8 %sums.1 = (bf16[64,3072]{1,0:T(8,128)(2,1)}, f32[1,1536]{1,0:T(1,128)}) custom-call(bf16[64,3072]{1,0:T(8,128)(2,1)S(1)} %collective-permute-done.4.kept_ref, bf16[64,3072]{1,0:T(8,128)(2,1)S(1)} %collective-permute-done.5.sent_ref, f32[1,1536]{1,0:T(1,128)S(1)} %get-tuple-element.29.gate_kept_ref, f32[1,1536]{1,0:T(1,128)S(1)} %collective-permute-done.6.gate_sent_ref), custom_call_target="tpu_custom_call" | custom-call | tf_op jit(solution)/shard_map/sums/pallas_call | solution.py:645
  (1 shorter events, 0.0 us)
Async XLA Ops:
  0.6 11.8 %collective-permute-start = (bf16[64,3072]{1,0:T(8,128)(2,1)}, bf16[64,3072]{1,0:T(8,128)(2,1)S(1)}, u32[]{:S(2)}, u32[]{:S(2)}) collective-permute-start(bf16[64,3072]{1,0:T(8,128)(2,1)} %bitcast.9), channel_id=1, source_target_pairs={{0,16},{4,20},{8,24},{12,28},{16,0},{20,4},{24,8},{28,12},{1,17},{... | collective-permute-start | bytes 1179656 | tf_op jit(solution)/shard_map/ppermute | solution.py:665
  2.7 19.2 %collective-permute-start.3 = (bf16[64,3072]{1,0:T(8,128)(2,1)}, bf16[64,3072]{1,0:T(8,128)(2,1)S(1)}, u32[]{:S(2)}, u32[]{:S(2)}) collective-permute-start(bf16[64,3072]{1,0:T(8,128)(2,1)} %bitcast.7), channel_id=1, source_target_pairs={{0,16},{4,20},{8,24},{12,28},{16,0},{20,4},{24,8},{28,12},{1,17},{... | collective-permute-start | bytes 1179656 | tf_op jit(solution)/shard_map/ppermute | solution.py:665
  2.8 9.6 %copy-start.1 = (bf16[1,64,3072]{2,1,0:T(8,128)(2,1)S(1)}, bf16[1,64,3072]{2,1,0:T(8,128)(2,1)}, u32[]{:S(2)}) copy-start(bf16[1,64,3072]{2,1,0:T(8,128)(2,1)} %param.9) | copy-start | bytes 1179652
  2.8 9.6 %copy-start.2 = (f32[1,3072]{1,0:T(1,128)S(1)}, f32[1,3072]{1,0:T(1,128)}, u32[]{:S(2)}) copy-start(f32[1,3072]{1,0:T(1,128)} %gate_ref.3) | copy-start | bytes 36868
  2.8 9.6 %copy-start.3 = (f32[1,128]{1,0:T(1,128)S(1)}, f32[1,128]{1,0:T(1,128)}, u32[]{:S(2)}) copy-start(f32[1,128]{1,0:T(1,128)} %query_gain_ref.3) | copy-start | bytes 1540
  2.8 9.6 %copy-start.4 = (f32[1,128]{1,0:T(1,128)S(1)}, f32[1,128]{1,0:T(1,128)}, u32[]{:S(2)}) copy-start(f32[1,128]{1,0:T(1,128)} %key_gain_ref.3) | copy-start | bytes 1540
  2.8 9.6 %copy-start.5 = (s32[2,27]{1,0:T(2,128)S(1)}, s32[2,27]{1,0:T(2,128)}, u32[]{:S(2)}) copy-start(s32[2,27]{1,0:T(2,128)} %neighbours_ref.1) | copy-start | bytes 652
  2.8 9.6 %copy-start.6 = (s32[2]{0:T(128)S(1)}, s32[2]{0:T(128)}, u32[]{:S(2)}) copy-start(s32[2]{0:T(128)} %tile_slot_ref.1) | copy-start | bytes 28
  12.5 9.5 %copy-start = (bf16[1,64,3072]{2,1,0:T(8,128)(2,1)S(1)}, bf16[1,64,3072]{2,1,0:T(8,128)(2,1)}, u32[]{:S(2)}) copy-start(bf16[1,64,3072]{2,1,0:T(8,128)(2,1)} %param.10) | copy-start | bytes 1179652
  17.9 12.7 %collective-permute-start.2 = (bf16[64,3072]{1,0:T(8,128)(2,1)S(1)}, bf16[64,3072]{1,0:T(8,128)(2,1)S(1)}, u32[]{:S(2)}, u32[]{:S(2)}) collective-permute-start(bf16[64,3072]{1,0:T(8,128)(2,1)S(1)} %get-tuple-element.20), channel_id=1, source_target_pairs={{0,20},{4,24},{8,28},{12,16},{16,4},{20,8},{24,12},{28,0},{1,21},{... | collective-permute-start | bytes 1179656 | tf_op jit(solution)/shard_map/ppermute | solution.py:665
  21.9 9.7 %collective-permute-start.1 = (bf16[64,3072]{1,0:T(8,128)(2,1)S(1)}, bf16[64,3072]{1,0:T(8,128)(2,1)S(1)}, u32[]{:S(2)}, u32[]{:S(2)}) collective-permute-start(bf16[64,3072]{1,0:T(8,128)(2,1)S(1)} %get-tuple-element.19), channel_id=1, source_target_pairs={{0,4},{4,8},{8,12},{12,0},{16,20},{20,24},{24,28},{28,16},{1,5},{5... | collective-permute-start | bytes 1179656 | tf_op jit(solution)/shard_map/ppermute | solution.py:665
  28.6 11.0 %collective-permute-start.4 = (bf16[64,3072]{1,0:T(8,128)(2,1)S(1)}, bf16[64,3072]{1,0:T(8,128)(2,1)S(1)}, u32[]{:S(2)}, u32[]{:S(2)}) collective-permute-start(bf16[64,3072]{1,0:T(8,128)(2,1)S(1)} %get-tuple-element.27), channel_id=1, source_target_pairs={{0,12},{4,0},{8,4},{12,8},{16,28},{20,16},{24,20},{28,24},{1,13},{... | collective-permute-start | bytes 1179656 | tf_op jit(solution)/shard_map/ppermute | solution.py:665
  29.1 11.9 %collective-permute-start.5 = (bf16[64,3072]{1,0:T(8,128)(2,1)S(1)}, bf16[64,3072]{1,0:T(8,128)(2,1)S(1)}, u32[]{:S(2)}, u32[]{:S(2)}) collective-permute-start(bf16[64,3072]{1,0:T(8,128)(2,1)S(1)} %get-tuple-element.28), channel_id=1, source_target_pairs={{0,28},{4,16},{8,20},{12,24},{16,12},{20,0},{24,4},{28,8},{1,29},{... | collective-permute-start | bytes 1179656 | tf_op jit(solution)/shard_map/ppermute | solution.py:665
  29.5 10.0 %collective-permute-start.6 = (f32[1,1536]{1,0:T(1,128)S(1)}, f32[1,1536]{1,0:T(1,128)S(1)}, u32[]{:S(2)}, u32[]{:S(2)}) collective-permute-start(f32[1,1536]{1,0:T(1,128)S(1)} %get-tuple-element.30), channel_id=1, source_target_pairs={{0,16},{4,20},{8,24},{12,28},{16,0},{20,4},{24,8},{28,12},{1,17},{... | collective-permute-start | bytes 18440 | tf_op jit(solution)/shard_map/ppermute | solution.py:665

commit v19 on v16

--- a/solution.py
+++ b/solution.py
@@ -14,7 +14,7 @@
 BF16 = jnp.bfloat16
 MIB = 1024 * 1024
 GROUP = 4
-TURNED = 6
+TURNED = 4
 
 
 def passed_along(block, axis, distance):
@@ -294,7 +294,7 @@
             pltpu.VMEM((slots, rows, heads, width), weight.dtype),
             pltpu.SemaphoreType.DMA((slots,)),
         ],
-        compiler_params=params(6),
+        compiler_params=params(9),
         cost_estimate=pl.CostEstimate(
             flops=0, bytes_accessed=4 * depth * heads * width, transcendentals=0
         ),
@@ -680,7 +680,7 @@
     upstream = output_grad[0]
     out_local = out_weight[0]
     other_stream = routed(stream, 1, 0)
-    weight, turned_weight = regroup(qkv_weight[0], 128, 4, TURNED)
+    weight, turned_weight = regroup(qkv_weight[0], 128, 6, TURNED)
     other_upstream = routed(upstream, 1, 0)
     projected, inverse, probs, attention, kept, sent, out_local = forward(
         neighbours,

time: 41.9 us -> 42.5 us (1.014)
  starting transfers between devices: 7.49 us -> 8.08 us
  waiting for transfers between devices: 10.2 us -> 10.7 us
    pallas_call x1, Pallas kernels: 9.55 us -> 8.46 us  [regroup(): pl.pallas_call(regroup_kernel, out_shape=(pltpu.VMEM(out, weight.dtype),...]
    pallas_call x1, Pallas kernels: 6.61 us -> 7.24 us  [backward(): pl.pallas_call(backward_kernel, out_shape=(jax.ShapeDtypeStruct((1, model...]
    ppermute x7, starting transfers between devices: 7.49 us -> 8.08 us  [routed(): return lax.ppermute(block, ('seq', 'pipe'), route)]
    ppermute x7, waiting for transfers between devices: 10.2 us -> 10.7 us  [routed(): return lax.ppermute(block, ('seq', 'pipe'), route)]
  transfers between devices with their start and end apart: 7 -> 7, of which waited for: 4 -> 5; matrix products, arithmetic and copies ran while one was open for 2% -> 2% of each run, Pallas kernels for 52% -> 50%
where the time goes in v19:
time: 42.5 us; the launch traced here: 42.3 us
  Pallas kernels  22 us (52%)
  waiting for transfers between devices  10.7 us (25%)
  starting transfers between devices  8.08 us (19%)
  other arithmetic  0.85 us (2%)
  between operations  0.72 us (2%)
    ppermute x7, waiting for transfers between devices, routed(): return lax.ppermute(block, ('seq', 'pipe'), route)  10.7 us
    pallas_call x1, Pallas kernels, regroup(): pl.pallas_call(regroup_kernel, out_shape=(pltpu.VMEM(out, weight.dtype),...  8.46 us
    ppermute x7, starting transfers between devices, routed(): return lax.ppermute(block, ('seq', 'pipe'), route)  8.08 us
    pallas_call x1, Pallas kernels, backward(): pl.pallas_call(backward_kernel, out_shape=(jax.ShapeDtypeStruct((1, model...  7.24 us
    pallas_call x1, Pallas kernels, forward(): pl.pallas_call(forward_kernel, out_shape=(jax.ShapeDtypeStruct((groups, t...  5.46 us
  transfers between devices with their start and end apart: 7, of which 5 were waited for; matrix products, arithmetic and copies ran while one was open for 2% of the time, Pallas kernels for 50%

profile of v19, /device:TPU:1, one launch (start us, length us, event | category | flops | bytes accessed | tf_op | source)
XLA Modules:
  0.0 42.3 jit_solution(7820843185411080202)
XLA Ops:
  0.6 2.1 %collective-permute-start = (bf16[64,3072]{1,0:T(8,128)(2,1)}, bf16[64,3072]{1,0:T(8,128)(2,1)S(1)}, u32[]{:S(2)}, u32[]{:S(2)}) collective-permute-start(bf16[64,3072]{1,0:T(8,128)(2,1)} %bitcast.8), channel_id=1, source_target_pairs={{0,16},{4,20},{8,24},{12,28},{16,0},{20,4},{24,8},{28,12},{1,17},{... | collective-permute-start | bytes 1179656 | tf_op jit(solution)/shard_map/ppermute | solution.py:665
  2.7 0.1 collective-permute-start.3
  2.8 0.0 copy-start.1
  2.8 0.0 copy-start.2
  2.8 0.0 copy-start.3
  2.8 0.0 copy-start.5
  2.8 0.0 copy-start.6
  2.8 8.5 %regroup.1 = (bf16[2,3072,1536]{2,1,0:T(8,128)(2,1)S(1)}, bf16[1536,3072]{1,0:T(8,128)(2,1)S(1)}) custom-call(bf16[3072,8,384]{2,1,0:T(8,128)(2,1)} %bitcast.10), custom_call_target="tpu_custom_call" | custom-call | bytes 37748736 | tf_op jit(solution)/shard_map/regroup/pallas_call | solution.py:285
  11.3 0.5 %collective-permute-done.other_ref = bf16[64,3072]{1,0:T(8,128)(2,1)S(1)} collective-permute-done((bf16[64,3072]{1,0:T(8,128)(2,1)}, bf16[64,3072]{1,0:T(8,128)(2,1)S(1)}, u32[]{:S(2)}, u32[]{:S(2)}) %collective-permute-start) | collective-permute-done | bytes 393248 | tf_op jit(solution)/shard_map/ppermute | solution.py:665
  11.8 0.0 copy-done.1
  11.8 0.0 copy-done.2
  11.8 0.0 copy-done.3
  11.8 0.0 copy-done.4
  11.8 0.0 copy-done.5
  11.8 0.0 copy-done.6
  11.8 0.0 copy-start
  11.8 5.5 %attention_forward.1 = (f32[2,128,1536]{2,1,0:T(8,128)S(1)}, f32[2,128,8]{2,1,0:T(8,128)S(1)}, bf16[8,128,128]{2,1,0:T(8,128)(2,1)S(1)}, f32[128,3072]{1,0:T(8,1...) custom-call(s32[2,27]{1,0:T(2,128)S(1)} %copy-done.5, ...), custom_call_target="tpu_custom_call" | custom-call | flops 3221225472 | bytes 25165824 | tf_op jit(solution)/shard_map/attention_forward/pallas_call | solution.py:434
  17.3 4.7 %collective-permute-start.2 = (bf16[64,3072]{1,0:T(8,128)(2,1)S(1)}, bf16[64,3072]{1,0:T(8,128)(2,1)S(1)}, u32[]{:S(2)}, u32[]{:S(2)}) collective-permute-start(bf16[64,3072]{1,0:T(8,128)(2,1)S(1)} %get-tuple-element.22), channel_id=1, source_target_pairs={{0,20},{4,24},{8,28},{12,16},{16,4},{20,8},{24,12},{28,0},{1,21},{... | collective-permute-start | bytes 1179656 | tf_op jit(solution)/shard_map/ppermute | solution.py:665
  22.0 0.0 collective-permute-start.1
  22.0 0.0 collective-permute-done.3.other_ref
  22.0 0.0 copy-done
  22.0 7.2 %attention_backward.1 = (f32[1,1536]{1,0:T(1,128)S(1)}, f32[1,1536]{1,0:T(1,128)S(1)}, bf16[64,3072]{1,0:T(8,128)(2,1)S(1)}, bf16[64,3072]{1,0:T(8,128)(2,1)S(1)}) custom-call(bf16[64,3072]{1,0:T(8,128)(2,1)S(1)} %bitcast.7, bf16[64,3072]{1,0:T(8,128)(2,1)S(1)} %collective-permute-done.3.other_ref, bf16[1024,3072]{1,0:T(8,128)(2,1)S(1)} %get-tuple-element.23.out_weight_ref, ...), custom_call_target="tpu_custom_call" | custom-call | flops 3221225472 | bytes 25165824 | tf_op jit(solution)/shard_map/attention_backward/pallas_call | solution.py:599
  29.3 0.8 %collective-permute-start.4 = (bf16[64,3072]{1,0:T(8,128)(2,1)S(1)}, bf16[64,3072]{1,0:T(8,128)(2,1)S(1)}, u32[]{:S(2)}, u32[]{:S(2)}) collective-permute-start(bf16[64,3072]{1,0:T(8,128)(2,1)S(1)} %get-tuple-element.31), channel_id=1, source_target_pairs={{0,28},{4,16},{8,20},{12,24},{16,12},{20,0},{24,4},{28,8},{1,29},{... | collective-permute-start | bytes 1179656 | tf_op jit(solution)/shard_map/ppermute | solution.py:665
  30.1 0.0 collective-permute-start.5
  30.1 0.1 collective-permute-done.2
  30.2 0.8 %collective-permute-done.1 = bf16[64,3072]{1,0:T(8,128)(2,1)S(1)} collective-permute-done((bf16[64,3072]{1,0:T(8,128)(2,1)S(1)}, bf16[64,3072]{1,0:T(8,128)(2,1)S(1)}, u32[]{:S(2)}, u32[]{:S(2)}) %collective-permute-start.1) | collective-permute-done | bytes 393248 | tf_op jit(solution)/shard_map/ppermute | solution.py:665
  31.0 0.8 %add_convert_fusion = bf16[64,3072]{1,0:T(8,128)(2,1)} fusion(bf16[64,3072]{1,0:T(8,128)(2,1)S(1)} %collective-permute-done.2, bf16[64,3072]{1,0:T(8,128)(2,1)S(1)} %collective-permute-done.1), kind=kLoop, calls=%fused_computation | loop fusion | flops 786432 | bytes 1179648 | tf_op jit(solution)/shard_map/convert_element_type | solution.py:714
  31.8 0.4 collective-permute-start.6
  32.2 8.6 %collective-permute-done.4.sent_ref = bf16[64,3072]{1,0:T(8,128)(2,1)S(1)} collective-permute-done((bf16[64,3072]{1,0:T(8,128)(2,1)S(1)}, bf16[64,3072]{1,0:T(8,128)(2,1)S(1)}, u32[]{:S(2)}, u32[]{:S(2)}) %collective-permute-start.4) | collective-permute-done | bytes 393248 | tf_op jit(solution)/shard_map/ppermute | solution.py:665
  40.8 0.7 %collective-permute-done.5.kept_ref = bf16[64,3072]{1,0:T(8,128)(2,1)S(1)} collective-permute-done((bf16[64,3072]{1,0:T(8,128)(2,1)S(1)}, bf16[64,3072]{1,0:T(8,128)(2,1)S(1)}, u32[]{:S(2)}, u32[]{:S(2)}) %collective-permute-start.5) | collective-permute-done | bytes 393248 | tf_op jit(solution)/shard_map/ppermute | solution.py:665
  41.5 0.0 collective-permute-done.6.gate_sent_ref
  41.5 0.8 %sums.1 = (bf16[64,3072]{1,0:T(8,128)(2,1)}, f32[1,1536]{1,0:T(1,128)}) custom-call(bf16[64,3072]{1,0:T(8,128)(2,1)S(1)} %collective-permute-done.4.sent_ref, bf16[64,3072]{1,0:T(8,128)(2,1)S(1)} %collective-permute-done.5.kept_ref, f32[1,1536]{1,0:T(1,128)S(1)} %get-tuple-element.33.gate_kept_ref, f32[1,1536]{1,0:T(1,128)S(1)} %collective-permute-done.6.gate_sent_ref), custom_call_target="tpu_custom_call" | custom-call | tf_op jit(solution)/shard_map/sums/pallas_call | solution.py:645
  (1 shorter events, 0.0 us)
Async XLA Ops:
  0.6 11.2 %collective-permute-start = (bf16[64,3072]{1,0:T(8,128)(2,1)}, bf16[64,3072]{1,0:T(8,128)(2,1)S(1)}, u32[]{:S(2)}, u32[]{:S(2)}) collective-permute-start(bf16[64,3072]{1,0:T(8,128)(2,1)} %bitcast.8), channel_id=1, source_target_pairs={{0,16},{4,20},{8,24},{12,28},{16,0},{20,4},{24,8},{28,12},{1,17},{... | collective-permute-start | bytes 1179656 | tf_op jit(solution)/shard_map/ppermute | solution.py:665
  2.7 19.3 %collective-permute-start.3 = (bf16[64,3072]{1,0:T(8,128)(2,1)}, bf16[64,3072]{1,0:T(8,128)(2,1)S(1)}, u32[]{:S(2)}, u32[]{:S(2)}) collective-permute-start(bf16[64,3072]{1,0:T(8,128)(2,1)} %bitcast.6), channel_id=1, source_target_pairs={{0,16},{4,20},{8,24},{12,28},{16,0},{20,4},{24,8},{28,12},{1,17},{... | collective-permute-start | bytes 1179656 | tf_op jit(solution)/shard_map/ppermute | solution.py:665
  2.8 9.0 %copy-start.1 = (bf16[1,64,3072]{2,1,0:T(8,128)(2,1)S(1)}, bf16[1,64,3072]{2,1,0:T(8,128)(2,1)}, u32[]{:S(2)}) copy-start(bf16[1,64,3072]{2,1,0:T(8,128)(2,1)} %param.9) | copy-start | bytes 1179652
  2.8 9.0 %copy-start.2 = (f32[1,3072]{1,0:T(1,128)S(1)}, f32[1,3072]{1,0:T(1,128)}, u32[]{:S(2)}) copy-start(f32[1,3072]{1,0:T(1,128)} %gate_ref.3) | copy-start | bytes 36868
  2.8 9.0 %copy-start.3 = (f32[1,128]{1,0:T(1,128)S(1)}, f32[1,128]{1,0:T(1,128)}, u32[]{:S(2)}) copy-start(f32[1,128]{1,0:T(1,128)} %query_gain_ref.3) | copy-start | bytes 1540
  2.8 9.0 %copy-start.4 = (f32[1,128]{1,0:T(1,128)S(1)}, f32[1,128]{1,0:T(1,128)}, u32[]{:S(2)}) copy-start(f32[1,128]{1,0:T(1,128)} %key_gain_ref.3) | copy-start | bytes 1540
  2.8 9.0 %copy-start.5 = (s32[2,27]{1,0:T(2,128)S(1)}, s32[2,27]{1,0:T(2,128)}, u32[]{:S(2)}) copy-start(s32[2,27]{1,0:T(2,128)} %neighbours_ref.1) | copy-start | bytes 652
  2.8 9.0 %copy-start.6 = (s32[2]{0:T(128)S(1)}, s32[2]{0:T(128)}, u32[]{:S(2)}) copy-start(s32[2]{0:T(128)} %tile_slot_ref.1) | copy-start | bytes 28
  11.8 10.2 %copy-start = (bf16[1,64,3072]{2,1,0:T(8,128)(2,1)S(1)}, bf16[1,64,3072]{2,1,0:T(8,128)(2,1)}, u32[]{:S(2)}) copy-start(bf16[1,64,3072]{2,1,0:T(8,128)(2,1)} %param.10) | copy-start | bytes 1179652
  17.3 12.9 %collective-permute-start.2 = (bf16[64,3072]{1,0:T(8,128)(2,1)S(1)}, bf16[64,3072]{1,0:T(8,128)(2,1)S(1)}, u32[]{:S(2)}, u32[]{:S(2)}) collective-permute-start(bf16[64,3072]{1,0:T(8,128)(2,1)S(1)} %get-tuple-element.22), channel_id=1, source_target_pairs={{0,20},{4,24},{8,28},{12,16},{16,4},{20,8},{24,12},{28,0},{1,21},{... | collective-permute-start | bytes 1179656 | tf_op jit(solution)/shard_map/ppermute | solution.py:665
  22.0 8.9 %collective-permute-start.1 = (bf16[64,3072]{1,0:T(8,128)(2,1)S(1)}, bf16[64,3072]{1,0:T(8,128)(2,1)S(1)}, u32[]{:S(2)}, u32[]{:S(2)}) collective-permute-start(bf16[64,3072]{1,0:T(8,128)(2,1)S(1)} %get-tuple-element.21), channel_id=1, source_target_pairs={{0,4},{4,8},{8,12},{12,0},{16,20},{20,24},{24,28},{28,16},{1,5},{5... | collective-permute-start | bytes 1179656 | tf_op jit(solution)/shard_map/ppermute | solution.py:665
  29.3 11.5 %collective-permute-start.4 = (bf16[64,3072]{1,0:T(8,128)(2,1)S(1)}, bf16[64,3072]{1,0:T(8,128)(2,1)S(1)}, u32[]{:S(2)}, u32[]{:S(2)}) collective-permute-start(bf16[64,3072]{1,0:T(8,128)(2,1)S(1)} %get-tuple-element.31), channel_id=1, source_target_pairs={{0,28},{4,16},{8,20},{12,24},{16,12},{20,0},{24,4},{28,8},{1,29},{... | collective-permute-start | bytes 1179656 | tf_op jit(solution)/shard_map/ppermute | solution.py:665
  30.1 11.4 %collective-permute-start.5 = (bf16[64,3072]{1,0:T(8,128)(2,1)S(1)}, bf16[64,3072]{1,0:T(8,128)(2,1)S(1)}, u32[]{:S(2)}, u32[]{:S(2)}) collective-permute-start(bf16[64,3072]{1,0:T(8,128)(2,1)S(1)} %get-tuple-element.32), channel_id=1, source_target_pairs={{0,12},{4,0},{8,4},{12,8},{16,28},{20,16},{24,20},{28,24},{1,13},{... | collective-permute-start | bytes 1179656 | tf_op jit(solution)/shard_map/ppermute | solution.py:665
  31.8 9.7 %collective-permute-start.6 = (f32[1,1536]{1,0:T(1,128)S(1)}, f32[1,1536]{1,0:T(1,128)S(1)}, u32[]{:S(2)}, u32[]{:S(2)}) collective-permute-start(f32[1,1536]{1,0:T(1,128)S(1)} %get-tuple-element.34), channel_id=1, source_target_pairs={{0,16},{4,20},{8,24},{12,28},{16,0},{20,4},{24,8},{28,12},{1,17},{... | collective-permute-start | bytes 18440 | tf_op jit(solution)/shard_map/ppermute | solution.py:665

commit v20 on v16

--- a/solution.py
+++ b/solution.py
@@ -693,8 +693,8 @@
         key_gain,
         gate_scale,
     )
+    sent = routed(sent, 1, 1)
     kept = routed(kept, 0, 1)
-    sent = routed(sent, 1, 1)
     gate_kept, gate_sent, grad_kept, grad_sent = backward(
         upstream,
         other_upstream,
@@ -711,7 +711,7 @@
     )
     grad_sent = routed(grad_sent, 1, -1)
     grad_kept = routed(grad_kept, 0, -1)
-    segment_output = (kept.astype(F32) + sent.astype(F32)).astype(BF16)
+    segment_output = (sent.astype(F32) + kept.astype(F32)).astype(BF16)
     segment_output, gate_sent = lax.optimization_barrier((segment_output, gate_sent))
     gate_sent = routed(gate_sent, 1, 0)
     token_grad, gate_grad = sums(grad_sent, grad_kept, gate_kept, gate_sent)

time: 41.9 us -> 41.9 us (level)
  starting transfers between devices: 7.49 us -> 9.41 us
  waiting for transfers between devices: 10.2 us -> 8.31 us
    ppermute x7, starting transfers between devices: 7.49 us -> 9.41 us  [routed(): return lax.ppermute(block, ('seq', 'pipe'), route)]
    ppermute x7, waiting for transfers between devices: 10.2 us -> 8.31 us  [routed(): return lax.ppermute(block, ('seq', 'pipe'), route)]
where the time goes in v20:
time: 41.9 us; the launch traced here: 41.7 us
  Pallas kernels  22.4 us (53%)
  starting transfers between devices  9.41 us (22%)
  waiting for transfers between devices  8.31 us (20%)
  other arithmetic  0.84 us (2%)
  between operations  0.74 us (2%)
    pallas_call x1, Pallas kernels, regroup(): pl.pallas_call(regroup_kernel, out_shape=(pltpu.VMEM(out, weight.dtype),...  9.55 us
    ppermute x7, starting transfers between devices, routed(): return lax.ppermute(block, ('seq', 'pipe'), route)  9.41 us
    ppermute x7, waiting for transfers between devices, routed(): return lax.ppermute(block, ('seq', 'pipe'), route)  8.31 us
    pallas_call x1, Pallas kernels, backward(): pl.pallas_call(backward_kernel, out_shape=(jax.ShapeDtypeStruct((1, model...  6.58 us
    pallas_call x1, Pallas kernels, forward(): pl.pallas_call(forward_kernel, out_shape=(jax.ShapeDtypeStruct((groups, t...  5.38 us
    pallas_call x1, Pallas kernels, sums(): pl.pallas_call(sums_kernel, out_shape=(jax.ShapeDtypeStruct(kept.shape, B...  0.84 us
    convert_element_type x1, other arithmetic, pair_body(): segment_output = (sent.astype(F32) + kept.astype(F32)).astype(BF16)  0.84 us
  transfers between devices with their start and end apart: 7, of which 4 were waited for; matrix products, arithmetic and copies ran while one was open for 2% of the time, Pallas kernels for 52%

profile of v20, /device:TPU:1, one launch (start us, length us, event | category | flops | bytes accessed | tf_op | source)
XLA Modules:
  0.0 41.7 jit_solution(17268185869518036472)
XLA Ops:
  0.6 2.1 %collective-permute-start = (bf16[64,3072]{1,0:T(8,128)(2,1)}, bf16[64,3072]{1,0:T(8,128)(2,1)S(1)}, u32[]{:S(2)}, u32[]{:S(2)}) collective-permute-start(bf16[64,3072]{1,0:T(8,128)(2,1)} %bitcast.8), channel_id=1, source_target_pairs={{0,16},{4,20},{8,24},{12,28},{16,0},{20,4},{24,8},{28,12},{1,17},{... | collective-permute-start | bytes 1179656 | tf_op jit(solution)/shard_map/ppermute | solution.py:665
  2.7 0.1 collective-permute-start.3
  2.8 0.0 copy-start.1
  2.8 0.0 copy-start.2
  2.8 0.0 copy-start.3
  2.8 0.0 copy-start.5
  2.8 0.0 copy-start.6
  2.8 9.6 %regroup.1 = (bf16[2,3072,1536]{2,1,0:T(8,128)(2,1)S(1)}, bf16[2304,3072]{1,0:T(8,128)(2,1)S(1)}) custom-call(bf16[3072,8,384]{2,1,0:T(8,128)(2,1)} %bitcast.10), custom_call_target="tpu_custom_call" | custom-call | bytes 37748736 | tf_op jit(solution)/shard_map/regroup/pallas_call | solution.py:285
  12.4 0.0 collective-permute-done.other_ref
  12.4 0.0 copy-done.1
  12.4 0.0 copy-done.2
  12.4 0.0 copy-done.3
  12.5 0.0 copy-done.4
  12.5 0.0 copy-done.5
  12.5 0.0 copy-done.6
  12.5 0.0 copy-start
  12.5 5.4 %attention_forward.1 = (f32[2,128,1536]{2,1,0:T(8,128)S(1)}, f32[2,128,8]{2,1,0:T(8,128)S(1)}, bf16[8,128,128]{2,1,0:T(8,128)(2,1)S(1)}, f32[128,3072]{1,0:T(8,1...) custom-call(s32[2,27]{1,0:T(2,128)S(1)} %copy-done.5, ...), custom_call_target="tpu_custom_call" | custom-call | flops 3221225472 | bytes 25165824 | tf_op jit(solution)/shard_map/attention_forward/pallas_call | solution.py:434
  17.9 3.1 %collective-permute-start.2 = (bf16[64,3072]{1,0:T(8,128)(2,1)S(1)}, bf16[64,3072]{1,0:T(8,128)(2,1)S(1)}, u32[]{:S(2)}, u32[]{:S(2)}) collective-permute-start(bf16[64,3072]{1,0:T(8,128)(2,1)S(1)} %get-tuple-element.22), channel_id=1, source_target_pairs={{0,4},{4,8},{8,12},{12,0},{16,20},{20,24},{24,28},{28,16},{1,5},{5... | collective-permute-start | bytes 1179656 | tf_op jit(solution)/shard_map/ppermute | solution.py:665
  21.0 1.0 %collective-permute-start.1 = (bf16[64,3072]{1,0:T(8,128)(2,1)S(1)}, bf16[64,3072]{1,0:T(8,128)(2,1)S(1)}, u32[]{:S(2)}, u32[]{:S(2)}) collective-permute-start(bf16[64,3072]{1,0:T(8,128)(2,1)S(1)} %get-tuple-element.21), channel_id=1, source_target_pairs={{0,20},{4,24},{8,28},{12,16},{16,4},{20,8},{24,12},{28,0},{1,21},{... | collective-permute-start | bytes 1179656 | tf_op jit(solution)/shard_map/ppermute | solution.py:665
  22.0 0.0 collective-permute-done.3.other_ref
  22.0 0.0 copy-done
  22.0 6.6 %attention_backward.1 = (f32[1,1536]{1,0:T(1,128)S(1)}, f32[1,1536]{1,0:T(1,128)S(1)}, bf16[64,3072]{1,0:T(8,128)(2,1)S(1)}, bf16[64,3072]{1,0:T(8,128)(2,1)S(1)}) custom-call(bf16[64,3072]{1,0:T(8,128)(2,1)S(1)} %bitcast.7, bf16[64,3072]{1,0:T(8,128)(2,1)S(1)} %collective-permute-done.3.other_ref, bf16[1024,3072]{1,0:T(8,128)(2,1)S(1)} %get-tuple-element.23.out_weight_ref, ...), custom_call_target="tpu_custom_call" | custom-call | flops 3221225472 | bytes 25165824 | tf_op jit(solution)/shard_map/attention_backward/pallas_call | solution.py:599
  28.6 0.8 %collective-permute-start.4 = (bf16[64,3072]{1,0:T(8,128)(2,1)S(1)}, bf16[64,3072]{1,0:T(8,128)(2,1)S(1)}, u32[]{:S(2)}, u32[]{:S(2)}) collective-permute-start(bf16[64,3072]{1,0:T(8,128)(2,1)S(1)} %get-tuple-element.31), channel_id=1, source_target_pairs={{0,28},{4,16},{8,20},{12,24},{16,12},{20,0},{24,4},{28,8},{1,29},{... | collective-permute-start | bytes 1179656 | tf_op jit(solution)/shard_map/ppermute | solution.py:665
  29.4 0.0 collective-permute-start.5
  29.4 0.2 collective-permute-done.2
  29.6 2.0 %collective-permute-done.1 = bf16[64,3072]{1,0:T(8,128)(2,1)S(1)} collective-permute-done((bf16[64,3072]{1,0:T(8,128)(2,1)S(1)}, bf16[64,3072]{1,0:T(8,128)(2,1)S(1)}, u32[]{:S(2)}, u32[]{:S(2)}) %collective-permute-start.1) | collective-permute-done | bytes 393248 | tf_op jit(solution)/shard_map/ppermute | solution.py:665
  31.6 0.8 %add_convert_fusion = bf16[64,3072]{1,0:T(8,128)(2,1)} fusion(bf16[64,3072]{1,0:T(8,128)(2,1)S(1)} %collective-permute-done.2, bf16[64,3072]{1,0:T(8,128)(2,1)S(1)} %collective-permute-done.1), kind=kLoop, calls=%fused_computation | loop fusion | flops 786432 | bytes 1179648 | tf_op jit(solution)/shard_map/convert_element_type | solution.py:714
  32.5 2.3 %collective-permute-start.6 = (f32[1,1536]{1,0:T(1,128)S(1)}, f32[1,1536]{1,0:T(1,128)S(1)}, u32[]{:S(2)}, u32[]{:S(2)}) collective-permute-start(f32[1,1536]{1,0:T(1,128)S(1)} %get-tuple-element.34), channel_id=1, source_target_pairs={{0,16},{4,20},{8,24},{12,28},{16,0},{20,4},{24,8},{28,12},{1,17},{... | collective-permute-start | bytes 18440 | tf_op jit(solution)/shard_map/ppermute | solution.py:665
  34.8 5.4 %collective-permute-done.4.sent_ref = bf16[64,3072]{1,0:T(8,128)(2,1)S(1)} collective-permute-done((bf16[64,3072]{1,0:T(8,128)(2,1)S(1)}, bf16[64,3072]{1,0:T(8,128)(2,1)S(1)}, u32[]{:S(2)}, u32[]{:S(2)}) %collective-permute-start.4) | collective-permute-done | bytes 393248 | tf_op jit(solution)/shard_map/ppermute | solution.py:665
  40.1 0.7 %collective-permute-done.5.kept_ref = bf16[64,3072]{1,0:T(8,128)(2,1)S(1)} collective-permute-done((bf16[64,3072]{1,0:T(8,128)(2,1)S(1)}, bf16[64,3072]{1,0:T(8,128)(2,1)S(1)}, u32[]{:S(2)}, u32[]{:S(2)}) %collective-permute-start.5) | collective-permute-done | bytes 393248 | tf_op jit(solution)/shard_map/ppermute | solution.py:665
  40.9 0.0 collective-permute-done.6.gate_sent_ref
  40.9 0.8 %sums.1 = (bf16[64,3072]{1,0:T(8,128)(2,1)}, f32[1,1536]{1,0:T(1,128)}) custom-call(bf16[64,3072]{1,0:T(8,128)(2,1)S(1)} %collective-permute-done.4.sent_ref, bf16[64,3072]{1,0:T(8,128)(2,1)S(1)} %collective-permute-done.5.kept_ref, f32[1,1536]{1,0:T(1,128)S(1)} %get-tuple-element.33.gate_kept_ref, f32[1,1536]{1,0:T(1,128)S(1)} %collective-permute-done.6.gate_sent_ref), custom_call_target="tpu_custom_call" | custom-call | tf_op jit(solution)/shard_map/sums/pallas_call | solution.py:645
  (1 shorter events, 0.0 us)
Async XLA Ops:
  0.6 11.8 %collective-permute-start = (bf16[64,3072]{1,0:T(8,128)(2,1)}, bf16[64,3072]{1,0:T(8,128)(2,1)S(1)}, u32[]{:S(2)}, u32[]{:S(2)}) collective-permute-start(bf16[64,3072]{1,0:T(8,128)(2,1)} %bitcast.8), channel_id=1, source_target_pairs={{0,16},{4,20},{8,24},{12,28},{16,0},{20,4},{24,8},{28,12},{1,17},{... | collective-permute-start | bytes 1179656 | tf_op jit(solution)/shard_map/ppermute | solution.py:665
  2.7 19.3 %collective-permute-start.3 = (bf16[64,3072]{1,0:T(8,128)(2,1)}, bf16[64,3072]{1,0:T(8,128)(2,1)S(1)}, u32[]{:S(2)}, u32[]{:S(2)}) collective-permute-start(bf16[64,3072]{1,0:T(8,128)(2,1)} %bitcast.6), channel_id=1, source_target_pairs={{0,16},{4,20},{8,24},{12,28},{16,0},{20,4},{24,8},{28,12},{1,17},{... | collective-permute-start | bytes 1179656 | tf_op jit(solution)/shard_map/ppermute | solution.py:665
  2.8 9.6 %copy-start.1 = (bf16[1,64,3072]{2,1,0:T(8,128)(2,1)S(1)}, bf16[1,64,3072]{2,1,0:T(8,128)(2,1)}, u32[]{:S(2)}) copy-start(bf16[1,64,3072]{2,1,0:T(8,128)(2,1)} %param.9) | copy-start | bytes 1179652
  2.8 9.6 %copy-start.2 = (f32[1,3072]{1,0:T(1,128)S(1)}, f32[1,3072]{1,0:T(1,128)}, u32[]{:S(2)}) copy-start(f32[1,3072]{1,0:T(1,128)} %gate_ref.3) | copy-start | bytes 36868
  2.8 9.6 %copy-start.3 = (f32[1,128]{1,0:T(1,128)S(1)}, f32[1,128]{1,0:T(1,128)}, u32[]{:S(2)}) copy-start(f32[1,128]{1,0:T(1,128)} %query_gain_ref.3) | copy-start | bytes 1540
  2.8 9.6 %copy-start.4 = (f32[1,128]{1,0:T(1,128)S(1)}, f32[1,128]{1,0:T(1,128)}, u32[]{:S(2)}) copy-start(f32[1,128]{1,0:T(1,128)} %key_gain_ref.3) | copy-start | bytes 1540
  2.8 9.6 %copy-start.5 = (s32[2,27]{1,0:T(2,128)S(1)}, s32[2,27]{1,0:T(2,128)}, u32[]{:S(2)}) copy-start(s32[2,27]{1,0:T(2,128)} %neighbours_ref.1) | copy-start | bytes 652
  2.8 9.6 %copy-start.6 = (s32[2]{0:T(128)S(1)}, s32[2]{0:T(128)}, u32[]{:S(2)}) copy-start(s32[2]{0:T(128)} %tile_slot_ref.1) | copy-start | bytes 28
  12.5 9.5 %copy-start = (bf16[1,64,3072]{2,1,0:T(8,128)(2,1)S(1)}, bf16[1,64,3072]{2,1,0:T(8,128)(2,1)}, u32[]{:S(2)}) copy-start(bf16[1,64,3072]{2,1,0:T(8,128)(2,1)} %param.10) | copy-start | bytes 1179652
  17.9 11.7 %collective-permute-start.2 = (bf16[64,3072]{1,0:T(8,128)(2,1)S(1)}, bf16[64,3072]{1,0:T(8,128)(2,1)S(1)}, u32[]{:S(2)}, u32[]{:S(2)}) collective-permute-start(bf16[64,3072]{1,0:T(8,128)(2,1)S(1)} %get-tuple-element.22), channel_id=1, source_target_pairs={{0,4},{4,8},{8,12},{12,0},{16,20},{20,24},{24,28},{28,16},{1,5},{5... | collective-permute-start | bytes 1179656 | tf_op jit(solution)/shard_map/ppermute | solution.py:665
  21.0 10.6 %collective-permute-start.1 = (bf16[64,3072]{1,0:T(8,128)(2,1)S(1)}, bf16[64,3072]{1,0:T(8,128)(2,1)S(1)}, u32[]{:S(2)}, u32[]{:S(2)}) collective-permute-start(bf16[64,3072]{1,0:T(8,128)(2,1)S(1)} %get-tuple-element.21), channel_id=1, source_target_pairs={{0,20},{4,24},{8,28},{12,16},{16,4},{20,8},{24,12},{28,0},{1,21},{... | collective-permute-start | bytes 1179656 | tf_op jit(solution)/shard_map/ppermute | solution.py:665
  28.6 11.5 %collective-permute-start.4 = (bf16[64,3072]{1,0:T(8,128)(2,1)S(1)}, bf16[64,3072]{1,0:T(8,128)(2,1)S(1)}, u32[]{:S(2)}, u32[]{:S(2)}) collective-permute-start(bf16[64,3072]{1,0:T(8,128)(2,1)S(1)} %get-tuple-element.31), channel_id=1, source_target_pairs={{0,28},{4,16},{8,20},{12,24},{16,12},{20,0},{24,4},{28,8},{1,29},{... | collective-permute-start | bytes 1179656 | tf_op jit(solution)/shard_map/ppermute | solution.py:665
  29.4 11.4 %collective-permute-start.5 = (bf16[64,3072]{1,0:T(8,128)(2,1)S(1)}, bf16[64,3072]{1,0:T(8,128)(2,1)S(1)}, u32[]{:S(2)}, u32[]{:S(2)}) collective-permute-start(bf16[64,3072]{1,0:T(8,128)(2,1)S(1)} %get-tuple-element.32), channel_id=1, source_target_pairs={{0,12},{4,0},{8,4},{12,8},{16,28},{20,16},{24,20},{28,24},{1,13},{... | collective-permute-start | bytes 1179656 | tf_op jit(solution)/shard_map/ppermute | solution.py:665
  32.5 8.4 %collective-permute-start.6 = (f32[1,1536]{1,0:T(1,128)S(1)}, f32[1,1536]{1,0:T(1,128)S(1)}, u32[]{:S(2)}, u32[]{:S(2)}) collective-permute-start(f32[1,1536]{1,0:T(1,128)S(1)} %get-tuple-element.34), channel_id=1, source_target_pairs={{0,16},{4,20},{8,24},{12,28},{16,0},{20,4},{24,8},{28,12},{1,17},{... | collective-permute-start | bytes 18440 | tf_op jit(solution)/shard_map/ppermute | solution.py:665
